TPU v7x, 32 devices: a whole 2x2x4 slice. The times are simulated.
32 devices in a mesh: fsdp: 16 (over z, y, x), row: 2 (over core).
Axes of the slice: x: 2, y: 2, z: 4, core: 2. Of those that a mesh axis runs over, the one named last changes fastest.
Arguments:
- tokens: bfloat16 [32768, 768], P(('fsdp', 'row')), may hold values from -6 to 6
- cotangent: bfloat16 [32768, 768], P(('fsdp', 'row')), may hold values from -6 to 6
- counts: int32 [32, 2], P(('fsdp', 'row')), may hold values from 0 to 1, as said below
- lengths: int32 [64], P(('fsdp', 'row')), may hold values from 128 to 512, as said below
- w_qkv: float32 [768, 2304], P('fsdp', 'row'), may hold values from -0.21875 to 0.21875
- w_out: float32 [768, 768], P('fsdp', 'row'), may hold values from -1.25 to 1.25
- w_up: float32 [768, 3072], P('fsdp', 'row'), may hold values from -0.21875 to 0.21875
- w_down: float32 [768, 3072], P('fsdp', 'row'), may hold values from -0.109375 to 0.109375
- vectors: float32 [12, 768], P('row', 'fsdp'), may hold values from -1.2 to 1.3
- mom_qkv: float32 [768, 2304], P('fsdp', 'row'), may hold values from -256 to 256
- mom_out: float32 [768, 768], P('fsdp', 'row'), may hold values from -64 to 64
- mom_up: float32 [768, 3072], P('fsdp', 'row'), may hold values from -128 to 128
- mom_down: float32 [768, 3072], P('fsdp', 'row'), may hold values from -256 to 256
- adam_first: float32 [12, 768], P('row', 'fsdp'), may hold values from -182.82953 to 182.82953
- adam_second: float32 [12, 768], P('row', 'fsdp'), may hold values from 6.5536 to 27852.8
Outputs:
- layer_out: bfloat16 [32768, 768], P(('fsdp', 'row'))
- input_grad: float32 [32768, 768], P(('fsdp', 'row'))
- grad_qkv: float32 [768, 2304], P('fsdp', 'row')
- grad_out: float32 [768, 768], P('fsdp', 'row')
- grad_up: float32 [768, 3072], P('fsdp', 'row')
- grad_down: float32 [768, 3072], P('fsdp', 'row')
- grad_vectors: float32 [12, 768], P('row', 'fsdp')
- moment_qkv: float32 [768, 2304], P('fsdp', 'row')
- moment_out: float32 [768, 768], P('fsdp', 'row')
- moment_up: float32 [768, 3072], P('fsdp', 'row')
- moment_down: float32 [768, 3072], P('fsdp', 'row')
- weight_qkv: float32 [768, 2304], P('fsdp', 'row')
- weight_out: float32 [768, 768], P('fsdp', 'row')
- weight_up: float32 [768, 3072], P('fsdp', 'row')
- weight_down: float32 [768, 3072], P('fsdp', 'row')
- first_moment: float32 [12, 768], P('row', 'fsdp')
- second_moment: float32 [12, 768], P('row', 'fsdp')
- new_vectors: float32 [12, 768], P('row', 'fsdp')
Inputs may be any that keep to these rules, and one draw needn't show every extreme that they name: `counts`: some micro-batch of some group is full. `lengths`: some slot is not padded.
All inputs are finite; a program needn't handle non-finite values.
Results may differ from a plain program's by a relative error of at most 0.013.
The roundings to bfloat16 on the way count: a program that leaves them out, or rounds other values in their place, can miss the bound.
Values may be sent and summed in bfloat16 or wider, within the bound.
No kernel may reach another device: no remote copies, remote signals or barrier semaphores. Data moves between devices by JAX's collectives and lax.ppermute only.
A program may use at most 256 MiB of HBM per device.

v0:
```python
import math

import jax
import jax.numpy as jnp
from jax import lax
from jax.sharding import PartitionSpec as P

D = 768
FF = 3072
HEADS = 12
HEAD_DIM = 64
SEQ = 512
CAP = 1
MICRO = 2
NS_ITERS = 5
STEP = 10


norm_eps = 1e-05
mask_fill = -1e30
poly_first = 3.4445
poly_second = -4.775
poly_third = 2.0315
muon_rate = 0.2
adam_rate = 0.8
decay_rate = 0.01
moment_decay = 0.5
beta_first = 0.9
beta_second = 0.98
adam_eps = 1e-06


def matmul(former, latter):
    return jnp.dot(former, latter, preferred_element_type=jnp.float32)


def matmul_tn(former, latter):
    return lax.dot_general(
        former, latter, (((0,), (0,)), ((), ())), preferred_element_type=jnp.float32
    )


def matmul_nt(former, latter):
    return lax.dot_general(
        former, latter, (((1,), (1,)), ((), ())), preferred_element_type=jnp.float32
    )


def exact_dot(former, latter):
    return jnp.dot(
        former, latter, precision=lax.Precision.HIGHEST, preferred_element_type=jnp.float32
    )


def exact_dot_nt(former, latter):
    return lax.dot_general(
        former,
        latter,
        (((1,), (1,)), ((), ())),
        precision=lax.Precision.HIGHEST,
        preferred_element_type=jnp.float32,
    )


def norm_rows(values, scaling, offset):
    center = values - jnp.mean(values, axis=-1, keepdims=True)
    spread = jnp.mean(center * center, axis=-1, keepdims=True)
    return center * lax.rsqrt(spread + norm_eps) * scaling + offset


def exact_gelu(values):
    return jax.nn.gelu(values, approximate=False)


def unpack_vectors(vector_rows):
    up_rows = FF // D
    floats = vector_rows.astype(jnp.float32)
    return (
        floats[0],
        floats[1],
        floats[2],
        floats[3],
        floats[4],
        floats[5 : 5 + up_rows].reshape(FF),
        floats[5 + up_rows],
        floats[6 + up_rows],
        floats[7 + up_rows],
    )


def score_block(query_heads, key_heads, key_valid):
    raw_scores = jnp.einsum(
        "cqhd,ckhd->chqk", query_heads, key_heads, preferred_element_type=jnp.float32
    ) / math.sqrt(HEAD_DIM)
    return jnp.where(key_valid[:, None, None, :], raw_scores, mask_fill)


def gather_weights(w_qkv, w_out, w_up, w_down, vectors):
    halves = (
        lax.all_gather(w_qkv.astype(jnp.bfloat16), "row", axis=1, tiled=True),
        lax.all_gather(w_out.astype(jnp.bfloat16), "row", axis=1, tiled=True),
        lax.all_gather(w_up.astype(jnp.bfloat16), "row", axis=1, tiled=True),
        lax.all_gather(w_down.astype(jnp.bfloat16), "row", axis=1, tiled=True),
        lax.all_gather(vectors.astype(jnp.bfloat16), "row", axis=0, tiled=True),
    )
    return (
        lax.all_gather(halves[0], "fsdp", axis=0, tiled=True),
        lax.all_gather(halves[1], "fsdp", axis=0, tiled=True),
        lax.all_gather(halves[2], "fsdp", axis=0, tiled=True),
        lax.all_gather(halves[3], "fsdp", axis=0, tiled=True),
        lax.all_gather(halves[4], "fsdp", axis=1, tiled=True),
    )


def reduce_grads(grad_parts):
    row_sums = (
        lax.psum_scatter(grad_parts[0], "fsdp", scatter_dimension=0, tiled=True),
        lax.psum_scatter(grad_parts[1], "fsdp", scatter_dimension=0, tiled=True),
        lax.psum_scatter(grad_parts[2], "fsdp", scatter_dimension=0, tiled=True),
        lax.psum_scatter(grad_parts[3], "fsdp", scatter_dimension=0, tiled=True),
        lax.psum_scatter(grad_parts[4], "fsdp", scatter_dimension=1, tiled=True),
    )
    return (
        lax.psum_scatter(row_sums[0], "row", scatter_dimension=1, tiled=True),
        lax.psum_scatter(row_sums[1], "row", scatter_dimension=1, tiled=True),
        lax.psum_scatter(row_sums[2], "row", scatter_dimension=1, tiled=True),
        lax.psum_scatter(row_sums[3], "row", scatter_dimension=1, tiled=True),
        lax.psum_scatter(row_sums[4], "row", scatter_dimension=0, tiled=True),
    )


def micro_step(rows_in, cot_rows, live_slots, seq_lengths, forward_set, backward_set):
    qkv_weight, out_weight, up_weight, down_weight, vector_rows = forward_set
    (
        bias_query,
        bias_value,
        bias_out,
        gain_attn,
        shift_attn,
        bias_up,
        bias_down,
        gain_ffn,
        shift_ffn,
    ) = unpack_vectors(vector_rows)
    micro_rows = rows_in.shape[0]
    head_shape = (CAP, SEQ, HEADS, HEAD_DIM)
    key_valid = jnp.arange(SEQ)[None, :] < seq_lengths[:, None]
    projected = matmul(rows_in, qkv_weight)
    query_heads = (projected[:, :D] + bias_query).astype(jnp.bfloat16).reshape(head_shape)
    key_heads = projected[:, D : 2 * D].astype(jnp.bfloat16).reshape(head_shape)
    value_heads = (projected[:, 2 * D :] + bias_value).astype(jnp.bfloat16).reshape(head_shape)
    scores = score_block(query_heads, key_heads, key_valid)
    top_score = jnp.max(scores, axis=-1, keepdims=True)
    exp_scores = jnp.exp(scores - top_score)
    row_total = jnp.sum(exp_scores, axis=-1, keepdims=True)
    log_total = top_score + jnp.log(row_total)
    prob_low = (exp_scores / row_total).astype(jnp.bfloat16)
    context = jnp.einsum(
        "chqk,ckhd->cqhd", prob_low, value_heads, preferred_element_type=jnp.float32
    )
    context_low = context.reshape(micro_rows, D).astype(jnp.bfloat16)
    attended = matmul(context_low, out_weight) + bias_out
    resid_one = rows_in.astype(jnp.float32) + attended
    hidden, pull_one = jax.vjp(norm_rows, resid_one, gain_attn, shift_attn)
    hidden_low = hidden.astype(jnp.bfloat16)
    pre_act = matmul(hidden_low, up_weight) + bias_up
    activated, pull_gelu = jax.vjp(exact_gelu, pre_act)
    act_low = activated.astype(jnp.bfloat16)
    branch = matmul_nt(act_low, down_weight) + bias_down
    layer_rows, pull_two = jax.vjp(norm_rows, hidden + branch, gain_ffn, shift_ffn)
    qkv_weight, out_weight, up_weight, down_weight, vector_rows = backward_set
    valid_rows = (live_slots[:, None] & key_valid).reshape(micro_rows)
    masked = cot_rows.astype(jnp.float32) * valid_rows[:, None].astype(jnp.float32)
    top_grad, gain_two, shift_two = pull_two(masked)
    branch_low = top_grad.astype(jnp.bfloat16)
    down_bias = jnp.sum(branch_low, axis=0, dtype=jnp.float32)
    down_grad = matmul_tn(branch_low, act_low)
    act_grad = matmul(branch_low, down_weight)
    pre_low = pull_gelu(act_grad)[0].astype(jnp.bfloat16)
    up_bias = jnp.sum(pre_low, axis=0, dtype=jnp.float32)
    up_grad = matmul_tn(hidden_low, pre_low)
    hidden_grad = top_grad + matmul_nt(pre_low, up_weight)
    skip_grad, gain_one, shift_one = pull_one(hidden_grad)
    attn_low = skip_grad.astype(jnp.bfloat16)
    out_bias = jnp.sum(attn_low, axis=0, dtype=jnp.float32)
    out_grad = matmul_tn(context_low, attn_low)
    context_grad = matmul_nt(attn_low, out_weight).astype(jnp.bfloat16).reshape(head_shape)
    scores = score_block(query_heads, key_heads, key_valid)
    attn_probs = jnp.exp(scores - log_total)
    prob_grad = jnp.einsum(
        "cqhd,ckhd->chqk", context_grad, value_heads, preferred_element_type=jnp.float32
    )
    value_grad = jnp.einsum(
        "chqk,cqhd->ckhd",
        attn_probs.astype(jnp.bfloat16),
        context_grad,
        preferred_element_type=jnp.float32,
    ).astype(jnp.bfloat16)
    row_dot = jnp.sum(attn_probs * prob_grad, axis=-1, keepdims=True)
    score_grad = (attn_probs * (prob_grad - row_dot)).astype(jnp.bfloat16)
    query_grad = (
        jnp.einsum("chqk,ckhd->cqhd", score_grad, key_heads, preferred_element_type=jnp.float32)
        / math.sqrt(HEAD_DIM)
    ).astype(jnp.bfloat16)
    key_grad = (
        jnp.einsum("chqk,cqhd->ckhd", score_grad, query_heads, preferred_element_type=jnp.float32)
        / math.sqrt(HEAD_DIM)
    ).astype(jnp.bfloat16)
    qkv_low = jnp.concatenate(
        [
            query_grad.reshape(micro_rows, D),
            key_grad.reshape(micro_rows, D),
            value_grad.reshape(micro_rows, D),
        ],
        axis=1,
    )
    column_sums = jnp.sum(qkv_low, axis=0, dtype=jnp.float32)
    qkv_grad = matmul_tn(rows_in, qkv_low)
    input_grad = skip_grad + matmul_nt(qkv_low, qkv_weight)
    vector_grad = jnp.concatenate(
        [
            jnp.stack([column_sums[:D], column_sums[2 * D :], out_bias, gain_one, shift_one]),
            up_bias.reshape(FF // D, D),
            jnp.stack([down_bias, gain_two, shift_two]),
        ],
        axis=0,
    )
    return (
        layer_rows.astype(jnp.bfloat16),
        input_grad,
        (qkv_grad, out_grad, up_grad, down_grad, vector_grad),
    )


def per_device(
    tokens,
    cotangent,
    counts,
    lengths,
    w_qkv,
    w_out,
    w_up,
    w_down,
    vectors,
    mom_qkv,
    mom_out,
    mom_up,
    mom_down,
    adam_first,
    adam_second,
):
    micro_rows = CAP * SEQ
    layer_parts = []
    input_parts = []
    totals = None
    for micro_index in range(MICRO):
        first_row = micro_index * micro_rows
        rows_in = tokens[first_row : first_row + micro_rows]
        cot_rows = cotangent[first_row : first_row + micro_rows]
        seq_lengths = lengths[micro_index * CAP : (micro_index + 1) * CAP]
        live_slots = jnp.arange(CAP) < counts[0, micro_index]
        forward_set = gather_weights(w_qkv, w_out, w_up, w_down, vectors)
        backward_set = gather_weights(w_qkv, w_out, w_up, w_down, vectors)
        layer_rows, grad_rows, grad_parts = micro_step(
            rows_in, cot_rows, live_slots, seq_lengths, forward_set, backward_set
        )
        layer_parts.append(layer_rows)
        input_parts.append(grad_rows)
        totals = grad_parts if totals is None else jax.tree.map(jnp.add, totals, grad_parts)
    totals = reduce_grads(totals)
    grad_qkv, grad_out, grad_up, grad_down, grad_vectors = totals
    moments = (
        moment_decay * mom_qkv + grad_qkv,
        moment_decay * mom_out + grad_out,
        moment_decay * mom_up + grad_up,
        moment_decay * mom_down + grad_down,
    )
    iterate = moments
    for sweep_index in range(NS_ITERS):
        full_cols = (
            lax.all_gather(iterate[0], "fsdp", axis=0, tiled=True),
            lax.all_gather(iterate[1], "fsdp", axis=0, tiled=True),
            lax.all_gather(iterate[2], "fsdp", axis=0, tiled=True),
            lax.all_gather(iterate[3], "fsdp", axis=0, tiled=True),
        )
        partial_value = tuple(
            (exact_dot_nt(own_rows, col_block) for own_rows, col_block in zip(iterate, full_cols))
        )
        gram_part = lax.psum(
            (partial_value[0], partial_value[1], partial_value[2], partial_value[3]), "row"
        )
        gram_full = (
            lax.all_gather(gram_part[0], "fsdp", axis=0, tiled=True),
            lax.all_gather(gram_part[1], "fsdp", axis=0, tiled=True),
            lax.all_gather(gram_part[2], "fsdp", axis=0, tiled=True),
            lax.all_gather(gram_part[3], "fsdp", axis=0, tiled=True),
        )
        if sweep_index == 0:
            scales = tuple((jnp.sqrt(jnp.trace(whole)) + 1e-07 for whole in gram_full))
            iterate = tuple((member / scale for member, scale in zip(iterate, scales)))
            full_cols = tuple((member / scale for member, scale in zip(full_cols, scales)))
            gram_part = tuple(
                (member / (scale * scale) for member, scale in zip(gram_part, scales))
            )
            gram_full = tuple(
                (member / (scale * scale) for member, scale in zip(gram_full, scales))
            )
        iterate = tuple(
            (
                poly_first * current
                + exact_dot(
                    poly_second * gram_rows + poly_third * exact_dot(gram_rows, gram_whole),
                    col_block,
                )
                for current, gram_rows, gram_whole, col_block in zip(
                    iterate, gram_part, gram_full, full_cols
                )
            )
        )
    masters = (w_qkv, w_out, w_up, w_down)
    columns = (3 * D, D, FF, FF)
    updated = tuple(
        (
            master * (1.0 - muon_rate * decay_rate)
            - muon_rate * 0.2 * math.sqrt(count) * ortho_rows
            for master, count, ortho_rows in zip(masters, columns, iterate)
        )
    )
    first_moment = beta_first * adam_first + (1.0 - beta_first) * grad_vectors
    second_moment = beta_second * adam_second + (1.0 - beta_second) * grad_vectors * grad_vectors
    direction = (
        first_moment
        / (1.0 - beta_first**STEP)
        / (jnp.sqrt(second_moment / (1.0 - beta_second**STEP)) + adam_eps)
    )
    new_vectors = vectors - adam_rate * (direction + decay_rate * vectors)
    return (
        jnp.concatenate(layer_parts, axis=0),
        jnp.concatenate(input_parts, axis=0),
        grad_qkv,
        grad_out,
        grad_up,
        grad_down,
        grad_vectors,
        moments[0],
        moments[1],
        moments[2],
        moments[3],
        updated[0],
        updated[1],
        updated[2],
        updated[3],
        first_moment,
        second_moment,
        new_vectors,
    )


def solution(mesh):
    return jax.shard_map(
        per_device,
        mesh=mesh,
        in_specs=(
            P(("fsdp", "row"), None),
            P(("fsdp", "row"), None),
            P(("fsdp", "row"), None),
            P(("fsdp", "row")),
            P("fsdp", "row"),
            P("fsdp", "row"),
            P("fsdp", "row"),
            P("fsdp", "row"),
            P("row", "fsdp"),
            P("fsdp", "row"),
            P("fsdp", "row"),
            P("fsdp", "row"),
            P("fsdp", "row"),
            P("row", "fsdp"),
            P("row", "fsdp"),
        ),
        out_specs=(
            P(("fsdp", "row"), None),
            P(("fsdp", "row"), None),
            P("fsdp", "row"),
            P("fsdp", "row"),
            P("fsdp", "row"),
            P("fsdp", "row"),
            P("row", "fsdp"),
            P("fsdp", "row"),
            P("fsdp", "row"),
            P("fsdp", "row"),
            P("fsdp", "row"),
            P("fsdp", "row"),
            P("fsdp", "row"),
            P("fsdp", "row"),
            P("fsdp", "row"),
            P("row", "fsdp"),
            P("row", "fsdp"),
            P("row", "fsdp"),
        ),
        check_vma=False,
    )
```

profile of v0, /device:TPU:0, one launch (start us, length us, event | category | flops | bytes accessed | tf_op | source)
XLA Modules:
  0.0 4122.5 jit_solution(15943063162518068400)
XLA Ops:
  21.9 42.8 %all-gather.1 = bf16[16,48,12]{1,2,0:T(8,128)(2,1)S(1)} all-gather(bf16[1,48,12]{1,2,0:T(8,128)(2,1)S(1)} %bitcast.282), channel_id=1, replica_groups=mesh['fsdp'=16,'row'=2] {'fsdp'}, dimensions={0}, use_global_device_ids=true | all-gather | bytes 19584 | tf_op jit(solution)/shard_map/all_gather | solution.py:111
  71.7 13.4 all-gather.47.cloned.1.call-done
  105.3 37.3 all-gather.49.cloned.1.call-done
  161.5 63.1 %all-gather.51.cloned.1.call-done = bf16[768,3072]{1,0:T(8,128)(2,1)} async-done(((bf16[48,3072]{1,0:T(8,128)(2,1)}), bf16[768,3072]{1,0:T(8,128)(2,1)}) %all-gather.51.cloned.1.call-update) | async-done | bytes 4718608 | tf_op jit(solution)/shard_map/all_gather | solution.py:109
  232.0 35.2 multiply_convert_fusion.3
  267.2 39.2 all-gather.53.cloned.1.call-done
  325.9 16.5 convert_reduce_fusion.1
  364.0 10.6 multiply_reduce_fusion.1
  406.8 11.0 multiply_reduce_fusion
  439.7 8.1 copy.138
  471.4 51.3 %reduce-scatter.16.cloned.1.call-done = f32[48,768]{1,0:T(8,128)} async-done(((f32[768,768]{1,0:T(8,128)}), f32[48,768]{1,0:T(8,128)}) %reduce-scatter.16.cloned.1.call-update) | async-done | bytes 147472 | tf_op jit(solution)/shard_map/reduce_scatter | solution.py:118
  522.8 156.3 %reduce-scatter.28.cloned.1.call-done = f32[48,2304]{1,0:T(8,128)} async-done(((f32[768,2304]{1,0:T(8,128)}), f32[48,2304]{1,0:T(8,128)}) %reduce-scatter.28.cloned.1.call-update) | async-done | bytes 442384 | tf_op jit(solution)/shard_map/reduce_scatter | solution.py:117
  679.2 176.6 %reduce-scatter.24.cloned.1.call-done = f32[48,3072]{1,0:T(8,128)} async-done(((f32[768,3072]{1,0:T(8,128)}), f32[48,3072]{1,0:T(8,128)}) %reduce-scatter.24.cloned.1.call-update) | async-done | bytes 589840 | tf_op jit(solution)/shard_map/reduce_scatter | solution.py:120
  856.0 175.4 %reduce-scatter.20.cloned.1.call-done = f32[48,3072]{1,0:T(8,128)} async-done(((f32[768,3072]{1,0:T(8,128)}), f32[48,3072]{1,0:T(8,128)}) %reduce-scatter.20.cloned.1.call-update) | async-done | bytes 589840 | tf_op jit(solution)/shard_map/reduce_scatter | solution.py:119
  1031.4 9.3 reduce-scatter.18.cloned.1.call-done
  1042.3 10.2 reduce-scatter.14.cloned.1.call-done
  1054.2 10.3 reduce-scatter.26.cloned.1.call-done
  1066.3 10.2 reduce-scatter.22.cloned.1.call-done
  1078.5 58.7 %all-gather.75.cloned.1.call-done = f32[768,384]{1,0:T(8,128)} async-done(((f32[48,384]{1,0:T(8,128)}), f32[768,384]{1,0:T(8,128)}) %all-gather.75.cloned.1.call-update) | async-done | bytes 1179664 | tf_op jit(solution)/shard_map/all_gather | solution.py:282
  1140.4 70.2 %all-gather.55.cloned.1.call-done = f32[768,1152]{1,0:T(8,128)} async-done(((f32[48,1152]{1,0:T(8,128)}), f32[768,1152]{1,0:T(8,128)}) %all-gather.55.cloned.1.call-update) | async-done | bytes 3538960 | tf_op jit(solution)/shard_map/all_gather | solution.py:281
  1216.6 76.2 %all-gather.115.cloned.1.call-done = f32[768,1536]{1,0:T(8,128)} async-done(((f32[48,1536]{1,0:T(8,128)}), f32[768,1536]{1,0:T(8,128)}) %all-gather.115.cloned.1.call-update) | async-done | bytes 4718608 | tf_op jit(solution)/shard_map/all_gather | solution.py:284
  1300.2 74.9 %all-gather.95.cloned.1.call-done = f32[768,1536]{1,0:T(8,128)} async-done(((f32[48,1536]{1,0:T(8,128)}), f32[768,1536]{1,0:T(8,128)}) %all-gather.95.cloned.1.call-update) | async-done | bytes 4718608 | tf_op jit(solution)/shard_map/all_gather | solution.py:283
  1382.7 17.7 all-reduce.20.cloned.1.call-done
  1402.9 64.0 %all-gather.77.cloned.1.call-done = f32[768,768]{1,0:T(8,128)} async-done(((f32[48,768]{1,0:T(8,128)}), f32[768,768]{1,0:T(8,128)}) %all-gather.77.cloned.1.call-update) | async-done | bytes 2359312 | tf_op jit(solution)/shard_map/all_gather | solution.py:294
  1474.8 56.4 %all-gather.57.cloned.1.call-done = f32[768,768]{1,0:T(8,128)} async-done(((f32[48,768]{1,0:T(8,128)}), f32[768,768]{1,0:T(8,128)}) %all-gather.57.cloned.1.call-update) | async-done | bytes 2359312 | tf_op jit(solution)/shard_map/all_gather | solution.py:293
  1540.6 54.8 %all-gather.117.cloned.1.call-done = f32[768,768]{1,0:T(8,128)} async-done(((f32[48,768]{1,0:T(8,128)}), f32[768,768]{1,0:T(8,128)}) %all-gather.117.cloned.1.call-update) | async-done | bytes 2359312 | tf_op jit(solution)/shard_map/all_gather | solution.py:296
  1605.8 53.9 %all-gather.97.cloned.1.call-done = f32[768,768]{1,0:T(8,128)} async-done(((f32[48,768]{1,0:T(8,128)}), f32[768,768]{1,0:T(8,128)}) %all-gather.97.cloned.1.call-update) | async-done | bytes 2359312 | tf_op jit(solution)/shard_map/all_gather | solution.py:295
  1670.3 48.1 %all-gather.79.cloned.1.call-done = f32[768,384]{1,0:T(8,128)} async-done(((f32[48,384]{1,0:T(8,128)}), f32[768,384]{1,0:T(8,128)}) %all-gather.79.cloned.1.call-update) | async-done | bytes 1179664 | tf_op jit(solution)/shard_map/all_gather | solution.py:282
  1721.6 70.8 %all-gather.59.cloned.1.call-done = f32[768,1152]{1,0:T(8,128)} async-done(((f32[48,1152]{1,0:T(8,128)}), f32[768,1152]{1,0:T(8,128)}) %all-gather.59.cloned.1.call-update) | async-done | bytes 3538960 | tf_op jit(solution)/shard_map/all_gather | solution.py:281
  1798.4 76.6 %all-gather.119.cloned.1.call-done = f32[768,1536]{1,0:T(8,128)} async-done(((f32[48,1536]{1,0:T(8,128)}), f32[768,1536]{1,0:T(8,128)}) %all-gather.119.cloned.1.call-update) | async-done | bytes 4718608 | tf_op jit(solution)/shard_map/all_gather | solution.py:284
  1882.4 75.5 %all-gather.99.cloned.1.call-done = f32[768,1536]{1,0:T(8,128)} async-done(((f32[48,1536]{1,0:T(8,128)}), f32[768,1536]{1,0:T(8,128)}) %all-gather.99.cloned.1.call-update) | async-done | bytes 4718608 | tf_op jit(solution)/shard_map/all_gather | solution.py:283
  1965.3 17.7 all-reduce.18.cloned.1.call-done
  1985.4 63.8 %all-gather.81.cloned.1.call-done = f32[768,768]{1,0:T(8,128)} async-done(((f32[48,768]{1,0:T(8,128)}), f32[768,768]{1,0:T(8,128)}) %all-gather.81.cloned.1.call-update) | async-done | bytes 2359312 | tf_op jit(solution)/shard_map/all_gather | solution.py:294
  2055.1 58.1 %all-gather.61.cloned.1.call-done = f32[768,768]{1,0:T(8,128)} async-done(((f32[48,768]{1,0:T(8,128)}), f32[768,768]{1,0:T(8,128)}) %all-gather.61.cloned.1.call-update) | async-done | bytes 2359312 | tf_op jit(solution)/shard_map/all_gather | solution.py:293
  2120.0 57.1 %all-gather.121.cloned.1.call-done = f32[768,768]{1,0:T(8,128)} async-done(((f32[48,768]{1,0:T(8,128)}), f32[768,768]{1,0:T(8,128)}) %all-gather.121.cloned.1.call-update) | async-done | bytes 2359312 | tf_op jit(solution)/shard_map/all_gather | solution.py:296
  2186.4 54.5 %all-gather.101.cloned.1.call-done = f32[768,768]{1,0:T(8,128)} async-done(((f32[48,768]{1,0:T(8,128)}), f32[768,768]{1,0:T(8,128)}) %all-gather.101.cloned.1.call-update) | async-done | bytes 2359312 | tf_op jit(solution)/shard_map/all_gather | solution.py:295
  2250.5 48.7 %all-gather.83.cloned.1.call-done = f32[768,384]{1,0:T(8,128)} async-done(((f32[48,384]{1,0:T(8,128)}), f32[768,384]{1,0:T(8,128)}) %all-gather.83.cloned.1.call-update) | async-done | bytes 1179664 | tf_op jit(solution)/shard_map/all_gather | solution.py:282
  2302.3 70.4 %all-gather.63.cloned.1.call-done = f32[768,1152]{1,0:T(8,128)} async-done(((f32[48,1152]{1,0:T(8,128)}), f32[768,1152]{1,0:T(8,128)}) %all-gather.63.cloned.1.call-update) | async-done | bytes 3538960 | tf_op jit(solution)/shard_map/all_gather | solution.py:281
  2378.7 76.2 %all-gather.123.cloned.1.call-done = f32[768,1536]{1,0:T(8,128)} async-done(((f32[48,1536]{1,0:T(8,128)}), f32[768,1536]{1,0:T(8,128)}) %all-gather.123.cloned.1.call-update) | async-done | bytes 4718608 | tf_op jit(solution)/shard_map/all_gather | solution.py:284
  2462.4 75.1 %all-gather.103.cloned.1.call-done = f32[768,1536]{1,0:T(8,128)} async-done(((f32[48,1536]{1,0:T(8,128)}), f32[768,1536]{1,0:T(8,128)}) %all-gather.103.cloned.1.call-update) | async-done | bytes 4718608 | tf_op jit(solution)/shard_map/all_gather | solution.py:283
  2544.9 17.7 all-reduce.16.cloned.1.call-done
  2564.7 64.4 %all-gather.85.cloned.1.call-done = f32[768,768]{1,0:T(8,128)} async-done(((f32[48,768]{1,0:T(8,128)}), f32[768,768]{1,0:T(8,128)}) %all-gather.85.cloned.1.call-update) | async-done | bytes 2359312 | tf_op jit(solution)/shard_map/all_gather | solution.py:294
  2635.0 58.3 %all-gather.65.cloned.1.call-done = f32[768,768]{1,0:T(8,128)} async-done(((f32[48,768]{1,0:T(8,128)}), f32[768,768]{1,0:T(8,128)}) %all-gather.65.cloned.1.call-update) | async-done | bytes 2359312 | tf_op jit(solution)/shard_map/all_gather | solution.py:293
  2700.2 57.4 %all-gather.125.cloned.1.call-done = f32[768,768]{1,0:T(8,128)} async-done(((f32[48,768]{1,0:T(8,128)}), f32[768,768]{1,0:T(8,128)}) %all-gather.125.cloned.1.call-update) | async-done | bytes 2359312 | tf_op jit(solution)/shard_map/all_gather | solution.py:296
  2767.0 54.8 %all-gather.105.cloned.1.call-done = f32[768,768]{1,0:T(8,128)} async-done(((f32[48,768]{1,0:T(8,128)}), f32[768,768]{1,0:T(8,128)}) %all-gather.105.cloned.1.call-update) | async-done | bytes 2359312 | tf_op jit(solution)/shard_map/all_gather | solution.py:295
  2831.3 49.2 %all-gather.87.cloned.1.call-done = f32[768,384]{1,0:T(8,128)} async-done(((f32[48,384]{1,0:T(8,128)}), f32[768,384]{1,0:T(8,128)}) %all-gather.87.cloned.1.call-update) | async-done | bytes 1179664 | tf_op jit(solution)/shard_map/all_gather | solution.py:282
  2883.7 70.7 %all-gather.67.cloned.1.call-done = f32[768,1152]{1,0:T(8,128)} async-done(((f32[48,1152]{1,0:T(8,128)}), f32[768,1152]{1,0:T(8,128)}) %all-gather.67.cloned.1.call-update) | async-done | bytes 3538960 | tf_op jit(solution)/shard_map/all_gather | solution.py:281
  2960.5 76.8 %all-gather.127.cloned.1.call-done = f32[768,1536]{1,0:T(8,128)} async-done(((f32[48,1536]{1,0:T(8,128)}), f32[768,1536]{1,0:T(8,128)}) %all-gather.127.cloned.1.call-update) | async-done | bytes 4718608 | tf_op jit(solution)/shard_map/all_gather | solution.py:284
  3044.6 75.3 %all-gather.107.cloned.1.call-done = f32[768,1536]{1,0:T(8,128)} async-done(((f32[48,1536]{1,0:T(8,128)}), f32[768,1536]{1,0:T(8,128)}) %all-gather.107.cloned.1.call-update) | async-done | bytes 4718608 | tf_op jit(solution)/shard_map/all_gather | solution.py:283
  3127.4 17.7 all-reduce.14.cloned.1.call-done
  3147.3 63.9 %all-gather.89.cloned.1.call-done = f32[768,768]{1,0:T(8,128)} async-done(((f32[48,768]{1,0:T(8,128)}), f32[768,768]{1,0:T(8,128)}) %all-gather.89.cloned.1.call-update) | async-done | bytes 2359312 | tf_op jit(solution)/shard_map/all_gather | solution.py:294
  3217.1 57.9 %all-gather.69.cloned.1.call-done = f32[768,768]{1,0:T(8,128)} async-done(((f32[48,768]{1,0:T(8,128)}), f32[768,768]{1,0:T(8,128)}) %all-gather.69.cloned.1.call-update) | async-done | bytes 2359312 | tf_op jit(solution)/shard_map/all_gather | solution.py:293
  3281.9 56.9 %all-gather.129.cloned.1.call-done = f32[768,768]{1,0:T(8,128)} async-done(((f32[48,768]{1,0:T(8,128)}), f32[768,768]{1,0:T(8,128)}) %all-gather.129.cloned.1.call-update) | async-done | bytes 2359312 | tf_op jit(solution)/shard_map/all_gather | solution.py:296
  3348.2 54.5 %all-gather.109.cloned.1.call-done = f32[768,768]{1,0:T(8,128)} async-done(((f32[48,768]{1,0:T(8,128)}), f32[768,768]{1,0:T(8,128)}) %all-gather.109.cloned.1.call-update) | async-done | bytes 2359312 | tf_op jit(solution)/shard_map/all_gather | solution.py:295
  3412.6 48.2 %all-gather.91.cloned.1.call-done = f32[768,384]{1,0:T(8,128)} async-done(((f32[48,384]{1,0:T(8,128)}), f32[768,384]{1,0:T(8,128)}) %all-gather.91.cloned.1.call-update) | async-done | bytes 1179664 | tf_op jit(solution)/shard_map/all_gather | solution.py:282
  3464.0 70.4 %all-gather.71.cloned.1.call-done = f32[768,1152]{1,0:T(8,128)} async-done(((f32[48,1152]{1,0:T(8,128)}), f32[768,1152]{1,0:T(8,128)}) %all-gather.71.cloned.1.call-update) | async-done | bytes 3538960 | tf_op jit(solution)/shard_map/all_gather | solution.py:281
  3540.4 76.2 %all-gather.131.cloned.1.call-done = f32[768,1536]{1,0:T(8,128)} async-done(((f32[48,1536]{1,0:T(8,128)}), f32[768,1536]{1,0:T(8,128)}) %all-gather.131.cloned.1.call-update) | async-done | bytes 4718608 | tf_op jit(solution)/shard_map/all_gather | solution.py:284
  3624.1 75.0 %all-gather.111.cloned.1.call-done = f32[768,1536]{1,0:T(8,128)} async-done(((f32[48,1536]{1,0:T(8,128)}), f32[768,1536]{1,0:T(8,128)}) %all-gather.111.cloned.1.call-update) | async-done | bytes 4718608 | tf_op jit(solution)/shard_map/all_gather | solution.py:283
  3699.1 7.5 fusion.187
  3748.4 104.4 %reduce-scatter.30.cloned.1.call-done = f32[48,12]{1,0:T(8,128)} async-done(((f32[768,12]{1,0:T(8,128)}), f32[48,12]{1,0:T(8,128)}) %reduce-scatter.30.cloned.1.call-update) | async-done | bytes 2320
  3856.7 60.3 %all-gather.93.cloned.1.call-done = f32[768,768]{1,0:T(8,128)} async-done(((f32[48,768]{1,0:T(8,128)}), f32[768,768]{1,0:T(8,128)}) %all-gather.93.cloned.1.call-update) | async-done | bytes 2359312 | tf_op jit(solution)/shard_map/all_gather | solution.py:294
  3921.6 59.4 %all-gather.133.cloned.1.call-done = f32[768,768]{1,0:T(8,128)} async-done(((f32[48,768]{1,0:T(8,128)}), f32[768,768]{1,0:T(8,128)}) %all-gather.133.cloned.1.call-update) | async-done | bytes 2359312 | tf_op jit(solution)/shard_map/all_gather | solution.py:296
  3984.1 60.8 %all-gather.113.cloned.1.call-done = f32[768,768]{1,0:T(8,128)} async-done(((f32[48,768]{1,0:T(8,128)}), f32[768,768]{1,0:T(8,128)}) %all-gather.113.cloned.1.call-update) | async-done | bytes 2359312 | tf_op jit(solution)/shard_map/all_gather | solution.py:295
  4060.3 48.4 %all-gather.73.cloned.1.call-done = f32[768,768]{1,0:T(8,128)} async-done(((f32[48,768]{1,0:T(8,128)}), f32[768,768]{1,0:T(8,128)}) %all-gather.73.cloned.1.call-update) | async-done | bytes 2359312 | tf_op jit(solution)/shard_map/all_gather | solution.py:293
  (594 shorter events, 519.0 us)
Async XLA Ops:
  7.2 77.9 %all-gather.47.cloned.1.call-start = ((), (), s32[]{:S(2)}) async-start(), calls=%async_computation.9 | async-start | bytes 3760128 | tf_op jit(solution)/shard_map/all_gather | solution.py:107
  10.6 132.0 %all-gather.49.cloned.1.call-start = ((), (), s32[]{:S(2)}) async-start(), calls=%async_computation.10 | async-start | bytes 1253376 | tf_op jit(solution)/shard_map/all_gather | solution.py:108
  13.5 211.0 %all-gather.51.cloned.1.call-start = ((), (), s32[]{:S(2)}) async-start(), calls=%async_computation.11 | async-start | bytes 5013504 | tf_op jit(solution)/shard_map/all_gather | solution.py:109
  16.7 289.6 %all-gather.53.cloned.1.call-start = ((), (), s32[]{:S(2)}) async-start(), calls=%async_computation.12 | async-start | bytes 5013504 | tf_op jit(solution)/shard_map/all_gather | solution.py:110
  19.9 502.8 %reduce-scatter.16.cloned.1.call-start = ((), (), s32[]{:S(2)}) async-start(), calls=%async_computation.14 | async-start | bytes 2506752 | tf_op jit(solution)/shard_map/reduce_scatter | solution.py:118
  395.5 283.6 %reduce-scatter.28.cloned.1.call-start = ((), (), s32[]{:S(2)}) async-start(), calls=%async_computation.60 | async-start | bytes 7520256 | tf_op jit(solution)/shard_map/reduce_scatter | solution.py:117
  447.9 408.0 %reduce-scatter.24.cloned.1.call-start = ((), (), s32[]{:S(2)}) async-start(), calls=%async_computation.18 | async-start | bytes 10027008 | tf_op jit(solution)/shard_map/reduce_scatter | solution.py:120
  459.3 572.1 %reduce-scatter.20.cloned.1.call-start = ((), (), s32[]{:S(2)}) async-start(), calls=%async_computation.16 | async-start | bytes 10027008 | tf_op jit(solution)/shard_map/reduce_scatter | solution.py:119
  471.3 569.3 %copy-start.95 = (f32[48,384]{1,0:T(8,128)S(1)}, f32[48,384]{1,0:T(8,128)}, u32[]{:S(2)}) copy-start(f32[48,384]{1,0:T(8,128)} %param.25) | copy-start | bytes 221188
  471.3 581.1 %copy-start.91 = (f32[48,1152]{1,0:T(8,128)S(1)}, f32[48,1152]{1,0:T(8,128)}, u32[]{:S(2)}) copy-start(f32[48,1152]{1,0:T(8,128)} %param.24) | copy-start | bytes 663556
  471.4 593.2 %copy-start.89 = (f32[48,1536]{1,0:T(8,128)S(1)}, f32[48,1536]{1,0:T(8,128)}, u32[]{:S(2)}) copy-start(f32[48,1536]{1,0:T(8,128)} %param.27) | copy-start | bytes 884740
  471.4 605.1 %copy-start.90 = (f32[48,1536]{1,0:T(8,128)S(1)}, f32[48,1536]{1,0:T(8,128)}, u32[]{:S(2)}) copy-start(f32[48,1536]{1,0:T(8,128)} %param.26) | copy-start | bytes 884740
  471.4 569.3 %reduce-scatter.18.cloned.1.call-start = ((), (), s32[]{:S(2)}) async-start(), calls=%async_computation.15 | async-start | bytes 221184 | tf_op jit(solution)/shard_map/reduce_scatter | solution.py:125
  522.8 529.7 %reduce-scatter.14.cloned.1.call-start = ((), (), s32[]{:S(2)}) async-start(), calls=%async_computation.13 | async-start | bytes 663552 | tf_op jit(solution)/shard_map/reduce_scatter | solution.py:124
  679.2 385.3 %reduce-scatter.26.cloned.1.call-start = ((), (), s32[]{:S(2)}) async-start(), calls=%async_computation.19 | async-start | bytes 884736 | tf_op jit(solution)/shard_map/reduce_scatter | solution.py:127
  855.9 220.6 %reduce-scatter.22.cloned.1.call-start = ((), (), s32[]{:S(2)}) async-start(), calls=%async_computation.17 | async-start | bytes 884736 | tf_op jit(solution)/shard_map/reduce_scatter | solution.py:126
  1031.3 105.9 %all-gather.75.cloned.1.call-start = ((), (), s32[]{:S(2)}) async-start(), calls=%async_computation.30 | async-start | bytes 1253376 | tf_op jit(solution)/shard_map/all_gather | solution.py:282
  1042.2 168.3 %all-gather.55.cloned.1.call-start = ((), (), s32[]{:S(2)}) async-start(), calls=%async_computation.20 | async-start | bytes 3760128 | tf_op jit(solution)/shard_map/all_gather | solution.py:281
  1054.1 238.7 %all-gather.115.cloned.1.call-start = ((), (), s32[]{:S(2)}) async-start(), calls=%async_computation.50 | async-start | bytes 5013504 | tf_op jit(solution)/shard_map/all_gather | solution.py:284
  1066.3 226.6 %copy-start.58 = (f32[48,1536]{1,0:T(8,128)S(1)}, f32[48,1536]{1,0:T(8,128)}, u32[]{:S(2)}) copy-start(f32[48,1536]{1,0:T(8,128)} %multiply_add_fusion.2) | copy-start | bytes 884740
  1066.3 308.9 %all-gather.95.cloned.1.call-start = ((), (), s32[]{:S(2)}) async-start(), calls=%async_computation.40 | async-start | bytes 5013504 | tf_op jit(solution)/shard_map/all_gather | solution.py:283
  1078.2 322.1 %all-reduce.20.cloned.1.call-start = ((), (), s32[]{:S(2)}) async-start(), calls=%async_computation.66 | async-start | bytes 1179648 | tf_op jit(solution)/shard_map/psum | solution.py:289
  1382.6 84.3 %all-gather.77.cloned.1.call-start = ((), (), s32[]{:S(2)}) async-start(), calls=%async_computation.31 | async-start | bytes 2506752 | tf_op jit(solution)/shard_map/all_gather | solution.py:294
  1400.3 130.9 %all-gather.57.cloned.1.call-start = ((), (), s32[]{:S(2)}) async-start(), calls=%async_computation.21 | async-start | bytes 2506752 | tf_op jit(solution)/shard_map/all_gather | solution.py:293
  1401.1 194.3 %all-gather.117.cloned.1.call-start = ((), (), s32[]{:S(2)}) async-start(), calls=%async_computation.51 | async-start | bytes 2506752 | tf_op jit(solution)/shard_map/all_gather | solution.py:296
  1401.7 258.0 %all-gather.97.cloned.1.call-start = ((), (), s32[]{:S(2)}) async-start(), calls=%async_computation.41 | async-start | bytes 2506752 | tf_op jit(solution)/shard_map/all_gather | solution.py:295
  1402.4 316.0 %all-gather.79.cloned.1.call-start = ((), (), s32[]{:S(2)}) async-start(), calls=%async_computation.32 | async-start | bytes 1253376 | tf_op jit(solution)/shard_map/all_gather | solution.py:282
  1474.8 317.6 %all-gather.59.cloned.1.call-start = ((), (), s32[]{:S(2)}) async-start(), calls=%async_computation.22 | async-start | bytes 3760128 | tf_op jit(solution)/shard_map/all_gather | solution.py:281
  1540.5 334.4 %all-gather.119.cloned.1.call-start = ((), (), s32[]{:S(2)}) async-start(), calls=%async_computation.52 | async-start | bytes 5013504 | tf_op jit(solution)/shard_map/all_gather | solution.py:284
  1605.7 352.1 %all-gather.99.cloned.1.call-start = ((), (), s32[]{:S(2)}) async-start(), calls=%async_computation.42 | async-start | bytes 5013504 | tf_op jit(solution)/shard_map/all_gather | solution.py:283
  1670.1 312.9 %all-reduce.18.cloned.1.call-start = ((), (), s32[]{:S(2)}) async-start(), calls=%async_computation.65 | async-start | bytes 1179648 | tf_op jit(solution)/shard_map/psum | solution.py:289
  1965.3 83.9 %all-gather.81.cloned.1.call-start = ((), (), s32[]{:S(2)}) async-start(), calls=%async_computation.33 | async-start | bytes 2506752 | tf_op jit(solution)/shard_map/all_gather | solution.py:294
  1983.0 130.1 %all-gather.61.cloned.1.call-start = ((), (), s32[]{:S(2)}) async-start(), calls=%async_computation.23 | async-start | bytes 2506752 | tf_op jit(solution)/shard_map/all_gather | solution.py:293
  1983.8 193.3 %all-gather.121.cloned.1.call-start = ((), (), s32[]{:S(2)}) async-start(), calls=%async_computation.53 | async-start | bytes 2506752 | tf_op jit(solution)/shard_map/all_gather | solution.py:296
  1984.5 256.3 %all-gather.101.cloned.1.call-start = ((), (), s32[]{:S(2)}) async-start(), calls=%async_computation.43 | async-start | bytes 2506752 | tf_op jit(solution)/shard_map/all_gather | solution.py:295
  1985.1 314.1 %all-gather.83.cloned.1.call-start = ((), (), s32[]{:S(2)}) async-start(), calls=%async_computation.34 | async-start | bytes 1253376 | tf_op jit(solution)/shard_map/all_gather | solution.py:282
  2055.0 317.7 %all-gather.63.cloned.1.call-start = ((), (), s32[]{:S(2)}) async-start(), calls=%async_computation.24 | async-start | bytes 3760128 | tf_op jit(solution)/shard_map/all_gather | solution.py:281
  2119.9 335.0 %all-gather.123.cloned.1.call-start = ((), (), s32[]{:S(2)}) async-start(), calls=%async_computation.54 | async-start | bytes 5013504 | tf_op jit(solution)/shard_map/all_gather | solution.py:284
  2186.3 351.1 %all-gather.103.cloned.1.call-start = ((), (), s32[]{:S(2)}) async-start(), calls=%async_computation.44 | async-start | bytes 5013504 | tf_op jit(solution)/shard_map/all_gather | solution.py:283
  2250.1 312.5 %all-reduce.16.cloned.1.call-start = ((), (), s32[]{:S(2)}) async-start(), calls=%async_computation.64 | async-start | bytes 1179648 | tf_op jit(solution)/shard_map/psum | solution.py:289
  2544.9 84.3 %all-gather.85.cloned.1.call-start = ((), (), s32[]{:S(2)}) async-start(), calls=%async_computation.35 | async-start | bytes 2506752 | tf_op jit(solution)/shard_map/all_gather | solution.py:294
  2562.6 130.7 %all-gather.65.cloned.1.call-start = ((), (), s32[]{:S(2)}) async-start(), calls=%async_computation.25 | async-start | bytes 2506752 | tf_op jit(solution)/shard_map/all_gather | solution.py:293
  2563.2 194.4 %all-gather.125.cloned.1.call-start = ((), (), s32[]{:S(2)}) async-start(), calls=%async_computation.55 | async-start | bytes 2506752 | tf_op jit(solution)/shard_map/all_gather | solution.py:296
  2563.9 257.8 %all-gather.105.cloned.1.call-start = ((), (), s32[]{:S(2)}) async-start(), calls=%async_computation.45 | async-start | bytes 2506752 | tf_op jit(solution)/shard_map/all_gather | solution.py:295
  2564.5 316.0 %all-gather.87.cloned.1.call-start = ((), (), s32[]{:S(2)}) async-start(), calls=%async_computation.36 | async-start | bytes 1253376 | tf_op jit(solution)/shard_map/all_gather | solution.py:282
  2635.0 319.4 %all-gather.67.cloned.1.call-start = ((), (), s32[]{:S(2)}) async-start(), calls=%async_computation.26 | async-start | bytes 3760128 | tf_op jit(solution)/shard_map/all_gather | solution.py:281
  2700.2 337.1 %all-gather.127.cloned.1.call-start = ((), (), s32[]{:S(2)}) async-start(), calls=%async_computation.56 | async-start | bytes 5013504 | tf_op jit(solution)/shard_map/all_gather | solution.py:284
  2766.9 353.0 %all-gather.107.cloned.1.call-start = ((), (), s32[]{:S(2)}) async-start(), calls=%async_computation.46 | async-start | bytes 5013504 | tf_op jit(solution)/shard_map/all_gather | solution.py:283
  2831.0 314.1 %all-reduce.14.cloned.1.call-start = ((), (), s32[]{:S(2)}) async-start(), calls=%async_computation.63 | async-start | bytes 1179648 | tf_op jit(solution)/shard_map/psum | solution.py:289
  3127.4 83.9 %all-gather.89.cloned.1.call-start = ((), (), s32[]{:S(2)}) async-start(), calls=%async_computation.37 | async-start | bytes 2506752 | tf_op jit(solution)/shard_map/all_gather | solution.py:294
  3145.1 129.9 %all-gather.69.cloned.1.call-start = ((), (), s32[]{:S(2)}) async-start(), calls=%async_computation.27 | async-start | bytes 2506752 | tf_op jit(solution)/shard_map/all_gather | solution.py:293
  3145.7 193.1 %all-gather.129.cloned.1.call-start = ((), (), s32[]{:S(2)}) async-start(), calls=%async_computation.57 | async-start | bytes 2506752 | tf_op jit(solution)/shard_map/all_gather | solution.py:296
  3146.3 256.4 %all-gather.109.cloned.1.call-start = ((), (), s32[]{:S(2)}) async-start(), calls=%async_computation.47 | async-start | bytes 2506752 | tf_op jit(solution)/shard_map/all_gather | solution.py:295
  3146.9 313.9 %all-gather.91.cloned.1.call-start = ((), (), s32[]{:S(2)}) async-start(), calls=%async_computation.38 | async-start | bytes 1253376 | tf_op jit(solution)/shard_map/all_gather | solution.py:282
  3217.1 317.2 %all-gather.71.cloned.1.call-start = ((), (), s32[]{:S(2)}) async-start(), calls=%async_computation.28 | async-start | bytes 3760128 | tf_op jit(solution)/shard_map/all_gather | solution.py:281
  3281.9 334.7 %all-gather.131.cloned.1.call-start = ((), (), s32[]{:S(2)}) async-start(), calls=%async_computation.58 | async-start | bytes 5013504 | tf_op jit(solution)/shard_map/all_gather | solution.py:284
  3348.1 351.0 %all-gather.111.cloned.1.call-start = ((), (), s32[]{:S(2)}) async-start(), calls=%async_computation.48 | async-start | bytes 5013504 | tf_op jit(solution)/shard_map/all_gather | solution.py:283
  3412.0 320.5 %all-reduce.12.cloned.1.call-start = ((), (), s32[]{:S(2)}) async-start(), calls=%async_computation.62 | async-start | bytes 1179648 | tf_op jit(solution)/shard_map/psum | solution.py:289
  3706.6 146.2 %reduce-scatter.30.cloned.1.call-start = ((), (), s32[]{:S(2)}) async-start(), calls=%async_computation.61 | async-start | bytes 417792
  3732.5 184.5 %all-gather.93.cloned.1.call-start = ((), (), s32[]{:S(2)}) async-start(), calls=%async_computation.39 | async-start | bytes 2506752 | tf_op jit(solution)/shard_map/all_gather | solution.py:294
  3733.2 247.7 %all-gather.133.cloned.1.call-start = ((), (), s32[]{:S(2)}) async-start(), calls=%async_computation.59 | async-start | bytes 2506752 | tf_op jit(solution)/shard_map/all_gather | solution.py:296
  3734.0 310.9 %all-gather.113.cloned.1.call-start = ((), (), s32[]{:S(2)}) async-start(), calls=%async_computation.49 | async-start | bytes 2506752 | tf_op jit(solution)/shard_map/all_gather | solution.py:295
  3734.7 373.9 %all-gather.73.cloned.1.call-start = ((), (), s32[]{:S(2)}) async-start(), calls=%async_computation.29 | async-start | bytes 2506752 | tf_op jit(solution)/shard_map/all_gather | solution.py:293
  3748.4 232.5 %copy-start.78 = (f32[48,768]{1,0:T(8,128)S(1)}, f32[48,768]{1,0:T(8,128)}, u32[]{:S(2)}) copy-start(f32[48,768]{1,0:T(8,128)} %get-tuple-element.79) | copy-start | bytes 442372
  (132 other events, 6132.0 us)
Sparse Core Ops, SparseCore 0:
  10.9 74.1 all-gather.46
  87.9 54.6 all-gather.48
  145.4 79.1 all-gather.50
  227.2 79.0 all-gather.52
  395.6 127.0 reduce-scatter.15
  528.8 150.2 reduce-scatter.27
  685.8 170.0 reduce-scatter.23
  861.6 169.7 reduce-scatter.19
  1034.2 6.4 reduce-scatter.17
  1043.4 8.9 reduce-scatter.13
  1055.3 9.1 reduce-scatter.25
  1067.3 9.1 reduce-scatter.21
  1079.9 57.2 all-gather.74
  1140.4 70.1 all-gather.54
  1213.8 78.9 all-gather.114
  1296.0 79.0 all-gather.94
  1382.7 17.5 all-reduce.19
  1403.4 63.4 all-gather.76
  1470.1 61.0 all-gather.56
  1534.2 61.0 all-gather.116
  1598.6 61.1 all-gather.96
  1663.5 54.9 all-gather.78
  1722.2 70.1 all-gather.58
  1795.9 78.9 all-gather.118
  1878.7 79.0 all-gather.98
  1965.4 17.5 all-reduce.17
  1985.7 63.4 all-gather.80
  2052.0 61.0 all-gather.60
  2115.9 61.0 all-gather.120
  2179.7 61.0 all-gather.100
  2244.2 54.9 all-gather.82
  2302.5 70.1 all-gather.62
  2375.9 78.9 all-gather.122
  2458.3 79.0 all-gather.102
  2545.0 17.5 all-reduce.15
  2565.6 63.4 all-gather.84
  2632.2 61.0 all-gather.64
  2696.5 61.0 all-gather.124
  2760.7 61.0 all-gather.104
  2825.5 54.9 all-gather.86
  2884.3 70.1 all-gather.66
  2958.2 78.9 all-gather.126
  3040.8 79.0 all-gather.106
  3127.5 17.5 all-reduce.13
  3147.7 63.4 all-gather.88
  3213.9 61.0 all-gather.68
  3277.7 61.0 all-gather.128
  3341.5 61.1 all-gather.108
  3405.9 54.9 all-gather.90
  3464.2 70.1 all-gather.70
  3537.6 78.9 all-gather.130
  3620.0 79.0 all-gather.110
  3706.8 17.5 all-reduce.11
  3732.6 120.1 reduce-scatter.29
  3855.6 61.3 all-gather.92
  3919.8 61.0 all-gather.132
  3983.7 61.0 all-gather.112
  4047.5 61.0 all-gather.72
where the time goes:
time: 4130 us; the launch traced here: 4120 us
  waiting for transfers between devices  3460 us (84%)
  matrix products  455 us (11%)
  other arithmetic  66.9 us (2%)
  local copies, waits for them, and re-layouts  57.9 us (1%)
  blocking collectives  55.5 us (1%)
    all_gather x5, waiting for transfers between devices, per_device(): lax.all_gather(iterate[3], 'fsdp', axis=0, tiled=True)  382 us
    all_gather x5, waiting for transfers between devices, per_device(): lax.all_gather(iterate[2], 'fsdp', axis=0, tiled=True)  376 us
    all_gather x5, waiting for transfers between devices, per_device(): lax.all_gather(iterate[0], 'fsdp', axis=0, tiled=True)  352 us
    all_gather x5, waiting for transfers between devices, per_device(): lax.all_gather(gram_part[1], 'fsdp', axis=0, tiled=True)  316 us
    all_gather x5, waiting for transfers between devices, per_device(): lax.all_gather(gram_part[3], 'fsdp', axis=0, tiled=True)  286 us
    all_gather x5, waiting for transfers between devices, per_device(): lax.all_gather(gram_part[0], 'fsdp', axis=0, tiled=True)  279 us
    all_gather x5, waiting for transfers between devices, per_device(): lax.all_gather(gram_part[2], 'fsdp', axis=0, tiled=True)  278 us
    all_gather x5, waiting for transfers between devices, per_device(): lax.all_gather(iterate[1], 'fsdp', axis=0, tiled=True)  253 us
  transfers between devices with their start and end apart: 58, of which 57 were waited for; matrix products, arithmetic and copies ran while one was open for 11% of the time, Pallas kernels for 0%

commit v1 on v0

v1 whole, which is shorter than its diff:
```python
import math

import jax
import jax.numpy as jnp
from jax import lax
from jax.sharding import PartitionSpec as P

D = 768
FF = 3072
HEADS = 12
HEAD_DIM = 64
SEQ = 512
CAP = 1
MICRO = 2
NS_ITERS = 5
STEP = 10

norm_eps = 1e-05
mask_fill = -1e30
poly_first = 3.4445
poly_second = -4.775
poly_third = 2.0315
muon_rate = 0.2
adam_rate = 0.8
decay_rate = 0.01
moment_decay = 0.5
beta_first = 0.9
beta_second = 0.98
adam_eps = 1e-06

SWAP = [(0, 1), (1, 0)]
VEC_PAD = 128
GROUP = 4


def matmul(former, latter):
    return jnp.dot(former, latter, preferred_element_type=jnp.float32)


def matmul_tn(former, latter):
    return lax.dot_general(
        former, latter, (((0,), (0,)), ((), ())), preferred_element_type=jnp.float32
    )


def matmul_nt(former, latter):
    return lax.dot_general(
        former, latter, (((1,), (1,)), ((), ())), preferred_element_type=jnp.float32
    )


def close_dot(former, latter):
    return jnp.dot(
        former, latter, precision=lax.Precision.HIGH, preferred_element_type=jnp.float32
    )


def flip(values, bit, size):
    return lax.ppermute(values, "fsdp", [(i, i ^ (1 << bit)) for i in range(size)])


def swap_cores(values):
    return lax.ppermute(values, "row", SWAP)


def bit_orders(size):
    count = size.bit_length() - 1
    every = list(range(count))[::-1]
    high, rest = every[:2], every[2:]
    half = len(rest) // 2
    return high, rest[:half] + rest[half:], rest[half:] + rest[:half]


def my_bit(bit):
    return (lax.axis_index("fsdp") >> bit) & 1


def gather_bits(values, have, bits, size):
    for bit in bits:
        arrived = flip(values, bit, size)
        place = sum(1 for other in have if other > bit)
        values = jnp.where(
            my_bit(bit) == 1,
            jnp.stack([arrived, values], axis=place),
            jnp.stack([values, arrived], axis=place),
        )
        have = have + [bit]
    return values, have


def gather_rows(values, cut, size):
    high, order_a, order_b = bit_orders(size)
    values, have = gather_bits(values, [], high, size)
    part_a, _ = gather_bits(values[..., :cut], have, order_a, size)
    part_b, _ = gather_bits(values[..., cut:], have, order_b, size)
    return part_a.reshape(D, -1), part_b.reshape(D, -1)


def reduce_bits(values, have, bits, size):
    for bit in bits:
        place = sum(1 for other in have if other > bit)
        mine = my_bit(bit)
        leaving = lax.dynamic_index_in_dim(values, 1 - mine, place, keepdims=False)
        kept = lax.dynamic_index_in_dim(values, mine, place, keepdims=False)
        values = kept + flip(leaving.astype(jnp.bfloat16), bit, size).astype(jnp.float32)
        have = [other for other in have if other != bit]
    return values, have


def reduce_rows(part_a, part_b, size):
    high, order_a, order_b = bit_orders(size)
    every = high + order_a
    shape = (2,) * len(every) + (D // size,)
    part_a = part_a.reshape(shape + (-1,))
    part_b = part_b.reshape(shape + (-1,))
    part_a, have = reduce_bits(part_a, every, order_a[::-1], size)
    part_b, have = reduce_bits(part_b, every, order_b[::-1], size)
    total = jnp.concatenate([part_a, part_b], axis=-1)
    total, _ = reduce_bits(total, have, high[::-1], size)
    return total


def column_halves(core, own, other):
    return jnp.where(
        core == 0,
        jnp.concatenate([own, other], axis=1),
        jnp.concatenate([other, own], axis=1),
    )


def chip_grad(core, former, latter):
    half = latter.shape[1] // 2
    leaving = matmul_tn(former, lax.dynamic_slice_in_dim(latter, (1 - core) * half, half, 1))
    arrived = swap_cores(leaving.astype(jnp.bfloat16))
    kept = matmul_tn(former, lax.dynamic_slice_in_dim(latter, core * half, half, 1))
    return kept + arrived.astype(jnp.float32)


def erf_gelu(pre_act):
    cdf = 0.5 * (1.0 + lax.erf(pre_act * math.sqrt(0.5)))
    pdf = jnp.exp(-0.5 * pre_act * pre_act) * (1.0 / math.sqrt(2.0 * math.pi))
    return pre_act * cdf, cdf + pre_act * pdf


def norm_parts(values):
    center = values - jnp.mean(values, axis=-1, keepdims=True)
    rstd = lax.rsqrt(jnp.mean(center * center, axis=-1, keepdims=True) + norm_eps)
    return center * rstd, rstd


def norm_pull(grad, gain, xhat, rstd):
    scaled = grad * gain
    return rstd * (
        scaled
        - jnp.mean(scaled, axis=-1, keepdims=True)
        - xhat * jnp.mean(scaled * xhat, axis=-1, keepdims=True)
    )


def column_sum(values):
    return jnp.sum(values, axis=0, dtype=jnp.float32)


def attend(query_heads, key_heads, key_valid):
    scores = jnp.einsum(
        "cqhd,ckhd->chqk", query_heads, key_heads, preferred_element_type=jnp.float32
    ) / math.sqrt(HEAD_DIM)
    return jnp.where(key_valid[:, None, None, :], scores, mask_fill)


def newton_schulz(gram, row_start, row_count):
    scale = jnp.sqrt(jnp.trace(gram)) + 1e-07
    gram = gram / (scale * scale)
    rows = None
    for sweep in range(NS_ITERS):
        square = close_dot(gram, gram)
        step = poly_second * gram + poly_third * square
        step = step + poly_first * jnp.eye(D, dtype=jnp.float32)
        if rows is None:
            rows = lax.dynamic_slice_in_dim(step, row_start, row_count, 0)
        else:
            rows = close_dot(rows, step)
        if sweep < NS_ITERS - 1:
            gram = close_dot(close_dot(step, gram), step)
    return rows / scale


def per_device(
    size,
    tokens,
    cotangent,
    counts,
    lengths,
    w_qkv,
    w_out,
    w_up,
    w_down,
    vectors,
    mom_qkv,
    mom_out,
    mom_up,
    mom_down,
    adam_first,
    adam_second,
):
    me = lax.axis_index("fsdp")
    core = lax.axis_index("row")
    slots = lengths.shape[0]
    rows = tokens.shape[0]
    up_rows = FF // D
    low = jnp.bfloat16

    vec_block = jnp.pad(vectors.T, ((0, 0), (0, VEC_PAD - vectors.shape[0]))).astype(low)
    first_block = jnp.concatenate([w_qkv.astype(low), vec_block], axis=1)
    first_a, first_b = gather_rows(first_block, 640, size)
    own_first = jnp.concatenate([first_a, first_b], axis=1)
    other_first = swap_cores(own_first)
    qkv_half = w_qkv.shape[1]
    qkv_weight = column_halves(core, own_first[:, :qkv_half], other_first[:, :qkv_half])
    vec_rows = vectors.shape[0]
    vec_own = own_first[:, qkv_half : qkv_half + vec_rows].T
    vec_other = other_first[:, qkv_half : qkv_half + vec_rows].T
    vec = jnp.where(
        core == 0,
        jnp.concatenate([vec_own, vec_other], axis=0),
        jnp.concatenate([vec_other, vec_own], axis=0),
    ).astype(jnp.float32)
    bias_query, bias_value, bias_out, gain_attn, shift_attn = (vec[i] for i in range(5))
    bias_up = vec[5 : 5 + up_rows].reshape(FF)
    bias_down, gain_ffn, shift_ffn = (vec[i] for i in range(5 + up_rows, 8 + up_rows))

    out_low, up_low, down_low = w_out.astype(low), w_up.astype(low), w_down.astype(low)
    second_block = jnp.concatenate([up_low, out_low, down_low], axis=1)
    second_a, second_b = gather_rows(second_block, 1792, size)
    other_a, other_b = swap_cores(second_a), swap_cores(second_b)
    up_half = w_up.shape[1]
    up_weight = column_halves(core, second_a[:, :up_half], other_a[:, :up_half])
    out_weight = column_halves(
        core,
        jnp.concatenate([second_a[:, up_half:], second_b[:, :128]], axis=1),
        jnp.concatenate([other_a[:, up_half:], other_b[:, :128]], axis=1),
    )
    down_weight = column_halves(core, second_b[:, 128:], other_b[:, 128:])

    head_shape = (slots, SEQ, HEADS, HEAD_DIM)
    key_valid = jnp.arange(SEQ)[None, :] < lengths[:, None]
    projected = matmul(tokens, qkv_weight)
    query = (projected[:, :D] + bias_query).astype(low).reshape(head_shape)
    key = projected[:, D : 2 * D].astype(low).reshape(head_shape)
    value = (projected[:, 2 * D :] + bias_value).astype(low).reshape(head_shape)
    scores = attend(query, key, key_valid)
    top_score = jnp.max(scores, axis=-1, keepdims=True)
    exp_scores = jnp.exp(scores - top_score)
    row_total = jnp.sum(exp_scores, axis=-1, keepdims=True)
    log_total = top_score + jnp.log(row_total)
    context = (
        jnp.einsum(
            "chqk,ckhd->cqhd",
            (exp_scores / row_total).astype(low),
            value,
            preferred_element_type=jnp.float32,
        )
        .reshape(rows, D)
        .astype(low)
    )
    resid_one = tokens.astype(jnp.float32) + (matmul(context, out_weight) + bias_out)
    xhat_one, rstd_one = norm_parts(resid_one)
    hidden = xhat_one * gain_attn + shift_attn
    hidden_low = hidden.astype(low)
    pre_act = matmul(hidden_low, up_weight) + bias_up
    activated, slope = erf_gelu(pre_act)
    act_low = activated.astype(low)
    branch = matmul_nt(act_low, down_weight) + bias_down
    xhat_two, rstd_two = norm_parts(hidden + branch)
    layer_out = (xhat_two * gain_ffn + shift_ffn).astype(low)

    live = jnp.arange(slots) % CAP < counts.reshape(-1)[jnp.arange(slots) // CAP]
    valid = (live[:, None] & key_valid).reshape(rows, 1).astype(jnp.float32)
    masked = cotangent.astype(jnp.float32) * valid
    gain_two = column_sum(masked * xhat_two)
    shift_two = column_sum(masked)
    top_grad = norm_pull(masked, gain_ffn, xhat_two, rstd_two)
    branch_low = top_grad.astype(low)
    down_bias = column_sum(branch_low)
    down_part = chip_grad(core, branch_low, act_low)
    pre_low = (matmul(branch_low, down_weight) * slope).astype(low)
    up_bias = column_sum(pre_low)
    up_part = chip_grad(core, hidden_low, pre_low)
    hidden_grad = top_grad + matmul_nt(pre_low, up_weight)
    gain_one = column_sum(hidden_grad * xhat_one)
    shift_one = column_sum(hidden_grad)
    skip_grad = norm_pull(hidden_grad, gain_attn, xhat_one, rstd_one)
    attn_low = skip_grad.astype(low)
    out_bias = column_sum(attn_low)
    out_part = chip_grad(core, context, attn_low)
    context_grad = matmul_nt(attn_low, out_weight).astype(low).reshape(head_shape)
    scores = attend(query, key, key_valid)
    probs = jnp.exp(scores - log_total)
    prob_grad = jnp.einsum(
        "cqhd,ckhd->chqk", context_grad, value, preferred_element_type=jnp.float32
    )
    value_grad = jnp.einsum(
        "chqk,cqhd->ckhd", probs.astype(low), context_grad, preferred_element_type=jnp.float32
    ).astype(low)
    row_dot = jnp.sum(probs * prob_grad, axis=-1, keepdims=True)
    score_grad = (probs * (prob_grad - row_dot)).astype(low)
    query_grad = (
        jnp.einsum("chqk,ckhd->cqhd", score_grad, key, preferred_element_type=jnp.float32)
        / math.sqrt(HEAD_DIM)
    ).astype(low)
    key_grad = (
        jnp.einsum("chqk,cqhd->ckhd", score_grad, query, preferred_element_type=jnp.float32)
        / math.sqrt(HEAD_DIM)
    ).astype(low)
    qkv_low = jnp.concatenate(
        [query_grad.reshape(rows, D), key_grad.reshape(rows, D), value_grad.reshape(rows, D)],
        axis=1,
    )
    qkv_part = chip_grad(core, tokens, qkv_low)
    query_bias, value_bias = column_sum(qkv_low[:, :D]), column_sum(qkv_low[:, 2 * D :])
    input_grad = skip_grad + matmul_nt(qkv_low, qkv_weight)

    half = up_half // 2
    grad_down = reduce_rows(down_part[:, :half], down_part[:, half:], size)
    grad_up = reduce_rows(up_part[:, :half], up_part[:, half:], size)
    last_part = jnp.concatenate([qkv_part, out_part], axis=1)
    grad_last = reduce_rows(last_part[:, :half], last_part[:, half:], size)
    grad_qkv, grad_out = grad_last[:, :qkv_half], grad_last[:, qkv_half:]
    vector_grad = jnp.concatenate(
        [
            jnp.stack([query_bias, value_bias, out_bias, gain_one, shift_one]),
            up_bias.reshape(up_rows, D),
            jnp.stack([down_bias, gain_two, shift_two]),
        ],
        axis=0,
    )
    grad_vectors = lax.psum_scatter(vector_grad, "fsdp", scatter_dimension=1, tiled=True)
    grad_vectors = lax.psum_scatter(grad_vectors, "row", scatter_dimension=0, tiled=True)

    moment_qkv = moment_decay * mom_qkv + grad_qkv
    moment_out = moment_decay * mom_out + grad_out
    moment_up = moment_decay * mom_up + grad_up
    moment_down = moment_decay * mom_down + grad_down

    def whole_columns(block):
        part_a, part_b = gather_rows(block, half, size)
        return jnp.concatenate([part_a, part_b], axis=1)

    down_cols = whole_columns(moment_down.astype(low))
    up_cols = whole_columns(moment_up.astype(low))
    last_cols = whole_columns(jnp.concatenate([moment_qkv, moment_out], axis=1).astype(low))
    columns = (last_cols[:, :qkv_half], last_cols[:, qkv_half:], up_cols, down_cols)

    place = me % GROUP
    gram = lax.switch(
        place,
        [
            lambda cols: matmul_nt(cols[0], cols[0]),
            lambda cols: matmul_nt(cols[1], cols[1]),
            lambda cols: matmul_nt(cols[2], cols[2]),
            lambda cols: matmul_nt(cols[3], cols[3]),
        ],
        columns,
    )
    gram = gram + swap_cores(gram)
    block_rows = D // size
    polar_rows = newton_schulz(gram, (me - place) * block_rows, GROUP * block_rows)
    polar_rows = polar_rows.reshape(GROUP, block_rows, D)
    arrived = []
    for offset in range(GROUP):
        block = lax.dynamic_index_in_dim(polar_rows, place ^ offset, 0, keepdims=False)
        if offset:
            block = lax.ppermute(block, "fsdp", [(i, i ^ offset) for i in range(size)])
        arrived.append(block)
    arrived = jnp.stack(arrived)
    masters = (w_qkv, w_out, w_up, w_down)
    counts_of = (3 * D, D, FF, FF)
    updated = []
    for index in range(GROUP):
        polar = lax.dynamic_index_in_dim(arrived, place ^ index, 0, keepdims=False)
        polar_high = polar.astype(low)
        polar_rest = (polar - polar_high.astype(jnp.float32)).astype(low)
        product = matmul(jnp.concatenate([polar_high, polar_rest], axis=0), columns[index])
        ortho = product[:block_rows] + product[block_rows:]
        updated.append(
            masters[index] * (1.0 - muon_rate * decay_rate)
            - muon_rate * 0.2 * math.sqrt(counts_of[index]) * ortho
        )

    first_moment = beta_first * adam_first + (1.0 - beta_first) * grad_vectors
    second_moment = beta_second * adam_second + (1.0 - beta_second) * grad_vectors * grad_vectors
    direction = (
        first_moment
        / (1.0 - beta_first**STEP)
        / (jnp.sqrt(second_moment / (1.0 - beta_second**STEP)) + adam_eps)
    )
    new_vectors = vectors - adam_rate * (direction + decay_rate * vectors)
    return (
        layer_out,
        input_grad,
        grad_qkv,
        grad_out,
        grad_up,
        grad_down,
        grad_vectors,
        moment_qkv,
        moment_out,
        moment_up,
        moment_down,
        updated[0],
        updated[1],
        updated[2],
        updated[3],
        first_moment,
        second_moment,
        new_vectors,
    )


def solution(mesh):
    size = mesh.shape["fsdp"]

    def run(*arrays):
        return per_device(size, *arrays)

    weight = P("fsdp", "row")
    vector = P("row", "fsdp")
    sample = P(("fsdp", "row"), None)
    return jax.shard_map(
        run,
        mesh=mesh,
        in_specs=(sample, sample, sample, P(("fsdp", "row")))
        + (weight,) * 4
        + (vector,)
        + (weight,) * 4
        + (vector,) * 2,
        out_specs=(sample, sample)
        + (weight,) * 4
        + (vector,)
        + (weight,) * 8
        + (vector,) * 3,
        check_vma=False,
    )
```

time: 4130 us -> 739 us (0.18)
  waiting for transfers between devices: 3460 us -> 253 us
  matrix products: 455 us -> 222 us
  starting transfers between devices: 4.91 us -> 67.5 us
  blocking collectives: 55.5 us -> 2.61 us
    all_gather x44 -> x0, waiting for transfers between devices: 2680 us -> none  [the longest x5 382 us: per_device(): lax.all_gather(iterate[3], 'fsdp', axis=0, tiled=True)]
    reduce_scatter x8 -> x0, waiting for transfers between devices: 600 us -> none  [the longest x1 177 us: reduce_grads(): lax.psum_scatter(grad_parts[3], 'fsdp', scatter_dimension=0, tiled=True)]
    dot_general x72 -> x23, matrix products: 315 us -> 120 us  [the longest x17 47.6 us: close_dot(): jnp.dot(former, latter, precision=lax.Precision.HIGH, preferred_element_t...]
    ppermute x0 -> x59, waiting for transfers between devices: none -> 144 us  [the longest x48 138 us: flip(): lax.ppermute(values, 'fsdp', [(i, i ^ 1 << bit) for i in range(size)])]
    psum x5 -> x0, waiting for transfers between devices: 70.6 us -> none  [per_device(): lax.psum((partial_value[0], partial_value[1], partial_value[2], partial_v...]
    ppermute x0 -> x59, starting transfers between devices: none -> 67.4 us  [the longest x48 62.3 us: flip(): lax.ppermute(values, 'fsdp', [(i, i ^ 1 << bit) for i in range(size)])]
    all_gather x6 -> x0, blocking collectives: 53.1 us -> none  [the longest x1 42.8 us: gather_weights(): lax.all_gather(halves[4], 'fsdp', axis=1, tiled=True)]
    unnamed x59 -> x2, waiting for transfers between devices: 115 us -> 109 us
  transfers between devices with their start and end apart: 58 -> 60, of which waited for: 57 -> 30; matrix products, arithmetic and copies ran while one was open for 11% -> 22% of each run, Pallas kernels for 0% -> 0%
where the time goes in v1:
time: 739 us; the launch traced here: 728 us
  waiting for transfers between devices  253 us (34%)
  matrix products  222 us (30%)
  other arithmetic  87.5 us (12%)
  local copies, waits for them, and re-layouts  77.9 us (11%)
  starting transfers between devices  67.5 us (9%)
  between operations  17.8 us (2%)
    ppermute x48, waiting for transfers between devices, flip(): lax.ppermute(values, 'fsdp', [(i, i ^ 1 << bit) for i in range(size)])  138 us
    unnamed x2, waiting for transfers between devices  109 us
    ppermute x48, starting transfers between devices, flip(): lax.ppermute(values, 'fsdp', [(i, i ^ 1 << bit) for i in range(size)])  62.3 us
    dot_general x17, matrix products, close_dot(): jnp.dot(former, latter, precision=lax.Precision.HIGH, preferred_element_t...  47.6 us
    dot_general x8, matrix products, matmul(): return jnp.dot(former, latter, preferred_element_type=jnp.float32)  36.5 us
    dot_general x5, matrix products, matmul_nt(): lax.dot_general(former, latter, (((1,), (1,)), ((), ())), preferred_eleme...  34 us
    dot_general x8, matrix products, matmul_tn(): lax.dot_general(former, latter, (((0,), (0,)), ((), ())), preferred_eleme...  31.6 us
    unnamed x202, local copies, waits for them, and re-layouts  23.7 us
  transfers between devices with their start and end apart: 60, of which 30 were waited for; matrix products, arithmetic and copies ran while one was open for 22% of the time, Pallas kernels for 0%

profile of v1, /device:TPU:0, one launch (start us, length us, event | category | flops | bytes accessed | tf_op | source)
XLA Modules:
  0.0 727.9 jit_solution(5440907182293936200)
XLA Ops:
  9.9 4.0 collective-permute-start
  23.5 5.7 collective-permute-start.1
  30.2 5.1 collective-permute-done.7
  36.7 3.8 collective-permute-done.1
  45.0 4.8 collective-permute-done.2
  59.9 3.9 collective-permute-done.5
  65.7 9.9 %collective-permute-done.11 = bf16[2,2,48,1664]{3,2,1,0:T(8,128)(2,1)S(1)} collective-permute-done((bf16[2,2,48,1664]{3,2,1,0:T(8,128)(2,1)S(1)}, bf16[2,2,48,1664]{3,2,1,0:T(8,128)(2,1)S(1)}, u32[]{:S(2)}, u32[]{:S(2)}) %collective-permute-start.11) | collective-permute-done | bytes 639008 | tf_op jit(solution)/shard_map/ppermute | solution.py:59
  85.3 19.7 %collective-permute-done.12 = bf16[2,2,2,48,1664]{4,3,1,0,2:T(8,128)(2,1)} collective-permute-done((bf16[2,2,2,48,1664]{4,3,1,0,2:T(8,128)(2,1)}, bf16[2,2,2,48,1664]{4,3,1,0,2:T(8,128)(2,1)}, u32[]{:S(2)}, u32[]{:S(2)}) %collective-permute-start.12) | collective-permute-done | bytes 1277984 | tf_op jit(solution)/shard_map/ppermute | solution.py:59
  110.3 3.2 slice.241
  118.4 3.2 slice.238
  126.8 4.0 convolution_bitcast_fusion
  130.8 3.7 copy-done.11
  138.7 5.5 fusion.14
  144.2 3.8 reshape.1194
  148.1 4.0 reshape.1195
  152.1 12.7 %fusion.12 = (f32[2,12,512]{2,1,0:T(8,128)S(1)}, f32[2,12,512,512]{2,3,1,0:T(8,128)}) fusion(pred[2,512]{1,0:T(4,128)(4,1)S(1)} %get-tuple-element.186, bf16[2,512,12,64]{1,0,3,2:T(2,128)(2,1)S(1)} %reshape.1196, bf16[2,512,12,64]{1,0,3,2:T(2,128)(2,1)} %reshape.1195), kind=kOutput, calls=%fused_computation.22 | convolution fusion | flops 824168448 | bytes 28361728 | tf_op jit(solution)/shard_map/cqhd,ckhd->chqk/dot_general | solution.py:165
  164.8 11.2 %fusion = f32[2,12,512]{2,1,0:T(8,128)S(1)} fusion(f32[2,12,512]{2,1,0:T(8,128)S(1)} %get-tuple-element.187, f32[2,12,512,512]{2,3,1,0:T(8,128)} %get-tuple-element.188, pred[2,512]{1,0:T(4,128)(4,1)S(1)} %get-tuple-element.186), kind=kLoop, calls=%fused_computation.7 | loop fusion | flops 25153536 | bytes 25265152 | tf_op jit(solution)/shard_map/reduce_sum | solution.py:254
  176.0 11.4 %fusion.57 = bf16[2,512,12,64]{1,3,2,0:T(8,128)(2,1)S(1)} fusion(f32[2,12,512]{2,1,0:T(8,128)S(1)} %fusion, f32[2,12,512]{2,1,0:T(8,128)S(1)} %get-tuple-element.187, f32[2,12,512,512]{2,3,1,0:T(8,128)} %get-tuple-element.188, pred[2,512]{1,0:T(4,128)(4,1)S(1)} %get-tuple-element.186, bf16[2,512,12,64]{1,0,3,2:T(2,128)(2,1)S(1)} %copy-done.12), kind=kOutput, calls=%fused_computation.112 | convolution fusion | flops 837550080 | bytes 28410880 | tf_op jit(solution)/shard_map/chqk,ckhd->cqhd/dot_general | solution.py:257
  199.6 12.5 %multiply_convert_fusion.1 = (bf16[1024,3072]{1,0:T(8,128)(2,1)}, f32[1024,3072]{1,0:T(8,128)}) fusion(f32[3072]{0:T(1024)S(1)} %add.389, bf16[1024,768]{0,1:T(8,128)(2,1)S(1)} %fusion.29, bf16[768,1536]{1,0:T(8,128)(2,1)S(1)} %slice.239, bf16[768,1536]{1,0:T(8,128)(2,1)S(1)} %copy-done.31, pred[]{:T(512)S(6)} %eq.26), kind=kOutput, calls=%fused_computation.19 | convolution fusion | flops 4871946240 | bytes 25178112 | tf_op jit(solution)/shard_map/dot_general | solution.py:37
  212.1 8.1 %fusion.264 = (f32[1024]{0:T(1024)S(1)}, f32[1024,768]{0,1:T(8,128)S(1)}) fusion(f32[768]{0:T(1024)S(1)} %get-tuple-element.91, bf16[1024,3072]{1,0:T(8,128)(2,1)} %get-tuple-element.191, bf16[768,1536]{1,0:T(8,128)(2,1)S(1)} %slice.242, bf16[768,1536]{1,0:T(8,128)(2,1)S(1)} %copy-done.30, pred[]{:T(512)S(6)} %eq.26, f32[768]{0:T(1024)S(1)} %get-tuple-element.92, ...), kind=kOutput, calls=%fused_computation.498 | convolution fusion | flops 4858575872 | bytes 17323008 | tf_op jit(solution)/shard_map/dot_general | solution.py:47
  222.9 3.3 convert_reduce_fusion.1
  226.3 16.6 %convert_reduce_fusion = (f32[3072]{0:T(1024)}, bf16[1024,3072]{1,0:T(8,128)(2,1)}) fusion(f32[1024,3072]{1,0:T(8,128)} %get-tuple-element.192, f32[3072]{0:T(1024)S(1)} %add.389, bf16[1024,768]{0,1:T(8,128)(2,1)S(1)} %get-tuple-element.124, bf16[768,1536]{1,0:T(8,128)(2,1)S(1)} %slice.242, bf16[768,1536]{1,0:T(8,128)(2,1)S(1)} %copy-done.30, pred[]{:T(512)S(6)} %eq.26), kind=kOutput, calls=%fused_computation.17 | convolution fusion | flops 4893963264 | bytes 25190400 | tf_op jit(solution)/shard_map/dot_general | solution.py:37
  242.9 10.6 %multiply_reduce_fusion.2 = (f32[768]{0:T(1024)}, f32[1024]{0:T(1024)S(1)}, f32[1024]{0:T(1024)S(1)}, f32[768]{0:T(1024)}, f32[1024,768]{0,1:T(8,128)S(1)}) fusion(f32[1024,768]{0,1:T(8,128)S(1)} %get-tuple-element.190, f32[1024]{0:T(1024)S(1)} %add_rsqrt_fusion.1, f32[1024]{0:T(1024)S(1)} %broadcast_multiply_fusion.5, f32[768]{0:T(1024)S(1)} %get-tuple-element.93, ...), kind=kOutput, calls=%fused_computation.46 | convolution fusion | flops 4868009984 | bytes 22069248 | tf_op jit(solution)/shard_map/dot_general | solution.py:47
  263.2 12.6 %convert_reduce_fusion.3 = (f32[12,64]{1,0:T(8,128)S(1)}, bf16[2,512,12,64]{1,3,2,0:T(8,128)(2,1)}) fusion(f32[2,12,512]{2,1,0:T(8,128)S(1)} %log_add_fusion, f32[2,12,512,512]{2,3,1,0:T(8,128)} %get-tuple-element.188, pred[2,512]{1,0:T(4,128)(4,1)S(1)} %get-tuple-element.186, bf16[2,512,12,64]{1,0,3,2:T(2,128)(2,1)} %reshape.1198), kind=kOutput, calls=%fused_computation.48 | convolution fusion | flops 832830720 | bytes 28364800 | tf_op jit(solution)/shard_map/chqk,cqhd->ckhd/dot_general | solution.py:302
  275.9 19.7 %multiply_reduce_fusion = (f32[2,12,512]{2,1,0:T(8,128)S(1)}, f32[2,12,512,512]{2,3,1,0:T(8,128)}) fusion(f32[2,12,512]{2,1,0:T(8,128)S(1)} %log_add_fusion, f32[2,12,512,512]{2,3,1,0:T(8,128)} %get-tuple-element.188, pred[2,512]{1,0:T(4,128)(4,1)S(1)} %get-tuple-element.186, bf16[2,512,12,64]{1,0,3,2:T(2,128)(2,1)S(1)} %copy-done.12, ...), kind=kOutput, calls=%fused_computation.2 | convolution fusion | flops 836751360 | bytes 53576704 | tf_op jit(solution)/shard_map/cqhd,ckhd->chqk/dot_general | solution.py:299
  295.6 22.1 %multiply_convert_fusion = bf16[2,12,512,512]{2,3,1,0:T(8,128)(2,1)} fusion(f32[2,12,512,512]{2,3,1,0:T(8,128)} %get-tuple-element.197, f32[2,12,512]{2,1,0:T(8,128)S(1)} %get-tuple-element.196, f32[2,12,512]{2,1,0:T(8,128)S(1)} %log_add_fusion, f32[2,12,512,512]{2,3,1,0:T(8,128)} %get-tuple-element.188, pred[2,512]{1,0:T(4,128)(4,1)S(1)} %get-tuple-element.186), kind=kLoop, calls=%fused_computation.1 | loop fusion | flops 37748736 | bytes 63013888 | tf_op jit(solution)/shard_map/convert_element_type | solution.py:306
  317.7 8.6 %fusion.56 = bf16[2,512,12,64]{1,3,2,0:T(8,128)(2,1)S(1)} fusion(bf16[2,12,512,512]{2,3,1,0:T(8,128)(2,1)} %multiply_convert_fusion, bf16[2,512,12,64]{1,0,3,2:T(2,128)(2,1)S(1)} %copy-done.6), kind=kOutput, calls=%fused_computation.111 | convolution fusion | flops 806879232 | bytes 15728640 | tf_op jit(solution)/shard_map/chqk,cqhd->ckhd/dot_general | solution.py:312
  326.3 6.9 convert_reduce_fusion.4
  341.0 3.8 fusion.28
  344.9 6.6 convolution_convert_fusion
  353.8 5.1 convolution_convert_fusion.1
  361.7 4.7 convert_add_fusion.2
  369.6 4.3 convert_add_fusion
  376.2 7.0 collective-permute-done.19
  389.3 13.4 %collective-permute-done.20 = bf16[2,2,48,768]{3,2,0,1:T(8,128)(2,1)S(1)} collective-permute-done((bf16[2,2,48,768]{3,2,0,1:T(8,128)(2,1)S(1)}, bf16[2,2,48,768]{3,2,0,1:T(8,128)(2,1)S(1)}, u32[]{:S(2)}, u32[]{:S(2)}) %collective-permute-start.20) | collective-permute-done | bytes 294944 | tf_op jit(solution)/shard_map/ppermute | solution.py:59
  405.1 5.7 collective-permute-done.21
  414.3 5.4 collective-permute-done.26
  423.6 3.1 collective-permute-start.37
  426.8 4.3 collective-permute-done.37
  435.9 5.4 collective-permute-done.38
  454.6 6.8 collective-permute-done.36
  473.7 3.6 collective-permute-done.50
  481.8 5.0 collective-permute-done.51
  493.4 3.4 collective-permute-done.47
  501.3 8.1 %collective-permute-done.52 = bf16[2,2,2,48,768]{4,3,1,0,2:T(8,128)(2,1)S(1)} collective-permute-done((bf16[2,2,2,48,768]{4,3,1,0,2:T(8,128)(2,1)S(1)}, bf16[2,2,2,48,768]{4,3,1,0,2:T(8,128)(2,1)S(1)}, u32[]{:S(2)}, u32[]{:S(2)}) %collective-permute-start.52) | collective-permute-done | bytes 589856 | tf_op jit(solution)/shard_map/ppermute | solution.py:59
  510.1 5.9 collective-permute-done.46
  520.3 3.3 conditional.1
  520.3 3.2 fusion.265
  526.3 9.5 %convolution_add_fusion.1 = f32[1024,768]{0,1:T(8,128)} fusion(bf16[1024,2304]{0,1:T(8,128)(2,1)} %copy-done.52, bf16[768,1152]{1,0:T(8,128)(2,1)} %copy-done.33, bf16[768,1152]{1,0:T(8,128)(2,1)} %fusion.47, pred[]{:T(512)S(6)} %eq.26, f32[1024]{0:T(1024)S(1)} %copy-done.79, f32[1024,768]{0,1:T(8,128)S(1)} %copy-done.3, f32[1024]{0:T(1024)S(1)} %copy-done.68, ...), kind=kOutput, calls=%fused_computation.105 | convolution fusion | flops 3646095360 | bytes 17714176 | tf_op jit(solution)/shard_map/dot_general | solution.py:47
  540.9 108.9 %reduce-scatter.4.cloned.1.call-done = f32[48,12]{1,0:T(8,128)} async-done(((f32[768,12]{1,0:T(8,128)}), f32[48,12]{1,0:T(8,128)}) %reduce-scatter.4.cloned.1.call-update) | async-done | bytes 2320
  653.2 3.3 select_reduce_fusion
  657.1 3.3 select_add_fusion.4
  663.6 3.2 fusion.269
  666.7 3.4 fusion.270
  670.1 3.4 fusion.39
  674.7 3.2 fusion.38
  677.9 3.1 fusion.271
  681.1 3.8 fusion.42
  686.1 3.2 fusion.41
  689.3 3.1 fusion.272
  692.5 3.6 fusion.45
  697.3 3.2 fusion.44
  700.5 3.2 fusion.273
  709.2 3.5 collective-permute-done.58
  (496 shorter events, 199.8 us)
Async XLA Ops:
  7.2 642.5 %reduce-scatter.4.cloned.1.call-start = ((), (), s32[]{:S(2)}) async-start(), calls=%async_computation.1 | async-start | bytes 417792
  9.9 12.6 %collective-permute-start = (bf16[48,1280]{1,0:T(8,128)(2,1)}, bf16[48,1280]{1,0:T(8,128)(2,1)}, u32[]{:S(2)}, u32[]{:S(2)}) collective-permute-start(bf16[48,1280]{1,0:T(8,128)(2,1)} %get-tuple-element.184), channel_id=1, source_target_pairs={{0,16},{2,18},{4,20},{6,22},{8,24},{10,26},{12,28},{14,30},{16,0},... | collective-permute-start | bytes 368648 | tf_op jit(solution)/shard_map/ppermute | solution.py:59
  17.7 17.7 %collective-permute-start.7 = (bf16[48,3456]{1,0:T(8,128)(2,1)}, bf16[48,3456]{1,0:T(8,128)(2,1)}, u32[]{:S(2)}, u32[]{:S(2)}) collective-permute-start(bf16[48,3456]{1,0:T(8,128)(2,1)} %get-tuple-element.178), channel_id=1, source_target_pairs={{0,16},{2,18},{4,20},{6,22},{8,24},{10,26},{12,28},{14,30},{16,0},... | collective-permute-start | bytes 995336 | tf_op jit(solution)/shard_map/ppermute | solution.py:59
  23.5 17.0 %collective-permute-start.1 = (bf16[2,48,1280]{2,1,0:T(8,128)(2,1)S(1)}, bf16[2,48,1280]{2,1,0:T(8,128)(2,1)S(1)}, u32[]{:S(2)}, u32[]{:S(2)}) collective-permute-start(bf16[2,48,1280]{2,1,0:T(8,128)(2,1)S(1)} %maximum_select_fusion.49), channel_id=1, source_target_pairs={{0,8},{2,10},{4,12},{6,14},{8,0},{10,2},{12,4},{14,6},{16,24},{18,... | collective-permute-start | bytes 737288 | tf_op jit(solution)/shard_map/ppermute | solution.py:59
  36.6 18.0 %collective-permute-start.8 = (bf16[2,48,3456]{2,1,0:T(8,128)(2,1)S(1)}, bf16[2,48,3456]{2,1,0:T(8,128)(2,1)S(1)}, u32[]{:S(2)}, u32[]{:S(2)}) collective-permute-start(bf16[2,48,3456]{2,1,0:T(8,128)(2,1)S(1)} %maximum_select_fusion.23), channel_id=1, source_target_pairs={{0,8},{2,10},{4,12},{6,14},{8,0},{10,2},{12,4},{14,6},{16,24},{18,... | collective-permute-start | bytes 1990664 | tf_op jit(solution)/shard_map/ppermute | solution.py:59
  40.7 9.8 %collective-permute-start.4 = (bf16[2,2,48,640]{3,2,1,0:T(8,128)(2,1)S(1)}, bf16[2,2,48,640]{3,2,1,0:T(8,128)(2,1)S(1)}, u32[]{:S(2)}, u32[]{:S(2)}) collective-permute-start(bf16[2,2,48,640]{3,2,1,0:T(8,128)(2,1)S(1)} %get-tuple-element.174), channel_id=1, source_target_pairs={{0,2},{2,0},{4,6},{6,4},{8,10},{10,8},{12,14},{14,12},{16,18},{18,... | collective-permute-start | bytes 737288 | tf_op jit(solution)/shard_map/ppermute | solution.py:59
  42.2 7.6 %collective-permute-start.2 = (bf16[2,2,48,640]{3,2,1,0:T(8,128)(2,1)S(1)}, bf16[2,2,48,640]{3,2,1,0:T(8,128)(2,1)S(1)}, u32[]{:S(2)}, u32[]{:S(2)}) collective-permute-start(bf16[2,2,48,640]{3,2,1,0:T(8,128)(2,1)S(1)} %get-tuple-element.175), channel_id=1, source_target_pairs={{0,4},{2,6},{4,0},{6,2},{8,12},{10,14},{12,8},{14,10},{16,20},{18,... | collective-permute-start | bytes 737288 | tf_op jit(solution)/shard_map/ppermute | solution.py:59
  49.9 14.2 %collective-permute-start.3 = (bf16[2,2,2,48,640]{4,3,1,0,2:T(8,128)(2,1)S(1)}, bf16[2,2,2,48,640]{4,3,1,0,2:T(8,128)(2,1)S(1)}, u32[]{:S(2)}, u32[]{:S(2)}) collective-permute-start(bf16[2,2,2,48,640]{4,3,1,0,2:T(8,128)(2,1)S(1)} %maximum_select_fusion.41), channel_id=1, source_target_pairs={{0,2},{2,0},{4,6},{6,4},{8,10},{10,8},{12,14},{14,12},{16,18},{18,... | collective-permute-start | bytes 1474568 | tf_op jit(solution)/shard_map/ppermute | solution.py:59
  50.6 13.2 %collective-permute-start.5 = (bf16[2,2,2,48,640]{4,3,1,0,2:T(8,128)(2,1)S(1)}, bf16[2,2,2,48,640]{4,3,1,0,2:T(8,128)(2,1)S(1)}, u32[]{:S(2)}, u32[]{:S(2)}) collective-permute-start(bf16[2,2,2,48,640]{4,3,1,0,2:T(8,128)(2,1)S(1)} %maximum_select_fusion.43), channel_id=1, source_target_pairs={{0,4},{2,6},{4,0},{6,2},{8,12},{10,14},{12,8},{14,10},{16,20},{18,... | collective-permute-start | bytes 1474568 | tf_op jit(solution)/shard_map/ppermute | solution.py:59
  55.9 19.7 %collective-permute-start.11 = (bf16[2,2,48,1664]{3,2,1,0:T(8,128)(2,1)S(1)}, bf16[2,2,48,1664]{3,2,1,0:T(8,128)(2,1)S(1)}, u32[]{:S(2)}, u32[]{:S(2)}) collective-permute-start(bf16[2,2,48,1664]{3,2,1,0:T(8,128)(2,1)S(1)} %get-tuple-element.141), channel_id=1, source_target_pairs={{0,2},{2,0},{4,6},{6,4},{8,10},{10,8},{12,14},{14,12},{16,18},{18,... | collective-permute-start | bytes 1916936 | tf_op jit(solution)/shard_map/ppermute | solution.py:59
  58.4 20.0 %collective-permute-start.9 = (bf16[2,2,48,1792]{3,2,1,0:T(8,128)(2,1)S(1)}, bf16[2,2,48,1792]{3,2,1,0:T(8,128)(2,1)S(1)}, u32[]{:S(2)}, u32[]{:S(2)}) collective-permute-start(bf16[2,2,48,1792]{3,2,1,0:T(8,128)(2,1)S(1)} %get-tuple-element.138), channel_id=1, source_target_pairs={{0,4},{2,6},{4,0},{6,2},{8,12},{10,14},{12,8},{14,10},{16,20},{18,... | collective-permute-start | bytes 2064392 | tf_op jit(solution)/shard_map/ppermute | solution.py:59
  65.7 56.5 %collective-permute-start.6 = (bf16[768,1280]{1,0:T(8,128)(2,1)}, bf16[768,1280]{1,0:T(8,128)(2,1)}, u32[]{:S(2)}, u32[]{:S(2)}) collective-permute-start(bf16[768,1280]{1,0:T(8,128)(2,1)} %pad_maximum_fusion.3), channel_id=1, source_target_pairs={{0,1},{1,0},{2,3},{3,2},{4,5},{5,4},{6,7},{7,6},{8,9},{9,8},{10,11... | collective-permute-start | bytes 5898248 | tf_op jit(solution)/shard_map/ppermute | solution.py:63
  76.9 28.2 %collective-permute-start.12 = (bf16[2,2,2,48,1664]{4,3,1,0,2:T(8,128)(2,1)}, bf16[2,2,2,48,1664]{4,3,1,0,2:T(8,128)(2,1)}, u32[]{:S(2)}, u32[]{:S(2)}) collective-permute-start(bf16[2,2,2,48,1664]{4,3,1,0,2:T(8,128)(2,1)} %maximum_select_fusion.8), channel_id=1, source_target_pairs={{0,4},{2,6},{4,0},{6,2},{8,12},{10,14},{12,8},{14,10},{16,20},{18,... | collective-permute-start | bytes 3833864 | tf_op jit(solution)/shard_map/ppermute | solution.py:59
  80.5 33.0 %collective-permute-start.10 = (bf16[2,2,2,48,1792]{4,3,1,0,2:T(8,128)(2,1)}, bf16[2,2,2,48,1792]{4,3,1,0,2:T(8,128)(2,1)}, u32[]{:S(2)}, u32[]{:S(2)}) collective-permute-start(bf16[2,2,2,48,1792]{4,3,1,0,2:T(8,128)(2,1)} %maximum_select_fusion.5), channel_id=1, source_target_pairs={{0,2},{2,0},{4,6},{6,4},{8,10},{10,8},{12,14},{14,12},{16,18},{18,... | collective-permute-start | bytes 4128776 | tf_op jit(solution)/shard_map/ppermute | solution.py:59
  113.5 76.1 %collective-permute-start.14 = (bf16[768,1664]{1,0:T(8,128)(2,1)}, bf16[768,1664]{1,0:T(8,128)(2,1)}, u32[]{:S(2)}, u32[]{:S(2)}) collective-permute-start(bf16[768,1664]{1,0:T(8,128)(2,1)} %bitcast.38), channel_id=1, source_target_pairs={{0,1},{1,0},{2,3},{3,2},{4,5},{5,4},{6,7},{7,6},{8,9},{9,8},{10,11... | collective-permute-start | bytes 7667720 | tf_op jit(solution)/shard_map/ppermute | solution.py:63
  121.7 71.1 %collective-permute-start.13 = (bf16[768,1792]{1,0:T(8,128)(2,1)}, bf16[768,1792]{1,0:T(8,128)(2,1)}, u32[]{:S(2)}, u32[]{:S(2)}) collective-permute-start(bf16[768,1792]{1,0:T(8,128)(2,1)} %bitcast.32), channel_id=1, source_target_pairs={{0,1},{1,0},{2,3},{3,2},{4,5},{5,4},{6,7},{7,6},{8,9},{9,8},{10,11... | collective-permute-start | bytes 8257544 | tf_op jit(solution)/shard_map/ppermute | solution.py:63
  124.8 128.7 %copy-start.69 = (f32[768]{0:T(1024)}, f32[768]{0:T(1024)S(1)}, u32[]{:S(2)}) copy-start(f32[768]{0:T(1024)S(1)} %get-tuple-element.93) | copy-start | bytes 9220
  195.6 57.9 %copy-start.2 = (f32[1024,768]{0,1:T(8,128)}, f32[1024,768]{0,1:T(8,128)S(1)}, u32[]{:S(2)}) copy-start(f32[1024,768]{0,1:T(8,128)S(1)} %get-tuple-element.190) | copy-start | bytes 9437188
  195.6 57.9 %copy-start.67 = (f32[1024]{0:T(1024)}, f32[1024]{0:T(1024)S(1)}, u32[]{:S(2)}) copy-start(f32[1024]{0:T(1024)S(1)} %broadcast_multiply_fusion.5) | copy-start | bytes 12292
  196.0 57.5 %copy-start.71 = (f32[1024]{0:T(1024)}, f32[1024]{0:T(1024)S(1)}, u32[]{:S(2)}) copy-start(f32[1024]{0:T(1024)S(1)} %add_rsqrt_fusion.1) | copy-start | bytes 12292
  344.8 16.9 %collective-permute-start.15 = (bf16[768,1152]{1,0:T(8,128)(2,1)}, bf16[768,1152]{1,0:T(8,128)(2,1)}, u32[]{:S(2)}, u32[]{:S(2)}) collective-permute-start(bf16[768,1152]{1,0:T(8,128)(2,1)} %fusion.28), channel_id=1, source_target_pairs={{0,1},{1,0},{2,3},{3,2},{4,5},{5,4},{6,7},{7,6},{8,9},{9,8},{10,11... | collective-permute-start | bytes 5308424 | tf_op jit(solution)/shard_map/ppermute | solution.py:63
  351.5 18.1 %collective-permute-start.30 = (bf16[768,1536]{1,0:T(8,128)(2,1)}, bf16[768,1536]{1,0:T(8,128)(2,1)}, u32[]{:S(2)}, u32[]{:S(2)}) collective-permute-start(bf16[768,1536]{1,0:T(8,128)(2,1)} %convolution_convert_fusion), channel_id=1, source_target_pairs={{0,1},{1,0},{2,3},{3,2},{4,5},{5,4},{6,7},{7,6},{8,9},{9,8},{10,11... | collective-permute-start | bytes 7077896 | tf_op jit(solution)/shard_map/ppermute | solution.py:63
  353.7 5.7 collective-permute-start.18
  358.9 27.3 %collective-permute-start.23 = (bf16[768,1536]{1,0:T(8,128)(2,1)S(1)}, bf16[768,1536]{1,0:T(8,128)(2,1)S(1)}, u32[]{:S(2)}, u32[]{:S(2)}) collective-permute-start(bf16[768,1536]{1,0:T(8,128)(2,1)S(1)} %convolution_convert_fusion.1), channel_id=1, source_target_pairs={{0,1},{1,0},{2,3},{3,2},{4,5},{5,4},{6,7},{7,6},{8,9},{9,8},{10,11... | collective-permute-start | bytes 7077896 | tf_op jit(solution)/shard_map/ppermute | solution.py:63
  366.9 16.2 %collective-permute-start.19 = (bf16[2,2,2,48,768]{4,3,0,1,2:T(8,128)(2,1)S(1)}, bf16[2,2,2,48,768]{4,3,0,1,2:T(8,128)(2,1)S(1)}, u32[]{:S(2)}, u32[]{:S(2)}) collective-permute-start(bf16[2,2,2,48,768]{4,3,0,1,2:T(8,128)(2,1)S(1)} %fusion.116), channel_id=1, source_target_pairs={{0,4},{2,6},{4,0},{6,2},{8,12},{10,14},{12,8},{14,10},{16,20},{18,... | collective-permute-start | bytes 1769480 | tf_op jit(solution)/shard_map/ppermute | solution.py:59
  368.5 16.3 %collective-permute-start.16 = (bf16[2,2,2,48,768]{4,3,0,1,2:T(8,128)(2,1)S(1)}, bf16[2,2,2,48,768]{4,3,0,1,2:T(8,128)(2,1)S(1)}, u32[]{:S(2)}, u32[]{:S(2)}) collective-permute-start(bf16[2,2,2,48,768]{4,3,0,1,2:T(8,128)(2,1)S(1)} %fusion.115), channel_id=1, source_target_pairs={{0,2},{2,0},{4,6},{6,4},{8,10},{10,8},{12,14},{14,12},{16,18},{18,... | collective-permute-start | bytes 1769480 | tf_op jit(solution)/shard_map/ppermute | solution.py:59
  374.5 37.8 %collective-permute-start.33 = (bf16[2,2,2,48,768]{4,3,0,1,2:T(8,128)(2,1)S(1)}, bf16[2,2,2,48,768]{4,3,0,1,2:T(8,128)(2,1)S(1)}, u32[]{:S(2)}, u32[]{:S(2)}) collective-permute-start(bf16[2,2,2,48,768]{4,3,0,1,2:T(8,128)(2,1)S(1)} %fusion.120), channel_id=1, source_target_pairs={{0,4},{2,6},{4,0},{6,2},{8,12},{10,14},{12,8},{14,10},{16,20},{18,... | collective-permute-start | bytes 1769480 | tf_op jit(solution)/shard_map/ppermute | solution.py:59
  375.1 38.5 %collective-permute-start.31 = (bf16[2,2,2,48,768]{4,3,0,1,2:T(8,128)(2,1)S(1)}, bf16[2,2,2,48,768]{4,3,0,1,2:T(8,128)(2,1)S(1)}, u32[]{:S(2)}, u32[]{:S(2)}) collective-permute-start(bf16[2,2,2,48,768]{4,3,0,1,2:T(8,128)(2,1)S(1)} %fusion.119), channel_id=1, source_target_pairs={{0,2},{2,0},{4,6},{6,4},{8,10},{10,8},{12,14},{14,12},{16,18},{18,... | collective-permute-start | bytes 1769480 | tf_op jit(solution)/shard_map/ppermute | solution.py:59
  383.3 19.3 %collective-permute-start.20 = (bf16[2,2,48,768]{3,2,0,1:T(8,128)(2,1)S(1)}, bf16[2,2,48,768]{3,2,0,1:T(8,128)(2,1)S(1)}, u32[]{:S(2)}, u32[]{:S(2)}) collective-permute-start(bf16[2,2,48,768]{3,2,0,1:T(8,128)(2,1)S(1)} %fusion.138), channel_id=1, source_target_pairs={{0,2},{2,0},{4,6},{6,4},{8,10},{10,8},{12,14},{14,12},{16,18},{18,... | collective-permute-start | bytes 884744 | tf_op jit(solution)/shard_map/ppermute | solution.py:59
  385.0 17.7 %collective-permute-start.17 = (bf16[2,2,48,768]{3,2,0,1:T(8,128)(2,1)S(1)}, bf16[2,2,48,768]{3,2,0,1:T(8,128)(2,1)S(1)}, u32[]{:S(2)}, u32[]{:S(2)}) collective-permute-start(bf16[2,2,48,768]{3,2,0,1:T(8,128)(2,1)S(1)} %fusion.137), channel_id=1, source_target_pairs={{0,4},{2,6},{4,0},{6,2},{8,12},{10,14},{12,8},{14,10},{16,20},{18,... | collective-permute-start | bytes 884744 | tf_op jit(solution)/shard_map/ppermute | solution.py:59
  402.8 7.9 %collective-permute-start.21 = (bf16[2,48,1536]{2,1,0:T(8,128)(2,1)S(1)}, bf16[2,48,1536]{2,1,0:T(8,128)(2,1)S(1)}, u32[]{:S(2)}, u32[]{:S(2)}) collective-permute-start(bf16[2,48,1536]{2,1,0:T(8,128)(2,1)S(1)} %fusion.143), channel_id=1, source_target_pairs={{0,8},{2,10},{4,12},{6,14},{8,0},{10,2},{12,4},{14,6},{16,24},{18,... | collective-permute-start | bytes 884744 | tf_op jit(solution)/shard_map/ppermute | solution.py:59
  403.3 16.3 %collective-permute-start.26 = (bf16[2,2,2,48,768]{4,3,0,1,2:T(8,128)(2,1)S(1)}, bf16[2,2,2,48,768]{4,3,0,1,2:T(8,128)(2,1)S(1)}, u32[]{:S(2)}, u32[]{:S(2)}) collective-permute-start(bf16[2,2,2,48,768]{4,3,0,1,2:T(8,128)(2,1)S(1)} %fusion.118), channel_id=1, source_target_pairs={{0,4},{2,6},{4,0},{6,2},{8,12},{10,14},{12,8},{14,10},{16,20},{18,... | collective-permute-start | bytes 1769480 | tf_op jit(solution)/shard_map/ppermute | solution.py:59
  404.0 17.0 %collective-permute-start.24 = (bf16[2,2,2,48,768]{4,3,0,1,2:T(8,128)(2,1)S(1)}, bf16[2,2,2,48,768]{4,3,0,1,2:T(8,128)(2,1)S(1)}, u32[]{:S(2)}, u32[]{:S(2)}) collective-permute-start(bf16[2,2,2,48,768]{4,3,0,1,2:T(8,128)(2,1)S(1)} %fusion.117), channel_id=1, source_target_pairs={{0,2},{2,0},{4,6},{6,4},{8,10},{10,8},{12,14},{14,12},{16,18},{18,... | collective-permute-start | bytes 1769480 | tf_op jit(solution)/shard_map/ppermute | solution.py:59
  410.9 11.2 %collective-permute-start.22 = (bf16[48,1536]{1,0:T(8,128)(2,1)S(1)}, bf16[48,1536]{1,0:T(8,128)(2,1)S(1)}, u32[]{:S(2)}, u32[]{:S(2)}) collective-permute-start(bf16[48,1536]{1,0:T(8,128)(2,1)S(1)} %fusion.154), channel_id=1, source_target_pairs={{0,16},{2,18},{4,20},{6,22},{8,24},{10,26},{12,28},{14,30},{16,0},... | collective-permute-start | bytes 442376 | tf_op jit(solution)/shard_map/ppermute | solution.py:59
  412.4 20.9 %collective-permute-start.34 = (bf16[2,2,48,768]{3,2,0,1:T(8,128)(2,1)S(1)}, bf16[2,2,48,768]{3,2,0,1:T(8,128)(2,1)S(1)}, u32[]{:S(2)}, u32[]{:S(2)}) collective-permute-start(bf16[2,2,48,768]{3,2,0,1:T(8,128)(2,1)S(1)} %fusion.142), channel_id=1, source_target_pairs={{0,2},{2,0},{4,6},{6,4},{8,10},{10,8},{12,14},{14,12},{16,18},{18,... | collective-permute-start | bytes 884744 | tf_op jit(solution)/shard_map/ppermute | solution.py:59
  413.7 19.7 %collective-permute-start.32 = (bf16[2,2,48,768]{3,2,0,1:T(8,128)(2,1)S(1)}, bf16[2,2,48,768]{3,2,0,1:T(8,128)(2,1)S(1)}, u32[]{:S(2)}, u32[]{:S(2)}) collective-permute-start(bf16[2,2,48,768]{3,2,0,1:T(8,128)(2,1)S(1)} %fusion.141), channel_id=1, source_target_pairs={{0,4},{2,6},{4,0},{6,2},{8,12},{10,14},{12,8},{14,10},{16,20},{18,... | collective-permute-start | bytes 884744 | tf_op jit(solution)/shard_map/ppermute | solution.py:59
  419.9 13.8 %collective-permute-start.27 = (bf16[2,2,48,768]{3,2,0,1:T(8,128)(2,1)S(1)}, bf16[2,2,48,768]{3,2,0,1:T(8,128)(2,1)S(1)}, u32[]{:S(2)}, u32[]{:S(2)}) collective-permute-start(bf16[2,2,48,768]{3,2,0,1:T(8,128)(2,1)S(1)} %fusion.140), channel_id=1, source_target_pairs={{0,2},{2,0},{4,6},{6,4},{8,10},{10,8},{12,14},{14,12},{16,18},{18,... | collective-permute-start | bytes 884744 | tf_op jit(solution)/shard_map/ppermute | solution.py:59
  421.1 12.6 %collective-permute-start.25 = (bf16[2,2,48,768]{3,2,0,1:T(8,128)(2,1)S(1)}, bf16[2,2,48,768]{3,2,0,1:T(8,128)(2,1)S(1)}, u32[]{:S(2)}, u32[]{:S(2)}) collective-permute-start(bf16[2,2,48,768]{3,2,0,1:T(8,128)(2,1)S(1)} %fusion.139), channel_id=1, source_target_pairs={{0,4},{2,6},{4,0},{6,2},{8,12},{10,14},{12,8},{14,10},{16,20},{18,... | collective-permute-start | bytes 884744 | tf_op jit(solution)/shard_map/ppermute | solution.py:59
  423.6 7.4 %collective-permute-start.37 = (bf16[48,1536]{1,0:T(8,128)(2,1)S(1)}, bf16[48,1536]{1,0:T(8,128)(2,1)S(1)}, u32[]{:S(2)}, u32[]{:S(2)}) collective-permute-start(bf16[48,1536]{1,0:T(8,128)(2,1)S(1)} %pad_maximum_fusion.9), channel_id=1, source_target_pairs={{0,16},{2,18},{4,20},{6,22},{8,24},{10,26},{12,28},{14,30},{16,0},... | collective-permute-start | bytes 442376 | tf_op jit(solution)/shard_map/ppermute | solution.py:59
  431.1 10.2 %collective-permute-start.38 = (bf16[2,48,1536]{2,1,0:T(8,128)(2,1)S(1)}, bf16[2,48,1536]{2,1,0:T(8,128)(2,1)S(1)}, u32[]{:S(2)}, u32[]{:S(2)}) collective-permute-start(bf16[2,48,1536]{2,1,0:T(8,128)(2,1)S(1)} %maximum_select_fusion.45), channel_id=1, source_target_pairs={{0,8},{2,10},{4,12},{6,14},{8,0},{10,2},{12,4},{14,6},{16,24},{18,... | collective-permute-start | bytes 884744 | tf_op jit(solution)/shard_map/ppermute | solution.py:59
  433.6 13.7 %collective-permute-start.35 = (bf16[2,48,1536]{2,1,0:T(8,128)(2,1)S(1)}, bf16[2,48,1536]{2,1,0:T(8,128)(2,1)S(1)}, u32[]{:S(2)}, u32[]{:S(2)}) collective-permute-start(bf16[2,48,1536]{2,1,0:T(8,128)(2,1)S(1)} %fusion.145), channel_id=1, source_target_pairs={{0,8},{2,10},{4,12},{6,14},{8,0},{10,2},{12,4},{14,6},{16,24},{18,... | collective-permute-start | bytes 884744 | tf_op jit(solution)/shard_map/ppermute | solution.py:59
  433.8 17.9 %collective-permute-start.28 = (bf16[2,48,1536]{2,1,0:T(8,128)(2,1)S(1)}, bf16[2,48,1536]{2,1,0:T(8,128)(2,1)S(1)}, u32[]{:S(2)}, u32[]{:S(2)}) collective-permute-start(bf16[2,48,1536]{2,1,0:T(8,128)(2,1)S(1)} %fusion.144), channel_id=1, source_target_pairs={{0,8},{2,10},{4,12},{6,14},{8,0},{10,2},{12,4},{14,6},{16,24},{18,... | collective-permute-start | bytes 884744 | tf_op jit(solution)/shard_map/ppermute | solution.py:59
  441.5 24.6 %collective-permute-start.39 = (bf16[2,2,48,768]{3,2,1,0:T(8,128)(2,1)S(1)}, bf16[2,2,48,768]{3,2,1,0:T(8,128)(2,1)S(1)}, u32[]{:S(2)}, u32[]{:S(2)}) collective-permute-start(bf16[2,2,48,768]{3,2,1,0:T(8,128)(2,1)S(1)} %copy.301), channel_id=1, source_target_pairs={{0,4},{2,6},{4,0},{6,2},{8,12},{10,14},{12,8},{14,10},{16,20},{18,... | collective-permute-start | bytes 884744 | tf_op jit(solution)/shard_map/ppermute | solution.py:59
  444.3 23.1 %collective-permute-start.41 = (bf16[2,2,48,768]{3,2,0,1:T(8,128)(2,1)S(1)}, bf16[2,2,48,768]{3,2,0,1:T(8,128)(2,1)S(1)}, u32[]{:S(2)}, u32[]{:S(2)}) collective-permute-start(bf16[2,2,48,768]{3,2,0,1:T(8,128)(2,1)S(1)} %get-tuple-element.169), channel_id=1, source_target_pairs={{0,2},{2,0},{4,6},{6,4},{8,10},{10,8},{12,14},{14,12},{16,18},{18,... | collective-permute-start | bytes 884744 | tf_op jit(solution)/shard_map/ppermute | solution.py:59
  447.4 14.0 %collective-permute-start.36 = (bf16[48,1536]{1,0:T(8,128)(2,1)S(1)}, bf16[48,1536]{1,0:T(8,128)(2,1)S(1)}, u32[]{:S(2)}, u32[]{:S(2)}) collective-permute-start(bf16[48,1536]{1,0:T(8,128)(2,1)S(1)} %fusion.156), channel_id=1, source_target_pairs={{0,16},{2,18},{4,20},{6,22},{8,24},{10,26},{12,28},{14,30},{16,0},... | collective-permute-start | bytes 442376 | tf_op jit(solution)/shard_map/ppermute | solution.py:59
  451.8 12.8 %collective-permute-start.29 = (bf16[48,1536]{1,0:T(8,128)(2,1)S(1)}, bf16[48,1536]{1,0:T(8,128)(2,1)S(1)}, u32[]{:S(2)}, u32[]{:S(2)}) collective-permute-start(bf16[48,1536]{1,0:T(8,128)(2,1)S(1)} %fusion.155), channel_id=1, source_target_pairs={{0,16},{2,18},{4,20},{6,22},{8,24},{10,26},{12,28},{14,30},{16,0},... | collective-permute-start | bytes 442376 | tf_op jit(solution)/shard_map/ppermute | solution.py:59
  462.3 7.3 %collective-permute-start.49 = (bf16[48,1536]{1,0:T(8,128)(2,1)S(1)}, bf16[48,1536]{1,0:T(8,128)(2,1)S(1)}, u32[]{:S(2)}, u32[]{:S(2)}) collective-permute-start(bf16[48,1536]{1,0:T(8,128)(2,1)S(1)} %get-tuple-element.111), channel_id=1, source_target_pairs={{0,16},{2,18},{4,20},{6,22},{8,24},{10,26},{12,28},{14,30},{16,0},... | collective-permute-start | bytes 442376 | tf_op jit(solution)/shard_map/ppermute | solution.py:59
  465.5 7.5 %collective-permute-start.43 = (bf16[48,1536]{1,0:T(8,128)(2,1)S(1)}, bf16[48,1536]{1,0:T(8,128)(2,1)S(1)}, u32[]{:S(2)}, u32[]{:S(2)}) collective-permute-start(bf16[48,1536]{1,0:T(8,128)(2,1)S(1)} %get-tuple-element.114), channel_id=1, source_target_pairs={{0,16},{2,18},{4,20},{6,22},{8,24},{10,26},{12,28},{14,30},{16,0},... | collective-permute-start | bytes 442376 | tf_op jit(solution)/shard_map/ppermute | solution.py:59
  466.2 33.1 %collective-permute-start.40 = (bf16[2,2,2,48,768]{4,3,1,0,2:T(8,128)(2,1)S(1)}, bf16[2,2,2,48,768]{4,3,1,0,2:T(8,128)(2,1)S(1)}, u32[]{:S(2)}, u32[]{:S(2)}) collective-permute-start(bf16[2,2,2,48,768]{4,3,1,0,2:T(8,128)(2,1)S(1)} %maximum_select_fusion.28), channel_id=1, source_target_pairs={{0,2},{2,0},{4,6},{6,4},{8,10},{10,8},{12,14},{14,12},{16,18},{18,... | collective-permute-start | bytes 1769480 | tf_op jit(solution)/shard_map/ppermute | solution.py:59
  467.4 30.4 %collective-permute-start.42 = (bf16[2,2,2,48,768]{4,3,0,1,2:T(8,128)(2,1)S(1)}, bf16[2,2,2,48,768]{4,3,0,1,2:T(8,128)(2,1)S(1)}, u32[]{:S(2)}, u32[]{:S(2)}) collective-permute-start(bf16[2,2,2,48,768]{4,3,0,1,2:T(8,128)(2,1)S(1)} %maximum_select_fusion.30), channel_id=1, source_target_pairs={{0,4},{2,6},{4,0},{6,2},{8,12},{10,14},{12,8},{14,10},{16,20},{18,... | collective-permute-start | bytes 1769480 | tf_op jit(solution)/shard_map/ppermute | solution.py:59
  469.7 7.6 %collective-permute-start.50 = (bf16[2,48,1536]{2,1,0:T(8,128)(2,1)S(1)}, bf16[2,48,1536]{2,1,0:T(8,128)(2,1)S(1)}, u32[]{:S(2)}, u32[]{:S(2)}) collective-permute-start(bf16[2,48,1536]{2,1,0:T(8,128)(2,1)S(1)} %maximum_select_fusion.47), channel_id=1, source_target_pairs={{0,8},{2,10},{4,12},{6,14},{8,0},{10,2},{12,4},{14,6},{16,24},{18,... | collective-permute-start | bytes 884744 | tf_op jit(solution)/shard_map/ppermute | solution.py:59
  473.1 7.4 %collective-permute-start.44 = (bf16[2,48,1536]{2,1,0:T(8,128)(2,1)S(1)}, bf16[2,48,1536]{2,1,0:T(8,128)(2,1)S(1)}, u32[]{:S(2)}, u32[]{:S(2)}) collective-permute-start(bf16[2,48,1536]{2,1,0:T(8,128)(2,1)S(1)} %maximum_select_fusion.46), channel_id=1, source_target_pairs={{0,8},{2,10},{4,12},{6,14},{8,0},{10,2},{12,4},{14,6},{16,24},{18,... | collective-permute-start | bytes 884744 | tf_op jit(solution)/shard_map/ppermute | solution.py:59
  477.6 10.3 %collective-permute-start.53 = (bf16[2,2,48,768]{3,2,1,0:T(8,128)(2,1)S(1)}, bf16[2,2,48,768]{3,2,1,0:T(8,128)(2,1)S(1)}, u32[]{:S(2)}, u32[]{:S(2)}) collective-permute-start(bf16[2,2,48,768]{3,2,1,0:T(8,128)(2,1)S(1)} %get-tuple-element.156), channel_id=1, source_target_pairs={{0,2},{2,0},{4,6},{6,4},{8,10},{10,8},{12,14},{14,12},{16,18},{18,... | collective-permute-start | bytes 884744 | tf_op jit(solution)/shard_map/ppermute | solution.py:59
  478.7 8.1 %collective-permute-start.51 = (bf16[2,2,48,768]{3,2,1,0:T(8,128)(2,1)S(1)}, bf16[2,2,48,768]{3,2,1,0:T(8,128)(2,1)S(1)}, u32[]{:S(2)}, u32[]{:S(2)}) collective-permute-start(bf16[2,2,48,768]{3,2,1,0:T(8,128)(2,1)S(1)} %get-tuple-element.157), channel_id=1, source_target_pairs={{0,4},{2,6},{4,0},{6,2},{8,12},{10,14},{12,8},{14,10},{16,20},{18,... | collective-permute-start | bytes 884744 | tf_op jit(solution)/shard_map/ppermute | solution.py:59
  480.6 11.6 %collective-permute-start.45 = (bf16[2,2,48,768]{3,2,1,0:T(8,128)(2,1)S(1)}, bf16[2,2,48,768]{3,2,1,0:T(8,128)(2,1)S(1)}, u32[]{:S(2)}, u32[]{:S(2)}) collective-permute-start(bf16[2,2,48,768]{3,2,1,0:T(8,128)(2,1)S(1)} %get-tuple-element.165), channel_id=1, source_target_pairs={{0,4},{2,6},{4,0},{6,2},{8,12},{10,14},{12,8},{14,10},{16,20},{18,... | collective-permute-start | bytes 884744 | tf_op jit(solution)/shard_map/ppermute | solution.py:59
  486.9 9.9 %collective-permute-start.47 = (bf16[2,2,48,768]{3,2,1,0:T(8,128)(2,1)S(1)}, bf16[2,2,48,768]{3,2,1,0:T(8,128)(2,1)S(1)}, u32[]{:S(2)}, u32[]{:S(2)}) collective-permute-start(bf16[2,2,48,768]{3,2,1,0:T(8,128)(2,1)S(1)} %get-tuple-element.164), channel_id=1, source_target_pairs={{0,2},{2,0},{4,6},{6,4},{8,10},{10,8},{12,14},{14,12},{16,18},{18,... | collective-permute-start | bytes 884744 | tf_op jit(solution)/shard_map/ppermute | solution.py:59
  487.9 21.5 %collective-permute-start.52 = (bf16[2,2,2,48,768]{4,3,1,0,2:T(8,128)(2,1)S(1)}, bf16[2,2,2,48,768]{4,3,1,0,2:T(8,128)(2,1)S(1)}, u32[]{:S(2)}, u32[]{:S(2)}) collective-permute-start(bf16[2,2,2,48,768]{4,3,1,0,2:T(8,128)(2,1)S(1)} %maximum_select_fusion.37), channel_id=1, source_target_pairs={{0,2},{2,0},{4,6},{6,4},{8,10},{10,8},{12,14},{14,12},{16,18},{18,... | collective-permute-start | bytes 1769480 | tf_op jit(solution)/shard_map/ppermute | solution.py:59
  492.2 17.5 %collective-permute-start.54 = (bf16[2,2,2,48,768]{4,3,1,0,2:T(8,128)(2,1)S(1)}, bf16[2,2,2,48,768]{4,3,1,0,2:T(8,128)(2,1)S(1)}, u32[]{:S(2)}, u32[]{:S(2)}) collective-permute-start(bf16[2,2,2,48,768]{4,3,1,0,2:T(8,128)(2,1)S(1)} %maximum_select_fusion.38), channel_id=1, source_target_pairs={{0,4},{2,6},{4,0},{6,2},{8,12},{10,14},{12,8},{14,10},{16,20},{18,... | collective-permute-start | bytes 1769480 | tf_op jit(solution)/shard_map/ppermute | solution.py:59
  496.8 19.2 %collective-permute-start.46 = (bf16[2,2,2,48,768]{4,3,1,0,2:T(8,128)(2,1)S(1)}, bf16[2,2,2,48,768]{4,3,1,0,2:T(8,128)(2,1)S(1)}, u32[]{:S(2)}, u32[]{:S(2)}) collective-permute-start(bf16[2,2,2,48,768]{4,3,1,0,2:T(8,128)(2,1)S(1)} %maximum_select_fusion.33), channel_id=1, source_target_pairs={{0,2},{2,0},{4,6},{6,4},{8,10},{10,8},{12,14},{14,12},{16,18},{18,... | collective-permute-start | bytes 1769480 | tf_op jit(solution)/shard_map/ppermute | solution.py:59
  497.9 18.4 %collective-permute-start.48 = (bf16[2,2,2,48,768]{4,3,1,0,2:T(8,128)(2,1)S(1)}, bf16[2,2,2,48,768]{4,3,1,0,2:T(8,128)(2,1)S(1)}, u32[]{:S(2)}, u32[]{:S(2)}) collective-permute-start(bf16[2,2,2,48,768]{4,3,1,0,2:T(8,128)(2,1)S(1)} %maximum_select_fusion.35), channel_id=1, source_target_pairs={{0,4},{2,6},{4,0},{6,2},{8,12},{10,14},{12,8},{14,10},{16,20},{18,... | collective-permute-start | bytes 1769480 | tf_op jit(solution)/shard_map/ppermute | solution.py:59
  523.5 129.6 %collective-permute-start.55 = (f32[768,768]{1,0:T(8,128)}, f32[768,768]{1,0:T(8,128)}, u32[]{:S(2)}, u32[]{:S(2)}) collective-permute-start(f32[768,768]{1,0:T(8,128)} %get-tuple-element.206), channel_id=1, source_target_pairs={{0,1},{1,0},{2,3},{3,2},{4,5},{5,4},{6,7},{7,6},{8,9},{9,8},{10,11... | collective-permute-start | bytes 7077896 | tf_op jit(solution)/shard_map/ppermute | solution.py:63
  705.0 7.7 %collective-permute-start.58 = (f32[48,768]{1,0:T(8,128)S(1)}, f32[48,768]{1,0:T(8,128)S(1)}, u32[]{:S(2)}, u32[]{:S(2)}) collective-permute-start(f32[48,768]{1,0:T(8,128)S(1)} %get-tuple-element.149), channel_id=1, source_target_pairs={{0,6},{2,4},{4,2},{6,0},{8,14},{10,12},{12,10},{14,8},{16,22},{18,... | collective-permute-start | bytes 442376 | tf_op jit(solution)/shard_map/ppermute | solution.py:373
  707.4 7.7 %collective-permute-start.57 = (f32[48,768]{1,0:T(8,128)S(1)}, f32[48,768]{1,0:T(8,128)S(1)}, u32[]{:S(2)}, u32[]{:S(2)}) collective-permute-start(f32[48,768]{1,0:T(8,128)S(1)} %get-tuple-element.150), channel_id=1, source_target_pairs={{0,4},{2,6},{4,0},{6,2},{8,12},{10,14},{12,8},{14,10},{16,20},{18,... | collective-permute-start | bytes 442376 | tf_op jit(solution)/shard_map/ppermute | solution.py:373
  708.0 7.1 collective-permute-start.56
  (90 other events, 511.8 us)
Sparse Core Ops, SparseCore 0:
  526.4 123.3 reduce-scatter.3

commit v2 on v1

v2 whole, which is shorter than its diff:
```python
import functools
import math

import jax
import jax.numpy as jnp
from jax import lax
from jax.experimental import pallas as pl
from jax.experimental.pallas import tpu as pltpu
from jax.sharding import PartitionSpec as P

D = 768
FF = 3072
HEADS = 12
HEAD_DIM = 64
SEQ = 512
CAP = 1
MICRO = 2
NS_ITERS = 5
STEP = 10

norm_eps = 1e-05
mask_fill = -1e30
poly_first = 3.4445
poly_second = -4.775
poly_third = 2.0315
muon_rate = 0.2
adam_rate = 0.8
decay_rate = 0.01
moment_decay = 0.5
beta_first = 0.9
beta_second = 0.98
adam_eps = 1e-06

SWAP = [(0, 1), (1, 0)]
VEC_PAD = 128
GROUP = 4
TILE = 256
ROWS = 256
VROWS = 8 + FF // D
PAIR = 2 * HEAD_DIM
PAIRS = HEADS // 2
BLOCKS = 3 * PAIRS
INFO = 1 + CAP * MICRO
WIDE = FF // 2
ORDER = (tuple(range(9)), tuple(range(12, 18)) + tuple(range(9, 12)))
SPOTS = tuple(
    tuple((ORDER[core] + ORDER[1 - core]).index(block) for block in range(BLOCKS))
    for core in range(2)
)


def matmul(former, latter):
    return jnp.dot(former, latter, preferred_element_type=jnp.float32)


def matmul_tn(former, latter):
    return lax.dot_general(
        former, latter, (((0,), (0,)), ((), ())), preferred_element_type=jnp.float32
    )


def matmul_nt(former, latter):
    return lax.dot_general(
        former, latter, (((1,), (1,)), ((), ())), preferred_element_type=jnp.float32
    )


def flip(values, mask, size):
    return lax.ppermute(values, "fsdp", [(i, i ^ mask) for i in range(size)])


def swap_cores(values):
    return lax.ppermute(values, "row", SWAP)


def together(*values):
    return lax.optimization_barrier(values)


def my_bit(bit):
    return (lax.axis_index("fsdp") >> bit) & 1


def pair_of(bit):
    return (lax.axis_index("fsdp") >> bit) & 3


def send_four(values, bit, size):
    return [values] + [flip(values, step << bit, size) for step in (1, 2, 3)]


def sort_four(pieces, bit, axis):
    low, high = my_bit(bit) == 1, my_bit(bit + 1) == 1
    first = jnp.where(low, jnp.stack(pieces[1::-1], axis), jnp.stack(pieces[:2], axis))
    second = jnp.where(low, jnp.stack(pieces[:1:-1], axis), jnp.stack(pieces[2:], axis))
    return jnp.where(
        high,
        jnp.concatenate([second, first], axis),
        jnp.concatenate([first, second], axis),
    )


def merge_rows(values):
    return values.reshape(-1, values.shape[-1])


def send_high(block, size):
    return send_four(block, size.bit_length() - 3, size)


def sort_high(pieces, size):
    return sort_four(pieces, size.bit_length() - 3, 0)


def send_low(values, size):
    for bit in range(size.bit_length() - 5, 0, -2):
        values = sort_four(send_four(values, bit, size), bit, -3)
    return send_four(values, 0, size)


def sort_low(pieces):
    return merge_rows(sort_four(pieces, 0, -3))


def pick_four(parts, axis, place):
    return [lax.dynamic_index_in_dim(part, place, axis, keepdims=False) for part in parts]


def leave_four(parts, axis, bit, size):
    mine = pair_of(bit)
    kept = pick_four(parts, axis, mine)
    arrived = []
    for step in (1, 2, 3):
        leaving = pick_four(parts, axis, mine ^ step)
        leaving = jnp.concatenate([part.astype(jnp.bfloat16) for part in leaving], axis=-1)
        arrived.append(flip(leaving, step << bit, size))
    return kept, arrived


def add_four(kept, arrived):
    totals, place = [], 0
    for part in kept:
        cols = slice(place, place + part.shape[-1])
        place = cols.stop
        for piece in arrived:
            part = part + piece[..., cols].astype(jnp.float32)
        totals.append(part)
    return totals


def leave_low(parts, size):
    shape = (4,) * ((size.bit_length() - 1) // 2) + (D // size, -1)
    parts = [part.reshape(shape) for part in parts]
    return leave_four(parts, len(shape) - 3, 0, size)


def leave_high(kept, arrived, size):
    parts = add_four(kept, arrived)
    for bit in range(2, size.bit_length() - 3, 2):
        parts = add_four(*leave_four(parts, parts[0].ndim - 3, bit, size))
    return leave_four(parts, 0, size.bit_length() - 3, size)


erf_slope = 0.3275911
erf_terms = (1.061405429, -1.453152027, 1.421413741, -0.284496736, 0.254829592)


def gelu_parts(pre_act):
    bell = jnp.exp(pre_act * pre_act * -0.5)
    inverse = 1.0 / (1.0 + jnp.abs(pre_act) * (erf_slope * math.sqrt(0.5)))
    poly = 0.5 * erf_terms[0] * inverse + 0.5 * erf_terms[1]
    for term in erf_terms[2:]:
        poly = poly * inverse + 0.5 * term
    tail = poly * inverse * bell
    cdf = jnp.where(pre_act < 0.0, tail, 1.0 - tail)
    return pre_act * cdf, cdf + pre_act * bell * (1.0 / math.sqrt(2.0 * math.pi))


def norm_parts(values):
    center = values - jnp.mean(values, axis=-1, keepdims=True)
    rstd = lax.rsqrt(jnp.mean(center * center, axis=-1, keepdims=True) + norm_eps)
    return center * rstd, rstd


def norm_pull(grad, gain, xhat, rstd):
    scaled = grad * gain
    return rstd * (
        scaled
        - jnp.mean(scaled, axis=-1, keepdims=True)
        - xhat * jnp.mean(scaled * xhat, axis=-1, keepdims=True)
    )


def head_lanes(shape, h):
    lane = lax.broadcasted_iota(jnp.int32, shape, 1)
    return (lane >= HEAD_DIM) if h else (lane < HEAD_DIM), lane == (0 if h else HEAD_DIM)

def masked_pair(q, k, length, h):
    inside, spare = head_lanes(q.shape, h)
    zero = jnp.zeros_like(q)
    q_in = jnp.where(inside, q * jnp.bfloat16(0.125), zero)
    q_aug = jnp.where(spare, jnp.ones_like(q), q_in)
    row = lax.broadcasted_iota(jnp.int32, q.shape, 0)
    fill = jnp.where(row < length, 0.0, mask_fill).astype(jnp.bfloat16)
    k_aug = jnp.where(inside, k, jnp.where(spare, fill, zero))
    return q_in, q_aug, k_aug, inside

def fwd_kernel(info, q_ref, k_ref, v_ref, ctx_ref, lse_ref):
    length = info[1 + pl.program_id(0)]
    q, k, v = q_ref[...], k_ref[...], v_ref[...]
    tops = []
    for h in range(2):
        _, q_aug, k_aug, _ = masked_pair(q, k, length, h)
        scores = matmul_nt(k_aug, q_aug)
        top = jnp.max(scores, axis=0, keepdims=True)
        e = jnp.exp(scores - top)
        total = jnp.sum(e, axis=0, keepdims=True)
        p = (e * (1.0 / total)).astype(jnp.bfloat16)
        lse_ref[0, 0, h:h+1, :] = top + jnp.log(total)
        tops.append(matmul_tn(v, p))
    ctx = jnp.concatenate([tops[0][:HEAD_DIM], tops[1][HEAD_DIM:]], axis=0)
    ctx_ref[...] = jnp.transpose(ctx).astype(jnp.bfloat16)

def bwd_kernel(slot, skipped, info, q_ref, k_ref, v_ref, g_ref, lse_ref, *refs):
    own_ref, other_ref, key_ref, sum_ref = refs[skipped:]
    length = info[1 + slot]
    q, k, v, g = q_ref[...], k_ref[...], v_ref[...], g_ref[...]
    dv = dk = dqt = None
    for h in range(2):
        q_in, q_aug, k_aug, inside = masked_pair(q, k, length, h)
        g_in = jnp.where(inside, g, jnp.zeros_like(g))
        scores = matmul_nt(k_aug, q_aug)
        p = jnp.exp(scores - lse_ref[0, 0, h:h+1, :])
        dp = matmul_nt(v, g_in)
        dv_h = matmul(p.astype(jnp.bfloat16), g_in)
        rd = jnp.sum(p * dp, axis=0, keepdims=True)
        ds = (p * (dp - rd)).astype(jnp.bfloat16)
        dk_h = matmul(ds, q_in)
        k_in = jnp.where(inside, k * jnp.bfloat16(0.125), jnp.zeros_like(k))
        dq_h = matmul_tn(k_in, ds)
        dv = dv_h if dv is None else dv + dv_h
        dk = dk_h if dk is None else dk + dk_h
        dqt = dq_h if dqt is None else dqt + dq_h
    dq = jnp.transpose(dqt).astype(jnp.bfloat16)
    dv = dv.astype(jnp.bfloat16)
    early = info[0] == 0
    own_ref[...] = jnp.where(early, dq, dv)
    other_ref[...] = jnp.where(early, dv, dq)
    key_ref[...] = dk.astype(jnp.bfloat16)
    sum_ref[0, 0, 0:1, :] = jnp.sum(dq.astype(jnp.float32), axis=0, keepdims=True)
    sum_ref[0, 0, 1:2, :] = jnp.sum(dv.astype(jnp.float32), axis=0, keepdims=True)


def pick(kind):
    def spot(s, p, info):
        return s, info[INFO + kind * PAIRS + p]

    return pl.BlockSpec((SEQ, PAIR), spot)


def pair_spec():
    return pl.BlockSpec((SEQ, PAIR), lambda s, p, info: (s, p))


def pair_rows(width):
    return pl.BlockSpec((1, 1, 2, width), lambda s, p, info: (s, p, 0, 0))


def attention(info, qkv, slots):
    rows = qkv.shape[0]
    return pl.pallas_call(
        fwd_kernel,
        grid_spec=pltpu.PrefetchScalarGridSpec(
            num_scalar_prefetch=1,
            grid=(slots, PAIRS),
            in_specs=[pick(kind) for kind in range(3)],
            out_specs=[pair_spec(), pair_rows(SEQ)],
        ),
        out_shape=[
            jax.ShapeDtypeStruct((rows, D), jnp.bfloat16),
            jax.ShapeDtypeStruct((slots, PAIRS, 2, SEQ), jnp.float32),
        ],
        cost_estimate=pl.CostEstimate(
            flops=20 << 30, bytes_accessed=8 << 20, transcendentals=slots * HEADS * SEQ * SEQ
        ),
        name="attention",
    )(info, qkv, qkv, qkv)


def attention_pull(info, qkv, grad, log_total, slots, slot, parts):
    rows = qkv.shape[0]

    def at_slot(spec):
        return pl.BlockSpec(
            spec.block_shape, lambda s, p, info: spec.index_map(slot, p, info)
        )

    def key_spot(s, p, info):
        return s, lax.rem(p + info[0] * (PAIRS // 2), PAIRS)

    table = jax.ShapeDtypeStruct((rows, D), jnp.bfloat16)
    before = [] if parts is None else list(parts)
    return pl.pallas_call(
        functools.partial(bwd_kernel, slot, len(before)),
        grid_spec=pltpu.PrefetchScalarGridSpec(
            num_scalar_prefetch=1,
            grid=(1, PAIRS),
            in_specs=[at_slot(pick(kind)) for kind in range(3)]
            + [at_slot(pair_spec()), at_slot(pair_rows(SEQ))]
            + [pl.BlockSpec(memory_space=pl.ANY)] * len(before),
            out_specs=[
                at_slot(pair_spec()),
                at_slot(pair_spec()),
                at_slot(pl.BlockSpec((SEQ, PAIR), key_spot)),
                at_slot(pair_rows(PAIR)),
            ],
        ),
        out_shape=[table] * 3 + [jax.ShapeDtypeStruct((slots, PAIRS, 2, PAIR), jnp.float32)],
        input_output_aliases={6 + place: place for place in range(len(before))},
        cost_estimate=pl.CostEstimate(
            flops=14 << 30, bytes_accessed=8 << 20, transcendentals=HEADS * SEQ * SEQ
        ),
        name="attention_pull",
    )(info, qkv, qkv, qkv, grad, log_total, *before)


def join_halves(core, own, other):
    return jnp.where(
        core == 0,
        jnp.concatenate([own, other], axis=1),
        jnp.concatenate([other, own], axis=1),
    )


def vector_kernel(info, own_ref, other_ref, vec_ref, bias_ref, own_bias_ref, other_bias_ref):
    early_core = info[0] == 0
    rows = VROWS // 2
    own = jnp.transpose(own_ref[...].astype(jnp.float32))[:rows]
    other = jnp.transpose(other_ref[...].astype(jnp.float32))[:rows]
    vec = jnp.concatenate(
        [jnp.where(early_core, own, other), jnp.where(early_core, other, own)], axis=0
    )
    vec_ref[0:VROWS, :] = vec
    up_rows = FF // D
    for place in range(up_rows):
        early, late = 5 + place, 5 + (place + up_rows // 2) % up_rows
        row = jnp.where(early_core, vec[early : early + 1], vec[late : late + 1])
        bias_ref[0:1, place * D : (place + 1) * D] = row
    own_bias_ref[...] = jnp.zeros_like(own_bias_ref)
    other_bias_ref[...] = jnp.zeros_like(other_bias_ref)
    own_bias_ref[0:1, :D] = jnp.where(early_core, vec[0:1], vec[1:2])
    other_bias_ref[0:1, :D] = jnp.where(early_core, vec[1:2], vec[0:1])


def vector_tables(info, own, other):
    half = own.shape[1] - VEC_PAD
    spec = pl.BlockSpec((D, VEC_PAD), lambda i: (0, half // VEC_PAD))
    shapes = [(16, D), (8, FF), (8, half), (8, half)]
    return pl.pallas_call(
        vector_kernel,
        grid=(1,),
        in_specs=[pl.BlockSpec(memory_space=pltpu.SMEM), spec, spec],
        out_specs=[pl.BlockSpec(shape, lambda i: (0, 0)) for shape in shapes],
        out_shape=[jax.ShapeDtypeStruct(shape, jnp.float32) for shape in shapes],
        name="vector_tables",
    )(info, own, other)


def vector_grad_kernel(info, low_ref, high_ref, bias_ref, head_ref, out_ref):
    early_core = info[0] == 0
    out_ref[...] = jnp.zeros_like(out_ref)
    for pair in range(PAIRS):
        cols = slice(pair * PAIR, (pair + 1) * PAIR)
        out_ref[0:2, cols] = jnp.sum(head_ref[:, pair], axis=0)
    out_ref[2:5, :] = low_ref[0:3, :]
    up_rows = FF // D
    for place in range(up_rows):
        late = (place + up_rows // 2) % up_rows
        out_ref[5 + place : 6 + place, :] = jnp.where(
            early_core,
            bias_ref[0:1, place * D : (place + 1) * D],
            bias_ref[0:1, late * D : (late + 1) * D],
        )
    out_ref[5 + up_rows : 8 + up_rows, :] = high_ref[0:3, :]


def vector_grads(info, low_sums, high_sums, bias_sums, head_sums):
    whole = pl.BlockSpec(memory_space=pltpu.VMEM)
    return pl.pallas_call(
        vector_grad_kernel,
        in_specs=[pl.BlockSpec(memory_space=pltpu.SMEM)] + [whole] * 4,
        out_specs=whole,
        out_shape=jax.ShapeDtypeStruct((16, D), jnp.float32),
        name="vector_grads",
    )(info, low_sums, high_sums, bias_sums, head_sums)


def hidden_pieces(own, other):
    return [
        (ref, slice(first, first + D), place + first)
        for place, ref in ((0, own), (WIDE, other))
        for first in range(0, WIDE, D)
    ]


OUT_COLS = slice(WIDE, WIDE + D // 2)


def raise_kernel(
    info, vec_ref, bias_ref, x_ref, ctx_ref, own, other, xhat_ref, rstd_ref, low_ref, act_ref, slope_ref
):
    ctx = ctx_ref[...]
    attended = join_halves(info[0], matmul(ctx, own[:, OUT_COLS]), matmul(ctx, other[:, OUT_COLS]))
    xhat, rstd = norm_parts(x_ref[...].astype(jnp.float32) + (attended + vec_ref[2:3, :]))
    xhat_ref[...] = xhat
    rstd_ref[...] = jnp.broadcast_to(rstd, rstd_ref.shape)
    hidden = (xhat * vec_ref[3:4, :] + vec_ref[4:5, :]).astype(jnp.bfloat16)
    low_ref[...] = hidden
    for ref, cols, place in hidden_pieces(own, other):
        spot = slice(place, place + D)
        act, slope = gelu_parts(matmul(hidden, ref[:, cols]) + bias_ref[0:1, spot])
        act_ref[:, spot] = act.astype(jnp.bfloat16)
        slope_ref[:, spot] = slope.astype(jnp.bfloat16)


def add_sums(ref, sums):
    first = pl.program_id(0) == 0
    for place, values in enumerate(sums):
        total = jnp.sum(values, axis=0, keepdims=True)
        spot = slice(place, place + 1)
        ref[spot, :] = jnp.where(first, total, ref[spot, :] + total)


def lower_kernel(
    info, vec_ref, xhat_ref, act_ref, cot_ref, own, other, out_ref, grad_ref, low_ref, sum_ref
):
    first = pl.program_id(0) * ROWS
    branch = vec_ref[9:10, :]
    for ref, cols, place in hidden_pieces(own, other):
        branch = branch + matmul_nt(act_ref[:, place : place + D], ref[:, cols])
    hidden = xhat_ref[...] * vec_ref[3:4, :] + vec_ref[4:5, :]
    xhat, rstd = norm_parts(hidden + branch)
    gain = vec_ref[10:11, :]
    out_ref[...] = (xhat * gain + vec_ref[11:12, :]).astype(jnp.bfloat16)
    limit = info[INFO + BLOCKS + lax.div(first, SEQ)]
    row = lax.broadcasted_iota(jnp.int32, (ROWS, 1), 0) + lax.rem(first, SEQ)
    cot = jnp.where(row < limit, cot_ref[...].astype(jnp.float32), 0.0)
    grad = norm_pull(cot, gain, xhat, rstd)
    grad_ref[...] = grad
    low = grad.astype(jnp.bfloat16)
    low_ref[...] = low
    add_sums(sum_ref, (low.astype(jnp.float32), cot * xhat, cot))


def pull_kernel(
    info,
    vec_ref,
    xhat_ref,
    rstd_ref,
    slope_ref,
    grad_ref,
    low_ref,
    up_own,
    up_other,
    own,
    other,
    pre_ref,
    skip_ref,
    attn_ref,
    ctx_ref,
    sum_ref,
    bias_ref,
):
    core = info[0]
    low = low_ref[...]
    hidden_grad = grad_ref[...]
    for down, up in zip(hidden_pieces(own, other), hidden_pieces(up_own, up_other)):
        ref, cols, place = down
        spot = slice(place, place + D)
        pre = matmul(low, ref[:, cols]) * slope_ref[:, spot].astype(jnp.float32)
        pre = pre.astype(jnp.bfloat16)
        pre_ref[:, spot] = pre
        hidden_grad = hidden_grad + matmul_nt(pre, up[0][:, up[1]])
    xhat = xhat_ref[...]
    skip = norm_pull(hidden_grad, vec_ref[3:4, :], xhat, rstd_ref[:, 0:1])
    skip_ref[...] = skip
    attn = skip.astype(jnp.bfloat16)
    attn_ref[...] = attn
    left, right = attn[:, : D // 2], attn[:, D // 2 :]
    ctx = matmul_nt(jnp.where(core == 0, left, right), up_own[:, OUT_COLS])
    ctx = ctx + matmul_nt(jnp.where(core == 0, right, left), up_other[:, OUT_COLS])
    ctx_ref[...] = ctx.astype(jnp.bfloat16)
    add_sums(sum_ref, (attn.astype(jnp.float32), hidden_grad * xhat, hidden_grad))
    add_sums(bias_ref, (pre_ref[...].astype(jnp.float32),))


def row_spec(width):
    return pl.BlockSpec((ROWS, width), lambda i: (i, 0))


def whole_spec():
    return pl.BlockSpec(memory_space=pltpu.VMEM)


def row_call(kernel, name, in_specs, rows, outs, sums, flops, operands):
    shapes = [jax.ShapeDtypeStruct((rows, width), kind) for width, kind in outs]
    shapes += [jax.ShapeDtypeStruct((8, width), jnp.float32) for width in sums]
    return pl.pallas_call(
        kernel,
        grid=(rows // ROWS,),
        in_specs=[pl.BlockSpec(memory_space=pltpu.SMEM)] + in_specs,
        out_specs=[row_spec(width) for width, kind in outs]
        + [pl.BlockSpec((8, width), lambda i: (0, 0)) for width in sums],
        out_shape=shapes,
        compiler_params=pltpu.CompilerParams(vmem_limit_bytes=52 << 20),
        cost_estimate=pl.CostEstimate(
            flops=flops, bytes_accessed=24 << 20, transcendentals=rows * FF
        ),
        name=name,
    )(*operands)


def raise_rows(info, vec, bias, tokens, context, own, other):
    low, full = jnp.bfloat16, jnp.float32
    return row_call(
        raise_kernel,
        "raise_rows",
        [whole_spec()] * 2 + [row_spec(D)] * 2 + [whole_spec()] * 2,
        tokens.shape[0],
        [(D, full), (PAIR, full), (D, low), (FF, low), (FF, low)],
        [],
        14 << 30,
        (info, vec, bias, tokens, context, own, other),
    )


def lower_rows(info, vec, xhat, act, cotangent, own, other):
    low, full = jnp.bfloat16, jnp.float32
    return row_call(
        lower_kernel,
        "lower_rows",
        [whole_spec(), row_spec(D), row_spec(FF), row_spec(D)] + [whole_spec()] * 2,
        act.shape[0],
        [(D, low), (D, full), (D, low)],
        [D],
        9 << 30,
        (info, vec, xhat, act, cotangent, own, other),
    )


def pull_rows(info, vec, xhat, rstd, slope, grad, low_grad, up, down):
    low, full = jnp.bfloat16, jnp.float32
    return row_call(
        pull_kernel,
        "pull_rows",
        [whole_spec(), row_spec(D), row_spec(PAIR), row_spec(FF), row_spec(D), row_spec(D)]
        + [whole_spec()] * 4,
        xhat.shape[0],
        [(FF, low), (D, full), (D, low), (D, low)],
        [D, FF],
        18 << 30,
        (info, vec, xhat, rstd, slope, grad, low_grad, *up, *down),
    )


def split_low(values):
    high = values.astype(jnp.bfloat16)
    return high, (values - high.astype(jnp.float32)).astype(jnp.bfloat16)

def store_split(values, where, high_ref, rest_ref):
    high_ref[where], rest_ref[where] = split_low(values)

def close_product(left, right, rows, cols):
    left_high, left_rest = left[0][rows, :], left[1][rows, :]
    right_high, right_rest = right[0][:, cols], right[1][:, cols]
    return matmul(
        jnp.concatenate([left_high, left_high, left_rest], axis=1),
        jnp.concatenate([right_high, right_rest, right_high], axis=0),
    )


def mirrored_product(left, right, finish):
    for first in range(0, D, TILE):
        rows = slice(first, first + TILE)
        wide = close_product(left, right, rows, slice(first, D))
        for last in range(first, D, TILE):
            tile = wide[:, last - first : last - first + TILE]
            cols = slice(last, last + TILE)
            finish(tile, rows, cols)
            if first < last:
                finish(jnp.transpose(tile), cols, rows)


def polar_kernel(
    start_ref,
    own_ref,
    other_ref,
    cols_ref,
    polar_ref,
    out_ref,
    gram,
    a_high,
    a_rest,
    q_high,
    q_rest,
    b_high,
    b_rest,
    r_high,
    r_rest,
):
    a, q, b, r = (a_high, a_rest), (q_high, q_rest), (b_high, b_rest), (r_high, r_rest)
    count = out_ref.shape[0]
    start = pl.multiple_of(start_ref[0], 8)
    whole = own_ref[...] + other_ref[...]
    row = lax.broadcasted_iota(jnp.int32, (D, D), 0)
    col = lax.broadcasted_iota(jnp.int32, (D, D), 1)
    scale = jnp.sqrt(jnp.sum(jnp.where(row == col, whole, 0.0), keepdims=True)) + 1e-07
    gram[...] = whole / (scale * scale)
    rows = lax.broadcasted_iota(jnp.int32, (count, D), 0) + start
    cols = lax.broadcasted_iota(jnp.int32, (count, D), 1)
    out_ref[...] = jnp.where(rows == cols, 1.0, 0.0)

    def sweep(index, carry):
        every = slice(0, D)
        store_split(gram[...], (every, every), a_high, a_rest)

        def step_tile(tile, where_rows, where_cols):
            step = poly_second * gram[where_rows, where_cols] + poly_third * tile
            if where_rows == where_cols:
                tile_row = lax.broadcasted_iota(jnp.int32, (TILE, TILE), 0)
                tile_col = lax.broadcasted_iota(jnp.int32, (TILE, TILE), 1)
                step = step + jnp.where(tile_row == tile_col, poly_first, 0.0)
            store_split(step, (where_rows, where_cols), q_high, q_rest)

        mirrored_product(a, a, step_tile)
        store_split(out_ref[...], (slice(0, count), every), r_high, r_rest)
        out_ref[...] = close_product(r, q, slice(0, count), every)

        @pl.when(index < NS_ITERS - 1)
        def _():
            def half_tile(tile, where_rows, where_cols):
                store_split(tile, (where_rows, where_cols), b_high, b_rest)

            def gram_tile(tile, where_rows, where_cols):
                gram[where_rows, where_cols] = tile

            mirrored_product(q, a, half_tile)
            mirrored_product(b, q, gram_tile)

        return carry

    lax.fori_loop(0, NS_ITERS, sweep, 0)
    both = jnp.concatenate(split_low(out_ref[...] / scale), axis=0)
    for place in range(0, cols_ref.shape[1], D):
        spot = slice(place, place + D)
        product = matmul(both, cols_ref[:, spot])
        polar_ref[:, spot] = (product[:count] + product[count:]).astype(jnp.bfloat16)

def polar_rows(start, own, other, columns, count):
    half = pltpu.VMEM((D, D), jnp.bfloat16)
    short = pltpu.VMEM((count, D), jnp.bfloat16)
    return pl.pallas_call(
        polar_kernel,
        in_specs=[pl.BlockSpec(memory_space=pltpu.SMEM)]
        + [pl.BlockSpec(memory_space=pltpu.VMEM)] * 3,
        out_specs=pl.BlockSpec(memory_space=pltpu.VMEM),
        out_shape=jax.ShapeDtypeStruct((count, columns.shape[1]), jnp.bfloat16),
        scratch_shapes=[pltpu.VMEM((count, D), jnp.float32), pltpu.VMEM((D, D), jnp.float32)]
        + [half] * 6
        + [short] * 2,
        compiler_params=pltpu.CompilerParams(vmem_limit_bytes=40 << 20),
        name="polar_rows",
    )(start, own, other, columns)


def per_device(
    size,
    tokens,
    cotangent,
    counts,
    lengths,
    w_qkv,
    w_out,
    w_up,
    w_down,
    vectors,
    mom_qkv,
    mom_out,
    mom_up,
    mom_down,
    adam_first,
    adam_second,
):
    me = lax.axis_index("fsdp")
    core = lax.axis_index("row")
    slots = lengths.shape[0]
    rows = tokens.shape[0]
    up_rows = FF // D
    low = jnp.bfloat16

    block_rows = D // size
    qkv_half, up_half = w_qkv.shape[1], w_up.shape[1]
    vec_rows = vectors.shape[0]
    narrow = qkv_half - D

    def pick_core(early, late):
        return jnp.where(core == 0, early, late)

    def turn(values, cut):
        return pick_core(values, jnp.concatenate([values[:, cut:], values[:, :cut]], axis=1))

    vec_block = jnp.pad(vectors.T, ((0, 0), (0, VEC_PAD - vec_rows))).astype(low)
    first_block = jnp.concatenate([turn(w_qkv.astype(low), narrow), vec_block], axis=1)
    second_block = jnp.concatenate([w_up.astype(low), w_out.astype(low)], axis=1)
    third_block = w_down.astype(low)
    first_pieces = together(*send_high(first_block, size), second_block)
    second_block = first_pieces[-1]
    first_pieces = send_low(sort_high(first_pieces[:4], size), size)
    second_pieces = send_high(second_block, size)
    *pieces, third_block = together(*first_pieces, *second_pieces, third_block)
    first_own = sort_low(pieces[:4])
    second_pieces = send_low(sort_high(pieces[4:], size), size)
    third_pieces = send_high(third_block, size)
    first_other = swap_cores(first_own)

    spots = pick_core(jnp.array(SPOTS[0], jnp.int32), jnp.array(SPOTS[1], jnp.int32))
    live = jnp.arange(slots) % CAP < counts.reshape(-1)[jnp.arange(slots) // CAP]
    info = jnp.concatenate(
        [core.reshape(1).astype(jnp.int32), lengths, spots, jnp.where(live, lengths, 0)]
    )
    vec, bias_up, bias_own, bias_other = vector_tables(info, first_own, first_other)
    qkv_own, qkv_other = first_own[:, :qkv_half], first_other[:, :qkv_half]
    projected = jnp.concatenate(
        [
            (matmul(tokens, qkv_own) + bias_own[:1]).astype(low),
            (matmul(tokens, qkv_other) + bias_other[:1]).astype(low),
        ],
        axis=1,
    )
    context, log_total = attention(info, projected, slots)
    context, *pieces = together(context, *second_pieces, *third_pieces)
    second_own = sort_low(pieces[:4])
    third_pieces = send_low(sort_high(pieces[4:], size), size)
    second_other = swap_cores(second_own)
    xhat_one, rstd_one, hidden_low, act_low, slope = raise_rows(
        info, vec, bias_up, tokens, context, second_own, second_other
    )
    act_low, *third_pieces = together(act_low, *third_pieces)
    third_own = sort_low(third_pieces)
    third_other = swap_cores(third_own)
    layer_out, top_grad, branch_low, high_sums = lower_rows(
        info, vec, xhat_one, act_low, cotangent, third_own, third_other
    )

    leaving = matmul_tn(branch_low, act_low[:, up_half:]).astype(low)
    leaving, branch_low = together(leaving, branch_low)
    down_arrived = swap_cores(leaving)
    down_own = matmul_tn(branch_low, act_low[:, :up_half])
    down_own, down_arrived, branch_low = together(down_own, down_arrived, branch_low)
    down_kept, down_sent = leave_low([down_own + down_arrived.astype(jnp.float32)], size)
    pre_low, skip_grad, attn_low, context_grad, low_sums, bias_sums = pull_rows(
        info,
        vec,
        xhat_one,
        rstd_one,
        slope,
        top_grad,
        branch_low,
        (second_own, second_other),
        (third_own, third_other),
    )
    pre_low, *down_sent = together(pre_low, *down_sent)
    down_kept, down_sent = leave_high(down_kept, down_sent, size)
    out_own = pick_core(attn_low[:, : D // 2], attn_low[:, D // 2 :])
    out_other = pick_core(attn_low[:, D // 2 :], attn_low[:, : D // 2])
    leaving = jnp.concatenate(
        [
            matmul_tn(hidden_low, pre_low[:, up_half:]).astype(low),
            matmul_tn(context, out_other).astype(low),
        ],
        axis=1,
    )
    leaving, context_grad = together(leaving, context_grad)
    wide_arrived = swap_cores(leaving)
    up_own = matmul_tn(hidden_low, pre_low[:, :up_half])
    out_own = matmul_tn(context, out_own)
    up_own, out_own, wide_arrived, context_grad = together(
        up_own, out_own, wide_arrived, context_grad
    )
    wide_arrived = wide_arrived.astype(jnp.float32)
    wide_kept, wide_sent = leave_low(
        [up_own + wide_arrived[:, :up_half], out_own + wide_arrived[:, up_half:]], size
    )
    parts = attention_pull(info, projected, context_grad, log_total, slots, 0, None)
    parts, wide_sent, down_sent = together(parts, wide_sent, down_sent)
    (grad_down,) = add_four(down_kept, down_sent)
    moment_down = moment_decay * mom_down + grad_down
    down_pieces = send_high(moment_down.astype(low), size)
    wide_kept, wide_sent = leave_high(wide_kept, wide_sent, size)
    for slot in range(1, slots):
        parts = attention_pull(info, projected, context_grad, log_total, slots, slot, parts)
    parts, wide_sent, down_pieces = together(parts, wide_sent, down_pieces)
    main_own, main_other, keys, head_sums = parts
    grad_own = jnp.concatenate([main_own, keys[:, :narrow]], axis=1)
    grad_other = jnp.concatenate([main_other, keys[:, narrow:]], axis=1)
    leaving = matmul_tn(tokens, grad_other).astype(low)
    leaving, grad_own = together(leaving, grad_own)
    qkv_arrived = swap_cores(leaving)
    vector_grad = vector_grads(info, low_sums, high_sums, bias_sums, head_sums)
    vector_grad = vector_grad + swap_cores(vector_grad)
    vector_part = pick_core(vector_grad[:vec_rows], vector_grad[vec_rows : 2 * vec_rows])
    vector_part = jnp.pad(vector_part, ((0, VEC_PAD - vec_rows), (0, 0))).T
    grad_up, grad_out = add_four(wide_kept, wide_sent)
    moment_up = moment_decay * mom_up + grad_up
    moment_out = moment_decay * mom_out + grad_out
    wide_block = jnp.concatenate([moment_up.astype(low), moment_out.astype(low)], axis=1)
    qkv_part = matmul_tn(tokens, grad_own)
    qkv_part, vector_part, qkv_arrived, wide_block, grad_own = together(
        qkv_part, vector_part, qkv_arrived, wide_block, grad_own
    )
    qkv_kept, qkv_sent = leave_low(
        [qkv_part + qkv_arrived.astype(jnp.float32), vector_part], size
    )
    wide_pieces = send_high(wide_block, size)
    input_grad = skip_grad + matmul_nt(grad_own, qkv_own) + matmul_nt(grad_other, qkv_other)
    down_rows = merge_rows(sort_high(down_pieces, size))
    input_grad, down_rows, qkv_sent, wide_pieces = together(
        input_grad, down_rows, qkv_sent, wide_pieces
    )
    qkv_kept, qkv_sent = leave_high(qkv_kept, qkv_sent, size)
    wide_rows = merge_rows(sort_high(wide_pieces, size))
    mom_turned = turn(mom_qkv, narrow)
    wide_rows, mom_turned, qkv_sent = together(wide_rows, mom_turned, qkv_sent)
    grad_turned, grad_vectors = add_four(qkv_kept, qkv_sent)
    qkv_pieces = send_high((moment_decay * mom_turned + grad_turned).astype(low), size)
    grad_qkv = turn(grad_turned, D)
    moment_qkv = moment_decay * mom_qkv + grad_qkv
    grad_vectors = grad_vectors[:, :vec_rows].T
    grad_qkv, moment_qkv, qkv_pieces = together(grad_qkv, moment_qkv, qkv_pieces)

    qkv_rows = merge_rows(sort_high(qkv_pieces, size))
    place = me % GROUP

    def widen(values):
        return jnp.pad(values, ((0, 0), (0, WIDE - values.shape[1])))

    matrices = (
        widen(qkv_rows),
        widen(wide_rows[:, up_half:]),
        wide_rows[:, :up_half],
        down_rows,
    )

    def matrix_at(which):
        lower = jnp.where(which == 0, matrices[0], matrices[1])
        upper = jnp.where(which == 2, matrices[2], matrices[3])
        return jnp.where(which < 2, lower, upper)

    pieces = []
    for step in range(GROUP):
        piece = matrix_at(place ^ step).reshape(-1, block_rows, WIDE)
        pieces.append(flip(piece, step, size) if step else piece)
    columns = sort_low(pieces)
    for bit in range(2, size.bit_length() - 3, 2):
        columns = sort_low(send_four(columns.reshape(4, -1, WIDE), bit, size))
    gram = matmul_nt(columns, columns)
    start = ((me - place) * block_rows).reshape(1).astype(jnp.int32)
    polar = polar_rows(start, gram, swap_cores(gram), columns, GROUP * block_rows)
    polar = polar.reshape(GROUP, block_rows, WIDE)
    arrived = []
    for step in range(GROUP):
        block = lax.dynamic_index_in_dim(polar, place ^ step, 0, keepdims=False)
        arrived.append(flip(block, step, size) if step else block)
    arrived = sort_four(arrived, 0, 0)
    masters = (w_qkv, w_out, w_up, w_down)
    counts_of = (3 * D, D, FF, FF)
    updated = []
    for index in range(GROUP):
        ortho = arrived[index][:, : masters[index].shape[1]].astype(jnp.float32)
        if index == 0:
            ortho = turn(ortho, D)
        updated.append(
            masters[index] * (1.0 - muon_rate * decay_rate)
            - muon_rate * 0.2 * math.sqrt(counts_of[index]) * ortho
        )

    first_moment = beta_first * adam_first + (1.0 - beta_first) * grad_vectors
    second_moment = beta_second * adam_second + (1.0 - beta_second) * grad_vectors * grad_vectors
    direction = (
        first_moment
        / (1.0 - beta_first**STEP)
        / (jnp.sqrt(second_moment / (1.0 - beta_second**STEP)) + adam_eps)
    )
    new_vectors = vectors - adam_rate * (direction + decay_rate * vectors)
    return (
        layer_out,
        input_grad,
        grad_qkv,
        grad_out,
        grad_up,
        grad_down,
        grad_vectors,
        moment_qkv,
        moment_out,
        moment_up,
        moment_down,
        updated[0],
        updated[1],
        updated[2],
        updated[3],
        first_moment,
        second_moment,
        new_vectors,
    )


def solution(mesh):
    size = mesh.shape["fsdp"]

    def run(*arrays):
        return per_device(size, *arrays)

    weight = P("fsdp", "row")
    vector = P("row", "fsdp")
    sample = P(("fsdp", "row"), None)
    return jax.shard_map(
        run,
        mesh=mesh,
        in_specs=(sample, sample, sample, P(("fsdp", "row")))
        + (weight,) * 4
        + (vector,)
        + (weight,) * 4
        + (vector,) * 2,
        out_specs=(sample, sample)
        + (weight,) * 4
        + (vector,)
        + (weight,) * 8
        + (vector,) * 3,
        check_vma=False,
    )
```

time: 739 us -> 504 us (0.68)
  the two profiles are of different devices: /device:TPU:0 before, /device:TPU:9 now
where the time goes in v2:
time: 504 us; the launch traced here: 497 us
  Pallas kernels  143 us (28%)
  waiting for transfers between devices  142 us (28%)
  starting transfers between devices  63.7 us (13%)
  local copies, waits for them, and re-layouts  51.9 us (10%)
  matrix products  48.2 us (10%)
  other arithmetic  46.2 us (9%)
    ppermute x51, waiting for transfers between devices, flip(): return lax.ppermute(values, 'fsdp', [(i, i ^ mask) for i in range(size)])  138 us
    pallas_call x3, Pallas kernels, row_call(): pl.pallas_call(kernel, grid=(rows // ROWS,), in_specs=[pl.BlockSpec(memor...  56.7 us
    ppermute x51, starting transfers between devices, flip(): return lax.ppermute(values, 'fsdp', [(i, i ^ mask) for i in range(size)])  53.4 us
    pallas_call x1, Pallas kernels, polar_rows(): pl.pallas_call(polar_kernel, in_specs=[pl.BlockSpec(memory_space=pltpu.SM...  33.5 us
    pallas_call x2, Pallas kernels, attention_pull(): pl.pallas_call(functools.partial(bwd_kernel, slot, len(before)), grid_spe...  29.6 us
    dot_general x8, matrix products, matmul_tn(): lax.dot_general(former, latter, (((0,), (0,)), ((), ())), preferred_eleme...  27 us
    unnamed x159, local copies, waits for them, and re-layouts  25.5 us
    pallas_call x1, Pallas kernels, attention(): pl.pallas_call(fwd_kernel, grid_spec=pltpu.PrefetchScalarGridSpec(num_sca...  19.4 us
  transfers between devices with their start and end apart: 59, of which 25 were waited for; matrix products, arithmetic and copies ran while one was open for 18% of the time, Pallas kernels for 19%

profile of v2, /device:TPU:9, one launch (start us, length us, event | category | flops | bytes accessed | tf_op | source)
XLA Modules:
  0.0 497.3 jit_solution(3063839951187868182)
XLA Ops:
  2.5 2.5 collective-permute-start.1
  6.7 3.6 collective-permute-done.1
  10.3 5.0 %collective-permute-done.2 = bf16[48,1280]{1,0:T(8,128)(2,1)S(1)} collective-permute-done((bf16[48,1280]{1,0:T(8,128)(2,1)S(1)}, bf16[48,1280]{1,0:T(8,128)(2,1)S(1)}, u32[]{:S(2)}, u32[]{:S(2)}) %collective-permute-start.2) | collective-permute-done | bytes 122912 | tf_op jit(solution)/shard_map/ppermute | solution.py:69
  18.2 2.9 collective-permute-start.7
  21.1 1.8 collective-permute-done.6
  26.9 9.5 %collective-permute-done.8 = bf16[48,1920]{1,0:T(8,128)(2,1)S(1)} collective-permute-done((bf16[48,1920]{1,0:T(8,128)(2,1)S(1)}, bf16[48,1920]{1,0:T(8,128)(2,1)S(1)}, u32[]{:S(2)}, u32[]{:S(2)}) %collective-permute-start.8) | collective-permute-done | bytes 184352 | tf_op jit(solution)/shard_map/ppermute | solution.py:69
  38.3 3.3 collective-permute-start.9
  45.9 2.9 collective-permute-start.14
  48.8 1.9 vector_tables.1
  52.3 4.3 fusion.8
  56.6 3.7 fusion
  60.3 2.5 pad_maximum_fusion.q_ref.k_ref.v_ref
  62.8 19.4 %attention.1 = (bf16[1024,768]{1,0:T(8,128)(2,1)}, f32[2,6,2,512]{3,2,1,0:T(2,128)}) custom-call(s32[23]{0:T(128)} %pad_add_fusion.info, bf16[1024,2304]{1,0:T(8,128)(2,1)} %pad_maximum_fusion.q_ref.k_ref.v_ref, bf16[1024,2304]{1,0:T(8,128)(2,1)} %pad_maximum_fusion.q_ref.k_ref.v_ref, bf16[1024,2304]{1,0:T(8,128)(2,1)} %pad_maximum_fusion.q_ref.k_ref.v_ref), custom_call_target="tpu_custom_call" | custom-call | flops 21474836480 | bytes 8388608 | tf_op jit(solution)/shard_map/attention/pallas_call | solution.py:271
  82.2 2.1 maximum_select_fusion.4
  93.5 21.8 %raise_rows.1 = (f32[1024,768]{1,0:T(8,128)}, f32[1024,128]{1,0:T(8,128)S(1)}, bf16[1024,768]{1,0:T(8,128)(2,1)}, bf16[1024,3072]{1,0:T(8,128)(2,1)}, bf16[1024,3072]{1,0:T(8,128)(2,1)}) custom-call(s32[23]{0:T(128)S(1)} %copy-done.6, f32[16,768]{1,0:T(8,128)S(1)} %copy-done.8, f32[8,3072]{1,0:T(8,128)S(1)} %copy-done.7, bf16[1024,768]{1,0:T(8,128)(2,1)} %x_ref.1, ...), custom_call_target="tpu_custom_call" | custom-call | flops 15032385536 | bytes 25165824 | tf_op jit(solution)/shard_map/raise_rows/pallas_call | solution.py:508
  115.3 1.8 collective-permute-done.19
  119.6 4.2 collective-permute-done.20.other
  125.1 13.3 %lower_rows.1 = (bf16[1024,768]{1,0:T(8,128)(2,1)}, f32[1024,768]{1,0:T(8,128)}, bf16[1024,768]{1,0:T(8,128)(2,1)S(1)}, f32[8,768]{1,0:T(8,128)S(1)}) custom-call(s32[23]{0:T(128)S(1)} %copy-done.6, f32[16,768]{1,0:T(8,128)S(1)} %copy-done.8, f32[1024,768]{1,0:T(8,128)} %get-tuple-element.162.xhat_ref, bf16[1024,3072]{1,0:T(8,128)(2,1)} %get-tuple-element.168.act_ref, ...), custom_call_target="tpu_custom_call" | custom-call | flops 9663676416 | bytes 25165824 | tf_op jit(solution)/shard_map/lower_rows/pallas_call | solution.py:508
  138.5 4.5 convolution_convert_fusion.1
  143.5 4.6 fusion.4
  148.1 2.5 convert_add_fusion
  153.5 21.5 %pull_rows.1 = (bf16[1024,3072]{1,0:T(8,128)(2,1)}, f32[1024,768]{1,0:T(8,128)}, bf16[1024,768]{1,0:T(8,128)(2,1)}, bf16[1024,768]{1,0:T(8,128)(2,1)}, f32[8,768]{1,0:T(8,128)S(1)}, /*index=5*/f32[8,3072]{1,0:T(8,128)S(1)}) custom-call(s32[23]{0:T(128)S(1)} %copy-done.6, f32[16,768]{1,0:T(8,128)S(1)} %copy-done.8, f32[1024,768]{1,0:T(8,128)} %get-tuple-element.162.xhat_ref, ...), custom_call_target="tpu_custom_call" | custom-call | flops 19327352832 | bytes 25165824 | tf_op jit(solution)/shard_map/pull_rows/pallas_call | solution.py:508
  175.1 2.5 convolution_convert_fusion.3
  179.2 4.9 convolution_convert_fusion
  184.2 1.8 pad_maximum_fusion.1
  188.9 3.6 fusion.27
  196.1 1.7 collective-permute-start.30
  197.9 2.7 fusion.2
  200.6 2.2 convert_element_type.371
  203.9 1.8 copy-done.9
  211.4 14.7 %attention_pull.2 = (bf16[1024,768]{1,0:T(8,128)(2,1)}, bf16[1024,768]{1,0:T(8,128)(2,1)}, bf16[1024,768]{1,0:T(8,128)(2,1)}, f32[2,6,2,128]{3,2,1,0:T(2,128)}) custom-call(s32[23]{0:T(128)} %pad_add_fusion.info, bf16[1024,2304]{1,0:T(8,128)(2,1)} %pad_maximum_fusion.q_ref.k_ref.v_ref, bf16[1024,2304]{1,0:T(8,128)(2,1)} %pad_maximum_fusion.q_ref.k_ref.v_ref, ...), custom_call_target="tpu_custom_call" | custom-call | flops 15032385536 | bytes 8388608 | tf_op jit(solution)/shard_map/attention_pull/pallas_call | solution.py:303
  226.2 15.9 %collective-permute-done.27 = bf16[4,48,1920]{2,1,0:T(8,128)(2,1)} collective-permute-done((bf16[4,48,1920]{2,1,0:T(8,128)(2,1)}, bf16[4,48,1920]{2,1,0:T(8,128)(2,1)}, u32[]{:S(2)}, u32[]{:S(2)}) %collective-permute-start.27) | collective-permute-done | bytes 737312 | tf_op jit(solution)/shard_map/ppermute | solution.py:69
  242.1 2.0 fusion.98
  244.0 1.8 collective-permute-start.35
  247.0 1.9 fusion.21
  251.3 3.3 collective-permute-start.33
  255.4 14.8 %attention_pull.3 = (bf16[1024,768]{1,0:T(8,128)(2,1)}, bf16[1024,768]{1,0:T(8,128)(2,1)}, bf16[1024,768]{1,0:T(8,128)(2,1)}, f32[2,6,2,128]{3,2,1,0:T(2,128)}) custom-call(s32[23]{0:T(128)} %pad_add_fusion.info, bf16[1024,2304]{1,0:T(8,128)(2,1)} %pad_maximum_fusion.q_ref.k_ref.v_ref, ...), custom_call_target="tpu_custom_call", output_to_operand_aliasing={{0}: (6, {}), {1}: (7, {}), {2}: (8, {}), {3}: (9, {})} | custom-call | flops 15032385536 | bytes 8388608 | tf_op jit(solution)/shard_map/attention_pull/pallas_call | solution.py:303
  271.8 2.7 collective-permute-done.33
  282.3 2.1 fusion.7
  288.4 2.1 convolution_bitcast_fusion
  292.0 2.2 collective-permute-start.43
  295.7 3.0 copy.284
  298.7 1.8 fusion.51
  300.6 2.0 copy.285
  306.0 4.4 fusion.12
  310.7 5.4 %add_add_fusion = f32[1024,768]{1,0:T(8,128)} fusion(f32[1024,768]{1,0:T(8,128)S(1)} %copy-done.66, f32[1024,768]{1,0:T(8,128)S(1)} %fusion.12, bf16[768,1280]{1,0:T(8,128)(2,1)} %collective-permute-done.9.other_ref, bf16[1024,384]{1,0:T(8,128)(2,1)S(1)} %copy-done.32, bf16[1024,768]{1,0:T(8,128)(2,1)S(1)} %copy-done.68), kind=kOutput, calls=%fused_computation.12 | convolution fusion | flops 1818230784 | bytes 13565952 | tf_op jit(solution)/shard_map/dot_general | solution.py:63
  316.4 11.9 %collective-permute-done.41 = bf16[4,48,1280]{2,1,0:T(8,128)(2,1)S(1)} collective-permute-done((bf16[4,48,1280]{2,1,0:T(8,128)(2,1)S(1)}, bf16[4,48,1280]{2,1,0:T(8,128)(2,1)S(1)}, u32[]{:S(2)}, u32[]{:S(2)}) %collective-permute-start.41) | collective-permute-done | bytes 491552 | tf_op jit(solution)/shard_map/ppermute | solution.py:69
  333.6 3.3 collective-permute-start.47
  340.8 13.5 %collective-permute-done.48 = bf16[48,1280]{0,1:T(8,128)(2,1)S(1)} collective-permute-done((bf16[48,1280]{0,1:T(8,128)(2,1)S(1)}, bf16[48,1280]{0,1:T(8,128)(2,1)S(1)}, u32[]{:S(2)}, u32[]{:S(2)}) %collective-permute-start.48) | collective-permute-done | bytes 122912 | tf_op jit(solution)/shard_map/ppermute | solution.py:69
  354.2 6.1 %collective-permute-done.47 = bf16[48,1280]{0,1:T(8,128)(2,1)S(1)} collective-permute-done((bf16[48,1280]{0,1:T(8,128)(2,1)}, bf16[48,1280]{0,1:T(8,128)(2,1)S(1)}, u32[]{:S(2)}, u32[]{:S(2)}) %collective-permute-start.47) | collective-permute-done | bytes 122912 | tf_op jit(solution)/shard_map/ppermute | solution.py:69
  361.2 2.1 collective-permute-start.49
  364.6 9.7 %collective-permute-done.49 = bf16[48,1152]{0,1:T(8,128)(2,1)S(1)} collective-permute-done((bf16[48,1152]{0,1:T(8,128)(2,1)S(1)}, bf16[48,1152]{0,1:T(8,128)(2,1)S(1)}, u32[]{:S(2)}, u32[]{:S(2)}) %collective-permute-start.49) | collective-permute-done | bytes 110624 | tf_op jit(solution)/shard_map/ppermute | solution.py:69
  374.3 2.1 collective-permute-done.50
  376.4 12.7 %collective-permute-done.51 = bf16[48,1152]{0,1:T(8,128)(2,1)S(1)} collective-permute-done((bf16[48,1152]{0,1:T(8,128)(2,1)S(1)}, bf16[48,1152]{0,1:T(8,128)(2,1)S(1)}, u32[]{:S(2)}, u32[]{:S(2)}) %collective-permute-start.51) | collective-permute-done | bytes 110624 | tf_op jit(solution)/shard_map/ppermute | solution.py:69
  398.0 10.9 %collective-permute-done.52 = bf16[4,48,1536]{2,1,0:T(8,128)(2,1)} collective-permute-done((bf16[4,48,1536]{2,1,0:T(8,128)(2,1)}, bf16[4,48,1536]{2,1,0:T(8,128)(2,1)}, u32[]{:S(2)}, u32[]{:S(2)}) %collective-permute-start.52) | collective-permute-done | bytes 589856 | tf_op jit(solution)/shard_map/ppermute | solution.py:69
  408.9 15.3 %collective-permute-done.53 = bf16[4,48,1536]{2,1,0:T(8,128)(2,1)} collective-permute-done((bf16[4,48,1536]{2,1,0:T(8,128)(2,1)}, bf16[4,48,1536]{2,1,0:T(8,128)(2,1)}, u32[]{:S(2)}, u32[]{:S(2)}) %collective-permute-start.53) | collective-permute-done | bytes 589856 | tf_op jit(solution)/shard_map/ppermute | solution.py:69
  424.2 1.8 maximum_select_fusion.8
  426.9 3.5 fusion.101.own_ref
  430.8 2.2 copy.307
  433.0 2.1 copy.308
  439.7 33.5 %polar_rows.1 = bf16[192,1536]{1,0:T(8,128)(2,1)S(1)} custom-call(s32[1]{0:T(128)} %bitcast.99.start_ref, f32[768,768]{1,0:T(8,128)} %fusion.101.own_ref, f32[768,768]{1,0:T(8,128)} %collective-permute-done.55.other_ref, bf16[768,1536]{1,0:T(8,128)(2,1)S(1)} %bitcast.273), custom_call_target="tpu_custom_call" | custom-call | tf_op jit(solution)/shard_map/polar_rows/pallas_call | solution.py:662
  479.2 4.6 collective-permute-done.56
  483.7 3.8 collective-permute-done.57
  489.3 1.7 copy.305
  (381 shorter events, 113.1 us)
Async XLA Ops:
  0.7 41.0 %copy-start = (s32[1,2]{1,0:T(1,128)S(1)}, s32[1,2]{1,0:T(1,128)}, u32[]{:S(2)}) copy-start(s32[1,2]{1,0:T(1,128)} %param.19) | copy-start | bytes 28
  2.4 4.3 collective-permute-start
  2.5 7.8 %collective-permute-start.1 = (bf16[48,1280]{1,0:T(8,128)(2,1)S(1)}, bf16[48,1280]{1,0:T(8,128)(2,1)S(1)}, u32[]{:S(2)}, u32[]{:S(2)}) collective-permute-start(bf16[48,1280]{1,0:T(8,128)(2,1)S(1)} %fusion.68), channel_id=1, source_target_pairs={{0,16},{2,18},{4,20},{6,22},{8,24},{10,26},{12,28},{14,30},{16,0},... | collective-permute-start | bytes 368648 | tf_op jit(solution)/shard_map/ppermute | solution.py:69
  5.0 10.3 %collective-permute-start.2 = (bf16[48,1280]{1,0:T(8,128)(2,1)S(1)}, bf16[48,1280]{1,0:T(8,128)(2,1)S(1)}, u32[]{:S(2)}, u32[]{:S(2)}) collective-permute-start(bf16[48,1280]{1,0:T(8,128)(2,1)S(1)} %fusion.68), channel_id=1, source_target_pairs={{0,24},{2,26},{4,28},{6,30},{8,16},{10,18},{12,20},{14,22},{16,8},... | collective-permute-start | bytes 368648 | tf_op jit(solution)/shard_map/ppermute | solution.py:69
  15.5 21.0 %collective-permute-start.3 = (bf16[4,48,1280]{2,1,0:T(8,128)(2,1)S(1)}, bf16[4,48,1280]{2,1,0:T(8,128)(2,1)S(1)}, u32[]{:S(2)}, u32[]{:S(2)}) collective-permute-start(bf16[4,48,1280]{2,1,0:T(8,128)(2,1)S(1)} %maximum_select_fusion.18), channel_id=1, source_target_pairs={{0,2},{2,0},{4,6},{6,4},{8,10},{10,8},{12,14},{14,12},{16,18},{18,... | collective-permute-start | bytes 1474568 | tf_op jit(solution)/shard_map/ppermute | solution.py:69
  16.7 19.7 %collective-permute-start.4 = (bf16[4,48,1280]{2,1,0:T(8,128)(2,1)S(1)}, bf16[4,48,1280]{2,1,0:T(8,128)(2,1)S(1)}, u32[]{:S(2)}, u32[]{:S(2)}) collective-permute-start(bf16[4,48,1280]{2,1,0:T(8,128)(2,1)S(1)} %maximum_select_fusion.18), channel_id=1, source_target_pairs={{0,4},{2,6},{4,0},{6,2},{8,12},{10,14},{12,8},{14,10},{16,20},{18,... | collective-permute-start | bytes 1474568 | tf_op jit(solution)/shard_map/ppermute | solution.py:69
  18.0 19.7 %collective-permute-start.5 = (bf16[4,48,1280]{2,1,0:T(8,128)(2,1)S(1)}, bf16[4,48,1280]{2,1,0:T(8,128)(2,1)S(1)}, u32[]{:S(2)}, u32[]{:S(2)}) collective-permute-start(bf16[4,48,1280]{2,1,0:T(8,128)(2,1)S(1)} %maximum_select_fusion.18), channel_id=1, source_target_pairs={{0,6},{2,4},{4,2},{6,0},{8,14},{10,12},{12,10},{14,8},{16,22},{18,... | collective-permute-start | bytes 1474568 | tf_op jit(solution)/shard_map/ppermute | solution.py:69
  18.2 4.7 collective-permute-start.6
  18.2 8.8 %collective-permute-start.7 = (bf16[48,1920]{1,0:T(8,128)(2,1)S(1)}, bf16[48,1920]{1,0:T(8,128)(2,1)S(1)}, u32[]{:S(2)}, u32[]{:S(2)}) collective-permute-start(bf16[48,1920]{1,0:T(8,128)(2,1)S(1)} %pad_maximum_fusion.17), channel_id=1, source_target_pairs={{0,16},{2,18},{4,20},{6,22},{8,24},{10,26},{12,28},{14,30},{16,0},... | collective-permute-start | bytes 552968 | tf_op jit(solution)/shard_map/ppermute | solution.py:69
  22.9 13.5 %collective-permute-start.8 = (bf16[48,1920]{1,0:T(8,128)(2,1)S(1)}, bf16[48,1920]{1,0:T(8,128)(2,1)S(1)}, u32[]{:S(2)}, u32[]{:S(2)}) collective-permute-start(bf16[48,1920]{1,0:T(8,128)(2,1)S(1)} %pad_maximum_fusion.17), channel_id=1, source_target_pairs={{0,24},{2,26},{4,28},{6,30},{8,16},{10,18},{12,20},{14,22},{16,8},... | collective-permute-start | bytes 552968 | tf_op jit(solution)/shard_map/ppermute | solution.py:69
  38.3 7.6 %collective-permute-start.9 = (bf16[768,1280]{1,0:T(8,128)(2,1)S(1)}, bf16[768,1280]{1,0:T(8,128)(2,1)}, u32[]{:S(2)}, u32[]{:S(2)}) collective-permute-start(bf16[768,1280]{1,0:T(8,128)(2,1)S(1)} %bitcast.281), channel_id=1, source_target_pairs={{0,1},{1,0},{2,3},{3,2},{4,5},{5,4},{6,7},{7,6},{8,9},{9,8},{10,11... | collective-permute-start | bytes 5898248 | tf_op jit(solution)/shard_map/ppermute | solution.py:73
  43.2 38.9 %collective-permute-start.10 = (bf16[4,48,1920]{2,1,0:T(8,128)(2,1)S(1)}, bf16[4,48,1920]{2,1,0:T(8,128)(2,1)S(1)}, u32[]{:S(2)}, u32[]{:S(2)}) collective-permute-start(bf16[4,48,1920]{2,1,0:T(8,128)(2,1)S(1)} %maximum_select_fusion.12), channel_id=1, source_target_pairs={{0,2},{2,0},{4,6},{6,4},{8,10},{10,8},{12,14},{14,12},{16,18},{18,... | collective-permute-start | bytes 2211848 | tf_op jit(solution)/shard_map/ppermute | solution.py:69
  44.2 37.9 %collective-permute-start.11 = (bf16[4,48,1920]{2,1,0:T(8,128)(2,1)S(1)}, bf16[4,48,1920]{2,1,0:T(8,128)(2,1)}, u32[]{:S(2)}, u32[]{:S(2)}) collective-permute-start(bf16[4,48,1920]{2,1,0:T(8,128)(2,1)S(1)} %maximum_select_fusion.12), channel_id=1, source_target_pairs={{0,4},{2,6},{4,0},{6,2},{8,12},{10,14},{12,8},{14,10},{16,20},{18,... | collective-permute-start | bytes 2211848 | tf_op jit(solution)/shard_map/ppermute | solution.py:69
  44.8 37.4 %collective-permute-start.12 = (bf16[4,48,1920]{2,1,0:T(8,128)(2,1)S(1)}, bf16[4,48,1920]{2,1,0:T(8,128)(2,1)}, u32[]{:S(2)}, u32[]{:S(2)}) collective-permute-start(bf16[4,48,1920]{2,1,0:T(8,128)(2,1)S(1)} %maximum_select_fusion.12), channel_id=1, source_target_pairs={{0,6},{2,4},{4,2},{6,0},{8,14},{10,12},{12,10},{14,8},{16,22},{18,... | collective-permute-start | bytes 2211848 | tf_op jit(solution)/shard_map/ppermute | solution.py:69
  45.9 16.8 %collective-permute-start.13 = (bf16[48,1536]{1,0:T(8,128)(2,1)}, bf16[48,1536]{1,0:T(8,128)(2,1)}, u32[]{:S(2)}, u32[]{:S(2)}) collective-permute-start(bf16[48,1536]{1,0:T(8,128)(2,1)} %convert_element_type.356), channel_id=1, source_target_pairs={{0,8},{2,10},{4,12},{6,14},{8,0},{10,2},{12,4},{14,6},{16,24},{18,... | collective-permute-start | bytes 442376 | tf_op jit(solution)/shard_map/ppermute | solution.py:69
  45.9 36.2 %collective-permute-start.14 = (bf16[48,1536]{1,0:T(8,128)(2,1)}, bf16[48,1536]{1,0:T(8,128)(2,1)}, u32[]{:S(2)}, u32[]{:S(2)}) collective-permute-start(bf16[48,1536]{1,0:T(8,128)(2,1)} %convert_element_type.356), channel_id=1, source_target_pairs={{0,16},{2,18},{4,20},{6,22},{8,24},{10,26},{12,28},{14,30},{16,0},... | collective-permute-start | bytes 442376 | tf_op jit(solution)/shard_map/ppermute | solution.py:69
  62.7 19.4 %collective-permute-start.15 = (bf16[48,1536]{1,0:T(8,128)(2,1)S(1)}, bf16[48,1536]{1,0:T(8,128)(2,1)S(1)}, u32[]{:S(2)}, u32[]{:S(2)}) collective-permute-start(bf16[48,1536]{1,0:T(8,128)(2,1)S(1)} %copy-done.36), channel_id=1, source_target_pairs={{0,24},{2,26},{4,28},{6,30},{8,16},{10,18},{12,20},{14,22},{16,8},... | collective-permute-start | bytes 442376 | tf_op jit(solution)/shard_map/ppermute | solution.py:69
  85.4 6.5 %collective-permute-start.16 = (bf16[768,1920]{1,0:T(8,128)(2,1)S(1)}, bf16[768,1920]{1,0:T(8,128)(2,1)S(1)}, u32[]{:S(2)}, u32[]{:S(2)}) collective-permute-start(bf16[768,1920]{1,0:T(8,128)(2,1)S(1)} %bitcast.294), channel_id=1, source_target_pairs={{0,1},{1,0},{2,3},{3,2},{4,5},{5,4},{6,7},{7,6},{8,9},{9,8},{10,11... | collective-permute-start | bytes 8847368 | tf_op jit(solution)/shard_map/ppermute | solution.py:73
  89.1 26.2 %collective-permute-start.17 = (bf16[4,48,1536]{2,1,0:T(8,128)(2,1)S(1)}, bf16[4,48,1536]{2,1,0:T(8,128)(2,1)S(1)}, u32[]{:S(2)}, u32[]{:S(2)}) collective-permute-start(bf16[4,48,1536]{2,1,0:T(8,128)(2,1)S(1)} %maximum_select_fusion.14), channel_id=1, source_target_pairs={{0,2},{2,0},{4,6},{6,4},{8,10},{10,8},{12,14},{14,12},{16,18},{18,... | collective-permute-start | bytes 1769480 | tf_op jit(solution)/shard_map/ppermute | solution.py:69
  90.1 25.2 %collective-permute-start.18 = (bf16[4,48,1536]{2,1,0:T(8,128)(2,1)S(1)}, bf16[4,48,1536]{2,1,0:T(8,128)(2,1)S(1)}, u32[]{:S(2)}, u32[]{:S(2)}) collective-permute-start(bf16[4,48,1536]{2,1,0:T(8,128)(2,1)S(1)} %maximum_select_fusion.14), channel_id=1, source_target_pairs={{0,4},{2,6},{4,0},{6,2},{8,12},{10,14},{12,8},{14,10},{16,20},{18,... | collective-permute-start | bytes 1769480 | tf_op jit(solution)/shard_map/ppermute | solution.py:69
  90.6 26.5 %collective-permute-start.19 = (bf16[4,48,1536]{2,1,0:T(8,128)(2,1)S(1)}, bf16[4,48,1536]{2,1,0:T(8,128)(2,1)S(1)}, u32[]{:S(2)}, u32[]{:S(2)}) collective-permute-start(bf16[4,48,1536]{2,1,0:T(8,128)(2,1)S(1)} %maximum_select_fusion.14), channel_id=1, source_target_pairs={{0,6},{2,4},{4,2},{6,0},{8,14},{10,12},{12,10},{14,8},{16,22},{18,... | collective-permute-start | bytes 1769480 | tf_op jit(solution)/shard_map/ppermute | solution.py:69
  118.1 5.6 %collective-permute-start.20 = (bf16[768,1536]{1,0:T(8,128)(2,1)S(1)}, bf16[768,1536]{1,0:T(8,128)(2,1)S(1)}, u32[]{:S(2)}, u32[]{:S(2)}) collective-permute-start(bf16[768,1536]{1,0:T(8,128)(2,1)S(1)} %bitcast.299), channel_id=1, source_target_pairs={{0,1},{1,0},{2,3},{3,2},{4,5},{5,4},{6,7},{7,6},{8,9},{9,8},{10,11... | collective-permute-start | bytes 7077896 | tf_op jit(solution)/shard_map/ppermute | solution.py:73
  143.0 5.0 %collective-permute-start.21 = (bf16[768,1536]{1,0:T(8,128)(2,1)}, bf16[768,1536]{1,0:T(8,128)(2,1)}, u32[]{:S(2)}, u32[]{:S(2)}) collective-permute-start(bf16[768,1536]{1,0:T(8,128)(2,1)} %convolution_convert_fusion.1), channel_id=1, source_target_pairs={{0,1},{1,0},{2,3},{3,2},{4,5},{5,4},{6,7},{7,6},{8,9},{9,8},{10,11... | collective-permute-start | bytes 7077896 | tf_op jit(solution)/shard_map/ppermute | solution.py:73
  150.8 26.9 %collective-permute-start.22 = (bf16[4,48,1536]{2,1,0:T(8,128)(2,1)S(1)}, bf16[4,48,1536]{2,1,0:T(8,128)(2,1)S(1)}, u32[]{:S(2)}, u32[]{:S(2)}) collective-permute-start(bf16[4,48,1536]{2,1,0:T(8,128)(2,1)S(1)} %get-tuple-element.388), channel_id=1, source_target_pairs={{0,2},{2,0},{4,6},{6,4},{8,10},{10,8},{12,14},{14,12},{16,18},{18,... | collective-permute-start | bytes 1769480 | tf_op jit(solution)/shard_map/ppermute | solution.py:69
  151.4 26.3 %collective-permute-start.23 = (bf16[4,48,1536]{2,1,0:T(8,128)(2,1)S(1)}, bf16[4,48,1536]{2,1,0:T(8,128)(2,1)S(1)}, u32[]{:S(2)}, u32[]{:S(2)}) collective-permute-start(bf16[4,48,1536]{2,1,0:T(8,128)(2,1)S(1)} %get-tuple-element.387), channel_id=1, source_target_pairs={{0,4},{2,6},{4,0},{6,2},{8,12},{10,14},{12,8},{14,10},{16,20},{18,... | collective-permute-start | bytes 1769480 | tf_op jit(solution)/shard_map/ppermute | solution.py:69
  152.6 25.8 %collective-permute-start.24 = (bf16[4,48,1536]{2,1,0:T(8,128)(2,1)S(1)}, bf16[4,48,1536]{2,1,0:T(8,128)(2,1)S(1)}, u32[]{:S(2)}, u32[]{:S(2)}) collective-permute-start(bf16[4,48,1536]{2,1,0:T(8,128)(2,1)S(1)} %get-tuple-element.386), channel_id=1, source_target_pairs={{0,6},{2,4},{4,2},{6,0},{8,14},{10,12},{12,10},{14,8},{16,22},{18,... | collective-permute-start | bytes 1769480 | tf_op jit(solution)/shard_map/ppermute | solution.py:69
  186.0 14.6 %collective-permute-start.25 = (bf16[768,1920]{1,0:T(8,128)(2,1)}, bf16[768,1920]{1,0:T(8,128)(2,1)}, u32[]{:S(2)}, u32[]{:S(2)}) collective-permute-start(bf16[768,1920]{1,0:T(8,128)(2,1)} %pad_maximum_fusion.1), channel_id=1, source_target_pairs={{0,1},{1,0},{2,3},{3,2},{4,5},{5,4},{6,7},{7,6},{8,9},{9,8},{10,11... | collective-permute-start | bytes 8847368 | tf_op jit(solution)/shard_map/ppermute | solution.py:73
  195.0 15.8 %collective-permute-start.29 = (bf16[48,1536]{1,0:T(8,128)(2,1)S(1)}, bf16[48,1536]{1,0:T(8,128)(2,1)S(1)}, u32[]{:S(2)}, u32[]{:S(2)}) collective-permute-start(bf16[48,1536]{1,0:T(8,128)(2,1)S(1)} %get-tuple-element.406), channel_id=1, source_target_pairs={{0,8},{2,10},{4,12},{6,14},{8,0},{10,2},{12,4},{14,6},{16,24},{18,... | collective-permute-start | bytes 442376 | tf_op jit(solution)/shard_map/ppermute | solution.py:69
  196.1 30.0 %collective-permute-start.30 = (bf16[48,1536]{1,0:T(8,128)(2,1)}, bf16[48,1536]{1,0:T(8,128)(2,1)S(1)}, u32[]{:S(2)}, u32[]{:S(2)}) collective-permute-start(bf16[48,1536]{1,0:T(8,128)(2,1)} %get-tuple-element.405), channel_id=1, source_target_pairs={{0,16},{2,18},{4,20},{6,22},{8,24},{10,26},{12,28},{14,30},{16,0},... | collective-permute-start | bytes 442376 | tf_op jit(solution)/shard_map/ppermute | solution.py:69
  197.9 28.3 %collective-permute-start.31 = (bf16[48,1536]{1,0:T(8,128)(2,1)}, bf16[48,1536]{1,0:T(8,128)(2,1)}, u32[]{:S(2)}, u32[]{:S(2)}) collective-permute-start(bf16[48,1536]{1,0:T(8,128)(2,1)} %get-tuple-element.404), channel_id=1, source_target_pairs={{0,24},{2,26},{4,28},{6,30},{8,16},{10,18},{12,20},{14,22},{16,8},... | collective-permute-start | bytes 442376 | tf_op jit(solution)/shard_map/ppermute | solution.py:69
  206.6 19.5 %collective-permute-start.28 = (bf16[4,48,1920]{2,1,0:T(8,128)(2,1)}, bf16[4,48,1920]{2,1,0:T(8,128)(2,1)S(1)}, u32[]{:S(2)}, u32[]{:S(2)}) collective-permute-start(bf16[4,48,1920]{2,1,0:T(8,128)(2,1)} %pad_maximum_fusion.10), channel_id=1, source_target_pairs={{0,6},{2,4},{4,2},{6,0},{8,14},{10,12},{12,10},{14,8},{16,22},{18,... | collective-permute-start | bytes 2211848 | tf_op jit(solution)/shard_map/ppermute | solution.py:69
  208.8 33.3 %collective-permute-start.27 = (bf16[4,48,1920]{2,1,0:T(8,128)(2,1)}, bf16[4,48,1920]{2,1,0:T(8,128)(2,1)}, u32[]{:S(2)}, u32[]{:S(2)}) collective-permute-start(bf16[4,48,1920]{2,1,0:T(8,128)(2,1)} %pad_maximum_fusion.9), channel_id=1, source_target_pairs={{0,4},{2,6},{4,0},{6,2},{8,12},{10,14},{12,8},{14,10},{16,20},{18,... | collective-permute-start | bytes 2211848 | tf_op jit(solution)/shard_map/ppermute | solution.py:69
  210.7 31.3 %collective-permute-start.26 = (bf16[4,48,1920]{2,1,0:T(8,128)(2,1)}, bf16[4,48,1920]{2,1,0:T(8,128)(2,1)}, u32[]{:S(2)}, u32[]{:S(2)}) collective-permute-start(bf16[4,48,1920]{2,1,0:T(8,128)(2,1)} %pad_maximum_fusion.8), channel_id=1, source_target_pairs={{0,2},{2,0},{4,6},{6,4},{8,10},{10,8},{12,14},{14,12},{16,18},{18,... | collective-permute-start | bytes 2211848 | tf_op jit(solution)/shard_map/ppermute | solution.py:69
  244.0 10.6 %collective-permute-start.35 = (bf16[48,1536]{1,0:T(8,128)(2,1)S(1)}, bf16[48,1536]{1,0:T(8,128)(2,1)S(1)}, u32[]{:S(2)}, u32[]{:S(2)}) collective-permute-start(bf16[48,1536]{1,0:T(8,128)(2,1)S(1)} %get-tuple-element.233), channel_id=1, source_target_pairs={{0,8},{2,10},{4,12},{6,14},{8,0},{10,2},{12,4},{14,6},{16,24},{18,... | collective-permute-start | bytes 442376 | tf_op jit(solution)/shard_map/ppermute | solution.py:69
  245.8 24.4 %collective-permute-start.36 = (bf16[48,1536]{1,0:T(8,128)(2,1)S(1)}, bf16[48,1536]{1,0:T(8,128)(2,1)}, u32[]{:S(2)}, u32[]{:S(2)}) collective-permute-start(bf16[48,1536]{1,0:T(8,128)(2,1)S(1)} %get-tuple-element.233), channel_id=1, source_target_pairs={{0,16},{2,18},{4,20},{6,22},{8,24},{10,26},{12,28},{14,30},{16,0},... | collective-permute-start | bytes 442376 | tf_op jit(solution)/shard_map/ppermute | solution.py:69
  246.7 23.5 %collective-permute-start.37 = (bf16[48,1536]{1,0:T(8,128)(2,1)S(1)}, bf16[48,1536]{1,0:T(8,128)(2,1)}, u32[]{:S(2)}, u32[]{:S(2)}) collective-permute-start(bf16[48,1536]{1,0:T(8,128)(2,1)S(1)} %get-tuple-element.233), channel_id=1, source_target_pairs={{0,24},{2,26},{4,28},{6,30},{8,16},{10,18},{12,20},{14,22},{16,8},... | collective-permute-start | bytes 442376 | tf_op jit(solution)/shard_map/ppermute | solution.py:69
  250.1 21.8 %collective-permute-start.34 = (bf16[48,1920]{1,0:T(8,128)(2,1)S(1)}, bf16[48,1920]{1,0:T(8,128)(2,1)S(1)}, u32[]{:S(2)}, u32[]{:S(2)}) collective-permute-start(bf16[48,1920]{1,0:T(8,128)(2,1)S(1)} %pad_maximum_fusion.20), channel_id=1, source_target_pairs={{0,24},{2,26},{4,28},{6,30},{8,16},{10,18},{12,20},{14,22},{16,8},... | collective-permute-start | bytes 552968 | tf_op jit(solution)/shard_map/ppermute | solution.py:69
  251.3 23.2 %collective-permute-start.33 = (bf16[48,1920]{1,0:T(8,128)(2,1)S(1)}, bf16[48,1920]{1,0:T(8,128)(2,1)S(1)}, u32[]{:S(2)}, u32[]{:S(2)}) collective-permute-start(bf16[48,1920]{1,0:T(8,128)(2,1)S(1)} %pad_maximum_fusion.19), channel_id=1, source_target_pairs={{0,16},{2,18},{4,20},{6,22},{8,24},{10,26},{12,28},{14,30},{16,0},... | collective-permute-start | bytes 552968 | tf_op jit(solution)/shard_map/ppermute | solution.py:69
  255.3 19.2 %collective-permute-start.32 = (bf16[48,1920]{1,0:T(8,128)(2,1)S(1)}, bf16[48,1920]{1,0:T(8,128)(2,1)S(1)}, u32[]{:S(2)}, u32[]{:S(2)}) collective-permute-start(bf16[48,1920]{1,0:T(8,128)(2,1)S(1)} %pad_maximum_fusion.18), channel_id=1, source_target_pairs={{0,8},{2,10},{4,12},{6,14},{8,0},{10,2},{12,4},{14,6},{16,24},{18,... | collective-permute-start | bytes 552968 | tf_op jit(solution)/shard_map/ppermute | solution.py:69
  276.1 15.0 %collective-permute-start.38 = (f32[16,768]{1,0:T(8,128)}, f32[16,768]{1,0:T(8,128)S(1)}, u32[]{:S(2)}, u32[]{:S(2)}) collective-permute-start(f32[16,768]{1,0:T(8,128)} %vector_grads.1), channel_id=1, source_target_pairs={{0,1},{1,0},{2,3},{3,2},{4,5},{5,4},{6,7},{7,6},{8,9},{9,8},{10,11... | collective-permute-start | bytes 147464 | tf_op jit(solution)/shard_map/ppermute | solution.py:73
  284.4 7.5 %collective-permute-start.39 = (bf16[768,1152]{0,1:T(8,128)(2,1)S(1)}, bf16[768,1152]{0,1:T(8,128)(2,1)S(1)}, u32[]{:S(2)}, u32[]{:S(2)}) collective-permute-start(bf16[768,1152]{0,1:T(8,128)(2,1)S(1)} %fusion.7), channel_id=1, source_target_pairs={{0,1},{1,0},{2,3},{3,2},{4,5},{5,4},{6,7},{7,6},{8,9},{9,8},{10,11... | collective-permute-start | bytes 5308424 | tf_op jit(solution)/shard_map/ppermute | solution.py:73
  292.0 18.5 %collective-permute-start.43 = (bf16[48,1920]{1,0:T(8,128)(2,1)}, bf16[48,1920]{1,0:T(8,128)(2,1)}, u32[]{:S(2)}, u32[]{:S(2)}) collective-permute-start(bf16[48,1920]{1,0:T(8,128)(2,1)} %pad_maximum_fusion.21), channel_id=1, source_target_pairs={{0,8},{2,10},{4,12},{6,14},{8,0},{10,2},{12,4},{14,6},{16,24},{18,... | collective-permute-start | bytes 552968 | tf_op jit(solution)/shard_map/ppermute | solution.py:69
  294.2 21.9 %collective-permute-start.44 = (bf16[48,1920]{1,0:T(8,128)(2,1)}, bf16[48,1920]{1,0:T(8,128)(2,1)}, u32[]{:S(2)}, u32[]{:S(2)}) collective-permute-start(bf16[48,1920]{1,0:T(8,128)(2,1)} %pad_maximum_fusion.21), channel_id=1, source_target_pairs={{0,16},{2,18},{4,20},{6,22},{8,24},{10,26},{12,28},{14,30},{16,0},... | collective-permute-start | bytes 552968 | tf_op jit(solution)/shard_map/ppermute | solution.py:69
  295.1 21.0 %collective-permute-start.45 = (bf16[48,1920]{1,0:T(8,128)(2,1)}, bf16[48,1920]{1,0:T(8,128)(2,1)}, u32[]{:S(2)}, u32[]{:S(2)}) collective-permute-start(bf16[48,1920]{1,0:T(8,128)(2,1)} %pad_maximum_fusion.21), channel_id=1, source_target_pairs={{0,24},{2,26},{4,28},{6,30},{8,16},{10,18},{12,20},{14,22},{16,8},... | collective-permute-start | bytes 552968 | tf_op jit(solution)/shard_map/ppermute | solution.py:69
  303.7 12.8 %collective-permute-start.42 = (bf16[4,48,1280]{2,1,0:T(8,128)(2,1)S(1)}, bf16[4,48,1280]{2,1,0:T(8,128)(2,1)S(1)}, u32[]{:S(2)}, u32[]{:S(2)}) collective-permute-start(bf16[4,48,1280]{2,1,0:T(8,128)(2,1)S(1)} %pad_maximum_fusion.15), channel_id=1, source_target_pairs={{0,6},{2,4},{4,2},{6,0},{8,14},{10,12},{12,10},{14,8},{16,22},{18,... | collective-permute-start | bytes 1474568 | tf_op jit(solution)/shard_map/ppermute | solution.py:69
  305.0 23.3 %collective-permute-start.41 = (bf16[4,48,1280]{2,1,0:T(8,128)(2,1)S(1)}, bf16[4,48,1280]{2,1,0:T(8,128)(2,1)S(1)}, u32[]{:S(2)}, u32[]{:S(2)}) collective-permute-start(bf16[4,48,1280]{2,1,0:T(8,128)(2,1)S(1)} %pad_maximum_fusion.14), channel_id=1, source_target_pairs={{0,4},{2,6},{4,0},{6,2},{8,12},{10,14},{12,8},{14,10},{16,20},{18,... | collective-permute-start | bytes 1474568 | tf_op jit(solution)/shard_map/ppermute | solution.py:69
  310.5 17.8 %collective-permute-start.40 = (bf16[4,48,1280]{2,1,0:T(8,128)(2,1)S(1)}, bf16[4,48,1280]{2,1,0:T(8,128)(2,1)S(1)}, u32[]{:S(2)}, u32[]{:S(2)}) collective-permute-start(bf16[4,48,1280]{2,1,0:T(8,128)(2,1)S(1)} %pad_maximum_fusion.13), channel_id=1, source_target_pairs={{0,2},{2,0},{4,6},{6,4},{8,10},{10,8},{12,14},{14,12},{16,18},{18,... | collective-permute-start | bytes 1474568 | tf_op jit(solution)/shard_map/ppermute | solution.py:69
  331.5 22.8 %collective-permute-start.48 = (bf16[48,1280]{0,1:T(8,128)(2,1)S(1)}, bf16[48,1280]{0,1:T(8,128)(2,1)S(1)}, u32[]{:S(2)}, u32[]{:S(2)}) collective-permute-start(bf16[48,1280]{0,1:T(8,128)(2,1)S(1)} %copy.291), channel_id=1, source_target_pairs={{0,24},{2,26},{4,28},{6,30},{8,16},{10,18},{12,20},{14,22},{16,8},... | collective-permute-start | bytes 368648 | tf_op jit(solution)/shard_map/ppermute | solution.py:69
  333.6 26.7 %collective-permute-start.47 = (bf16[48,1280]{0,1:T(8,128)(2,1)}, bf16[48,1280]{0,1:T(8,128)(2,1)S(1)}, u32[]{:S(2)}, u32[]{:S(2)}) collective-permute-start(bf16[48,1280]{0,1:T(8,128)(2,1)} %copy.290), channel_id=1, source_target_pairs={{0,16},{2,18},{4,20},{6,22},{8,24},{10,26},{12,28},{14,30},{16,0},... | collective-permute-start | bytes 368648 | tf_op jit(solution)/shard_map/ppermute | solution.py:69
  337.8 22.5 %collective-permute-start.46 = (bf16[48,1280]{0,1:T(8,128)(2,1)}, bf16[48,1280]{0,1:T(8,128)(2,1)S(1)}, u32[]{:S(2)}, u32[]{:S(2)}) collective-permute-start(bf16[48,1280]{0,1:T(8,128)(2,1)} %copy.289), channel_id=1, source_target_pairs={{0,8},{2,10},{4,12},{6,14},{8,0},{10,2},{12,4},{14,6},{16,24},{18,... | collective-permute-start | bytes 368648 | tf_op jit(solution)/shard_map/ppermute | solution.py:69
  361.2 13.1 %collective-permute-start.49 = (bf16[48,1152]{0,1:T(8,128)(2,1)S(1)}, bf16[48,1152]{0,1:T(8,128)(2,1)S(1)}, u32[]{:S(2)}, u32[]{:S(2)}) collective-permute-start(bf16[48,1152]{0,1:T(8,128)(2,1)S(1)} %get-tuple-element.255), channel_id=1, source_target_pairs={{0,8},{2,10},{4,12},{6,14},{8,0},{10,2},{12,4},{14,6},{16,24},{18,... | collective-permute-start | bytes 331784 | tf_op jit(solution)/shard_map/ppermute | solution.py:69
  363.3 13.1 %collective-permute-start.50 = (bf16[48,1152]{0,1:T(8,128)(2,1)S(1)}, bf16[48,1152]{0,1:T(8,128)(2,1)S(1)}, u32[]{:S(2)}, u32[]{:S(2)}) collective-permute-start(bf16[48,1152]{0,1:T(8,128)(2,1)S(1)} %get-tuple-element.255), channel_id=1, source_target_pairs={{0,16},{2,18},{4,20},{6,22},{8,24},{10,26},{12,28},{14,30},{16,0},... | collective-permute-start | bytes 331784 | tf_op jit(solution)/shard_map/ppermute | solution.py:69
  364.2 24.9 %collective-permute-start.51 = (bf16[48,1152]{0,1:T(8,128)(2,1)S(1)}, bf16[48,1152]{0,1:T(8,128)(2,1)S(1)}, u32[]{:S(2)}, u32[]{:S(2)}) collective-permute-start(bf16[48,1152]{0,1:T(8,128)(2,1)S(1)} %get-tuple-element.255), channel_id=1, source_target_pairs={{0,24},{2,26},{4,28},{6,30},{8,16},{10,18},{12,20},{14,22},{16,8},... | collective-permute-start | bytes 331784 | tf_op jit(solution)/shard_map/ppermute | solution.py:69
  395.1 13.8 %collective-permute-start.52 = (bf16[4,48,1536]{2,1,0:T(8,128)(2,1)}, bf16[4,48,1536]{2,1,0:T(8,128)(2,1)}, u32[]{:S(2)}, u32[]{:S(2)}) collective-permute-start(bf16[4,48,1536]{2,1,0:T(8,128)(2,1)} %bitcast.105), channel_id=1, source_target_pairs={{0,6},{2,4},{4,2},{6,0},{8,14},{10,12},{12,10},{14,8},{16,22},{18,... | collective-permute-start | bytes 1769480 | tf_op jit(solution)/shard_map/ppermute | solution.py:69
  396.6 27.6 %collective-permute-start.53 = (bf16[4,48,1536]{2,1,0:T(8,128)(2,1)}, bf16[4,48,1536]{2,1,0:T(8,128)(2,1)}, u32[]{:S(2)}, u32[]{:S(2)}) collective-permute-start(bf16[4,48,1536]{2,1,0:T(8,128)(2,1)} %bitcast.107), channel_id=1, source_target_pairs={{0,4},{2,6},{4,0},{6,2},{8,12},{10,14},{12,8},{14,10},{16,20},{18,... | collective-permute-start | bytes 1769480 | tf_op jit(solution)/shard_map/ppermute | solution.py:69
  397.5 28.6 %collective-permute-start.54 = (bf16[4,48,1536]{2,1,0:T(8,128)(2,1)}, bf16[4,48,1536]{2,1,0:T(8,128)(2,1)S(1)}, u32[]{:S(2)}, u32[]{:S(2)}) collective-permute-start(bf16[4,48,1536]{2,1,0:T(8,128)(2,1)} %bitcast.318), channel_id=1, source_target_pairs={{0,2},{2,0},{4,6},{6,4},{8,10},{10,8},{12,14},{14,12},{16,18},{18,... | collective-permute-start | bytes 1769480 | tf_op jit(solution)/shard_map/ppermute | solution.py:69
  430.3 9.3 %collective-permute-start.55 = (f32[768,768]{1,0:T(8,128)}, f32[768,768]{1,0:T(8,128)}, u32[]{:S(2)}, u32[]{:S(2)}) collective-permute-start(f32[768,768]{1,0:T(8,128)} %fusion.101.own_ref), channel_id=1, source_target_pairs={{0,1},{1,0},{2,3},{3,2},{4,5},{5,4},{6,7},{7,6},{8,9},{9,8},{10,11... | collective-permute-start | bytes 7077896 | tf_op jit(solution)/shard_map/ppermute | solution.py:73
  439.6 34.9 %slice-start.8 = ((bf16[48,1280]{0,1:T(8,128)(2,1)}), bf16[48,128]{0,1:T(8,128)(2,1)S(1)}, s32[]{:S(2)}) async-start(bf16[48,1280]{0,1:T(8,128)(2,1)} %copy-done.37), calls=%async_computation.8 | async-start | bytes 65536 | tf_op jit(solution)/shard_map/slice | solution.py:146
  439.6 34.9 %slice-start.9 = ((bf16[48,1280]{0,1:T(8,128)(2,1)}), bf16[48,128]{0,1:T(8,128)(2,1)S(1)}, s32[]{:S(2)}) async-start(bf16[48,1280]{0,1:T(8,128)(2,1)} %copy-done.38), calls=%async_computation.9 | async-start | bytes 65536 | tf_op jit(solution)/shard_map/slice | solution.py:146
  439.6 34.9 %slice-start.10 = ((bf16[48,1280]{0,1:T(8,128)(2,1)}), bf16[48,128]{0,1:T(8,128)(2,1)S(1)}, s32[]{:S(2)}) async-start(bf16[48,1280]{0,1:T(8,128)(2,1)} %copy-done.39), calls=%async_computation.10 | async-start | bytes 65536 | tf_op jit(solution)/shard_map/slice | solution.py:146
  439.6 34.9 %copy-start.56 = (f32[6,48]{1,0:T(8,128)S(1)}, f32[6,48]{1,0:T(8,128)}, u32[]{:S(2)}) copy-start(f32[6,48]{1,0:T(8,128)} %param.25) | copy-start | bytes 3460
  473.2 5.9 %collective-permute-start.58 = (bf16[48,1536]{1,0:T(8,128)(2,1)S(1)}, bf16[48,1536]{1,0:T(8,128)(2,1)S(1)}, u32[]{:S(2)}, u32[]{:S(2)}) collective-permute-start(bf16[48,1536]{1,0:T(8,128)(2,1)S(1)} %get-tuple-element.417), channel_id=1, source_target_pairs={{0,2},{2,0},{4,6},{6,4},{8,10},{10,8},{12,14},{14,12},{16,18},{18,... | collective-permute-start | bytes 442376 | tf_op jit(solution)/shard_map/ppermute | solution.py:69
  477.6 6.1 %collective-permute-start.56 = (bf16[48,1536]{1,0:T(8,128)(2,1)S(1)}, bf16[48,1536]{1,0:T(8,128)(2,1)S(1)}, u32[]{:S(2)}, u32[]{:S(2)}) collective-permute-start(bf16[48,1536]{1,0:T(8,128)(2,1)S(1)} %get-tuple-element.415), channel_id=1, source_target_pairs={{0,6},{2,4},{4,2},{6,0},{8,14},{10,12},{12,10},{14,8},{16,22},{18,... | collective-permute-start | bytes 442376 | tf_op jit(solution)/shard_map/ppermute | solution.py:69
  479.1 8.4 %collective-permute-start.57 = (bf16[48,1536]{1,0:T(8,128)(2,1)S(1)}, bf16[48,1536]{1,0:T(8,128)(2,1)S(1)}, u32[]{:S(2)}, u32[]{:S(2)}) collective-permute-start(bf16[48,1536]{1,0:T(8,128)(2,1)S(1)} %get-tuple-element.418), channel_id=1, source_target_pairs={{0,4},{2,6},{4,0},{6,2},{8,12},{10,14},{12,8},{14,10},{16,20},{18,... | collective-permute-start | bytes 442376 | tf_op jit(solution)/shard_map/ppermute | solution.py:69
  (76 other events, 515.7 us)

commit v3 on v2

--- a/solution.py
+++ b/solution.py
@@ -1,10 +1,10 @@
-import functools
 import math
 
 import jax
 import jax.numpy as jnp
 from jax import lax
 from jax.experimental import pallas as pl
+from jax.experimental.layout import Layout, with_layout_constraint
 from jax.experimental.pallas import tpu as pltpu
 from jax.sharding import PartitionSpec as P
 
@@ -35,8 +35,10 @@
 VEC_PAD = 128
 GROUP = 4
 TILE = 256
+CHUNK = 256
 ROWS = 256
 VROWS = 8 + FF // D
+SMALL = pl.CostEstimate(flops=1 << 20, bytes_accessed=1 << 16, transcendentals=0)
 PAIR = 2 * HEAD_DIM
 PAIRS = HEADS // 2
 BLOCKS = 3 * PAIRS
@@ -65,12 +67,16 @@
     )
 
 
+def by_rows(values):
+    return with_layout_constraint(values, Layout(major_to_minor=tuple(range(values.ndim))))
+
+
 def flip(values, mask, size):
-    return lax.ppermute(values, "fsdp", [(i, i ^ mask) for i in range(size)])
+    return by_rows(lax.ppermute(by_rows(values), "fsdp", [(i, i ^ mask) for i in range(size)]))
 
 
 def swap_cores(values):
-    return lax.ppermute(values, "row", SWAP)
+    return by_rows(lax.ppermute(by_rows(values), "row", SWAP))
 
 
 def together(*values):
@@ -126,15 +132,32 @@
     return [lax.dynamic_index_in_dim(part, place, axis, keepdims=False) for part in parts]
 
 
-def leave_four(parts, axis, bit, size):
+def split_four(parts, axis, bit):
     mine = pair_of(bit)
-    kept = pick_four(parts, axis, mine)
-    arrived = []
+    leaving = []
     for step in (1, 2, 3):
-        leaving = pick_four(parts, axis, mine ^ step)
-        leaving = jnp.concatenate([part.astype(jnp.bfloat16) for part in leaving], axis=-1)
-        arrived.append(flip(leaving, step << bit, size))
-    return kept, arrived
+        pieces = pick_four(parts, axis, mine ^ step)
+        leaving.append(jnp.concatenate([part.astype(jnp.bfloat16) for part in pieces], axis=-1))
+    return pick_four(parts, axis, mine), leaving
+
+
+def fly_four(leaving, bit, size):
+    return [flip(piece, step << bit, size) for step, piece in zip((1, 2, 3), leaving)]
+
+
+def split_two(parts, axis, bit):
+    mine = my_bit(bit)
+    pieces = pick_four(parts, axis, 1 - mine)
+    leaving = jnp.concatenate([part.astype(jnp.bfloat16) for part in pieces], axis=-1)
+    return pick_four(parts, axis, mine), leaving
+
+
+def place_two(values, arrived, bit, axis):
+    return jnp.where(
+        my_bit(bit) == 1,
+        jnp.stack([arrived, values], axis),
+        jnp.stack([values, arrived], axis),
+    )
 
 
 def add_four(kept, arrived):
@@ -148,17 +171,55 @@
     return totals
 
 
-def leave_low(parts, size):
+def split_low(parts, size):
     shape = (4,) * ((size.bit_length() - 1) // 2) + (D // size, -1)
     parts = [part.reshape(shape) for part in parts]
-    return leave_four(parts, len(shape) - 3, 0, size)
-
-
-def leave_high(kept, arrived, size):
+    return split_four(parts, len(shape) - 3, 0)
+
+
+def fly_low(leaving, size):
+    return fly_four(leaving, 0, size)
+
+
+def add_low(kept, arrived, size):
     parts = add_four(kept, arrived)
     for bit in range(2, size.bit_length() - 3, 2):
-        parts = add_four(*leave_four(parts, parts[0].ndim - 3, bit, size))
-    return leave_four(parts, 0, size.bit_length() - 3, size)
+        kept, leaving = split_four(parts, parts[0].ndim - 3, bit)
+        parts = add_four(kept, fly_four(leaving, bit, size))
+    return parts
+
+
+def split_high(kept, arrived, size):
+    return split_four(add_low(kept, arrived, size), 0, size.bit_length() - 3)
+
+
+def split_near(kept, arrived, size):
+    parts = [part.reshape((2, 2) + part.shape[1:]) for part in add_low(kept, arrived, size)]
+    return split_two(parts, 1, size.bit_length() - 3)
+
+
+def split_far(kept, arrived, size):
+    return split_two(add_four(kept, [arrived]), 0, size.bit_length() - 2)
+
+
+def fly_near(values, size):
+    return flip(values, 1 << size.bit_length() - 3, size)
+
+
+def fly_far(values, size):
+    return flip(values, 1 << size.bit_length() - 2, size)
+
+
+def place_far(values, arrived, size):
+    return place_two(values, arrived, size.bit_length() - 2, 0)
+
+
+def place_near(values, arrived, size):
+    return merge_rows(place_two(values, arrived, size.bit_length() - 3, 1))
+
+
+def fly_high(leaving, size):
+    return fly_four(leaving, size.bit_length() - 3, size)
 
 
 erf_slope = 0.3275911
@@ -191,64 +252,91 @@
     )
 
 
-def head_lanes(shape, h):
+def head_lanes(shape, head):
     lane = lax.broadcasted_iota(jnp.int32, shape, 1)
-    return (lane >= HEAD_DIM) if h else (lane < HEAD_DIM), lane == (0 if h else HEAD_DIM)
-
-def masked_pair(q, k, length, h):
-    inside, spare = head_lanes(q.shape, h)
-    zero = jnp.zeros_like(q)
-    q_in = jnp.where(inside, q * jnp.bfloat16(0.125), zero)
-    q_aug = jnp.where(spare, jnp.ones_like(q), q_in)
-    row = lax.broadcasted_iota(jnp.int32, q.shape, 0)
+    return (lane >= HEAD_DIM) if head else (lane < HEAD_DIM), lane == (0 if head else HEAD_DIM)
+
+
+def head_operands(query, key, length, head):
+    inside, spare = head_lanes(query.shape, head)
+    zero = jnp.zeros_like(query)
+    query_in = jnp.where(inside, query * jnp.bfloat16(0.125), zero)
+    query_mask = jnp.where(spare, jnp.ones_like(query), query_in)
+    row = lax.broadcasted_iota(jnp.int32, query.shape, 0)
     fill = jnp.where(row < length, 0.0, mask_fill).astype(jnp.bfloat16)
-    k_aug = jnp.where(inside, k, jnp.where(spare, fill, zero))
-    return q_in, q_aug, k_aug, inside
-
-def fwd_kernel(info, q_ref, k_ref, v_ref, ctx_ref, lse_ref):
+    key_mask = jnp.where(inside, key, jnp.where(spare, fill, zero))
+    return query_in, query_mask, key_mask, inside
+
+
+def attention_kernel(info, query_ref, key_ref, value_ref, ctx_ref, total_ref):
     length = info[1 + pl.program_id(0)]
-    q, k, v = q_ref[...], k_ref[...], v_ref[...]
-    tops = []
-    for h in range(2):
-        _, q_aug, k_aug, _ = masked_pair(q, k, length, h)
-        scores = matmul_nt(k_aug, q_aug)
-        top = jnp.max(scores, axis=0, keepdims=True)
-        e = jnp.exp(scores - top)
-        total = jnp.sum(e, axis=0, keepdims=True)
-        p = (e * (1.0 / total)).astype(jnp.bfloat16)
-        lse_ref[0, 0, h:h+1, :] = top + jnp.log(total)
-        tops.append(matmul_tn(v, p))
-    ctx = jnp.concatenate([tops[0][:HEAD_DIM], tops[1][HEAD_DIM:]], axis=0)
-    ctx_ref[...] = jnp.transpose(ctx).astype(jnp.bfloat16)
-
-def bwd_kernel(slot, skipped, info, q_ref, k_ref, v_ref, g_ref, lse_ref, *refs):
-    own_ref, other_ref, key_ref, sum_ref = refs[skipped:]
-    length = info[1 + slot]
-    q, k, v, g = q_ref[...], k_ref[...], v_ref[...], g_ref[...]
-    dv = dk = dqt = None
-    for h in range(2):
-        q_in, q_aug, k_aug, inside = masked_pair(q, k, length, h)
-        g_in = jnp.where(inside, g, jnp.zeros_like(g))
-        scores = matmul_nt(k_aug, q_aug)
-        p = jnp.exp(scores - lse_ref[0, 0, h:h+1, :])
-        dp = matmul_nt(v, g_in)
-        dv_h = matmul(p.astype(jnp.bfloat16), g_in)
-        rd = jnp.sum(p * dp, axis=0, keepdims=True)
-        ds = (p * (dp - rd)).astype(jnp.bfloat16)
-        dk_h = matmul(ds, q_in)
-        k_in = jnp.where(inside, k * jnp.bfloat16(0.125), jnp.zeros_like(k))
-        dq_h = matmul_tn(k_in, ds)
-        dv = dv_h if dv is None else dv + dv_h
-        dk = dk_h if dk is None else dk + dk_h
-        dqt = dq_h if dqt is None else dqt + dq_h
-    dq = jnp.transpose(dqt).astype(jnp.bfloat16)
-    dv = dv.astype(jnp.bfloat16)
+    query, key = query_ref[...], key_ref[...]
+    value = jnp.transpose(value_ref[...])
+    operands = [head_operands(query, key, length, head) for head in range(2)]
+    scores = [matmul_nt(operand[2], operand[1]) for operand in operands]
+    parts = []
+    for head in range(2):
+        top = jnp.max(scores[head], axis=0, keepdims=True)
+        powers = jnp.exp(scores[head] - top)
+        total = jnp.sum(powers, axis=0, keepdims=True)
+        probs = (powers * (1.0 / total)).astype(jnp.bfloat16)
+        total_ref[0, 0, head : head + 1, :] = top + jnp.log(total)
+        parts.append(matmul(value[head * HEAD_DIM : (head + 1) * HEAD_DIM], probs))
+    ctx_ref[...] = jnp.transpose(jnp.concatenate(parts, axis=0)).astype(jnp.bfloat16)
+
+
+def attention_pull_kernel(
+    info,
+    query_ref,
+    key_ref,
+    value_ref,
+    grad_ref,
+    total_ref,
+    own_ref,
+    other_ref,
+    keys_ref,
+    sum_ref,
+    queries_ref,
+):
+    length = info[1 + pl.program_id(0)]
+    query, key, value, grad = query_ref[...], key_ref[...], value_ref[...], grad_ref[...]
+    operands = [head_operands(query, key, length, head) for head in range(2)]
+    grads = [jnp.where(operand[3], grad, jnp.zeros_like(grad)) for operand in operands]
+    flat_key = jnp.transpose(key * jnp.bfloat16(0.125))
+    jobs = [(head, first) for first in range(0, SEQ, CHUNK) for head in range(2)]
+
+    def begin(head, first):
+        spot = slice(first, first + CHUNK)
+        return (
+            matmul_nt(operands[head][2], operands[head][1][spot]),
+            matmul_nt(value, grads[head][spot]),
+        )
+
+    ready = begin(*jobs[0])
+    key_grad = value_grad = jnp.zeros((SEQ, PAIR), jnp.float32)
+    flat = []
+    for index, (head, first) in enumerate(jobs):
+        scores, prob_grad = ready
+        if index + 1 < len(jobs):
+            ready = begin(*jobs[index + 1])
+        spot = slice(first, first + CHUNK)
+        probs = jnp.exp(scores - total_ref[0, 0, head : head + 1, spot])
+        row_dot = jnp.sum(probs * prob_grad, axis=0, keepdims=True)
+        score_grad = (probs * (prob_grad - row_dot)).astype(jnp.bfloat16)
+        value_grad += matmul(probs.astype(jnp.bfloat16), grads[head][spot])
+        key_grad += matmul(score_grad, operands[head][0][spot])
+        flat.append(matmul(flat_key[head * HEAD_DIM : (head + 1) * HEAD_DIM], score_grad))
+        if head:
+            queries_ref[spot, :] = jnp.transpose(jnp.concatenate(flat, axis=0)).astype(jnp.bfloat16)
+            flat = []
+    query_grad = queries_ref[...]
+    value_grad = value_grad.astype(jnp.bfloat16)
     early = info[0] == 0
-    own_ref[...] = jnp.where(early, dq, dv)
-    other_ref[...] = jnp.where(early, dv, dq)
-    key_ref[...] = dk.astype(jnp.bfloat16)
-    sum_ref[0, 0, 0:1, :] = jnp.sum(dq.astype(jnp.float32), axis=0, keepdims=True)
-    sum_ref[0, 0, 1:2, :] = jnp.sum(dv.astype(jnp.float32), axis=0, keepdims=True)
+    own_ref[...] = jnp.where(early, query_grad, value_grad)
+    other_ref[...] = jnp.where(early, value_grad, query_grad)
+    keys_ref[...] = key_grad.astype(jnp.bfloat16)
+    sum_ref[0, 0, 0:1, :] = jnp.sum(query_grad.astype(jnp.float32), axis=0, keepdims=True)
+    sum_ref[0, 0, 1:2, :] = jnp.sum(value_grad.astype(jnp.float32), axis=0, keepdims=True)
 
 
 def pick(kind):
@@ -269,7 +357,7 @@
 def attention(info, qkv, slots):
     rows = qkv.shape[0]
     return pl.pallas_call(
-        fwd_kernel,
+        attention_kernel,
         grid_spec=pltpu.PrefetchScalarGridSpec(
             num_scalar_prefetch=1,
             grid=(slots, PAIRS),
@@ -280,48 +368,36 @@
             jax.ShapeDtypeStruct((rows, D), jnp.bfloat16),
             jax.ShapeDtypeStruct((slots, PAIRS, 2, SEQ), jnp.float32),
         ],
-        cost_estimate=pl.CostEstimate(
-            flops=20 << 30, bytes_accessed=8 << 20, transcendentals=slots * HEADS * SEQ * SEQ
-        ),
+        cost_estimate=SMALL,
         name="attention",
     )(info, qkv, qkv, qkv)
 
 
-def attention_pull(info, qkv, grad, log_total, slots, slot, parts):
+def attention_pull(info, qkv, grad, log_total, slots):
     rows = qkv.shape[0]
-
-    def at_slot(spec):
-        return pl.BlockSpec(
-            spec.block_shape, lambda s, p, info: spec.index_map(slot, p, info)
-        )
 
     def key_spot(s, p, info):
         return s, lax.rem(p + info[0] * (PAIRS // 2), PAIRS)
 
     table = jax.ShapeDtypeStruct((rows, D), jnp.bfloat16)
-    before = [] if parts is None else list(parts)
     return pl.pallas_call(
-        functools.partial(bwd_kernel, slot, len(before)),
+        attention_pull_kernel,
         grid_spec=pltpu.PrefetchScalarGridSpec(
             num_scalar_prefetch=1,
-            grid=(1, PAIRS),
-            in_specs=[at_slot(pick(kind)) for kind in range(3)]
-            + [at_slot(pair_spec()), at_slot(pair_rows(SEQ))]
-            + [pl.BlockSpec(memory_space=pl.ANY)] * len(before),
+            grid=(slots, PAIRS),
+            in_specs=[pick(kind) for kind in range(3)] + [pair_spec(), pair_rows(SEQ)],
             out_specs=[
-                at_slot(pair_spec()),
-                at_slot(pair_spec()),
-                at_slot(pl.BlockSpec((SEQ, PAIR), key_spot)),
-                at_slot(pair_rows(PAIR)),
+                pair_spec(),
+                pair_spec(),
+                pl.BlockSpec((SEQ, PAIR), key_spot),
+                pair_rows(PAIR),
             ],
+            scratch_shapes=[pltpu.VMEM((SEQ, PAIR), jnp.bfloat16)],
         ),
         out_shape=[table] * 3 + [jax.ShapeDtypeStruct((slots, PAIRS, 2, PAIR), jnp.float32)],
-        input_output_aliases={6 + place: place for place in range(len(before))},
-        cost_estimate=pl.CostEstimate(
-            flops=14 << 30, bytes_accessed=8 << 20, transcendentals=HEADS * SEQ * SEQ
-        ),
+        cost_estimate=SMALL,
         name="attention_pull",
-    )(info, qkv, qkv, qkv, grad, log_total, *before)
+    )(info, qkv, qkv, qkv, grad, log_total)
 
 
 def join_halves(core, own, other):
@@ -407,7 +483,19 @@
 
 
 def raise_kernel(
-    info, vec_ref, bias_ref, x_ref, ctx_ref, own, other, xhat_ref, rstd_ref, low_ref, act_ref, slope_ref
+    info,
+    vec_ref,
+    bias_ref,
+    x_ref,
+    ctx_ref,
+    own,
+    other,
+    xhat_ref,
+    rstd_ref,
+    low_ref,
+    own_act_ref,
+    other_act_ref,
+    slope_ref,
 ):
     ctx = ctx_ref[...]
     attended = join_halves(info[0], matmul(ctx, own[:, OUT_COLS]), matmul(ctx, other[:, OUT_COLS]))
@@ -419,7 +507,8 @@
     for ref, cols, place in hidden_pieces(own, other):
         spot = slice(place, place + D)
         act, slope = gelu_parts(matmul(hidden, ref[:, cols]) + bias_ref[0:1, spot])
-        act_ref[:, spot] = act.astype(jnp.bfloat16)
+        act_ref = own_act_ref if place < WIDE else other_act_ref
+        act_ref[:, cols] = act.astype(jnp.bfloat16)
         slope_ref[:, spot] = slope.astype(jnp.bfloat16)
 
 
@@ -432,14 +521,11 @@
 
 
 def lower_kernel(
-    info, vec_ref, xhat_ref, act_ref, cot_ref, own, other, out_ref, grad_ref, low_ref, sum_ref
+    info, vec_ref, xhat_ref, first_ref, second_ref, cot_ref, out_ref, grad_ref, low_ref, sum_ref
 ):
     first = pl.program_id(0) * ROWS
-    branch = vec_ref[9:10, :]
-    for ref, cols, place in hidden_pieces(own, other):
-        branch = branch + matmul_nt(act_ref[:, place : place + D], ref[:, cols])
     hidden = xhat_ref[...] * vec_ref[3:4, :] + vec_ref[4:5, :]
-    xhat, rstd = norm_parts(hidden + branch)
+    xhat, rstd = norm_parts(hidden + (first_ref[...] + second_ref[...] + vec_ref[9:10, :]))
     gain = vec_ref[10:11, :]
     out_ref[...] = (xhat * gain + vec_ref[11:12, :]).astype(jnp.bfloat16)
     limit = info[INFO + BLOCKS + lax.div(first, SEQ)]
@@ -464,7 +550,8 @@
     up_other,
     own,
     other,
-    pre_ref,
+    own_pre_ref,
+    other_pre_ref,
     skip_ref,
     attn_ref,
     ctx_ref,
@@ -479,7 +566,8 @@
         spot = slice(place, place + D)
         pre = matmul(low, ref[:, cols]) * slope_ref[:, spot].astype(jnp.float32)
         pre = pre.astype(jnp.bfloat16)
-        pre_ref[:, spot] = pre
+        pre_ref = own_pre_ref if place < WIDE else other_pre_ref
+        pre_ref[:, cols] = pre
         hidden_grad = hidden_grad + matmul_nt(pre, up[0][:, up[1]])
     xhat = xhat_ref[...]
     skip = norm_pull(hidden_grad, vec_ref[3:4, :], xhat, rstd_ref[:, 0:1])
@@ -491,7 +579,8 @@
     ctx = ctx + matmul_nt(jnp.where(core == 0, right, left), up_other[:, OUT_COLS])
     ctx_ref[...] = ctx.astype(jnp.bfloat16)
     add_sums(sum_ref, (attn.astype(jnp.float32), hidden_grad * xhat, hidden_grad))
-    add_sums(bias_ref, (pre_ref[...].astype(jnp.float32),))
+    add_sums(bias_ref.at[:, :WIDE], (own_pre_ref[...].astype(jnp.float32),))
+    add_sums(bias_ref.at[:, WIDE:], (other_pre_ref[...].astype(jnp.float32),))
 
 
 def row_spec(width):
@@ -513,9 +602,7 @@
         + [pl.BlockSpec((8, width), lambda i: (0, 0)) for width in sums],
         out_shape=shapes,
         compiler_params=pltpu.CompilerParams(vmem_limit_bytes=52 << 20),
-        cost_estimate=pl.CostEstimate(
-            flops=flops, bytes_accessed=24 << 20, transcendentals=rows * FF
-        ),
+        cost_estimate=SMALL,
         name=name,
     )(*operands)
 
@@ -527,24 +614,24 @@
         "raise_rows",
         [whole_spec()] * 2 + [row_spec(D)] * 2 + [whole_spec()] * 2,
         tokens.shape[0],
-        [(D, full), (PAIR, full), (D, low), (FF, low), (FF, low)],
+        [(D, full), (PAIR, full), (D, low), (WIDE, low), (WIDE, low), (FF, low)],
         [],
         14 << 30,
         (info, vec, bias, tokens, context, own, other),
     )
 
 
-def lower_rows(info, vec, xhat, act, cotangent, own, other):
+def lower_rows(info, vec, xhat, first, second, cotangent):
     low, full = jnp.bfloat16, jnp.float32
     return row_call(
         lower_kernel,
         "lower_rows",
-        [whole_spec(), row_spec(D), row_spec(FF), row_spec(D)] + [whole_spec()] * 2,
-        act.shape[0],
+        [whole_spec()] + [row_spec(D)] * 4,
+        first.shape[0],
         [(D, low), (D, full), (D, low)],
         [D],
-        9 << 30,
-        (info, vec, xhat, act, cotangent, own, other),
+        4 << 30,
+        (info, vec, xhat, first, second, cotangent),
     )
 
 
@@ -556,19 +643,19 @@
         [whole_spec(), row_spec(D), row_spec(PAIR), row_spec(FF), row_spec(D), row_spec(D)]
         + [whole_spec()] * 4,
         xhat.shape[0],
-        [(FF, low), (D, full), (D, low), (D, low)],
+        [(WIDE, low), (WIDE, low), (D, full), (D, low), (D, low)],
         [D, FF],
         18 << 30,
         (info, vec, xhat, rstd, slope, grad, low_grad, *up, *down),
     )
 
 
-def split_low(values):
+def split_rest(values):
     high = values.astype(jnp.bfloat16)
     return high, (values - high.astype(jnp.float32)).astype(jnp.bfloat16)
 
 def store_split(values, where, high_ref, rest_ref):
-    high_ref[where], rest_ref[where] = split_low(values)
+    high_ref[where], rest_ref[where] = split_rest(values)
 
 def close_product(left, right, rows, cols):
     left_high, left_rest = left[0][rows, :], left[1][rows, :]
@@ -650,7 +737,7 @@
         return carry
 
     lax.fori_loop(0, NS_ITERS, sweep, 0)
-    both = jnp.concatenate(split_low(out_ref[...] / scale), axis=0)
+    both = jnp.concatenate(split_rest(out_ref[...] / scale), axis=0)
     for place in range(0, cols_ref.shape[1], D):
         spot = slice(place, place + D)
         product = matmul(both, cols_ref[:, spot])
@@ -713,15 +800,18 @@
     first_block = jnp.concatenate([turn(w_qkv.astype(low), narrow), vec_block], axis=1)
     second_block = jnp.concatenate([w_up.astype(low), w_out.astype(low)], axis=1)
     third_block = w_down.astype(low)
-    first_pieces = together(*send_high(first_block, size), second_block)
-    second_block = first_pieces[-1]
-    first_pieces = send_low(sort_high(first_pieces[:4], size), size)
-    second_pieces = send_high(second_block, size)
-    *pieces, third_block = together(*first_pieces, *second_pieces, third_block)
-    first_own = sort_low(pieces[:4])
-    second_pieces = send_low(sort_high(pieces[4:], size), size)
-    third_pieces = send_high(third_block, size)
+    near, far = size.bit_length() - 3, size.bit_length() - 2
+    steps = [1 << near, 1 << far, 3 << near]
+    first_pieces = send_high(first_block, size)
+    second_pieces = [second_block, flip(second_block, steps[0], size)]
+    first_pieces, second_pieces, third_block = together(first_pieces, second_pieces, third_block)
+    first_pieces = send_low(sort_high(first_pieces, size), size)
+    second_pieces += [flip(second_pieces[0], step, size) for step in steps[1:]]
+    first_pieces, second_pieces, third_block = together(first_pieces, second_pieces, third_block)
+    first_own = sort_low(first_pieces)
     first_other = swap_cores(first_own)
+    second_pieces = send_low(sort_high(second_pieces, size), size)
+    third_pieces = [third_block, flip(third_block, steps[0], size)]
 
     spots = pick_core(jnp.array(SPOTS[0], jnp.int32), jnp.array(SPOTS[1], jnp.int32))
     live = jnp.arange(slots) % CAP < counts.reshape(-1)[jnp.arange(slots) // CAP]
@@ -737,28 +827,35 @@
         ],
         axis=1,
     )
+    projected, third_pieces = together(projected, third_pieces)
+    third_pieces += [flip(third_pieces[0], step, size) for step in steps[1:]]
     context, log_total = attention(info, projected, slots)
-    context, *pieces = together(context, *second_pieces, *third_pieces)
-    second_own = sort_low(pieces[:4])
-    third_pieces = send_low(sort_high(pieces[4:], size), size)
+    context, second_pieces, third_pieces = together(context, second_pieces, third_pieces)
+    second_own = sort_low(second_pieces)
+    third_pieces = send_low(sort_high(third_pieces, size), size)
     second_other = swap_cores(second_own)
-    xhat_one, rstd_one, hidden_low, act_low, slope = raise_rows(
+    xhat_one, rstd_one, hidden_low, act_own, act_other, slope = raise_rows(
         info, vec, bias_up, tokens, context, second_own, second_other
     )
-    act_low, *third_pieces = together(act_low, *third_pieces)
+    act_own, act_other, *third_pieces = together(act_own, act_other, *third_pieces)
     third_own = sort_low(third_pieces)
     third_other = swap_cores(third_own)
+    branch = matmul_nt(act_own, third_own)
+    branch, third_other = together(branch, third_other)
     layer_out, top_grad, branch_low, high_sums = lower_rows(
-        info, vec, xhat_one, act_low, cotangent, third_own, third_other
-    )
-
-    leaving = matmul_tn(branch_low, act_low[:, up_half:]).astype(low)
+        info, vec, xhat_one, branch, matmul_nt(act_other, third_other), cotangent
+    )
+
+    full = jnp.float32
+    leaving = matmul_tn(branch_low, act_other).astype(low)
     leaving, branch_low = together(leaving, branch_low)
     down_arrived = swap_cores(leaving)
-    down_own = matmul_tn(branch_low, act_low[:, :up_half])
+    down_own = matmul_tn(branch_low, act_own)
     down_own, down_arrived, branch_low = together(down_own, down_arrived, branch_low)
-    down_kept, down_sent = leave_low([down_own + down_arrived.astype(jnp.float32)], size)
-    pre_low, skip_grad, attn_low, context_grad, low_sums, bias_sums = pull_rows(
+    down_kept, leaving = split_low([down_own + down_arrived.astype(full)], size)
+    leaving, branch_low = together(leaving, branch_low)
+    down_sent = fly_low(leaving, size)
+    pulled = pull_rows(
         info,
         vec,
         xhat_one,
@@ -769,74 +866,87 @@
         (second_own, second_other),
         (third_own, third_other),
     )
-    pre_low, *down_sent = together(pre_low, *down_sent)
-    down_kept, down_sent = leave_high(down_kept, down_sent, size)
+    pulled, down_sent = together(pulled, down_sent)
+    pre_own, pre_other, skip_grad, attn_low, context_grad, low_sums, bias_sums = pulled
+    down_kept, leaving = split_near(down_kept, down_sent, size)
+    leaving, pre_own, pre_other, attn_low = together(leaving, pre_own, pre_other, attn_low)
+    down_sent = fly_near(leaving, size)
+    up_leaving = matmul_tn(hidden_low, pre_other).astype(low)
+    up_leaving, pre_own, attn_low, down_sent = together(up_leaving, pre_own, attn_low, down_sent)
+    up_arrived = swap_cores(up_leaving)
+    down_kept, down_leaving = split_far(down_kept, down_sent, size)
     out_own = pick_core(attn_low[:, : D // 2], attn_low[:, D // 2 :])
     out_other = pick_core(attn_low[:, D // 2 :], attn_low[:, : D // 2])
-    leaving = jnp.concatenate(
-        [
-            matmul_tn(hidden_low, pre_low[:, up_half:]).astype(low),
-            matmul_tn(context, out_other).astype(low),
-        ],
-        axis=1,
-    )
-    leaving, context_grad = together(leaving, context_grad)
-    wide_arrived = swap_cores(leaving)
-    up_own = matmul_tn(hidden_low, pre_low[:, :up_half])
+    out_arrived = swap_cores(matmul_tn(context, out_other).astype(low))
+    up_own = matmul_tn(hidden_low, pre_own)
     out_own = matmul_tn(context, out_own)
-    up_own, out_own, wide_arrived, context_grad = together(
-        up_own, out_own, wide_arrived, context_grad
-    )
-    wide_arrived = wide_arrived.astype(jnp.float32)
-    wide_kept, wide_sent = leave_low(
-        [up_own + wide_arrived[:, :up_half], out_own + wide_arrived[:, up_half:]], size
-    )
-    parts = attention_pull(info, projected, context_grad, log_total, slots, 0, None)
-    parts, wide_sent, down_sent = together(parts, wide_sent, down_sent)
-    (grad_down,) = add_four(down_kept, down_sent)
+    up_own, out_own, up_arrived, out_arrived = together(up_own, out_own, up_arrived, out_arrived)
+    wide_kept, leaving = split_low(
+        [up_own + up_arrived.astype(full), out_own + out_arrived.astype(full)], size
+    )
+    leaving, down_leaving, context_grad = together(leaving, down_leaving, context_grad)
+    wide_sent = fly_low(leaving, size)
+    down_sent = fly_far(down_leaving, size)
+    parts = attention_pull(info, projected, context_grad, log_total, slots)
+    parts, down_sent = together(parts, down_sent)
+
+    grads = (parts[0], parts[1], parts[2][:, :narrow], parts[2][:, narrow:])
+    main_leaving = matmul_tn(tokens, grads[1]).astype(low)
+    keys_leaving = matmul_tn(tokens, grads[3]).astype(low)
+    vector_grad = vector_grads(info, low_sums, high_sums, bias_sums, parts[3])
+    main_leaving, keys_leaving, grads, vector_grad, wide_sent = together(
+        main_leaving, keys_leaving, grads, vector_grad, wide_sent
+    )
+    wide_kept, leaving = split_near(wide_kept, wide_sent, size)
+    leaving, grads = together(leaving, grads)
+    wide_sent = fly_near(leaving, size)
+    main_arrived, keys_arrived = swap_cores(main_leaving), swap_cores(keys_leaving)
+    main_part, keys_part = matmul_tn(tokens, grads[0]), matmul_tn(tokens, grads[2])
+    (grad_down,) = add_four(down_kept, [down_sent])
     moment_down = moment_decay * mom_down + grad_down
-    down_pieces = send_high(moment_down.astype(low), size)
-    wide_kept, wide_sent = leave_high(wide_kept, wide_sent, size)
-    for slot in range(1, slots):
-        parts = attention_pull(info, projected, context_grad, log_total, slots, slot, parts)
-    parts, wide_sent, down_pieces = together(parts, wide_sent, down_pieces)
-    main_own, main_other, keys, head_sums = parts
-    grad_own = jnp.concatenate([main_own, keys[:, :narrow]], axis=1)
-    grad_other = jnp.concatenate([main_other, keys[:, narrow:]], axis=1)
-    leaving = matmul_tn(tokens, grad_other).astype(low)
-    leaving, grad_own = together(leaving, grad_own)
-    qkv_arrived = swap_cores(leaving)
-    vector_grad = vector_grads(info, low_sums, high_sums, bias_sums, head_sums)
-    vector_grad = vector_grad + swap_cores(vector_grad)
-    vector_part = pick_core(vector_grad[:vec_rows], vector_grad[vec_rows : 2 * vec_rows])
-    vector_part = jnp.pad(vector_part, ((0, VEC_PAD - vec_rows), (0, 0))).T
-    grad_up, grad_out = add_four(wide_kept, wide_sent)
+    main_part, keys_part, main_arrived, keys_arrived, grads, moment_down = together(
+        main_part, keys_part, main_arrived, keys_arrived, grads, moment_down
+    )
+    qkv_kept, leaving = split_low(
+        [main_part + main_arrived.astype(full), keys_part + keys_arrived.astype(full)], size
+    )
+    leaving, grads, down_block = together(leaving, grads, moment_down.astype(low))
+    qkv_sent = fly_low(leaving, size)
+    down_sent = fly_far(down_block, size)
+    wide_sent, down_sent = together(wide_sent, down_sent)
+    wide_kept, wide_leaving = split_far(wide_kept, wide_sent, size)
+    wide_sent = fly_far(wide_leaving, size)
+    qkv_sent, wide_sent, down_sent = together(qkv_sent, wide_sent, down_sent)
+    grad_up, grad_out = add_four(wide_kept, [wide_sent])
     moment_up = moment_decay * mom_up + grad_up
     moment_out = moment_decay * mom_out + grad_out
     wide_block = jnp.concatenate([moment_up.astype(low), moment_out.astype(low)], axis=1)
-    qkv_part = matmul_tn(tokens, grad_own)
-    qkv_part, vector_part, qkv_arrived, wide_block, grad_own = together(
-        qkv_part, vector_part, qkv_arrived, wide_block, grad_own
-    )
-    qkv_kept, qkv_sent = leave_low(
-        [qkv_part + qkv_arrived.astype(jnp.float32), vector_part], size
-    )
-    wide_pieces = send_high(wide_block, size)
-    input_grad = skip_grad + matmul_nt(grad_own, qkv_own) + matmul_nt(grad_other, qkv_other)
-    down_rows = merge_rows(sort_high(down_pieces, size))
-    input_grad, down_rows, qkv_sent, wide_pieces = together(
-        input_grad, down_rows, qkv_sent, wide_pieces
-    )
-    qkv_kept, qkv_sent = leave_high(qkv_kept, qkv_sent, size)
-    wide_rows = merge_rows(sort_high(wide_pieces, size))
     mom_turned = turn(mom_qkv, narrow)
-    wide_rows, mom_turned, qkv_sent = together(wide_rows, mom_turned, qkv_sent)
-    grad_turned, grad_vectors = add_four(qkv_kept, qkv_sent)
-    qkv_pieces = send_high((moment_decay * mom_turned + grad_turned).astype(low), size)
+    qkv_kept, leaving = split_high(qkv_kept, qkv_sent, size)
+    down_pair = place_far(down_block, down_sent, size)
+    leaving, down_pair, wide_block, grads, vector_grad, mom_turned = together(
+        leaving, down_pair, wide_block, grads, vector_grad, mom_turned
+    )
+    qkv_sent = fly_high(leaving, size)
+    wide_sent = fly_far(wide_block, size)
+    down_sent = fly_near(down_pair, size)
+    qkv_sent, wide_sent, down_sent = together(qkv_sent, wide_sent, down_sent)
+    grad_main, grad_keys = add_four(qkv_kept, qkv_sent)
+    grad_turned = jnp.concatenate([grad_main, grad_keys], axis=1)
+    qkv_block = (moment_decay * mom_turned + grad_turned).astype(low)
+    wide_pair = place_far(wide_block, wide_sent, size)
+    qkv_block, grad_turned, wide_pair = together(qkv_block, grad_turned, wide_pair)
+    qkv_pieces = send_high(qkv_block, size)
+    wide_sent = fly_near(wide_pair, size)
+    vector_grad = vector_grad + swap_cores(vector_grad)
+    vector_arrived = flip(vector_grad, 1, size)
+    down_rows = place_near(down_pair, down_sent, size)
     grad_qkv = turn(grad_turned, D)
     moment_qkv = moment_decay * mom_qkv + grad_qkv
-    grad_vectors = grad_vectors[:, :vec_rows].T
-    grad_qkv, moment_qkv, qkv_pieces = together(grad_qkv, moment_qkv, qkv_pieces)
+    grad_qkv, moment_qkv, qkv_pieces, wide_sent, down_rows = together(
+        grad_qkv, moment_qkv, qkv_pieces, wide_sent, down_rows
+    )
+    wide_rows = place_near(wide_pair, wide_sent, size)
 
     qkv_rows = merge_rows(sort_high(qkv_pieces, size))
     place = me % GROUP
@@ -858,14 +968,41 @@
 
     pieces = []
     for step in range(GROUP):
-        piece = matrix_at(place ^ step).reshape(-1, block_rows, WIDE)
-        pieces.append(flip(piece, step, size) if step else piece)
+        pieces.append(matrix_at(place ^ step).reshape(-1, block_rows, WIDE))
+    pieces, grads, vector_grad, vector_arrived = together(
+        pieces, grads, vector_grad, vector_arrived
+    )
+    pieces = pieces[:1] + [flip(pieces[step], step, size) for step in range(1, GROUP)]
+    vector_grad = vector_grad + vector_arrived
+    vector_arrived = flip(vector_grad, 2, size)
+    input_grad = (
+        skip_grad
+        + matmul_nt(grads[0], qkv_own[:, :D])
+        + matmul_nt(grads[1], qkv_other[:, :D])
+        + matmul_nt(grads[2], qkv_own[:, D:])
+        + matmul_nt(grads[3], qkv_other[:, D:])
+    )
+    pieces, input_grad, vector_grad, vector_arrived = together(
+        pieces, input_grad, vector_grad, vector_arrived
+    )
     columns = sort_low(pieces)
     for bit in range(2, size.bit_length() - 3, 2):
         columns = sort_low(send_four(columns.reshape(4, -1, WIDE), bit, size))
     gram = matmul_nt(columns, columns)
     start = ((me - place) * block_rows).reshape(1).astype(jnp.int32)
-    polar = polar_rows(start, gram, swap_cores(gram), columns, GROUP * block_rows)
+    vector_grad = vector_grad + vector_arrived
+    gram, vector_grad = together(gram, vector_grad)
+    gram_arrived = swap_cores(gram)
+    vector_arrived = flip(vector_grad, 4, size)
+    gram_arrived, vector_arrived = together(gram_arrived, vector_arrived)
+    vector_grad = vector_grad + vector_arrived
+    polar = polar_rows(start, gram, gram_arrived, columns, GROUP * block_rows)
+    polar, vector_grad = together(polar, vector_grad)
+    for bit in range(3, size.bit_length() - 1):
+        vector_grad = vector_grad + flip(vector_grad, 1 << bit, size)
+    grad_vectors = lax.dynamic_slice(
+        vector_grad, (core * vec_rows, me * block_rows), (vec_rows, block_rows)
+    )
     polar = polar.reshape(GROUP, block_rows, WIDE)
     arrived = []
     for step in range(GROUP):

time: 504 us -> 421 us (0.84)
  the two profiles are of different devices: /device:TPU:9 before, /device:TPU:0 now
where the time goes in v3:
time: 421 us; the launch traced here: 415 us
  Pallas kernels  128 us (30%)
  waiting for transfers between devices  95.3 us (23%)
  starting transfers between devices  67.7 us (16%)
  matrix products  57.7 us (14%)
  other arithmetic  43.7 us (10%)
  local copies, waits for them, and re-layouts  20.1 us (5%)
    ppermute x51, waiting for transfers between devices, flip(): lax.ppermute(by_rows(values), 'fsdp', [(i, i ^ mask) for i in range(size)])  94.3 us
    ppermute x51, starting transfers between devices, flip(): lax.ppermute(by_rows(values), 'fsdp', [(i, i ^ mask) for i in range(size)])  66.3 us
    pallas_call x3, Pallas kernels, row_call(): pl.pallas_call(kernel, grid=(rows // ROWS,), in_specs=[pl.BlockSpec(memor...  50.8 us
    pallas_call x1, Pallas kernels, polar_rows(): pl.pallas_call(polar_kernel, in_specs=[pl.BlockSpec(memory_space=pltpu.SM...  33.2 us
    dot_general x10, matrix products, matmul_tn(): lax.dot_general(former, latter, (((0,), (0,)), ((), ())), preferred_eleme...  28.3 us
    pallas_call x1, Pallas kernels, attention_pull(): pl.pallas_call(attention_pull_kernel, grid_spec=pltpu.PrefetchScalarGridS...  23.8 us
    dot_general x7, matrix products, matmul_nt(): lax.dot_general(former, latter, (((1,), (1,)), ((), ())), preferred_eleme...  21.4 us
    pallas_call x1, Pallas kernels, attention(): pl.pallas_call(attention_kernel, grid_spec=pltpu.PrefetchScalarGridSpec(n...  16.9 us
  transfers between devices with their start and end apart: 61, of which 25 were waited for; matrix products, arithmetic and copies ran while one was open for 16% of the time, Pallas kernels for 21%

profile of v3, /device:TPU:0, one launch (start us, length us, event | category | flops | bytes accessed | tf_op | source)
XLA Modules:
  0.0 415.0 jit_solution(6687479774857487341)
XLA Ops:
  2.6 3.1 collective-permute-start.3
  7.7 3.0 collective-permute-start.1
  12.7 2.9 collective-permute-done
  16.0 4.5 %collective-permute-done.2 = bf16[48,1280]{1,0:T(8,128)(2,1)S(1)} collective-permute-done((bf16[48,1280]{1,0:T(8,128)(2,1)S(1)}, bf16[48,1280]{1,0:T(8,128)(2,1)S(1)}, u32[]{:S(2)}, u32[]{:S(2)}) %collective-permute-start.2) | collective-permute-done | bytes 122912 | tf_op jit(solution)/shard_map/ppermute | solution.py:75
  20.7 1.6 collective-permute-start.4
  24.3 3.5 collective-permute-start.7
  28.3 11.0 %collective-permute-done.7 = bf16[48,1920]{1,0:T(8,128)(2,1)S(1)} collective-permute-done((bf16[48,1920]{1,0:T(8,128)(2,1)S(1)}, bf16[48,1920]{1,0:T(8,128)(2,1)S(1)}, u32[]{:S(2)}, u32[]{:S(2)}) %collective-permute-start.7) | collective-permute-done | bytes 184352 | tf_op jit(solution)/shard_map/ppermute | solution.py:75
  39.3 5.7 %collective-permute-done.5 = bf16[4,48,1280]{2,1,0:T(8,128)(2,1)S(1)} collective-permute-done((bf16[4,48,1280]{2,1,0:T(8,128)(2,1)S(1)}, bf16[4,48,1280]{2,1,0:T(8,128)(2,1)S(1)}, u32[]{:S(2)}, u32[]{:S(2)}) %collective-permute-start.5) | collective-permute-done | bytes 491552 | tf_op jit(solution)/shard_map/ppermute | solution.py:75
  52.5 1.9 vector_tables.1
  56.0 4.3 %fusion.1 = bf16[1024,1152]{1,0:T(8,128)(2,1)S(1)} fusion(f32[1152]{0:T(1024)S(1)} %slice_reduce_fusion.1, bf16[1024,768]{1,0:T(8,128)(2,1)} %x_ref.1, bf16[768,1280]{1,0:T(8,128)(2,1)} %bitcast.318), kind=kOutput, calls=%fused_computation.11 | convolution fusion | flops 1814298624 | bytes 5706240 | tf_op jit(solution)/shard_map/dot_general | solution.py:55
  60.3 3.7 fusion
  63.9 2.5 pad_maximum_fusion.query_ref.key_ref.value_ref
  67.7 1.8 collective-permute-start.15
  69.4 16.9 %attention.1 = (bf16[1024,768]{1,0:T(8,128)(2,1)}, f32[2,6,2,512]{3,2,1,0:T(2,128)}) custom-call(s32[23]{0:T(128)} %pad_add_fusion.info, bf16[1024,2304]{1,0:T(8,128)(2,1)} %pad_maximum_fusion.query_ref.key_ref.value_ref, bf16[1024,2304]{1,0:T(8,128)(2,1)} %pad_maximum_fusion.query_ref.key_ref.value_ref, ...), custom_call_target="tpu_custom_call" | custom-call | flops 1048576 | bytes 65536 | tf_op jit(solution)/shard_map/attention/pallas_call | solution.py:359
  86.6 2.0 maximum_select_fusion.4
  89.6 2.0 maximum_select_fusion.23
  95.3 1.6 copy-done.12
  96.9 21.6 %raise_rows.1 = (f32[1024,768]{1,0:T(8,128)}, f32[1024,128]{1,0:T(8,128)S(1)}, bf16[1024,768]{1,0:T(8,128)(2,1)}, bf16[1024,1536]{1,0:T(8,128)(2,1)}, bf16[1024,...) custom-call(s32[23]{0:T(128)S(1)} %copy-done.6, f32[16,768]{1,0:T(8,128)S(1)} %copy-done.3, f32[8,3072]{1,0:T(8,128)S(1)} %copy-done.4, ...), custom_call_target="tpu_custom_call" | custom-call | flops 1048576 | bytes 65536 | tf_op jit(solution)/shard_map/raise_rows/pallas_call | solution.py:597
  118.7 1.6 collective-permute-done.19
  121.4 2.4 copy-done.18
  123.9 4.4 %fusion.83.first_ref = f32[1024,768]{1,0:T(8,128)} fusion(bf16[1024,1536]{1,0:T(8,128)(2,1)S(1)} %copy-done.18, bf16[768,1536]{1,0:T(8,128)(2,1)S(1)} %bitcast.322), kind=kOutput, calls=%fused_computation.214 | convolution fusion | flops 2415919104 | bytes 8650752 | tf_op jit(solution)/shard_map/dot_general | solution.py:65
  128.3 4.3 %fusion.84.second_ref = f32[1024,768]{1,0:T(8,128)} fusion(bf16[1024,1536]{1,0:T(8,128)(2,1)S(1)} %copy-done.62, bf16[768,1536]{1,0:T(8,128)(2,1)S(1)} %collective-permute-done.20.other), kind=kOutput, calls=%fused_computation.215 | convolution fusion | flops 2415919104 | bytes 8650752 | tf_op jit(solution)/shard_map/dot_general | solution.py:65
  132.6 7.7 %lower_rows.1 = (bf16[1024,768]{1,0:T(8,128)(2,1)}, f32[1024,768]{1,0:T(8,128)}, bf16[1024,768]{1,0:T(8,128)(2,1)S(1)}, f32[8,768]{1,0:T(8,128)S(1)}) custom-call(s32[23]{0:T(128)S(1)} %copy-done.6, f32[16,768]{1,0:T(8,128)S(1)} %copy-done.3, f32[1024,768]{1,0:T(8,128)} %get-tuple-element.240.xhat_ref, f32[1024,768]{1,0:T(8,128)} %fusion.83.first_ref, ...), custom_call_target="tpu_custom_call" | custom-call | flops 1048576 | bytes 65536 | tf_op jit(solution)/shard_map/lower_rows/pallas_call | solution.py:597
  140.3 4.3 %convolution_convert_fusion.1 = bf16[768,1536]{1,0:T(8,128)(2,1)} fusion(bf16[1024,768]{1,0:T(8,128)(2,1)S(1)} %get-tuple-element.266.low_ref, bf16[1024,1536]{1,0:T(8,128)(2,1)S(1)} %copy-done.62), kind=kOutput, calls=%fused_computation.7 | convolution fusion | flops 2417098752 | bytes 7077888 | tf_op jit(solution)/shard_map/dot_general | solution.py:59
  144.6 4.6 %fusion.85 = f32[768,1536]{1,0:T(8,128)S(1)} fusion(bf16[1024,768]{1,0:T(8,128)(2,1)S(1)} %get-tuple-element.266.low_ref, bf16[1024,1536]{1,0:T(8,128)(2,1)} %get-tuple-element.247), kind=kOutput, calls=%fused_computation.216 | convolution fusion | flops 2415919104 | bytes 9437184 | tf_op jit(solution)/shard_map/dot_general | solution.py:59
  149.4 2.5 convert_add_fusion.1
  151.9 2.1 copy-done.11
  158.6 21.5 %pull_rows.1 = (bf16[1024,1536]{1,0:T(8,128)(2,1)}, bf16[1024,1536]{1,0:T(8,128)(2,1)}, f32[1024,768]{1,0:T(8,128)}, bf16[1024,768]{1,0:T(8,128)(2,1)}, bf16[102...) custom-call(s32[23]{0:T(128)S(1)} %copy-done.6, f32[16,768]{1,0:T(8,128)S(1)} %copy-done.3, ...), custom_call_target="tpu_custom_call" | custom-call | flops 1048576 | bytes 65536 | tf_op jit(solution)/shard_map/pull_rows/pallas_call | solution.py:597
  180.1 2.7 collective-permute-done.23
  183.8 1.8 fusion.16
  186.5 4.3 %convolution_convert_fusion = bf16[768,1536]{1,0:T(8,128)(2,1)} fusion(bf16[1024,768]{1,0:T(8,128)(2,1)S(1)} %copy-done.34, bf16[1024,1536]{1,0:T(8,128)(2,1)S(1)} %copy-done.63), kind=kOutput, calls=%fused_computation.6 | convolution fusion | flops 2417098752 | bytes 7077888 | tf_op jit(solution)/shard_map/dot_general | solution.py:59
  190.8 3.1 collective-permute-done.25
  194.0 2.5 convolution_convert_fusion.4
  200.2 2.7 fusion.86
  203.1 2.5 convert_add_fusion
  205.6 2.2 copy-done.10
  210.9 1.7 collective-permute-start.28
  216.1 23.8 %attention_pull.1 = (bf16[1024,768]{1,0:T(8,128)(2,1)}, bf16[1024,768]{1,0:T(8,128)(2,1)}, bf16[1024,768]{1,0:T(8,128)(2,1)}, f32[2,6,2,128]{3,2,1,0:T(2,128)}) custom-call(s32[23]{0:T(128)} %pad_add_fusion.info, bf16[1024,2304]{1,0:T(8,128)(2,1)} %pad_maximum_fusion.query_ref.key_ref.value_ref, ...), custom_call_target="tpu_custom_call" | custom-call | flops 1048576 | bytes 65536 | tf_op jit(solution)/shard_map/attention_pull/pallas_call | solution.py:383
  239.9 4.6 %fusion.7 = bf16[768,768]{1,0:T(8,128)(2,1)} fusion(bf16[1024,768]{1,0:T(8,128)(2,1)} %get-tuple-element.384, bf16[1024,768]{1,0:T(8,128)(2,1)} %x_ref.1), kind=kOutput, calls=%fused_computation.23 | convolution fusion | flops 1208549376 | bytes 4325376 | tf_op jit(solution)/shard_map/dot_general | solution.py:59
  244.5 1.8 fusion.8
  246.3 1.6 vector_grads.1
  247.9 1.6 fusion.82
  251.5 2.0 fusion.14
  266.2 5.3 %collective-permute-done.38 = bf16[48,1536]{1,0:T(8,128)(2,1)S(1)} collective-permute-done((bf16[48,1536]{1,0:T(8,128)(2,1)S(1)}, bf16[48,1536]{1,0:T(8,128)(2,1)S(1)}, u32[]{:S(2)}, u32[]{:S(2)}) %collective-permute-start.38) | collective-permute-done | bytes 147488 | tf_op jit(solution)/shard_map/ppermute | solution.py:75
  274.7 9.3 %collective-permute-done.39 = bf16[48,1920]{1,0:T(8,128)(2,1)S(1)} collective-permute-done((bf16[48,1920]{1,0:T(8,128)(2,1)}, bf16[48,1920]{1,0:T(8,128)(2,1)S(1)}, u32[]{:S(2)}, u32[]{:S(2)}) %collective-permute-start.39) | collective-permute-done | bytes 184352 | tf_op jit(solution)/shard_map/ppermute | solution.py:75
  284.0 1.6 collective-permute-done.35
  291.5 1.7 collective-permute-start.43
  295.2 2.4 collective-permute-start.42
  297.6 10.6 %collective-permute-done.40 = bf16[48,1152]{1,0:T(8,128)(2,1)S(1)} collective-permute-done((bf16[48,1152]{1,0:T(8,128)(2,1)S(1)}, bf16[48,1152]{1,0:T(8,128)(2,1)S(1)}, u32[]{:S(2)}, u32[]{:S(2)}) %collective-permute-start.40) | collective-permute-done | bytes 110624 | tf_op jit(solution)/shard_map/ppermute | solution.py:75
  308.2 1.5 collective-permute-start.50
  311.1 2.1 collective-permute-start.45
  313.8 1.8 collective-permute-start.47
  317.6 5.6 %collective-permute-done.46 = bf16[48,1152]{1,0:T(8,128)(2,1)S(1)} collective-permute-done((bf16[48,1152]{1,0:T(8,128)(2,1)S(1)}, bf16[48,1152]{1,0:T(8,128)(2,1)S(1)}, u32[]{:S(2)}, u32[]{:S(2)}) %collective-permute-start.46) | collective-permute-done | bytes 110624 | tf_op jit(solution)/shard_map/ppermute | solution.py:75
  323.7 5.3 %collective-permute-done.48 = bf16[2,48,1920]{2,1,0:T(8,128)(2,1)S(1)} collective-permute-done((bf16[2,48,1920]{2,1,0:T(8,128)(2,1)S(1)}, bf16[2,48,1920]{2,1,0:T(8,128)(2,1)S(1)}, u32[]{:S(2)}, u32[]{:S(2)}) %collective-permute-start.48) | collective-permute-done | bytes 368672 | tf_op jit(solution)/shard_map/ppermute | solution.py:75
  334.8 1.6 fusion.11
  337.6 2.8 fusion.9
  340.5 3.8 add_add_fusion
  344.3 14.7 %collective-permute-done.54 = f32[16,768]{1,0:T(8,128)S(1)} collective-permute-done((f32[16,768]{1,0:T(8,128)S(1)}, f32[16,768]{1,0:T(8,128)S(1)}, u32[]{:S(2)}, u32[]{:S(2)}) %collective-permute-start.54) | collective-permute-done | bytes 49184 | tf_op jit(solution)/shard_map/ppermute | solution.py:75
  360.0 3.4 fusion.87.own_ref
  364.5 3.1 collective-permute-done.56
  368.3 33.2 %polar_rows.1 = bf16[192,1536]{1,0:T(8,128)(2,1)S(1)} custom-call(s32[1]{0:T(128)} %bitcast.103.start_ref, f32[768,768]{1,0:T(8,128)} %fusion.87.own_ref, f32[768,768]{1,0:T(8,128)} %collective-permute-done.55.other_ref, bf16[768,1536]{1,0:T(8,128)(2,1)S(1)} %bitcast.307), custom_call_target="tpu_custom_call" | custom-call | tf_op jit(solution)/shard_map/polar_rows/pallas_call | solution.py:749
  404.7 1.9 collective-permute-start.58
  408.1 1.7 collective-permute-done.60
  409.8 2.4 collective-permute-done.59
  (350 shorter events, 88.8 us)
Async XLA Ops:
  0.7 45.3 %copy-start = (s32[1,2]{1,0:T(1,128)S(1)}, s32[1,2]{1,0:T(1,128)}, u32[]{:S(2)}) copy-start(s32[1,2]{1,0:T(1,128)} %param.19) | copy-start | bytes 28
  2.6 17.9 %collective-permute-start.3 = (bf16[48,1920]{1,0:T(8,128)(2,1)S(1)}, bf16[48,1920]{1,0:T(8,128)(2,1)S(1)}, u32[]{:S(2)}, u32[]{:S(2)}) collective-permute-start(bf16[48,1920]{1,0:T(8,128)(2,1)S(1)} %pad_maximum_fusion.9), channel_id=1, source_target_pairs={{0,8},{2,10},{4,12},{6,14},{8,0},{10,2},{12,4},{14,6},{16,24},{18,... | collective-permute-start | bytes 552968 | tf_op jit(solution)/shard_map/ppermute | solution.py:75
  7.6 8.1 %collective-permute-start = (bf16[48,1280]{1,0:T(8,128)(2,1)S(1)}, bf16[48,1280]{1,0:T(8,128)(2,1)S(1)}, u32[]{:S(2)}, u32[]{:S(2)}) collective-permute-start(bf16[48,1280]{1,0:T(8,128)(2,1)S(1)} %fusion.66), channel_id=1, source_target_pairs={{0,8},{2,10},{4,12},{6,14},{8,0},{10,2},{12,4},{14,6},{16,24},{18,... | collective-permute-start | bytes 368648 | tf_op jit(solution)/shard_map/ppermute | solution.py:75
  7.7 8.4 %collective-permute-start.1 = (bf16[48,1280]{1,0:T(8,128)(2,1)S(1)}, bf16[48,1280]{1,0:T(8,128)(2,1)S(1)}, u32[]{:S(2)}, u32[]{:S(2)}) collective-permute-start(bf16[48,1280]{1,0:T(8,128)(2,1)S(1)} %fusion.66), channel_id=1, source_target_pairs={{0,16},{2,18},{4,20},{6,22},{8,24},{10,26},{12,28},{14,30},{16,0},... | collective-permute-start | bytes 368648 | tf_op jit(solution)/shard_map/ppermute | solution.py:75
  10.7 9.9 %collective-permute-start.2 = (bf16[48,1280]{1,0:T(8,128)(2,1)S(1)}, bf16[48,1280]{1,0:T(8,128)(2,1)S(1)}, u32[]{:S(2)}, u32[]{:S(2)}) collective-permute-start(bf16[48,1280]{1,0:T(8,128)(2,1)S(1)} %fusion.66), channel_id=1, source_target_pairs={{0,24},{2,26},{4,28},{6,30},{8,16},{10,18},{12,20},{14,22},{16,8},... | collective-permute-start | bytes 368648 | tf_op jit(solution)/shard_map/ppermute | solution.py:75
  20.7 18.6 %collective-permute-start.4 = (bf16[4,48,1280]{2,1,0:T(8,128)(2,1)S(1)}, bf16[4,48,1280]{2,1,0:T(8,128)(2,1)S(1)}, u32[]{:S(2)}, u32[]{:S(2)}) collective-permute-start(bf16[4,48,1280]{2,1,0:T(8,128)(2,1)S(1)} %maximum_select_fusion.17), channel_id=1, source_target_pairs={{0,2},{2,0},{4,6},{6,4},{8,10},{10,8},{12,14},{14,12},{16,18},{18,... | collective-permute-start | bytes 1474568 | tf_op jit(solution)/shard_map/ppermute | solution.py:75
  22.3 22.7 %collective-permute-start.5 = (bf16[4,48,1280]{2,1,0:T(8,128)(2,1)S(1)}, bf16[4,48,1280]{2,1,0:T(8,128)(2,1)S(1)}, u32[]{:S(2)}, u32[]{:S(2)}) collective-permute-start(bf16[4,48,1280]{2,1,0:T(8,128)(2,1)S(1)} %maximum_select_fusion.17), channel_id=1, source_target_pairs={{0,4},{2,6},{4,0},{6,2},{8,12},{10,14},{12,8},{14,10},{16,20},{18,... | collective-permute-start | bytes 1474568 | tf_op jit(solution)/shard_map/ppermute | solution.py:75
  23.8 21.2 %collective-permute-start.6 = (bf16[4,48,1280]{2,1,0:T(8,128)(2,1)S(1)}, bf16[4,48,1280]{2,1,0:T(8,128)(2,1)S(1)}, u32[]{:S(2)}, u32[]{:S(2)}) collective-permute-start(bf16[4,48,1280]{2,1,0:T(8,128)(2,1)S(1)} %maximum_select_fusion.17), channel_id=1, source_target_pairs={{0,6},{2,4},{4,2},{6,0},{8,14},{10,12},{12,10},{14,8},{16,22},{18,... | collective-permute-start | bytes 1474568 | tf_op jit(solution)/shard_map/ppermute | solution.py:75
  24.3 15.0 %collective-permute-start.7 = (bf16[48,1920]{1,0:T(8,128)(2,1)S(1)}, bf16[48,1920]{1,0:T(8,128)(2,1)S(1)}, u32[]{:S(2)}, u32[]{:S(2)}) collective-permute-start(bf16[48,1920]{1,0:T(8,128)(2,1)S(1)} %pad_maximum_fusion.9), channel_id=1, source_target_pairs={{0,16},{2,18},{4,20},{6,22},{8,24},{10,26},{12,28},{14,30},{16,0},... | collective-permute-start | bytes 552968 | tf_op jit(solution)/shard_map/ppermute | solution.py:75
  27.8 11.5 %collective-permute-start.8 = (bf16[48,1920]{1,0:T(8,128)(2,1)S(1)}, bf16[48,1920]{1,0:T(8,128)(2,1)S(1)}, u32[]{:S(2)}, u32[]{:S(2)}) collective-permute-start(bf16[48,1920]{1,0:T(8,128)(2,1)S(1)} %pad_maximum_fusion.9), channel_id=1, source_target_pairs={{0,24},{2,26},{4,28},{6,30},{8,16},{10,18},{12,20},{14,22},{16,8},... | collective-permute-start | bytes 552968 | tf_op jit(solution)/shard_map/ppermute | solution.py:75
  45.8 6.7 %collective-permute-start.9 = (bf16[768,1280]{1,0:T(8,128)(2,1)S(1)}, bf16[768,1280]{1,0:T(8,128)(2,1)}, u32[]{:S(2)}, u32[]{:S(2)}) collective-permute-start(bf16[768,1280]{1,0:T(8,128)(2,1)S(1)} %bitcast.316), channel_id=1, source_target_pairs={{0,1},{1,0},{2,3},{3,2},{4,5},{5,4},{6,7},{7,6},{8,9},{9,8},{10,11... | collective-permute-start | bytes 5898248 | tf_op jit(solution)/shard_map/ppermute | solution.py:79
  47.5 38.8 %collective-permute-start.11 = (bf16[4,48,1920]{2,1,0:T(8,128)(2,1)S(1)}, bf16[4,48,1920]{2,1,0:T(8,128)(2,1)S(1)}, u32[]{:S(2)}, u32[]{:S(2)}) collective-permute-start(bf16[4,48,1920]{2,1,0:T(8,128)(2,1)S(1)} %maximum_select_fusion.12), channel_id=1, source_target_pairs={{0,2},{2,0},{4,6},{6,4},{8,10},{10,8},{12,14},{14,12},{16,18},{18,... | collective-permute-start | bytes 2211848 | tf_op jit(solution)/shard_map/ppermute | solution.py:75
  48.8 37.5 %collective-permute-start.12 = (bf16[4,48,1920]{2,1,0:T(8,128)(2,1)S(1)}, bf16[4,48,1920]{2,1,0:T(8,128)(2,1)}, u32[]{:S(2)}, u32[]{:S(2)}) collective-permute-start(bf16[4,48,1920]{2,1,0:T(8,128)(2,1)S(1)} %maximum_select_fusion.12), channel_id=1, source_target_pairs={{0,4},{2,6},{4,0},{6,2},{8,12},{10,14},{12,8},{14,10},{16,20},{18,... | collective-permute-start | bytes 2211848 | tf_op jit(solution)/shard_map/ppermute | solution.py:75
  49.6 36.7 %collective-permute-start.13 = (bf16[4,48,1920]{2,1,0:T(8,128)(2,1)S(1)}, bf16[4,48,1920]{2,1,0:T(8,128)(2,1)}, u32[]{:S(2)}, u32[]{:S(2)}) collective-permute-start(bf16[4,48,1920]{2,1,0:T(8,128)(2,1)S(1)} %maximum_select_fusion.12), channel_id=1, source_target_pairs={{0,6},{2,4},{4,2},{6,0},{8,14},{10,12},{12,10},{14,8},{16,22},{18,... | collective-permute-start | bytes 2211848 | tf_op jit(solution)/shard_map/ppermute | solution.py:75
  51.1 15.4 %collective-permute-start.10 = (bf16[48,1536]{1,0:T(8,128)(2,1)}, bf16[48,1536]{1,0:T(8,128)(2,1)}, u32[]{:S(2)}, u32[]{:S(2)}) collective-permute-start(bf16[48,1536]{1,0:T(8,128)(2,1)} %convert_element_type.339), channel_id=1, source_target_pairs={{0,8},{2,10},{4,12},{6,14},{8,0},{10,2},{12,4},{14,6},{16,24},{18,... | collective-permute-start | bytes 442376 | tf_op jit(solution)/shard_map/ppermute | solution.py:75
  66.5 19.9 %collective-permute-start.14 = (bf16[48,1536]{1,0:T(8,128)(2,1)}, bf16[48,1536]{1,0:T(8,128)(2,1)S(1)}, u32[]{:S(2)}, u32[]{:S(2)}) collective-permute-start(bf16[48,1536]{1,0:T(8,128)(2,1)} %convert_element_type.339), channel_id=1, source_target_pairs={{0,16},{2,18},{4,20},{6,22},{8,24},{10,26},{12,28},{14,30},{16,0},... | collective-permute-start | bytes 442376 | tf_op jit(solution)/shard_map/ppermute | solution.py:75
  67.7 18.7 %collective-permute-start.15 = (bf16[48,1536]{1,0:T(8,128)(2,1)}, bf16[48,1536]{1,0:T(8,128)(2,1)S(1)}, u32[]{:S(2)}, u32[]{:S(2)}) collective-permute-start(bf16[48,1536]{1,0:T(8,128)(2,1)} %convert_element_type.339), channel_id=1, source_target_pairs={{0,24},{2,26},{4,28},{6,30},{8,16},{10,18},{12,20},{14,22},{16,8},... | collective-permute-start | bytes 442376 | tf_op jit(solution)/shard_map/ppermute | solution.py:75
  89.5 5.8 %collective-permute-start.16 = (bf16[768,1920]{1,0:T(8,128)(2,1)S(1)}, bf16[768,1920]{1,0:T(8,128)(2,1)S(1)}, u32[]{:S(2)}, u32[]{:S(2)}) collective-permute-start(bf16[768,1920]{1,0:T(8,128)(2,1)S(1)} %bitcast.309), channel_id=1, source_target_pairs={{0,1},{1,0},{2,3},{3,2},{4,5},{5,4},{6,7},{7,6},{8,9},{9,8},{10,11... | collective-permute-start | bytes 8847368 | tf_op jit(solution)/shard_map/ppermute | solution.py:79
  91.8 26.8 %collective-permute-start.17 = (bf16[4,48,1536]{2,1,0:T(8,128)(2,1)S(1)}, bf16[4,48,1536]{2,1,0:T(8,128)(2,1)S(1)}, u32[]{:S(2)}, u32[]{:S(2)}) collective-permute-start(bf16[4,48,1536]{2,1,0:T(8,128)(2,1)S(1)} %maximum_select_fusion.14), channel_id=1, source_target_pairs={{0,2},{2,0},{4,6},{6,4},{8,10},{10,8},{12,14},{14,12},{16,18},{18,... | collective-permute-start | bytes 1769480 | tf_op jit(solution)/shard_map/ppermute | solution.py:75
  93.1 25.6 %collective-permute-start.18 = (bf16[4,48,1536]{2,1,0:T(8,128)(2,1)S(1)}, bf16[4,48,1536]{2,1,0:T(8,128)(2,1)S(1)}, u32[]{:S(2)}, u32[]{:S(2)}) collective-permute-start(bf16[4,48,1536]{2,1,0:T(8,128)(2,1)S(1)} %maximum_select_fusion.14), channel_id=1, source_target_pairs={{0,4},{2,6},{4,0},{6,2},{8,12},{10,14},{12,8},{14,10},{16,20},{18,... | collective-permute-start | bytes 1769480 | tf_op jit(solution)/shard_map/ppermute | solution.py:75
  93.9 26.4 %collective-permute-start.19 = (bf16[4,48,1536]{2,1,0:T(8,128)(2,1)S(1)}, bf16[4,48,1536]{2,1,0:T(8,128)(2,1)S(1)}, u32[]{:S(2)}, u32[]{:S(2)}) collective-permute-start(bf16[4,48,1536]{2,1,0:T(8,128)(2,1)S(1)} %maximum_select_fusion.14), channel_id=1, source_target_pairs={{0,6},{2,4},{4,2},{6,0},{8,14},{10,12},{12,10},{14,8},{16,22},{18,... | collective-permute-start | bytes 1769480 | tf_op jit(solution)/shard_map/ppermute | solution.py:75
  121.4 6.9 %collective-permute-start.20 = (bf16[768,1536]{1,0:T(8,128)(2,1)S(1)}, bf16[768,1536]{1,0:T(8,128)(2,1)S(1)}, u32[]{:S(2)}, u32[]{:S(2)}) collective-permute-start(bf16[768,1536]{1,0:T(8,128)(2,1)S(1)} %bitcast.321), channel_id=1, source_target_pairs={{0,1},{1,0},{2,3},{3,2},{4,5},{5,4},{6,7},{7,6},{8,9},{9,8},{10,11... | collective-permute-start | bytes 7077896 | tf_op jit(solution)/shard_map/ppermute | solution.py:79
  144.6 4.9 %collective-permute-start.21 = (bf16[768,1536]{1,0:T(8,128)(2,1)}, bf16[768,1536]{1,0:T(8,128)(2,1)}, u32[]{:S(2)}, u32[]{:S(2)}) collective-permute-start(bf16[768,1536]{1,0:T(8,128)(2,1)} %convolution_convert_fusion.1), channel_id=1, source_target_pairs={{0,1},{1,0},{2,3},{3,2},{4,5},{5,4},{6,7},{7,6},{8,9},{9,8},{10,11... | collective-permute-start | bytes 7077896 | tf_op jit(solution)/shard_map/ppermute | solution.py:79
  155.1 25.0 %collective-permute-start.22 = (bf16[4,48,1536]{2,1,0:T(8,128)(2,1)}, bf16[4,48,1536]{2,1,0:T(8,128)(2,1)S(1)}, u32[]{:S(2)}, u32[]{:S(2)}) collective-permute-start(bf16[4,48,1536]{2,1,0:T(8,128)(2,1)} %get-tuple-element.274), channel_id=1, source_target_pairs={{0,2},{2,0},{4,6},{6,4},{8,10},{10,8},{12,14},{14,12},{16,18},{18,... | collective-permute-start | bytes 1769480 | tf_op jit(solution)/shard_map/ppermute | solution.py:75
  155.9 26.9 %collective-permute-start.23 = (bf16[4,48,1536]{2,1,0:T(8,128)(2,1)S(1)}, bf16[4,48,1536]{2,1,0:T(8,128)(2,1)S(1)}, u32[]{:S(2)}, u32[]{:S(2)}) collective-permute-start(bf16[4,48,1536]{2,1,0:T(8,128)(2,1)S(1)} %get-tuple-element.275), channel_id=1, source_target_pairs={{0,4},{2,6},{4,0},{6,2},{8,12},{10,14},{12,8},{14,10},{16,20},{18,... | collective-permute-start | bytes 1769480 | tf_op jit(solution)/shard_map/ppermute | solution.py:75
  157.4 26.3 %collective-permute-start.24 = (bf16[4,48,1536]{2,1,0:T(8,128)(2,1)S(1)}, bf16[4,48,1536]{2,1,0:T(8,128)(2,1)S(1)}, u32[]{:S(2)}, u32[]{:S(2)}) collective-permute-start(bf16[4,48,1536]{2,1,0:T(8,128)(2,1)S(1)} %get-tuple-element.276), channel_id=1, source_target_pairs={{0,6},{2,4},{4,2},{6,0},{8,14},{10,12},{12,10},{14,8},{16,22},{18,... | collective-permute-start | bytes 1769480 | tf_op jit(solution)/shard_map/ppermute | solution.py:75
  185.6 8.4 %collective-permute-start.25 = (bf16[2,48,1536]{2,1,0:T(8,128)(2,1)S(1)}, bf16[2,48,1536]{2,1,0:T(8,128)(2,1)S(1)}, u32[]{:S(2)}, u32[]{:S(2)}) collective-permute-start(bf16[2,48,1536]{2,1,0:T(8,128)(2,1)S(1)} %fusion.44), channel_id=1, source_target_pairs={{0,8},{2,10},{4,12},{6,14},{8,0},{10,2},{12,4},{14,6},{16,24},{18,... | collective-permute-start | bytes 884744 | tf_op jit(solution)/shard_map/ppermute | solution.py:75
  193.9 9.0 %collective-permute-start.26 = (bf16[768,1536]{1,0:T(8,128)(2,1)}, bf16[768,1536]{1,0:T(8,128)(2,1)}, u32[]{:S(2)}, u32[]{:S(2)}) collective-permute-start(bf16[768,1536]{1,0:T(8,128)(2,1)} %convolution_convert_fusion), channel_id=1, source_target_pairs={{0,1},{1,0},{2,3},{3,2},{4,5},{5,4},{6,7},{7,6},{8,9},{9,8},{10,11... | collective-permute-start | bytes 7077896 | tf_op jit(solution)/shard_map/ppermute | solution.py:79
  196.5 6.4 %collective-permute-start.27 = (bf16[768,384]{1,0:T(8,128)(2,1)S(1)}, bf16[768,384]{1,0:T(8,128)(2,1)S(1)}, u32[]{:S(2)}, u32[]{:S(2)}) collective-permute-start(bf16[768,384]{1,0:T(8,128)(2,1)S(1)} %convolution_convert_fusion.4), channel_id=1, source_target_pairs={{0,1},{1,0},{2,3},{3,2},{4,5},{5,4},{6,7},{7,6},{8,9},{9,8},{10,11... | collective-permute-start | bytes 1769480 | tf_op jit(solution)/shard_map/ppermute | solution.py:79
  210.9 29.0 %collective-permute-start.28 = (bf16[48,1536]{1,0:T(8,128)(2,1)S(1)}, bf16[48,1536]{1,0:T(8,128)(2,1)S(1)}, u32[]{:S(2)}, u32[]{:S(2)}) collective-permute-start(bf16[48,1536]{1,0:T(8,128)(2,1)S(1)} %fusion.56), channel_id=1, source_target_pairs={{0,16},{2,18},{4,20},{6,22},{8,24},{10,26},{12,28},{14,30},{16,0},... | collective-permute-start | bytes 442376 | tf_op jit(solution)/shard_map/ppermute | solution.py:75
  212.6 37.7 %collective-permute-start.29 = (bf16[4,48,1920]{2,1,0:T(8,128)(2,1)}, bf16[4,48,1920]{2,1,0:T(8,128)(2,1)S(1)}, u32[]{:S(2)}, u32[]{:S(2)}) collective-permute-start(bf16[4,48,1920]{2,1,0:T(8,128)(2,1)} %pad_maximum_fusion.1), channel_id=1, source_target_pairs={{0,2},{2,0},{4,6},{6,4},{8,10},{10,8},{12,14},{14,12},{16,18},{18,... | collective-permute-start | bytes 2211848 | tf_op jit(solution)/shard_map/ppermute | solution.py:75
  214.1 36.3 %collective-permute-start.30 = (bf16[4,48,1920]{2,1,0:T(8,128)(2,1)}, bf16[4,48,1920]{2,1,0:T(8,128)(2,1)}, u32[]{:S(2)}, u32[]{:S(2)}) collective-permute-start(bf16[4,48,1920]{2,1,0:T(8,128)(2,1)} %pad_maximum_fusion.2), channel_id=1, source_target_pairs={{0,4},{2,6},{4,0},{6,2},{8,12},{10,14},{12,8},{14,10},{16,20},{18,... | collective-permute-start | bytes 2211848 | tf_op jit(solution)/shard_map/ppermute | solution.py:75
  214.6 35.7 %collective-permute-start.31 = (bf16[4,48,1920]{2,1,0:T(8,128)(2,1)}, bf16[4,48,1920]{2,1,0:T(8,128)(2,1)}, u32[]{:S(2)}, u32[]{:S(2)}) collective-permute-start(bf16[4,48,1920]{2,1,0:T(8,128)(2,1)} %pad_maximum_fusion.3), channel_id=1, source_target_pairs={{0,6},{2,4},{4,2},{6,0},{8,14},{10,12},{12,10},{14,8},{16,22},{18,... | collective-permute-start | bytes 2211848 | tf_op jit(solution)/shard_map/ppermute | solution.py:75
  253.6 4.2 %collective-permute-start.32 = (bf16[768,768]{1,0:T(8,128)(2,1)S(1)}, bf16[768,768]{1,0:T(8,128)(2,1)S(1)}, u32[]{:S(2)}, u32[]{:S(2)}) collective-permute-start(bf16[768,768]{1,0:T(8,128)(2,1)S(1)} %copy-done.68), channel_id=1, source_target_pairs={{0,1},{1,0},{2,3},{3,2},{4,5},{5,4},{6,7},{7,6},{8,9},{9,8},{10,11... | collective-permute-start | bytes 3538952 | tf_op jit(solution)/shard_map/ppermute | solution.py:79
  253.8 4.0 collective-permute-start.33
  254.3 11.9 %collective-permute-start.37 = (bf16[2,48,1920]{2,1,0:T(8,128)(2,1)S(1)}, bf16[2,48,1920]{2,1,0:T(8,128)(2,1)S(1)}, u32[]{:S(2)}, u32[]{:S(2)}) collective-permute-start(bf16[2,48,1920]{2,1,0:T(8,128)(2,1)S(1)} %pad_maximum_fusion.7), channel_id=1, source_target_pairs={{0,8},{2,10},{4,12},{6,14},{8,0},{10,2},{12,4},{14,6},{16,24},{18,... | collective-permute-start | bytes 1105928 | tf_op jit(solution)/shard_map/ppermute | solution.py:75
  261.9 9.6 %collective-permute-start.38 = (bf16[48,1536]{1,0:T(8,128)(2,1)S(1)}, bf16[48,1536]{1,0:T(8,128)(2,1)S(1)}, u32[]{:S(2)}, u32[]{:S(2)}) collective-permute-start(bf16[48,1536]{1,0:T(8,128)(2,1)S(1)} %convert_element_type.405), channel_id=1, source_target_pairs={{0,16},{2,18},{4,20},{6,22},{8,24},{10,26},{12,28},{14,30},{16,0},... | collective-permute-start | bytes 442376 | tf_op jit(solution)/shard_map/ppermute | solution.py:75
  262.8 21.3 %collective-permute-start.34 = (bf16[4,48,1152]{2,1,0:T(8,128)(2,1)}, bf16[4,48,1152]{2,1,0:T(8,128)(2,1)}, u32[]{:S(2)}, u32[]{:S(2)}) collective-permute-start(bf16[4,48,1152]{2,1,0:T(8,128)(2,1)} %pad_maximum_fusion.4), channel_id=1, source_target_pairs={{0,2},{2,0},{4,6},{6,4},{8,10},{10,8},{12,14},{14,12},{16,18},{18,... | collective-permute-start | bytes 1327112 | tf_op jit(solution)/shard_map/ppermute | solution.py:75
  264.3 21.3 %collective-permute-start.35 = (bf16[4,48,1152]{2,1,0:T(8,128)(2,1)}, bf16[4,48,1152]{2,1,0:T(8,128)(2,1)}, u32[]{:S(2)}, u32[]{:S(2)}) collective-permute-start(bf16[4,48,1152]{2,1,0:T(8,128)(2,1)} %pad_maximum_fusion.5), channel_id=1, source_target_pairs={{0,4},{2,6},{4,0},{6,2},{8,12},{10,14},{12,8},{14,10},{16,20},{18,... | collective-permute-start | bytes 1327112 | tf_op jit(solution)/shard_map/ppermute | solution.py:75
  264.8 20.8 %collective-permute-start.36 = (bf16[4,48,1152]{2,1,0:T(8,128)(2,1)}, bf16[4,48,1152]{2,1,0:T(8,128)(2,1)}, u32[]{:S(2)}, u32[]{:S(2)}) collective-permute-start(bf16[4,48,1152]{2,1,0:T(8,128)(2,1)} %pad_maximum_fusion.6), channel_id=1, source_target_pairs={{0,6},{2,4},{4,2},{6,0},{8,14},{10,12},{12,10},{14,8},{16,22},{18,... | collective-permute-start | bytes 1327112 | tf_op jit(solution)/shard_map/ppermute | solution.py:75
  273.9 10.1 %collective-permute-start.39 = (bf16[48,1920]{1,0:T(8,128)(2,1)}, bf16[48,1920]{1,0:T(8,128)(2,1)S(1)}, u32[]{:S(2)}, u32[]{:S(2)}) collective-permute-start(bf16[48,1920]{1,0:T(8,128)(2,1)} %pad_maximum_fusion.10), channel_id=1, source_target_pairs={{0,16},{2,18},{4,20},{6,22},{8,24},{10,26},{12,28},{14,30},{16,0},... | collective-permute-start | bytes 552968 | tf_op jit(solution)/shard_map/ppermute | solution.py:75
  290.2 19.7 %collective-permute-start.44 = (bf16[2,48,1536]{2,1,0:T(8,128)(2,1)S(1)}, bf16[2,48,1536]{2,1,0:T(8,128)(2,1)S(1)}, u32[]{:S(2)}, u32[]{:S(2)}) collective-permute-start(bf16[2,48,1536]{2,1,0:T(8,128)(2,1)S(1)} %maximum_select_fusion.24), channel_id=1, source_target_pairs={{0,8},{2,10},{4,12},{6,14},{8,0},{10,2},{12,4},{14,6},{16,24},{18,... | collective-permute-start | bytes 884744 | tf_op jit(solution)/shard_map/ppermute | solution.py:75
  291.5 18.4 %collective-permute-start.43 = (bf16[48,1920]{1,0:T(8,128)(2,1)S(1)}, bf16[48,1920]{1,0:T(8,128)(2,1)S(1)}, u32[]{:S(2)}, u32[]{:S(2)}) collective-permute-start(bf16[48,1920]{1,0:T(8,128)(2,1)S(1)} %pad_maximum_fusion.11), channel_id=1, source_target_pairs={{0,16},{2,18},{4,20},{6,22},{8,24},{10,26},{12,28},{14,30},{16,0},... | collective-permute-start | bytes 552968 | tf_op jit(solution)/shard_map/ppermute | solution.py:75
  293.2 2.0 collective-permute-start.49
  293.2 15.0 %collective-permute-start.40 = (bf16[48,1152]{1,0:T(8,128)(2,1)S(1)}, bf16[48,1152]{1,0:T(8,128)(2,1)S(1)}, u32[]{:S(2)}, u32[]{:S(2)}) collective-permute-start(bf16[48,1152]{1,0:T(8,128)(2,1)S(1)} %pad_maximum_fusion.12), channel_id=1, source_target_pairs={{0,8},{2,10},{4,12},{6,14},{8,0},{10,2},{12,4},{14,6},{16,24},{18,... | collective-permute-start | bytes 331784 | tf_op jit(solution)/shard_map/ppermute | solution.py:75
  294.1 15.8 %collective-permute-start.41 = (bf16[48,1152]{1,0:T(8,128)(2,1)S(1)}, bf16[48,1152]{1,0:T(8,128)(2,1)S(1)}, u32[]{:S(2)}, u32[]{:S(2)}) collective-permute-start(bf16[48,1152]{1,0:T(8,128)(2,1)S(1)} %pad_maximum_fusion.13), channel_id=1, source_target_pairs={{0,16},{2,18},{4,20},{6,22},{8,24},{10,26},{12,28},{14,30},{16,0},... | collective-permute-start | bytes 331784 | tf_op jit(solution)/shard_map/ppermute | solution.py:75
  295.2 14.7 %collective-permute-start.42 = (bf16[48,1152]{1,0:T(8,128)(2,1)S(1)}, bf16[48,1152]{1,0:T(8,128)(2,1)S(1)}, u32[]{:S(2)}, u32[]{:S(2)}) collective-permute-start(bf16[48,1152]{1,0:T(8,128)(2,1)S(1)} %pad_maximum_fusion.14), channel_id=1, source_target_pairs={{0,24},{2,26},{4,28},{6,30},{8,16},{10,18},{12,20},{14,22},{16,8},... | collective-permute-start | bytes 331784 | tf_op jit(solution)/shard_map/ppermute | solution.py:75
  308.2 22.1 %collective-permute-start.50 = (f32[16,768]{1,0:T(8,128)S(1)}, f32[16,768]{1,0:T(8,128)S(1)}, u32[]{:S(2)}, u32[]{:S(2)}) collective-permute-start(f32[16,768]{1,0:T(8,128)S(1)} %add.343), channel_id=1, source_target_pairs={{0,2},{2,0},{4,6},{6,4},{8,10},{10,8},{12,14},{14,12},{16,18},{18,... | collective-permute-start | bytes 147464 | tf_op jit(solution)/shard_map/ppermute | solution.py:75
  311.1 6.5 %collective-permute-start.45 = (bf16[48,1152]{1,0:T(8,128)(2,1)S(1)}, bf16[48,1152]{1,0:T(8,128)(2,1)S(1)}, u32[]{:S(2)}, u32[]{:S(2)}) collective-permute-start(bf16[48,1152]{1,0:T(8,128)(2,1)S(1)} %get-tuple-element.370), channel_id=1, source_target_pairs={{0,8},{2,10},{4,12},{6,14},{8,0},{10,2},{12,4},{14,6},{16,24},{18,... | collective-permute-start | bytes 331784 | tf_op jit(solution)/shard_map/ppermute | solution.py:75
  313.1 10.1 %collective-permute-start.46 = (bf16[48,1152]{1,0:T(8,128)(2,1)S(1)}, bf16[48,1152]{1,0:T(8,128)(2,1)S(1)}, u32[]{:S(2)}, u32[]{:S(2)}) collective-permute-start(bf16[48,1152]{1,0:T(8,128)(2,1)S(1)} %get-tuple-element.370), channel_id=1, source_target_pairs={{0,16},{2,18},{4,20},{6,22},{8,24},{10,26},{12,28},{14,30},{16,0},... | collective-permute-start | bytes 331784 | tf_op jit(solution)/shard_map/ppermute | solution.py:75
  313.8 10.0 %collective-permute-start.47 = (bf16[48,1152]{1,0:T(8,128)(2,1)S(1)}, bf16[48,1152]{1,0:T(8,128)(2,1)S(1)}, u32[]{:S(2)}, u32[]{:S(2)}) collective-permute-start(bf16[48,1152]{1,0:T(8,128)(2,1)S(1)} %get-tuple-element.370), channel_id=1, source_target_pairs={{0,24},{2,26},{4,28},{6,30},{8,16},{10,18},{12,20},{14,22},{16,8},... | collective-permute-start | bytes 331784 | tf_op jit(solution)/shard_map/ppermute | solution.py:75
  315.6 13.5 %collective-permute-start.48 = (bf16[2,48,1920]{2,1,0:T(8,128)(2,1)S(1)}, bf16[2,48,1920]{2,1,0:T(8,128)(2,1)S(1)}, u32[]{:S(2)}, u32[]{:S(2)}) collective-permute-start(bf16[2,48,1920]{2,1,0:T(8,128)(2,1)S(1)} %maximum_select_fusion.21), channel_id=1, source_target_pairs={{0,8},{2,10},{4,12},{6,14},{8,0},{10,2},{12,4},{14,6},{16,24},{18,... | collective-permute-start | bytes 1105928 | tf_op jit(solution)/shard_map/ppermute | solution.py:75
  330.3 28.7 %collective-permute-start.51 = (bf16[4,48,1536]{2,1,0:T(8,128)(2,1)S(1)}, bf16[4,48,1536]{2,1,0:T(8,128)(2,1)S(1)}, u32[]{:S(2)}, u32[]{:S(2)}) collective-permute-start(bf16[4,48,1536]{2,1,0:T(8,128)(2,1)S(1)} %bitcast.361), channel_id=1, source_target_pairs={{0,2},{2,0},{4,6},{6,4},{8,10},{10,8},{12,14},{14,12},{16,18},{18,... | collective-permute-start | bytes 1769480 | tf_op jit(solution)/shard_map/ppermute | solution.py:75
  331.2 27.8 %collective-permute-start.52 = (bf16[4,48,1536]{2,1,0:T(8,128)(2,1)S(1)}, bf16[4,48,1536]{2,1,0:T(8,128)(2,1)S(1)}, u32[]{:S(2)}, u32[]{:S(2)}) collective-permute-start(bf16[4,48,1536]{2,1,0:T(8,128)(2,1)S(1)} %bitcast.360), channel_id=1, source_target_pairs={{0,4},{2,6},{4,0},{6,2},{8,12},{10,14},{12,8},{14,10},{16,20},{18,... | collective-permute-start | bytes 1769480 | tf_op jit(solution)/shard_map/ppermute | solution.py:75
  332.4 26.6 %collective-permute-start.53 = (bf16[4,48,1536]{2,1,0:T(8,128)(2,1)S(1)}, bf16[4,48,1536]{2,1,0:T(8,128)(2,1)S(1)}, u32[]{:S(2)}, u32[]{:S(2)}) collective-permute-start(bf16[4,48,1536]{2,1,0:T(8,128)(2,1)S(1)} %bitcast.359), channel_id=1, source_target_pairs={{0,6},{2,4},{4,2},{6,0},{8,14},{10,12},{12,10},{14,8},{16,22},{18,... | collective-permute-start | bytes 1769480 | tf_op jit(solution)/shard_map/ppermute | solution.py:75
  336.5 22.5 %collective-permute-start.54 = (f32[16,768]{1,0:T(8,128)S(1)}, f32[16,768]{1,0:T(8,128)S(1)}, u32[]{:S(2)}, u32[]{:S(2)}) collective-permute-start(f32[16,768]{1,0:T(8,128)S(1)} %add.348), channel_id=1, source_target_pairs={{0,4},{2,6},{4,0},{6,2},{8,12},{10,14},{12,8},{14,10},{16,20},{18,... | collective-permute-start | bytes 147464 | tf_op jit(solution)/shard_map/ppermute | solution.py:75
  363.4 4.9 %collective-permute-start.55 = (f32[768,768]{1,0:T(8,128)}, f32[768,768]{1,0:T(8,128)}, u32[]{:S(2)}, u32[]{:S(2)}) collective-permute-start(f32[768,768]{1,0:T(8,128)} %fusion.87.own_ref), channel_id=1, source_target_pairs={{0,1},{1,0},{2,3},{3,2},{4,5},{5,4},{6,7},{7,6},{8,9},{9,8},{10,11... | collective-permute-start | bytes 7077896 | tf_op jit(solution)/shard_map/ppermute | solution.py:79
  363.4 4.2 %collective-permute-start.56 = (f32[16,768]{1,0:T(8,128)S(1)}, f32[16,768]{1,0:T(8,128)S(1)}, u32[]{:S(2)}, u32[]{:S(2)}) collective-permute-start(f32[16,768]{1,0:T(8,128)S(1)} %add.349), channel_id=1, source_target_pairs={{0,8},{2,10},{4,12},{6,14},{8,0},{10,2},{12,4},{14,6},{16,24},{18,... | collective-permute-start | bytes 147464 | tf_op jit(solution)/shard_map/ppermute | solution.py:75
  368.3 39.1 %copy-start.56 = (f32[6,48]{1,0:T(8,128)S(1)}, f32[6,48]{1,0:T(8,128)}, u32[]{:S(2)}) copy-start(f32[6,48]{1,0:T(8,128)} %param.25) | copy-start | bytes 3460
  368.3 39.0 %copy-start.57 = (f32[6,48]{1,0:T(8,128)S(1)}, f32[6,48]{1,0:T(8,128)}, u32[]{:S(2)}) copy-start(f32[6,48]{1,0:T(8,128)} %param.31) | copy-start | bytes 3460
  401.5 5.8 %collective-permute-start.57 = (f32[16,768]{1,0:T(8,128)S(1)}, f32[16,768]{1,0:T(8,128)S(1)}, u32[]{:S(2)}, u32[]{:S(2)}) collective-permute-start(f32[16,768]{1,0:T(8,128)S(1)} %add.350), channel_id=1, source_target_pairs={{0,16},{2,18},{4,20},{6,22},{8,24},{10,26},{12,28},{14,30},{16,0},... | collective-permute-start | bytes 147464 | tf_op jit(solution)/shard_map/ppermute | solution.py:75
  403.0 6.8 %collective-permute-start.60 = (bf16[48,1536]{1,0:T(8,128)(2,1)S(1)}, bf16[48,1536]{1,0:T(8,128)(2,1)S(1)}, u32[]{:S(2)}, u32[]{:S(2)}) collective-permute-start(bf16[48,1536]{1,0:T(8,128)(2,1)S(1)} %get-tuple-element.444), channel_id=1, source_target_pairs={{0,2},{2,0},{4,6},{6,4},{8,10},{10,8},{12,14},{14,12},{16,18},{18,... | collective-permute-start | bytes 442376 | tf_op jit(solution)/shard_map/ppermute | solution.py:75
  403.4 8.8 %collective-permute-start.59 = (bf16[48,1536]{1,0:T(8,128)(2,1)S(1)}, bf16[48,1536]{1,0:T(8,128)(2,1)S(1)}, u32[]{:S(2)}, u32[]{:S(2)}) collective-permute-start(bf16[48,1536]{1,0:T(8,128)(2,1)S(1)} %get-tuple-element.445), channel_id=1, source_target_pairs={{0,4},{2,6},{4,0},{6,2},{8,12},{10,14},{12,8},{14,10},{16,20},{18,... | collective-permute-start | bytes 442376 | tf_op jit(solution)/shard_map/ppermute | solution.py:75
  404.7 7.5 %collective-permute-start.58 = (bf16[48,1536]{1,0:T(8,128)(2,1)S(1)}, bf16[48,1536]{1,0:T(8,128)(2,1)S(1)}, u32[]{:S(2)}, u32[]{:S(2)}) collective-permute-start(bf16[48,1536]{1,0:T(8,128)(2,1)S(1)} %get-tuple-element.442), channel_id=1, source_target_pairs={{0,6},{2,4},{4,2},{6,0},{8,14},{10,12},{12,10},{14,8},{16,22},{18,... | collective-permute-start | bytes 442376 | tf_op jit(solution)/shard_map/ppermute | solution.py:75
  (69 other events, 352.7 us)

commit v4 on v3

--- a/solution.py
+++ b/solution.py
@@ -294,9 +294,10 @@
     total_ref,
     own_ref,
     other_ref,
-    keys_ref,
     sum_ref,
     queries_ref,
+    out_buffer,
+    sems,
 ):
     length = info[1 + pl.program_id(0)]
     query, key, value, grad = query_ref[...], key_ref[...], value_ref[...], grad_ref[...]
@@ -332,9 +333,47 @@
     query_grad = queries_ref[...]
     value_grad = value_grad.astype(jnp.bfloat16)
     early = info[0] == 0
-    own_ref[...] = jnp.where(early, query_grad, value_grad)
-    other_ref[...] = jnp.where(early, value_grad, query_grad)
-    keys_ref[...] = key_grad.astype(jnp.bfloat16)
+    pair = pl.program_id(1)
+    step = pl.program_id(0) * PAIRS + pair
+    last = pl.num_programs(0) * PAIRS - 1
+    slot = lax.rem(step, 2)
+    rows = pl.ds(pl.multiple_of(pl.program_id(0) * SEQ, SEQ), SEQ)
+
+    def copy(which, ref, block, slot):
+        cols = pl.ds(pl.multiple_of(block * PAIR, PAIR), PAIR)
+        return pltpu.make_async_copy(
+            out_buffer.at[slot, which], ref.at[rows, cols], sems.at[slot, which]
+        )
+
+    def wait(slot):
+        for which in range(3):
+            copy(which, own_ref, 0, slot).wait()
+
+    @pl.when(step >= 2)
+    def _():
+        wait(slot)
+
+    out_buffer[slot, 0] = jnp.where(early, query_grad, value_grad)
+    out_buffer[slot, 1] = jnp.where(early, value_grad, query_grad)
+    out_buffer[slot, 2] = key_grad.astype(jnp.bfloat16)
+    copy(0, own_ref, pair, slot).start()
+    copy(1, other_ref, pair, slot).start()
+    key_block = PAIRS + lax.rem(pair, PAIRS // 2)
+    mine = (pair < PAIRS // 2) == early
+
+    @pl.when(mine)
+    def _():
+        copy(2, own_ref, key_block, slot).start()
+
+    @pl.when(jnp.logical_not(mine))
+    def _():
+        copy(2, other_ref, key_block, slot).start()
+
+    @pl.when(step == last)
+    def _():
+        wait(1 - slot)
+        wait(slot)
+
     sum_ref[0, 0, 0:1, :] = jnp.sum(query_grad.astype(jnp.float32), axis=0, keepdims=True)
     sum_ref[0, 0, 1:2, :] = jnp.sum(value_grad.astype(jnp.float32), axis=0, keepdims=True)
 
@@ -376,25 +415,21 @@
 def attention_pull(info, qkv, grad, log_total, slots):
     rows = qkv.shape[0]
 
-    def key_spot(s, p, info):
-        return s, lax.rem(p + info[0] * (PAIRS // 2), PAIRS)
-
-    table = jax.ShapeDtypeStruct((rows, D), jnp.bfloat16)
+    table = jax.ShapeDtypeStruct((rows, BLOCKS // 2 * PAIR), jnp.bfloat16)
     return pl.pallas_call(
         attention_pull_kernel,
         grid_spec=pltpu.PrefetchScalarGridSpec(
             num_scalar_prefetch=1,
             grid=(slots, PAIRS),
             in_specs=[pick(kind) for kind in range(3)] + [pair_spec(), pair_rows(SEQ)],
-            out_specs=[
-                pair_spec(),
-                pair_spec(),
-                pl.BlockSpec((SEQ, PAIR), key_spot),
-                pair_rows(PAIR),
+            out_specs=[pl.BlockSpec(memory_space=pl.ANY)] * 2 + [pair_rows(PAIR)],
+            scratch_shapes=[
+                pltpu.VMEM((SEQ, PAIR), jnp.bfloat16),
+                pltpu.VMEM((2, 3, SEQ, PAIR), jnp.bfloat16),
+                pltpu.SemaphoreType.DMA((2, 3)),
             ],
-            scratch_shapes=[pltpu.VMEM((SEQ, PAIR), jnp.bfloat16)],
         ),
-        out_shape=[table] * 3 + [jax.ShapeDtypeStruct((slots, PAIRS, 2, PAIR), jnp.float32)],
+        out_shape=[table] * 2 + [jax.ShapeDtypeStruct((slots, PAIRS, 2, PAIR), jnp.float32)],
         cost_estimate=SMALL,
         name="attention_pull",
     )(info, qkv, qkv, qkv, grad, log_total)
@@ -890,26 +925,17 @@
     parts = attention_pull(info, projected, context_grad, log_total, slots)
     parts, down_sent = together(parts, down_sent)
 
-    grads = (parts[0], parts[1], parts[2][:, :narrow], parts[2][:, narrow:])
-    main_leaving = matmul_tn(tokens, grads[1]).astype(low)
-    keys_leaving = matmul_tn(tokens, grads[3]).astype(low)
-    vector_grad = vector_grads(info, low_sums, high_sums, bias_sums, parts[3])
-    main_leaving, keys_leaving, grads, vector_grad, wide_sent = together(
-        main_leaving, keys_leaving, grads, vector_grad, wide_sent
-    )
+    leaving = matmul_tn(tokens, parts[1]).astype(low)
+    qkv_leaving, parts, wide_sent, down_sent = together(leaving, parts, wide_sent, down_sent)
     wide_kept, leaving = split_near(wide_kept, wide_sent, size)
-    leaving, grads = together(leaving, grads)
+    leaving, parts = together(leaving, parts)
     wide_sent = fly_near(leaving, size)
-    main_arrived, keys_arrived = swap_cores(main_leaving), swap_cores(keys_leaving)
-    main_part, keys_part = matmul_tn(tokens, grads[0]), matmul_tn(tokens, grads[2])
+    qkv_arrived = swap_cores(qkv_leaving)
+    qkv_part = matmul_tn(tokens, parts[0])
     (grad_down,) = add_four(down_kept, [down_sent])
     moment_down = moment_decay * mom_down + grad_down
-    main_part, keys_part, main_arrived, keys_arrived, grads, moment_down = together(
-        main_part, keys_part, main_arrived, keys_arrived, grads, moment_down
-    )
-    qkv_kept, leaving = split_low(
-        [main_part + main_arrived.astype(full), keys_part + keys_arrived.astype(full)], size
-    )
+    qkv_part, qkv_arrived, grads, moment_down = together(qkv_part, qkv_arrived, parts, moment_down)
+    qkv_kept, leaving = split_low([qkv_part + qkv_arrived.astype(full)], size)
     leaving, grads, down_block = together(leaving, grads, moment_down.astype(low))
     qkv_sent = fly_low(leaving, size)
     down_sent = fly_far(down_block, size)
@@ -917,22 +943,22 @@
     wide_kept, wide_leaving = split_far(wide_kept, wide_sent, size)
     wide_sent = fly_far(wide_leaving, size)
     qkv_sent, wide_sent, down_sent = together(qkv_sent, wide_sent, down_sent)
+    qkv_kept, leaving = split_high(qkv_kept, qkv_sent, size)
+    leaving, wide_sent, down_sent = together(leaving, wide_sent, down_sent)
+    qkv_sent = fly_high(leaving, size)
     grad_up, grad_out = add_four(wide_kept, [wide_sent])
     moment_up = moment_decay * mom_up + grad_up
     moment_out = moment_decay * mom_out + grad_out
     wide_block = jnp.concatenate([moment_up.astype(low), moment_out.astype(low)], axis=1)
+    wide_sent = fly_far(wide_block, size)
+    down_pair = place_far(down_block, down_sent, size)
+    down_sent = fly_near(down_pair, size)
     mom_turned = turn(mom_qkv, narrow)
-    qkv_kept, leaving = split_high(qkv_kept, qkv_sent, size)
-    down_pair = place_far(down_block, down_sent, size)
-    leaving, down_pair, wide_block, grads, vector_grad, mom_turned = together(
-        leaving, down_pair, wide_block, grads, vector_grad, mom_turned
-    )
-    qkv_sent = fly_high(leaving, size)
-    wide_sent = fly_far(wide_block, size)
-    down_sent = fly_near(down_pair, size)
-    qkv_sent, wide_sent, down_sent = together(qkv_sent, wide_sent, down_sent)
-    grad_main, grad_keys = add_four(qkv_kept, qkv_sent)
-    grad_turned = jnp.concatenate([grad_main, grad_keys], axis=1)
+    vector_grad = vector_grads(info, low_sums, high_sums, bias_sums, grads[2])
+    qkv_sent, wide_sent, down_sent, grads, vector_grad, mom_turned = together(
+        qkv_sent, wide_sent, down_sent, grads, vector_grad, mom_turned
+    )
+    (grad_turned,) = add_four(qkv_kept, qkv_sent)
     qkv_block = (moment_decay * mom_turned + grad_turned).astype(low)
     wide_pair = place_far(wide_block, wide_sent, size)
     qkv_block, grad_turned, wide_pair = together(qkv_block, grad_turned, wide_pair)
@@ -976,11 +1002,7 @@
     vector_grad = vector_grad + vector_arrived
     vector_arrived = flip(vector_grad, 2, size)
     input_grad = (
-        skip_grad
-        + matmul_nt(grads[0], qkv_own[:, :D])
-        + matmul_nt(grads[1], qkv_other[:, :D])
-        + matmul_nt(grads[2], qkv_own[:, D:])
-        + matmul_nt(grads[3], qkv_other[:, D:])
+        skip_grad + matmul_nt(grads[0], qkv_own) + matmul_nt(grads[1], qkv_other)
     )
     pieces, input_grad, vector_grad, vector_arrived = together(
         pieces, input_grad, vector_grad, vector_arrived

time: 421 us -> 412 us (0.979)
  waiting for transfers between devices: 95.3 us -> 89.4 us
    ppermute x51, waiting for transfers between devices: 94.3 us -> 87.9 us  [flip(): lax.ppermute(by_rows(values), 'fsdp', [(i, i ^ mask) for i in range(size)])]
    add x10 -> x7, other arithmetic: 8.65 us -> 6.44 us  [add_four(): part = part + piece[..., cols].astype(jnp.float32)]
    dot_general x10 -> x8, matrix products: 28.3 us -> 26.2 us  [matmul_tn(): lax.dot_general(former, latter, (((0,), (0,)), ((), ())), preferred_eleme...]
    unnamed x140 -> x126, local copies, waits for them, and re-layouts: 13.5 us -> 11.9 us
    dot_general x7 -> x5, matrix products: 21.4 us -> 20 us  [matmul_nt(): lax.dot_general(former, latter, (((1,), (1,)), ((), ())), preferred_eleme...]
  transfers between devices with their start and end apart: 61 -> 60, of which waited for: 25 -> 29; matrix products, arithmetic and copies ran while one was open for 16% -> 17% of each run, Pallas kernels for 21% -> 22%
where the time goes in v4:
time: 412 us; the launch traced here: 406 us
  Pallas kernels  130 us (32%)
  waiting for transfers between devices  89.4 us (22%)
  starting transfers between devices  71.1 us (17%)
  matrix products  54.1 us (13%)
  other arithmetic  40.3 us (10%)
  local copies, waits for them, and re-layouts  18.5 us (4%)
    ppermute x51, waiting for transfers between devices, flip(): lax.ppermute(by_rows(values), 'fsdp', [(i, i ^ mask) for i in range(size)])  87.9 us
    ppermute x51, starting transfers between devices, flip(): lax.ppermute(by_rows(values), 'fsdp', [(i, i ^ mask) for i in range(size)])  70.3 us
    pallas_call x3, Pallas kernels, row_call(): pl.pallas_call(kernel, grid=(rows // ROWS,), in_specs=[pl.BlockSpec(memor...  50.7 us
    pallas_call x1, Pallas kernels, polar_rows(): pl.pallas_call(polar_kernel, in_specs=[pl.BlockSpec(memory_space=pltpu.SM...  33.2 us
    dot_general x8, matrix products, matmul_tn(): lax.dot_general(former, latter, (((0,), (0,)), ((), ())), preferred_eleme...  26.2 us
    pallas_call x1, Pallas kernels, attention_pull(): pl.pallas_call(attention_pull_kernel, grid_spec=pltpu.PrefetchScalarGridS...  25.9 us
    dot_general x5, matrix products, matmul_nt(): lax.dot_general(former, latter, (((1,), (1,)), ((), ())), preferred_eleme...  20 us
    pallas_call x1, Pallas kernels, attention(): pl.pallas_call(attention_kernel, grid_spec=pltpu.PrefetchScalarGridSpec(n...  16.9 us
  transfers between devices with their start and end apart: 60, of which 29 were waited for; matrix products, arithmetic and copies ran while one was open for 17% of the time, Pallas kernels for 22%

profile of v4, /device:TPU:0, one launch (start us, length us, event | category | flops | bytes accessed | tf_op | source)
XLA Modules:
  0.0 405.6 jit_solution(1554675907201672182)
XLA Ops:
  2.6 3.1 collective-permute-start.3
  8.6 3.0 collective-permute-start.1
  13.6 2.3 collective-permute-done
  16.0 4.7 %collective-permute-done.2 = bf16[48,1280]{1,0:T(8,128)(2,1)S(1)} collective-permute-done((bf16[48,1280]{1,0:T(8,128)(2,1)S(1)}, bf16[48,1280]{1,0:T(8,128)(2,1)S(1)}, u32[]{:S(2)}, u32[]{:S(2)}) %collective-permute-start.2) | collective-permute-done | bytes 122912 | tf_op jit(solution)/shard_map/ppermute | solution.py:75
  20.8 1.6 collective-permute-start.4
  22.4 1.5 collective-permute-start.5
  24.4 4.3 %collective-permute-start.7 = (bf16[48,1920]{1,0:T(8,128)(2,1)S(1)}, bf16[48,1920]{1,0:T(8,128)(2,1)S(1)}, u32[]{:S(2)}, u32[]{:S(2)}) collective-permute-start(bf16[48,1920]{1,0:T(8,128)(2,1)S(1)} %pad_maximum_fusion.5), channel_id=1, source_target_pairs={{0,16},{2,18},{4,20},{6,22},{8,24},{10,26},{12,28},{14,30},{16,0},... | collective-permute-start | bytes 552968 | tf_op jit(solution)/shard_map/ppermute | solution.py:75
  29.2 11.2 %collective-permute-done.7 = bf16[48,1920]{1,0:T(8,128)(2,1)S(1)} collective-permute-done((bf16[48,1920]{1,0:T(8,128)(2,1)S(1)}, bf16[48,1920]{1,0:T(8,128)(2,1)S(1)}, u32[]{:S(2)}, u32[]{:S(2)}) %collective-permute-start.7) | collective-permute-done | bytes 184352 | tf_op jit(solution)/shard_map/ppermute | solution.py:75
  40.3 3.7 collective-permute-done.5
  50.1 3.7 collective-permute-start.10
  53.8 1.9 vector_tables.1
  57.3 4.3 %fusion.2 = bf16[1024,1152]{1,0:T(8,128)(2,1)S(1)} fusion(f32[1152]{0:T(1024)S(1)} %slice_reduce_fusion.1, bf16[1024,768]{1,0:T(8,128)(2,1)} %x_ref.1, bf16[768,1280]{1,0:T(8,128)(2,1)} %bitcast.280), kind=kOutput, calls=%fused_computation.15 | convolution fusion | flops 1814298624 | bytes 5706240 | tf_op jit(solution)/shard_map/dot_general | solution.py:55
  61.6 3.7 fusion
  65.3 2.5 pad_maximum_fusion.query_ref.key_ref.value_ref
  69.2 1.5 collective-permute-start.15
  70.7 16.9 %attention.1 = (bf16[1024,768]{1,0:T(8,128)(2,1)}, f32[2,6,2,512]{3,2,1,0:T(2,128)}) custom-call(s32[23]{0:T(128)} %pad_add_fusion.info, bf16[1024,2304]{1,0:T(8,128)(2,1)} %pad_maximum_fusion.query_ref.key_ref.value_ref, bf16[1024,2304]{1,0:T(8,128)(2,1)} %pad_maximum_fusion.query_ref.key_ref.value_ref, ...), custom_call_target="tpu_custom_call" | custom-call | flops 1048576 | bytes 65536 | tf_op jit(solution)/shard_map/attention/pallas_call | solution.py:398
  87.9 2.0 maximum_select_fusion.4
  90.9 1.5 maximum_select_fusion.23
  96.2 1.6 copy-done.12
  97.8 21.6 %raise_rows.1 = (f32[1024,768]{1,0:T(8,128)}, f32[1024,128]{1,0:T(8,128)S(1)}, bf16[1024,768]{1,0:T(8,128)(2,1)}, bf16[1024,1536]{1,0:T(8,128)(2,1)}, bf16[1024,...) custom-call(s32[23]{0:T(128)S(1)} %copy-done.6, f32[16,768]{1,0:T(8,128)S(1)} %copy-done.3, f32[8,3072]{1,0:T(8,128)S(1)} %copy-done.4, ...), custom_call_target="tpu_custom_call" | custom-call | flops 1048576 | bytes 65536 | tf_op jit(solution)/shard_map/raise_rows/pallas_call | solution.py:632
  119.8 1.6 collective-permute-done.19
  122.6 2.4 copy-done.17
  125.0 4.3 %fusion.68.first_ref = f32[1024,768]{1,0:T(8,128)} fusion(bf16[1024,1536]{1,0:T(8,128)(2,1)S(1)} %copy-done.17, bf16[768,1536]{1,0:T(8,128)(2,1)S(1)} %bitcast.274), kind=kOutput, calls=%fused_computation.181 | convolution fusion | flops 2415919104 | bytes 8650752 | tf_op jit(solution)/shard_map/dot_general | solution.py:65
  129.4 4.3 %fusion.69.second_ref = f32[1024,768]{1,0:T(8,128)} fusion(bf16[1024,1536]{1,0:T(8,128)(2,1)S(1)} %copy-done.57, bf16[768,1536]{1,0:T(8,128)(2,1)S(1)} %collective-permute-done.20.other), kind=kOutput, calls=%fused_computation.182 | convolution fusion | flops 2415919104 | bytes 8650752 | tf_op jit(solution)/shard_map/dot_general | solution.py:65
  133.7 7.7 %lower_rows.1 = (bf16[1024,768]{1,0:T(8,128)(2,1)}, f32[1024,768]{1,0:T(8,128)}, bf16[1024,768]{1,0:T(8,128)(2,1)S(1)}, f32[8,768]{1,0:T(8,128)S(1)}) custom-call(s32[23]{0:T(128)S(1)} %copy-done.6, f32[16,768]{1,0:T(8,128)S(1)} %copy-done.3, f32[1024,768]{1,0:T(8,128)} %get-tuple-element.227.xhat_ref, f32[1024,768]{1,0:T(8,128)} %fusion.68.first_ref, ...), custom_call_target="tpu_custom_call" | custom-call | flops 1048576 | bytes 65536 | tf_op jit(solution)/shard_map/lower_rows/pallas_call | solution.py:632
  141.4 4.2 %convolution_convert_fusion.1 = bf16[768,1536]{1,0:T(8,128)(2,1)} fusion(bf16[1024,768]{1,0:T(8,128)(2,1)S(1)} %get-tuple-element.253.low_ref, bf16[1024,1536]{1,0:T(8,128)(2,1)S(1)} %copy-done.57), kind=kOutput, calls=%fused_computation.9 | convolution fusion | flops 2417098752 | bytes 7077888 | tf_op jit(solution)/shard_map/dot_general | solution.py:59
  145.6 4.6 %fusion.70 = f32[768,1536]{1,0:T(8,128)S(1)} fusion(bf16[1024,768]{1,0:T(8,128)(2,1)S(1)} %get-tuple-element.253.low_ref, bf16[1024,1536]{1,0:T(8,128)(2,1)} %get-tuple-element.234), kind=kOutput, calls=%fused_computation.183 | convolution fusion | flops 2415919104 | bytes 9437184 | tf_op jit(solution)/shard_map/dot_general | solution.py:59
  150.5 2.5 convert_add_fusion.1
  153.0 2.1 copy-done.11
  159.6 21.4 %pull_rows.1 = (bf16[1024,1536]{1,0:T(8,128)(2,1)}, bf16[1024,1536]{1,0:T(8,128)(2,1)}, f32[1024,768]{1,0:T(8,128)}, bf16[1024,768]{1,0:T(8,128)(2,1)}, bf16[102...) custom-call(s32[23]{0:T(128)S(1)} %copy-done.6, f32[16,768]{1,0:T(8,128)S(1)} %copy-done.3, ...), custom_call_target="tpu_custom_call" | custom-call | flops 1048576 | bytes 65536 | tf_op jit(solution)/shard_map/pull_rows/pallas_call | solution.py:632
  181.1 2.7 collective-permute-done.23
  184.8 1.8 fusion.17
  187.5 4.3 %convolution_convert_fusion = bf16[768,1536]{1,0:T(8,128)(2,1)} fusion(bf16[1024,768]{1,0:T(8,128)(2,1)S(1)} %copy-done.29, bf16[1024,1536]{1,0:T(8,128)(2,1)S(1)} %copy-done.58), kind=kOutput, calls=%fused_computation.8 | convolution fusion | flops 2417098752 | bytes 7077888 | tf_op jit(solution)/shard_map/dot_general | solution.py:59
  191.8 3.1 collective-permute-done.25
  195.7 3.0 convolution_convert_fusion.3
  203.2 2.7 fusion.71
  214.5 2.0 collective-permute-start.28
  216.4 25.9 %attention_pull.1 = (bf16[1024,1152]{1,0:T(8,128)(2,1)}, bf16[1024,1152]{1,0:T(8,128)(2,1)}, f32[2,6,2,128]{3,2,1,0:T(2,128)}) custom-call(s32[23]{0:T(128)} %pad_add_fusion.info, bf16[1024,2304]{1,0:T(8,128)(2,1)} %pad_maximum_fusion.query_ref.key_ref.value_ref, bf16[1024,2304]{1,0:T(8,128)(2,1)} %pad_maximum_fusion.query_ref.key_ref.value_ref, ...), custom_call_target="tpu_custom_call" | custom-call | flops 1048576 | bytes 65536 | tf_op jit(solution)/shard_map/attention_pull/pallas_call | solution.py:419
  242.4 3.9 fusion.1
  246.7 1.9 fusion.15
  250.7 1.7 multiply_add_fusion.1
  252.3 2.4 convolution_bitcast_fusion
  256.3 2.3 collective-permute-start.37
  260.4 1.7 collective-permute-start.35
  263.4 3.0 collective-permute-done.37
  269.5 1.6 vector_grads.1
  271.1 8.7 %collective-permute-done.38 = bf16[48,1920]{1,0:T(8,128)(2,1)} collective-permute-done((bf16[48,1920]{1,0:T(8,128)(2,1)}, bf16[48,1920]{1,0:T(8,128)(2,1)}, u32[]{:S(2)}, u32[]{:S(2)}) %collective-permute-start.38) | collective-permute-done | bytes 184352 | tf_op jit(solution)/shard_map/ppermute | solution.py:75
  283.4 1.6 collective-permute-start.40
  285.1 1.6 collective-permute-start.41
  288.1 1.8 fusion.66
  290.4 2.6 collective-permute-start.42
  293.6 9.3 %collective-permute-done.42 = bf16[48,1920]{1,0:T(8,128)(2,1)S(1)} collective-permute-done((bf16[48,1920]{1,0:T(8,128)(2,1)S(1)}, bf16[48,1920]{1,0:T(8,128)(2,1)S(1)}, u32[]{:S(2)}, u32[]{:S(2)}) %collective-permute-start.42) | collective-permute-done | bytes 184352 | tf_op jit(solution)/shard_map/ppermute | solution.py:75
  303.3 2.5 collective-permute-start.45
  305.8 1.8 collective-permute-start.46
  310.4 2.9 collective-permute-done.45
  313.9 5.6 %collective-permute-done.47 = bf16[2,48,1920]{2,1,0:T(8,128)(2,1)S(1)} collective-permute-done((bf16[2,48,1920]{2,1,0:T(8,128)(2,1)S(1)}, bf16[2,48,1920]{2,1,0:T(8,128)(2,1)S(1)}, u32[]{:S(2)}, u32[]{:S(2)}) %collective-permute-start.47) | collective-permute-done | bytes 368672 | tf_op jit(solution)/shard_map/ppermute | solution.py:75
  324.3 2.2 fusion.6
  326.5 1.6 collective-permute-start.53
  328.1 5.7 %add_add_fusion = f32[1024,768]{1,0:T(8,128)} fusion(f32[1024,768]{1,0:T(8,128)S(1)} %copy-done.56, f32[1024,768]{1,0:T(8,128)S(1)} %fusion.6, bf16[1024,1152]{1,0:T(8,128)(2,1)S(1)} %copy-done.59, bf16[768,1280]{1,0:T(8,128)(2,1)} %collective-permute-done.9.other_ref), kind=kOutput, calls=%fused_computation.12 | convolution fusion | flops 1813512192 | bytes 13565952 | tf_op jit(solution)/shard_map/dot_general | solution.py:65
  333.7 15.5 %collective-permute-done.53 = f32[16,768]{1,0:T(8,128)S(1)} collective-permute-done((f32[16,768]{1,0:T(8,128)S(1)}, f32[16,768]{1,0:T(8,128)S(1)}, u32[]{:S(2)}, u32[]{:S(2)}) %collective-permute-start.53) | collective-permute-done | bytes 49184 | tf_op jit(solution)/shard_map/ppermute | solution.py:75
  350.2 3.4 fusion.72.own_ref
  355.1 2.7 collective-permute-done.55
  358.6 33.2 %polar_rows.1 = bf16[192,1536]{1,0:T(8,128)(2,1)S(1)} custom-call(s32[1]{0:T(128)} %bitcast.93.start_ref, f32[768,768]{1,0:T(8,128)} %fusion.72.own_ref, f32[768,768]{1,0:T(8,128)} %collective-permute-done.54.other_ref, bf16[768,1536]{1,0:T(8,128)(2,1)S(1)} %bitcast.264), custom_call_target="tpu_custom_call" | custom-call | tf_op jit(solution)/shard_map/polar_rows/pallas_call | solution.py:784
  399.9 1.5 collective-permute-done.58
  (317 shorter events, 83.0 us)
Async XLA Ops:
  0.7 44.3 %copy-start = (s32[1,2]{1,0:T(1,128)S(1)}, s32[1,2]{1,0:T(1,128)}, u32[]{:S(2)}) copy-start(s32[1,2]{1,0:T(1,128)} %param.19) | copy-start | bytes 28
  2.6 18.1 %collective-permute-start.3 = (bf16[48,1920]{1,0:T(8,128)(2,1)S(1)}, bf16[48,1920]{1,0:T(8,128)(2,1)S(1)}, u32[]{:S(2)}, u32[]{:S(2)}) collective-permute-start(bf16[48,1920]{1,0:T(8,128)(2,1)S(1)} %pad_maximum_fusion.5), channel_id=1, source_target_pairs={{0,8},{2,10},{4,12},{6,14},{8,0},{10,2},{12,4},{14,6},{16,24},{18,... | collective-permute-start | bytes 552968 | tf_op jit(solution)/shard_map/ppermute | solution.py:75
  8.5 7.5 %collective-permute-start = (bf16[48,1280]{1,0:T(8,128)(2,1)S(1)}, bf16[48,1280]{1,0:T(8,128)(2,1)S(1)}, u32[]{:S(2)}, u32[]{:S(2)}) collective-permute-start(bf16[48,1280]{1,0:T(8,128)(2,1)S(1)} %fusion.56), channel_id=1, source_target_pairs={{0,8},{2,10},{4,12},{6,14},{8,0},{10,2},{12,4},{14,6},{16,24},{18,... | collective-permute-start | bytes 368648 | tf_op jit(solution)/shard_map/ppermute | solution.py:75
  8.6 7.4 %collective-permute-start.1 = (bf16[48,1280]{1,0:T(8,128)(2,1)S(1)}, bf16[48,1280]{1,0:T(8,128)(2,1)S(1)}, u32[]{:S(2)}, u32[]{:S(2)}) collective-permute-start(bf16[48,1280]{1,0:T(8,128)(2,1)S(1)} %fusion.56), channel_id=1, source_target_pairs={{0,16},{2,18},{4,20},{6,22},{8,24},{10,26},{12,28},{14,30},{16,0},... | collective-permute-start | bytes 368648 | tf_op jit(solution)/shard_map/ppermute | solution.py:75
  11.6 9.1 %collective-permute-start.2 = (bf16[48,1280]{1,0:T(8,128)(2,1)S(1)}, bf16[48,1280]{1,0:T(8,128)(2,1)S(1)}, u32[]{:S(2)}, u32[]{:S(2)}) collective-permute-start(bf16[48,1280]{1,0:T(8,128)(2,1)S(1)} %fusion.56), channel_id=1, source_target_pairs={{0,24},{2,26},{4,28},{6,30},{8,16},{10,18},{12,20},{14,22},{16,8},... | collective-permute-start | bytes 368648 | tf_op jit(solution)/shard_map/ppermute | solution.py:75
  20.8 19.5 %collective-permute-start.4 = (bf16[4,48,1280]{2,1,0:T(8,128)(2,1)S(1)}, bf16[4,48,1280]{2,1,0:T(8,128)(2,1)S(1)}, u32[]{:S(2)}, u32[]{:S(2)}) collective-permute-start(bf16[4,48,1280]{2,1,0:T(8,128)(2,1)S(1)} %maximum_select_fusion.17), channel_id=1, source_target_pairs={{0,2},{2,0},{4,6},{6,4},{8,10},{10,8},{12,14},{14,12},{16,18},{18,... | collective-permute-start | bytes 1474568 | tf_op jit(solution)/shard_map/ppermute | solution.py:75
  22.4 21.6 %collective-permute-start.5 = (bf16[4,48,1280]{2,1,0:T(8,128)(2,1)S(1)}, bf16[4,48,1280]{2,1,0:T(8,128)(2,1)S(1)}, u32[]{:S(2)}, u32[]{:S(2)}) collective-permute-start(bf16[4,48,1280]{2,1,0:T(8,128)(2,1)S(1)} %maximum_select_fusion.17), channel_id=1, source_target_pairs={{0,4},{2,6},{4,0},{6,2},{8,12},{10,14},{12,8},{14,10},{16,20},{18,... | collective-permute-start | bytes 1474568 | tf_op jit(solution)/shard_map/ppermute | solution.py:75
  24.0 20.1 %collective-permute-start.6 = (bf16[4,48,1280]{2,1,0:T(8,128)(2,1)S(1)}, bf16[4,48,1280]{2,1,0:T(8,128)(2,1)S(1)}, u32[]{:S(2)}, u32[]{:S(2)}) collective-permute-start(bf16[4,48,1280]{2,1,0:T(8,128)(2,1)S(1)} %maximum_select_fusion.17), channel_id=1, source_target_pairs={{0,6},{2,4},{4,2},{6,0},{8,14},{10,12},{12,10},{14,8},{16,22},{18,... | collective-permute-start | bytes 1474568 | tf_op jit(solution)/shard_map/ppermute | solution.py:75
  24.4 15.9 %collective-permute-start.7 = (bf16[48,1920]{1,0:T(8,128)(2,1)S(1)}, bf16[48,1920]{1,0:T(8,128)(2,1)S(1)}, u32[]{:S(2)}, u32[]{:S(2)}) collective-permute-start(bf16[48,1920]{1,0:T(8,128)(2,1)S(1)} %pad_maximum_fusion.5), channel_id=1, source_target_pairs={{0,16},{2,18},{4,20},{6,22},{8,24},{10,26},{12,28},{14,30},{16,0},... | collective-permute-start | bytes 552968 | tf_op jit(solution)/shard_map/ppermute | solution.py:75
  28.7 11.6 %collective-permute-start.8 = (bf16[48,1920]{1,0:T(8,128)(2,1)S(1)}, bf16[48,1920]{1,0:T(8,128)(2,1)S(1)}, u32[]{:S(2)}, u32[]{:S(2)}) collective-permute-start(bf16[48,1920]{1,0:T(8,128)(2,1)S(1)} %pad_maximum_fusion.5), channel_id=1, source_target_pairs={{0,24},{2,26},{4,28},{6,30},{8,16},{10,18},{12,20},{14,22},{16,8},... | collective-permute-start | bytes 552968 | tf_op jit(solution)/shard_map/ppermute | solution.py:75
  44.9 8.9 %collective-permute-start.9 = (bf16[768,1280]{1,0:T(8,128)(2,1)S(1)}, bf16[768,1280]{1,0:T(8,128)(2,1)}, u32[]{:S(2)}, u32[]{:S(2)}) collective-permute-start(bf16[768,1280]{1,0:T(8,128)(2,1)S(1)} %bitcast.278), channel_id=1, source_target_pairs={{0,1},{1,0},{2,3},{3,2},{4,5},{5,4},{6,7},{7,6},{8,9},{9,8},{10,11... | collective-permute-start | bytes 5898248 | tf_op jit(solution)/shard_map/ppermute | solution.py:79
  46.6 41.1 %collective-permute-start.11 = (bf16[4,48,1920]{2,1,0:T(8,128)(2,1)S(1)}, bf16[4,48,1920]{2,1,0:T(8,128)(2,1)S(1)}, u32[]{:S(2)}, u32[]{:S(2)}) collective-permute-start(bf16[4,48,1920]{2,1,0:T(8,128)(2,1)S(1)} %maximum_select_fusion.12), channel_id=1, source_target_pairs={{0,2},{2,0},{4,6},{6,4},{8,10},{10,8},{12,14},{14,12},{16,18},{18,... | collective-permute-start | bytes 2211848 | tf_op jit(solution)/shard_map/ppermute | solution.py:75
  47.9 39.8 %collective-permute-start.12 = (bf16[4,48,1920]{2,1,0:T(8,128)(2,1)S(1)}, bf16[4,48,1920]{2,1,0:T(8,128)(2,1)}, u32[]{:S(2)}, u32[]{:S(2)}) collective-permute-start(bf16[4,48,1920]{2,1,0:T(8,128)(2,1)S(1)} %maximum_select_fusion.12), channel_id=1, source_target_pairs={{0,4},{2,6},{4,0},{6,2},{8,12},{10,14},{12,8},{14,10},{16,20},{18,... | collective-permute-start | bytes 2211848 | tf_op jit(solution)/shard_map/ppermute | solution.py:75
  48.7 38.9 %collective-permute-start.13 = (bf16[4,48,1920]{2,1,0:T(8,128)(2,1)S(1)}, bf16[4,48,1920]{2,1,0:T(8,128)(2,1)}, u32[]{:S(2)}, u32[]{:S(2)}) collective-permute-start(bf16[4,48,1920]{2,1,0:T(8,128)(2,1)S(1)} %maximum_select_fusion.12), channel_id=1, source_target_pairs={{0,6},{2,4},{4,2},{6,0},{8,14},{10,12},{12,10},{14,8},{16,22},{18,... | collective-permute-start | bytes 2211848 | tf_op jit(solution)/shard_map/ppermute | solution.py:75
  50.1 17.7 %collective-permute-start.10 = (bf16[48,1536]{1,0:T(8,128)(2,1)}, bf16[48,1536]{1,0:T(8,128)(2,1)}, u32[]{:S(2)}, u32[]{:S(2)}) collective-permute-start(bf16[48,1536]{1,0:T(8,128)(2,1)} %convert_element_type.276), channel_id=1, source_target_pairs={{0,8},{2,10},{4,12},{6,14},{8,0},{10,2},{12,4},{14,6},{16,24},{18,... | collective-permute-start | bytes 442376 | tf_op jit(solution)/shard_map/ppermute | solution.py:75
  67.8 19.8 %collective-permute-start.14 = (bf16[48,1536]{1,0:T(8,128)(2,1)S(1)}, bf16[48,1536]{1,0:T(8,128)(2,1)S(1)}, u32[]{:S(2)}, u32[]{:S(2)}) collective-permute-start(bf16[48,1536]{1,0:T(8,128)(2,1)S(1)} %copy-done.38), channel_id=1, source_target_pairs={{0,16},{2,18},{4,20},{6,22},{8,24},{10,26},{12,28},{14,30},{16,0},... | collective-permute-start | bytes 442376 | tf_op jit(solution)/shard_map/ppermute | solution.py:75
  69.2 18.4 %collective-permute-start.15 = (bf16[48,1536]{1,0:T(8,128)(2,1)S(1)}, bf16[48,1536]{1,0:T(8,128)(2,1)S(1)}, u32[]{:S(2)}, u32[]{:S(2)}) collective-permute-start(bf16[48,1536]{1,0:T(8,128)(2,1)S(1)} %copy-done.38), channel_id=1, source_target_pairs={{0,24},{2,26},{4,28},{6,30},{8,16},{10,18},{12,20},{14,22},{16,8},... | collective-permute-start | bytes 442376 | tf_op jit(solution)/shard_map/ppermute | solution.py:75
  90.8 5.4 %collective-permute-start.16 = (bf16[768,1920]{1,0:T(8,128)(2,1)S(1)}, bf16[768,1920]{1,0:T(8,128)(2,1)S(1)}, u32[]{:S(2)}, u32[]{:S(2)}) collective-permute-start(bf16[768,1920]{1,0:T(8,128)(2,1)S(1)} %bitcast.266), channel_id=1, source_target_pairs={{0,1},{1,0},{2,3},{3,2},{4,5},{5,4},{6,7},{7,6},{8,9},{9,8},{10,11... | collective-permute-start | bytes 8847368 | tf_op jit(solution)/shard_map/ppermute | solution.py:79
  92.5 26.8 %collective-permute-start.17 = (bf16[4,48,1536]{2,1,0:T(8,128)(2,1)S(1)}, bf16[4,48,1536]{2,1,0:T(8,128)(2,1)S(1)}, u32[]{:S(2)}, u32[]{:S(2)}) collective-permute-start(bf16[4,48,1536]{2,1,0:T(8,128)(2,1)S(1)} %maximum_select_fusion.14), channel_id=1, source_target_pairs={{0,2},{2,0},{4,6},{6,4},{8,10},{10,8},{12,14},{14,12},{16,18},{18,... | collective-permute-start | bytes 1769480 | tf_op jit(solution)/shard_map/ppermute | solution.py:75
  93.9 25.9 %collective-permute-start.18 = (bf16[4,48,1536]{2,1,0:T(8,128)(2,1)S(1)}, bf16[4,48,1536]{2,1,0:T(8,128)(2,1)S(1)}, u32[]{:S(2)}, u32[]{:S(2)}) collective-permute-start(bf16[4,48,1536]{2,1,0:T(8,128)(2,1)S(1)} %maximum_select_fusion.14), channel_id=1, source_target_pairs={{0,4},{2,6},{4,0},{6,2},{8,12},{10,14},{12,8},{14,10},{16,20},{18,... | collective-permute-start | bytes 1769480 | tf_op jit(solution)/shard_map/ppermute | solution.py:75
  94.7 26.8 %collective-permute-start.19 = (bf16[4,48,1536]{2,1,0:T(8,128)(2,1)S(1)}, bf16[4,48,1536]{2,1,0:T(8,128)(2,1)S(1)}, u32[]{:S(2)}, u32[]{:S(2)}) collective-permute-start(bf16[4,48,1536]{2,1,0:T(8,128)(2,1)S(1)} %maximum_select_fusion.14), channel_id=1, source_target_pairs={{0,6},{2,4},{4,2},{6,0},{8,14},{10,12},{12,10},{14,8},{16,22},{18,... | collective-permute-start | bytes 1769480 | tf_op jit(solution)/shard_map/ppermute | solution.py:75
  122.5 6.9 %collective-permute-start.20 = (bf16[768,1536]{1,0:T(8,128)(2,1)S(1)}, bf16[768,1536]{1,0:T(8,128)(2,1)S(1)}, u32[]{:S(2)}, u32[]{:S(2)}) collective-permute-start(bf16[768,1536]{1,0:T(8,128)(2,1)S(1)} %bitcast.273), channel_id=1, source_target_pairs={{0,1},{1,0},{2,3},{3,2},{4,5},{5,4},{6,7},{7,6},{8,9},{9,8},{10,11... | collective-permute-start | bytes 7077896 | tf_op jit(solution)/shard_map/ppermute | solution.py:79
  145.6 4.9 %collective-permute-start.21 = (bf16[768,1536]{1,0:T(8,128)(2,1)}, bf16[768,1536]{1,0:T(8,128)(2,1)}, u32[]{:S(2)}, u32[]{:S(2)}) collective-permute-start(bf16[768,1536]{1,0:T(8,128)(2,1)} %convolution_convert_fusion.1), channel_id=1, source_target_pairs={{0,1},{1,0},{2,3},{3,2},{4,5},{5,4},{6,7},{7,6},{8,9},{9,8},{10,11... | collective-permute-start | bytes 7077896 | tf_op jit(solution)/shard_map/ppermute | solution.py:79
  156.2 24.9 %collective-permute-start.22 = (bf16[4,48,1536]{2,1,0:T(8,128)(2,1)}, bf16[4,48,1536]{2,1,0:T(8,128)(2,1)S(1)}, u32[]{:S(2)}, u32[]{:S(2)}) collective-permute-start(bf16[4,48,1536]{2,1,0:T(8,128)(2,1)} %get-tuple-element.261), channel_id=1, source_target_pairs={{0,2},{2,0},{4,6},{6,4},{8,10},{10,8},{12,14},{14,12},{16,18},{18,... | collective-permute-start | bytes 1769480 | tf_op jit(solution)/shard_map/ppermute | solution.py:75
  156.9 26.9 %collective-permute-start.23 = (bf16[4,48,1536]{2,1,0:T(8,128)(2,1)S(1)}, bf16[4,48,1536]{2,1,0:T(8,128)(2,1)S(1)}, u32[]{:S(2)}, u32[]{:S(2)}) collective-permute-start(bf16[4,48,1536]{2,1,0:T(8,128)(2,1)S(1)} %get-tuple-element.262), channel_id=1, source_target_pairs={{0,4},{2,6},{4,0},{6,2},{8,12},{10,14},{12,8},{14,10},{16,20},{18,... | collective-permute-start | bytes 1769480 | tf_op jit(solution)/shard_map/ppermute | solution.py:75
  158.5 26.3 %collective-permute-start.24 = (bf16[4,48,1536]{2,1,0:T(8,128)(2,1)S(1)}, bf16[4,48,1536]{2,1,0:T(8,128)(2,1)S(1)}, u32[]{:S(2)}, u32[]{:S(2)}) collective-permute-start(bf16[4,48,1536]{2,1,0:T(8,128)(2,1)S(1)} %get-tuple-element.263), channel_id=1, source_target_pairs={{0,6},{2,4},{4,2},{6,0},{8,14},{10,12},{12,10},{14,8},{16,22},{18,... | collective-permute-start | bytes 1769480 | tf_op jit(solution)/shard_map/ppermute | solution.py:75
  186.6 8.4 %collective-permute-start.25 = (bf16[2,48,1536]{2,1,0:T(8,128)(2,1)S(1)}, bf16[2,48,1536]{2,1,0:T(8,128)(2,1)S(1)}, u32[]{:S(2)}, u32[]{:S(2)}) collective-permute-start(bf16[2,48,1536]{2,1,0:T(8,128)(2,1)S(1)} %fusion.42), channel_id=1, source_target_pairs={{0,8},{2,10},{4,12},{6,14},{8,0},{10,2},{12,4},{14,6},{16,24},{18,... | collective-permute-start | bytes 884744 | tf_op jit(solution)/shard_map/ppermute | solution.py:75
  195.7 10.2 %collective-permute-start.26 = (bf16[768,1536]{1,0:T(8,128)(2,1)}, bf16[768,1536]{1,0:T(8,128)(2,1)S(1)}, u32[]{:S(2)}, u32[]{:S(2)}) collective-permute-start(bf16[768,1536]{1,0:T(8,128)(2,1)} %convolution_convert_fusion), channel_id=1, source_target_pairs={{0,1},{1,0},{2,3},{3,2},{4,5},{5,4},{6,7},{7,6},{8,9},{9,8},{10,11... | collective-permute-start | bytes 7077896 | tf_op jit(solution)/shard_map/ppermute | solution.py:79
  198.7 7.1 %collective-permute-start.27 = (bf16[768,384]{1,0:T(8,128)(2,1)S(1)}, bf16[768,384]{1,0:T(8,128)(2,1)S(1)}, u32[]{:S(2)}, u32[]{:S(2)}) collective-permute-start(bf16[768,384]{1,0:T(8,128)(2,1)S(1)} %convolution_convert_fusion.3), channel_id=1, source_target_pairs={{0,1},{1,0},{2,3},{3,2},{4,5},{5,4},{6,7},{7,6},{8,9},{9,8},{10,11... | collective-permute-start | bytes 1769480 | tf_op jit(solution)/shard_map/ppermute | solution.py:79
  211.0 35.4 %collective-permute-start.29 = (bf16[4,48,1920]{2,1,0:T(8,128)(2,1)}, bf16[4,48,1920]{2,1,0:T(8,128)(2,1)S(1)}, u32[]{:S(2)}, u32[]{:S(2)}) collective-permute-start(bf16[4,48,1920]{2,1,0:T(8,128)(2,1)} %pad_maximum_fusion.1), channel_id=1, source_target_pairs={{0,2},{2,0},{4,6},{6,4},{8,10},{10,8},{12,14},{14,12},{16,18},{18,... | collective-permute-start | bytes 2211848 | tf_op jit(solution)/shard_map/ppermute | solution.py:75
  212.5 34.2 %collective-permute-start.30 = (bf16[4,48,1920]{2,1,0:T(8,128)(2,1)}, bf16[4,48,1920]{2,1,0:T(8,128)(2,1)}, u32[]{:S(2)}, u32[]{:S(2)}) collective-permute-start(bf16[4,48,1920]{2,1,0:T(8,128)(2,1)} %pad_maximum_fusion.2), channel_id=1, source_target_pairs={{0,4},{2,6},{4,0},{6,2},{8,12},{10,14},{12,8},{14,10},{16,20},{18,... | collective-permute-start | bytes 2211848 | tf_op jit(solution)/shard_map/ppermute | solution.py:75
  213.0 33.7 %collective-permute-start.31 = (bf16[4,48,1920]{2,1,0:T(8,128)(2,1)}, bf16[4,48,1920]{2,1,0:T(8,128)(2,1)}, u32[]{:S(2)}, u32[]{:S(2)}) collective-permute-start(bf16[4,48,1920]{2,1,0:T(8,128)(2,1)} %pad_maximum_fusion.3), channel_id=1, source_target_pairs={{0,6},{2,4},{4,2},{6,0},{8,14},{10,12},{12,10},{14,8},{16,22},{18,... | collective-permute-start | bytes 2211848 | tf_op jit(solution)/shard_map/ppermute | solution.py:75
  214.5 27.9 %collective-permute-start.28 = (bf16[48,1536]{1,0:T(8,128)(2,1)}, bf16[48,1536]{1,0:T(8,128)(2,1)}, u32[]{:S(2)}, u32[]{:S(2)}) collective-permute-start(bf16[48,1536]{1,0:T(8,128)(2,1)} %fusion.51), channel_id=1, source_target_pairs={{0,16},{2,18},{4,20},{6,22},{8,24},{10,26},{12,28},{14,30},{16,0},... | collective-permute-start | bytes 442376 | tf_op jit(solution)/shard_map/ppermute | solution.py:75
  246.7 8.1 %collective-permute-start.32 = (bf16[768,1152]{1,0:T(8,128)(2,1)S(1)}, bf16[768,1152]{1,0:T(8,128)(2,1)S(1)}, u32[]{:S(2)}, u32[]{:S(2)}) collective-permute-start(bf16[768,1152]{1,0:T(8,128)(2,1)S(1)} %fusion.1), channel_id=1, source_target_pairs={{0,1},{1,0},{2,3},{3,2},{4,5},{5,4},{6,7},{7,6},{8,9},{9,8},{10,11... | collective-permute-start | bytes 5308424 | tf_op jit(solution)/shard_map/ppermute | solution.py:79
  249.9 13.5 %collective-permute-start.36 = (bf16[2,48,1920]{2,1,0:T(8,128)(2,1)S(1)}, bf16[2,48,1920]{2,1,0:T(8,128)(2,1)S(1)}, u32[]{:S(2)}, u32[]{:S(2)}) collective-permute-start(bf16[2,48,1920]{2,1,0:T(8,128)(2,1)S(1)} %pad_maximum_fusion.4), channel_id=1, source_target_pairs={{0,8},{2,10},{4,12},{6,14},{8,0},{10,2},{12,4},{14,6},{16,24},{18,... | collective-permute-start | bytes 1105928 | tf_op jit(solution)/shard_map/ppermute | solution.py:75
  256.3 10.1 %collective-permute-start.37 = (bf16[48,1536]{1,0:T(8,128)(2,1)S(1)}, bf16[48,1536]{1,0:T(8,128)(2,1)S(1)}, u32[]{:S(2)}, u32[]{:S(2)}) collective-permute-start(bf16[48,1536]{1,0:T(8,128)(2,1)S(1)} %convert_element_type.333), channel_id=1, source_target_pairs={{0,16},{2,18},{4,20},{6,22},{8,24},{10,26},{12,28},{14,30},{16,0},... | collective-permute-start | bytes 442376 | tf_op jit(solution)/shard_map/ppermute | solution.py:75
  258.6 21.2 %collective-permute-start.33 = (bf16[4,48,1152]{2,1,0:T(8,128)(2,1)}, bf16[4,48,1152]{2,1,0:T(8,128)(2,1)}, u32[]{:S(2)}, u32[]{:S(2)}) collective-permute-start(bf16[4,48,1152]{2,1,0:T(8,128)(2,1)} %get-tuple-element.313), channel_id=1, source_target_pairs={{0,2},{2,0},{4,6},{6,4},{8,10},{10,8},{12,14},{14,12},{16,18},{18,... | collective-permute-start | bytes 1327112 | tf_op jit(solution)/shard_map/ppermute | solution.py:75
  259.1 21.5 %collective-permute-start.34 = (bf16[4,48,1152]{2,1,0:T(8,128)(2,1)}, bf16[4,48,1152]{2,1,0:T(8,128)(2,1)}, u32[]{:S(2)}, u32[]{:S(2)}) collective-permute-start(bf16[4,48,1152]{2,1,0:T(8,128)(2,1)} %get-tuple-element.314), channel_id=1, source_target_pairs={{0,4},{2,6},{4,0},{6,2},{8,12},{10,14},{12,8},{14,10},{16,20},{18,... | collective-permute-start | bytes 1327112 | tf_op jit(solution)/shard_map/ppermute | solution.py:75
  260.4 20.3 %collective-permute-start.35 = (bf16[4,48,1152]{2,1,0:T(8,128)(2,1)}, bf16[4,48,1152]{2,1,0:T(8,128)(2,1)}, u32[]{:S(2)}, u32[]{:S(2)}) collective-permute-start(bf16[4,48,1152]{2,1,0:T(8,128)(2,1)} %get-tuple-element.315), channel_id=1, source_target_pairs={{0,6},{2,4},{4,2},{6,0},{8,14},{10,12},{12,10},{14,8},{16,22},{18,... | collective-permute-start | bytes 1327112 | tf_op jit(solution)/shard_map/ppermute | solution.py:75
  268.7 11.1 %collective-permute-start.38 = (bf16[48,1920]{1,0:T(8,128)(2,1)}, bf16[48,1920]{1,0:T(8,128)(2,1)}, u32[]{:S(2)}, u32[]{:S(2)}) collective-permute-start(bf16[48,1920]{1,0:T(8,128)(2,1)} %pad_maximum_fusion.6), channel_id=1, source_target_pairs={{0,16},{2,18},{4,20},{6,22},{8,24},{10,26},{12,28},{14,30},{16,0},... | collective-permute-start | bytes 552968 | tf_op jit(solution)/shard_map/ppermute | solution.py:75
  282.2 10.8 %collective-permute-start.39 = (bf16[48,1152]{1,0:T(8,128)(2,1)S(1)}, bf16[48,1152]{1,0:T(8,128)(2,1)S(1)}, u32[]{:S(2)}, u32[]{:S(2)}) collective-permute-start(bf16[48,1152]{1,0:T(8,128)(2,1)S(1)} %get-tuple-element.325), channel_id=1, source_target_pairs={{0,8},{2,10},{4,12},{6,14},{8,0},{10,2},{12,4},{14,6},{16,24},{18,... | collective-permute-start | bytes 331784 | tf_op jit(solution)/shard_map/ppermute | solution.py:75
  283.4 10.2 %collective-permute-start.40 = (bf16[48,1152]{1,0:T(8,128)(2,1)S(1)}, bf16[48,1152]{1,0:T(8,128)(2,1)S(1)}, u32[]{:S(2)}, u32[]{:S(2)}) collective-permute-start(bf16[48,1152]{1,0:T(8,128)(2,1)S(1)} %get-tuple-element.326), channel_id=1, source_target_pairs={{0,16},{2,18},{4,20},{6,22},{8,24},{10,26},{12,28},{14,30},{16,0},... | collective-permute-start | bytes 331784 | tf_op jit(solution)/shard_map/ppermute | solution.py:75
  285.1 8.6 %collective-permute-start.41 = (bf16[48,1152]{1,0:T(8,128)(2,1)S(1)}, bf16[48,1152]{1,0:T(8,128)(2,1)S(1)}, u32[]{:S(2)}, u32[]{:S(2)}) collective-permute-start(bf16[48,1152]{1,0:T(8,128)(2,1)S(1)} %get-tuple-element.327), channel_id=1, source_target_pairs={{0,24},{2,26},{4,28},{6,30},{8,16},{10,18},{12,20},{14,22},{16,8},... | collective-permute-start | bytes 331784 | tf_op jit(solution)/shard_map/ppermute | solution.py:75
  290.0 12.9 %collective-permute-start.43 = (bf16[2,48,1536]{2,1,0:T(8,128)(2,1)S(1)}, bf16[2,48,1536]{2,1,0:T(8,128)(2,1)S(1)}, u32[]{:S(2)}, u32[]{:S(2)}) collective-permute-start(bf16[2,48,1536]{2,1,0:T(8,128)(2,1)S(1)} %maximum_select_fusion.24), channel_id=1, source_target_pairs={{0,8},{2,10},{4,12},{6,14},{8,0},{10,2},{12,4},{14,6},{16,24},{18,... | collective-permute-start | bytes 884744 | tf_op jit(solution)/shard_map/ppermute | solution.py:75
  290.4 12.6 %collective-permute-start.42 = (bf16[48,1920]{1,0:T(8,128)(2,1)S(1)}, bf16[48,1920]{1,0:T(8,128)(2,1)S(1)}, u32[]{:S(2)}, u32[]{:S(2)}) collective-permute-start(bf16[48,1920]{1,0:T(8,128)(2,1)S(1)} %get-tuple-element.421), channel_id=1, source_target_pairs={{0,16},{2,18},{4,20},{6,22},{8,24},{10,26},{12,28},{14,30},{16,0},... | collective-permute-start | bytes 552968 | tf_op jit(solution)/shard_map/ppermute | solution.py:75
  303.2 7.2 %collective-permute-start.44 = (bf16[48,1152]{1,0:T(8,128)(2,1)S(1)}, bf16[48,1152]{1,0:T(8,128)(2,1)S(1)}, u32[]{:S(2)}, u32[]{:S(2)}) collective-permute-start(bf16[48,1152]{1,0:T(8,128)(2,1)S(1)} %get-tuple-element.348), channel_id=1, source_target_pairs={{0,8},{2,10},{4,12},{6,14},{8,0},{10,2},{12,4},{14,6},{16,24},{18,... | collective-permute-start | bytes 331784 | tf_op jit(solution)/shard_map/ppermute | solution.py:75
  303.3 10.0 %collective-permute-start.45 = (bf16[48,1152]{1,0:T(8,128)(2,1)S(1)}, bf16[48,1152]{1,0:T(8,128)(2,1)S(1)}, u32[]{:S(2)}, u32[]{:S(2)}) collective-permute-start(bf16[48,1152]{1,0:T(8,128)(2,1)S(1)} %get-tuple-element.348), channel_id=1, source_target_pairs={{0,16},{2,18},{4,20},{6,22},{8,24},{10,26},{12,28},{14,30},{16,0},... | collective-permute-start | bytes 331784 | tf_op jit(solution)/shard_map/ppermute | solution.py:75
  305.8 8.1 %collective-permute-start.46 = (bf16[48,1152]{1,0:T(8,128)(2,1)S(1)}, bf16[48,1152]{1,0:T(8,128)(2,1)S(1)}, u32[]{:S(2)}, u32[]{:S(2)}) collective-permute-start(bf16[48,1152]{1,0:T(8,128)(2,1)S(1)} %get-tuple-element.348), channel_id=1, source_target_pairs={{0,24},{2,26},{4,28},{6,30},{8,16},{10,18},{12,20},{14,22},{16,8},... | collective-permute-start | bytes 331784 | tf_op jit(solution)/shard_map/ppermute | solution.py:75
  307.6 11.8 %collective-permute-start.47 = (bf16[2,48,1920]{2,1,0:T(8,128)(2,1)S(1)}, bf16[2,48,1920]{2,1,0:T(8,128)(2,1)S(1)}, u32[]{:S(2)}, u32[]{:S(2)}) collective-permute-start(bf16[2,48,1920]{2,1,0:T(8,128)(2,1)S(1)} %maximum_select_fusion.21), channel_id=1, source_target_pairs={{0,8},{2,10},{4,12},{6,14},{8,0},{10,2},{12,4},{14,6},{16,24},{18,... | collective-permute-start | bytes 1105928 | tf_op jit(solution)/shard_map/ppermute | solution.py:75
  307.6 1.2 collective-permute-start.48
  308.9 11.8 %collective-permute-start.49 = (f32[16,768]{1,0:T(8,128)S(1)}, f32[16,768]{1,0:T(8,128)S(1)}, u32[]{:S(2)}, u32[]{:S(2)}) collective-permute-start(f32[16,768]{1,0:T(8,128)S(1)} %add.300), channel_id=1, source_target_pairs={{0,2},{2,0},{4,6},{6,4},{8,10},{10,8},{12,14},{14,12},{16,18},{18,... | collective-permute-start | bytes 147464 | tf_op jit(solution)/shard_map/ppermute | solution.py:75
  320.7 28.5 %collective-permute-start.50 = (bf16[4,48,1536]{2,1,0:T(8,128)(2,1)S(1)}, bf16[4,48,1536]{2,1,0:T(8,128)(2,1)S(1)}, u32[]{:S(2)}, u32[]{:S(2)}) collective-permute-start(bf16[4,48,1536]{2,1,0:T(8,128)(2,1)S(1)} %bitcast.315), channel_id=1, source_target_pairs={{0,2},{2,0},{4,6},{6,4},{8,10},{10,8},{12,14},{14,12},{16,18},{18,... | collective-permute-start | bytes 1769480 | tf_op jit(solution)/shard_map/ppermute | solution.py:75
  322.1 27.1 %collective-permute-start.51 = (bf16[4,48,1536]{2,1,0:T(8,128)(2,1)S(1)}, bf16[4,48,1536]{2,1,0:T(8,128)(2,1)S(1)}, u32[]{:S(2)}, u32[]{:S(2)}) collective-permute-start(bf16[4,48,1536]{2,1,0:T(8,128)(2,1)S(1)} %bitcast.314), channel_id=1, source_target_pairs={{0,4},{2,6},{4,0},{6,2},{8,12},{10,14},{12,8},{14,10},{16,20},{18,... | collective-permute-start | bytes 1769480 | tf_op jit(solution)/shard_map/ppermute | solution.py:75
  323.1 26.1 %collective-permute-start.52 = (bf16[4,48,1536]{2,1,0:T(8,128)(2,1)S(1)}, bf16[4,48,1536]{2,1,0:T(8,128)(2,1)S(1)}, u32[]{:S(2)}, u32[]{:S(2)}) collective-permute-start(bf16[4,48,1536]{2,1,0:T(8,128)(2,1)S(1)} %bitcast.313), channel_id=1, source_target_pairs={{0,6},{2,4},{4,2},{6,0},{8,14},{10,12},{12,10},{14,8},{16,22},{18,... | collective-permute-start | bytes 1769480 | tf_op jit(solution)/shard_map/ppermute | solution.py:75
  326.5 22.7 %collective-permute-start.53 = (f32[16,768]{1,0:T(8,128)S(1)}, f32[16,768]{1,0:T(8,128)S(1)}, u32[]{:S(2)}, u32[]{:S(2)}) collective-permute-start(f32[16,768]{1,0:T(8,128)S(1)} %add.303), channel_id=1, source_target_pairs={{0,4},{2,6},{4,0},{6,2},{8,12},{10,14},{12,8},{14,10},{16,20},{18,... | collective-permute-start | bytes 147464 | tf_op jit(solution)/shard_map/ppermute | solution.py:75
  353.6 4.9 %collective-permute-start.54 = (f32[768,768]{1,0:T(8,128)}, f32[768,768]{1,0:T(8,128)}, u32[]{:S(2)}, u32[]{:S(2)}) collective-permute-start(f32[768,768]{1,0:T(8,128)} %fusion.72.own_ref), channel_id=1, source_target_pairs={{0,1},{1,0},{2,3},{3,2},{4,5},{5,4},{6,7},{7,6},{8,9},{9,8},{10,11... | collective-permute-start | bytes 7077896 | tf_op jit(solution)/shard_map/ppermute | solution.py:79
  353.7 4.2 %collective-permute-start.55 = (f32[16,768]{1,0:T(8,128)S(1)}, f32[16,768]{1,0:T(8,128)S(1)}, u32[]{:S(2)}, u32[]{:S(2)}) collective-permute-start(f32[16,768]{1,0:T(8,128)S(1)} %add.304), channel_id=1, source_target_pairs={{0,8},{2,10},{4,12},{6,14},{8,0},{10,2},{12,4},{14,6},{16,24},{18,... | collective-permute-start | bytes 147464 | tf_op jit(solution)/shard_map/ppermute | solution.py:75
  358.5 39.4 %copy-start.50 = (f32[6,48]{1,0:T(8,128)S(1)}, f32[6,48]{1,0:T(8,128)}, u32[]{:S(2)}) copy-start(f32[6,48]{1,0:T(8,128)} %param.25) | copy-start | bytes 3460
  358.5 39.3 %copy-start.51 = (f32[6,48]{1,0:T(8,128)S(1)}, f32[6,48]{1,0:T(8,128)}, u32[]{:S(2)}) copy-start(f32[6,48]{1,0:T(8,128)} %param.31) | copy-start | bytes 3460
  358.5 39.3 %copy-start.52 = (f32[6,48]{1,0:T(8,128)S(1)}, f32[6,48]{1,0:T(8,128)}, u32[]{:S(2)}) copy-start(f32[6,48]{1,0:T(8,128)} %param.30) | copy-start | bytes 3460
  391.8 6.1 %collective-permute-start.56 = (f32[16,768]{1,0:T(8,128)S(1)}, f32[16,768]{1,0:T(8,128)S(1)}, u32[]{:S(2)}, u32[]{:S(2)}) collective-permute-start(f32[16,768]{1,0:T(8,128)S(1)} %add.305), channel_id=1, source_target_pairs={{0,16},{2,18},{4,20},{6,22},{8,24},{10,26},{12,28},{14,30},{16,0},... | collective-permute-start | bytes 147464 | tf_op jit(solution)/shard_map/ppermute | solution.py:75
  393.0 6.8 %collective-permute-start.59 = (bf16[48,1536]{1,0:T(8,128)(2,1)S(1)}, bf16[48,1536]{1,0:T(8,128)(2,1)S(1)}, u32[]{:S(2)}, u32[]{:S(2)}) collective-permute-start(bf16[48,1536]{1,0:T(8,128)(2,1)S(1)} %get-tuple-element.418), channel_id=1, source_target_pairs={{0,2},{2,0},{4,6},{6,4},{8,10},{10,8},{12,14},{14,12},{16,18},{18,... | collective-permute-start | bytes 442376 | tf_op jit(solution)/shard_map/ppermute | solution.py:75
  393.9 7.5 %collective-permute-start.58 = (bf16[48,1536]{1,0:T(8,128)(2,1)S(1)}, bf16[48,1536]{1,0:T(8,128)(2,1)S(1)}, u32[]{:S(2)}, u32[]{:S(2)}) collective-permute-start(bf16[48,1536]{1,0:T(8,128)(2,1)S(1)} %get-tuple-element.419), channel_id=1, source_target_pairs={{0,4},{2,6},{4,0},{6,2},{8,12},{10,14},{12,8},{14,10},{16,20},{18,... | collective-permute-start | bytes 442376 | tf_op jit(solution)/shard_map/ppermute | solution.py:75
  395.4 7.5 %collective-permute-start.57 = (bf16[48,1536]{1,0:T(8,128)(2,1)S(1)}, bf16[48,1536]{1,0:T(8,128)(2,1)S(1)}, u32[]{:S(2)}, u32[]{:S(2)}) collective-permute-start(bf16[48,1536]{1,0:T(8,128)(2,1)S(1)} %get-tuple-element.416), channel_id=1, source_target_pairs={{0,6},{2,4},{4,2},{6,0},{8,14},{10,12},{12,10},{14,8},{16,22},{18,... | collective-permute-start | bytes 442376 | tf_op jit(solution)/shard_map/ppermute | solution.py:75
  (61 other events, 386.8 us)

commit v5 on v4

--- a/solution.py
+++ b/solution.py
@@ -35,6 +35,8 @@
 VEC_PAD = 128
 GROUP = 4
 TILE = 256
+PARTS = 2
+STRIDE = HEADS // 2 // PARTS
 CHUNK = 256
 ROWS = 256
 VROWS = 8 + FF // D
@@ -44,11 +46,6 @@
 BLOCKS = 3 * PAIRS
 INFO = 1 + CAP * MICRO
 WIDE = FF // 2
-ORDER = (tuple(range(9)), tuple(range(12, 18)) + tuple(range(9, 12)))
-SPOTS = tuple(
-    tuple((ORDER[core] + ORDER[1 - core]).index(block) for block in range(BLOCKS))
-    for core in range(2)
-)
 
 
 def matmul(former, latter):
@@ -129,7 +126,12 @@
 
 
 def pick_four(parts, axis, place):
-    return [lax.dynamic_index_in_dim(part, place, axis, keepdims=False) for part in parts]
+    picked = []
+    for part in parts:
+        terms = part if isinstance(part, tuple) else (part,)
+        blocks = [lax.dynamic_index_in_dim(term, place, axis, keepdims=False) for term in terms]
+        picked.append(sum(block.astype(jnp.float32) for block in blocks))
+    return picked
 
 
 def split_four(parts, axis, bit):
@@ -173,7 +175,7 @@
 
 def split_low(parts, size):
     shape = (4,) * ((size.bit_length() - 1) // 2) + (D // size, -1)
-    parts = [part.reshape(shape) for part in parts]
+    parts = [tuple(term.reshape(shape) for term in part) for part in parts]
     return split_four(parts, len(shape) - 3, 0)
 
 
@@ -270,19 +272,54 @@
 
 def attention_kernel(info, query_ref, key_ref, value_ref, ctx_ref, total_ref):
     length = info[1 + pl.program_id(0)]
-    query, key = query_ref[...], key_ref[...]
-    value = jnp.transpose(value_ref[...])
+    for pair in range(STRIDE):
+        cols = slice(pair * PAIR, (pair + 1) * PAIR)
+        query, key = query_ref[:, cols], key_ref[:, cols]
+        value = jnp.transpose(value_ref[:, cols])
+        operands = [head_operands(query, key, length, head) for head in range(2)]
+        scores = [matmul_nt(operand[2], operand[1]) for operand in operands]
+        parts = []
+        for head in range(2):
+            top = jnp.max(scores[head], axis=0, keepdims=True)
+            powers = jnp.exp(scores[head] - top)
+            total = jnp.sum(powers, axis=0, keepdims=True)
+            probs = (powers * (1.0 / total)).astype(jnp.bfloat16)
+            total_ref[0, pair, head : head + 1, :] = top + jnp.log(total)
+            parts.append(matmul(value[head * HEAD_DIM : (head + 1) * HEAD_DIM], probs))
+        ctx_ref[:, cols] = jnp.transpose(jnp.concatenate(parts, axis=0)).astype(jnp.bfloat16)
+
+
+def pull_pair(length, query, key, value, grad, total_ref, queries_ref):
     operands = [head_operands(query, key, length, head) for head in range(2)]
-    scores = [matmul_nt(operand[2], operand[1]) for operand in operands]
-    parts = []
-    for head in range(2):
-        top = jnp.max(scores[head], axis=0, keepdims=True)
-        powers = jnp.exp(scores[head] - top)
-        total = jnp.sum(powers, axis=0, keepdims=True)
-        probs = (powers * (1.0 / total)).astype(jnp.bfloat16)
-        total_ref[0, 0, head : head + 1, :] = top + jnp.log(total)
-        parts.append(matmul(value[head * HEAD_DIM : (head + 1) * HEAD_DIM], probs))
-    ctx_ref[...] = jnp.transpose(jnp.concatenate(parts, axis=0)).astype(jnp.bfloat16)
+    grads = [jnp.where(operand[3], grad, jnp.zeros_like(grad)) for operand in operands]
+    flat_key = jnp.transpose(key * jnp.bfloat16(0.125))
+    jobs = [(head, first) for first in range(0, SEQ, CHUNK) for head in range(2)]
+
+    def begin(head, first):
+        spot = slice(first, first + CHUNK)
+        return (
+            matmul_nt(operands[head][2], operands[head][1][spot]),
+            matmul_nt(value, grads[head][spot]),
+        )
+
+    ready = begin(*jobs[0])
+    key_grad = value_grad = jnp.zeros((SEQ, PAIR), jnp.float32)
+    flat = []
+    for index, (head, first) in enumerate(jobs):
+        scores, prob_grad = ready
+        if index + 1 < len(jobs):
+            ready = begin(*jobs[index + 1])
+        spot = slice(first, first + CHUNK)
+        probs = jnp.exp(scores - total_ref[head : head + 1, spot])
+        row_dot = jnp.sum(probs * prob_grad, axis=0, keepdims=True)
+        score_grad = (probs * (prob_grad - row_dot)).astype(jnp.bfloat16)
+        value_grad += matmul(probs.astype(jnp.bfloat16), grads[head][spot])
+        key_grad += matmul(score_grad, operands[head][0][spot])
+        flat.append(matmul(flat_key[head * HEAD_DIM : (head + 1) * HEAD_DIM], score_grad))
+        if head:
+            queries_ref[spot, :] = jnp.transpose(jnp.concatenate(flat, axis=0)).astype(jnp.bfloat16)
+            flat = []
+    return queries_ref[...], key_grad.astype(jnp.bfloat16), value_grad.astype(jnp.bfloat16)
 
 
 def attention_pull_kernel(
@@ -300,47 +337,16 @@
     sems,
 ):
     length = info[1 + pl.program_id(0)]
-    query, key, value, grad = query_ref[...], key_ref[...], value_ref[...], grad_ref[...]
-    operands = [head_operands(query, key, length, head) for head in range(2)]
-    grads = [jnp.where(operand[3], grad, jnp.zeros_like(grad)) for operand in operands]
-    flat_key = jnp.transpose(key * jnp.bfloat16(0.125))
-    jobs = [(head, first) for first in range(0, SEQ, CHUNK) for head in range(2)]
-
-    def begin(head, first):
-        spot = slice(first, first + CHUNK)
-        return (
-            matmul_nt(operands[head][2], operands[head][1][spot]),
-            matmul_nt(value, grads[head][spot]),
-        )
-
-    ready = begin(*jobs[0])
-    key_grad = value_grad = jnp.zeros((SEQ, PAIR), jnp.float32)
-    flat = []
-    for index, (head, first) in enumerate(jobs):
-        scores, prob_grad = ready
-        if index + 1 < len(jobs):
-            ready = begin(*jobs[index + 1])
-        spot = slice(first, first + CHUNK)
-        probs = jnp.exp(scores - total_ref[0, 0, head : head + 1, spot])
-        row_dot = jnp.sum(probs * prob_grad, axis=0, keepdims=True)
-        score_grad = (probs * (prob_grad - row_dot)).astype(jnp.bfloat16)
-        value_grad += matmul(probs.astype(jnp.bfloat16), grads[head][spot])
-        key_grad += matmul(score_grad, operands[head][0][spot])
-        flat.append(matmul(flat_key[head * HEAD_DIM : (head + 1) * HEAD_DIM], score_grad))
-        if head:
-            queries_ref[spot, :] = jnp.transpose(jnp.concatenate(flat, axis=0)).astype(jnp.bfloat16)
-            flat = []
-    query_grad = queries_ref[...]
-    value_grad = value_grad.astype(jnp.bfloat16)
     early = info[0] == 0
-    pair = pl.program_id(1)
-    step = pl.program_id(0) * PAIRS + pair
-    last = pl.num_programs(0) * PAIRS - 1
+    part = pl.program_id(1)
+    step = pl.program_id(0) * PARTS + part
+    last = pl.num_programs(0) * PARTS - 1
     slot = lax.rem(step, 2)
     rows = pl.ds(pl.multiple_of(pl.program_id(0) * SEQ, SEQ), SEQ)
+    width = STRIDE * PAIR
 
     def copy(which, ref, block, slot):
-        cols = pl.ds(pl.multiple_of(block * PAIR, PAIR), PAIR)
+        cols = pl.ds(pl.multiple_of(block * width, width), width)
         return pltpu.make_async_copy(
             out_buffer.at[slot, which], ref.at[rows, cols], sems.at[slot, which]
         )
@@ -353,44 +359,66 @@
     def _():
         wait(slot)
 
-    out_buffer[slot, 0] = jnp.where(early, query_grad, value_grad)
-    out_buffer[slot, 1] = jnp.where(early, value_grad, query_grad)
-    out_buffer[slot, 2] = key_grad.astype(jnp.bfloat16)
-    copy(0, own_ref, pair, slot).start()
-    copy(1, other_ref, pair, slot).start()
-    key_block = PAIRS + lax.rem(pair, PAIRS // 2)
-    mine = (pair < PAIRS // 2) == early
+    for pair in range(STRIDE):
+        cols = slice(pair * PAIR, (pair + 1) * PAIR)
+        query_grad, key_grad, value_grad = pull_pair(
+            length,
+            query_ref[:, cols],
+            key_ref[:, cols],
+            value_ref[:, cols],
+            grad_ref[:, cols],
+            total_ref.at[0, pair],
+            queries_ref.at[pair],
+        )
+        out_buffer[slot, 0, :, cols] = jnp.where(early, query_grad, value_grad)
+        out_buffer[slot, 1, :, cols] = jnp.where(early, value_grad, query_grad)
+        out_buffer[slot, 2, :, cols] = key_grad
+        for place, values in enumerate((query_grad, value_grad)):
+            total = jnp.sum(values.astype(jnp.float32), axis=0, keepdims=True)
+            sum_ref[0, pair, place : place + 1, :] = total
+    copy(0, own_ref, part, slot).start()
+    copy(1, other_ref, part, slot).start()
+    mine = (part == 0) == early
 
     @pl.when(mine)
     def _():
-        copy(2, own_ref, key_block, slot).start()
+        copy(2, own_ref, PARTS, slot).start()
 
     @pl.when(jnp.logical_not(mine))
     def _():
-        copy(2, other_ref, key_block, slot).start()
+        copy(2, other_ref, PARTS, slot).start()
 
     @pl.when(step == last)
     def _():
         wait(1 - slot)
         wait(slot)
 
-    sum_ref[0, 0, 0:1, :] = jnp.sum(query_grad.astype(jnp.float32), axis=0, keepdims=True)
-    sum_ref[0, 0, 1:2, :] = jnp.sum(value_grad.astype(jnp.float32), axis=0, keepdims=True)
-
-
-def pick(kind):
-    def spot(s, p, info):
-        return s, info[INFO + kind * PAIRS + p]
-
-    return pl.BlockSpec((SEQ, PAIR), spot)
-
-
-def pair_spec():
-    return pl.BlockSpec((SEQ, PAIR), lambda s, p, info: (s, p))
-
-
-def pair_rows(width):
-    return pl.BlockSpec((1, 1, 2, width), lambda s, p, info: (s, p, 0, 0))
+
+def pick(place):
+    def spot(s, t, info):
+        return s, place(t, info[0])
+
+    return pl.BlockSpec((SEQ, STRIDE * PAIR), spot)
+
+
+def query_place(part, core):
+    return 3 * core + part
+
+
+def key_place(part, core):
+    return lax.select(core == 0, 2 + 3 * part, 5 - 3 * part)
+
+
+def value_place(part, core):
+    return 3 - 3 * core + part
+
+
+def part_spec():
+    return pl.BlockSpec((SEQ, STRIDE * PAIR), lambda s, t, info: (s, t))
+
+
+def part_rows(width):
+    return pl.BlockSpec((1, STRIDE, 2, width), lambda s, t, info: (s, t, 0, 0))
 
 
 def attention(info, qkv, slots):
@@ -399,14 +427,15 @@
         attention_kernel,
         grid_spec=pltpu.PrefetchScalarGridSpec(
             num_scalar_prefetch=1,
-            grid=(slots, PAIRS),
-            in_specs=[pick(kind) for kind in range(3)],
-            out_specs=[pair_spec(), pair_rows(SEQ)],
+            grid=(slots, PARTS),
+            in_specs=[pick(query_place), pick(key_place), pick(value_place)],
+            out_specs=[part_spec(), part_rows(SEQ)],
         ),
         out_shape=[
             jax.ShapeDtypeStruct((rows, D), jnp.bfloat16),
             jax.ShapeDtypeStruct((slots, PAIRS, 2, SEQ), jnp.float32),
         ],
+        compiler_params=pltpu.CompilerParams(vmem_limit_bytes=52 << 20),
         cost_estimate=SMALL,
         name="attention",
     )(info, qkv, qkv, qkv)
@@ -414,22 +443,23 @@
 
 def attention_pull(info, qkv, grad, log_total, slots):
     rows = qkv.shape[0]
-
     table = jax.ShapeDtypeStruct((rows, BLOCKS // 2 * PAIR), jnp.bfloat16)
     return pl.pallas_call(
         attention_pull_kernel,
         grid_spec=pltpu.PrefetchScalarGridSpec(
             num_scalar_prefetch=1,
-            grid=(slots, PAIRS),
-            in_specs=[pick(kind) for kind in range(3)] + [pair_spec(), pair_rows(SEQ)],
-            out_specs=[pl.BlockSpec(memory_space=pl.ANY)] * 2 + [pair_rows(PAIR)],
+            grid=(slots, PARTS),
+            in_specs=[pick(query_place), pick(key_place), pick(value_place)]
+            + [part_spec(), part_rows(SEQ)],
+            out_specs=[pl.BlockSpec(memory_space=pl.ANY)] * 2 + [part_rows(PAIR)],
             scratch_shapes=[
-                pltpu.VMEM((SEQ, PAIR), jnp.bfloat16),
-                pltpu.VMEM((2, 3, SEQ, PAIR), jnp.bfloat16),
+                pltpu.VMEM((STRIDE, SEQ, PAIR), jnp.bfloat16),
+                pltpu.VMEM((2, 3, SEQ, STRIDE * PAIR), jnp.bfloat16),
                 pltpu.SemaphoreType.DMA((2, 3)),
             ],
         ),
         out_shape=[table] * 2 + [jax.ShapeDtypeStruct((slots, PAIRS, 2, PAIR), jnp.float32)],
+        compiler_params=pltpu.CompilerParams(vmem_limit_bytes=52 << 20),
         cost_estimate=SMALL,
         name="attention_pull",
     )(info, qkv, qkv, qkv, grad, log_total)
@@ -563,7 +593,7 @@
     xhat, rstd = norm_parts(hidden + (first_ref[...] + second_ref[...] + vec_ref[9:10, :]))
     gain = vec_ref[10:11, :]
     out_ref[...] = (xhat * gain + vec_ref[11:12, :]).astype(jnp.bfloat16)
-    limit = info[INFO + BLOCKS + lax.div(first, SEQ)]
+    limit = info[INFO + lax.div(first, SEQ)]
     row = lax.broadcasted_iota(jnp.int32, (ROWS, 1), 0) + lax.rem(first, SEQ)
     cot = jnp.where(row < limit, cot_ref[...].astype(jnp.float32), 0.0)
     grad = norm_pull(cot, gain, xhat, rstd)
@@ -732,15 +762,13 @@
 ):
     a, q, b, r = (a_high, a_rest), (q_high, q_rest), (b_high, b_rest), (r_high, r_rest)
     count = out_ref.shape[0]
-    start = pl.multiple_of(start_ref[0], 8)
+    start = pl.multiple_of(start_ref[0], 16)
     whole = own_ref[...] + other_ref[...]
     row = lax.broadcasted_iota(jnp.int32, (D, D), 0)
     col = lax.broadcasted_iota(jnp.int32, (D, D), 1)
     scale = jnp.sqrt(jnp.sum(jnp.where(row == col, whole, 0.0), keepdims=True)) + 1e-07
     gram[...] = whole / (scale * scale)
-    rows = lax.broadcasted_iota(jnp.int32, (count, D), 0) + start
-    cols = lax.broadcasted_iota(jnp.int32, (count, D), 1)
-    out_ref[...] = jnp.where(rows == cols, 1.0, 0.0)
+    whole_rows = (slice(0, count), slice(0, D))
 
     def sweep(index, carry):
         every = slice(0, D)
@@ -755,23 +783,36 @@
             store_split(step, (where_rows, where_cols), q_high, q_rest)
 
         mirrored_product(a, a, step_tile)
-        store_split(out_ref[...], (slice(0, count), every), r_high, r_rest)
-        out_ref[...] = close_product(r, q, slice(0, count), every)
-
-        @pl.when(index < NS_ITERS - 1)
+
+        @pl.when(index == 0)
         def _():
-            def half_tile(tile, where_rows, where_cols):
-                store_split(tile, (where_rows, where_cols), b_high, b_rest)
-
-            def gram_tile(tile, where_rows, where_cols):
-                gram[where_rows, where_cols] = tile
-
-            mirrored_product(q, a, half_tile)
-            mirrored_product(b, q, gram_tile)
-
+            rows = pl.ds(start, count)
+            out_ref[...] = q_high[rows, :].astype(jnp.float32) + q_rest[rows, :].astype(jnp.float32)
+
+        @pl.when(index > 0)
+        def _():
+            store_split(out_ref[...], whole_rows, r_high, r_rest)
+            out_ref[...] = close_product(r, q, slice(0, count), every)
+
+        def half_tile(tile, where_rows, where_cols):
+            store_split(tile, (where_rows, where_cols), b_high, b_rest)
+
+        def gram_tile(tile, where_rows, where_cols):
+            gram[where_rows, where_cols] = tile
+
+        mirrored_product(q, a, half_tile)
+        mirrored_product(b, q, gram_tile)
         return carry
 
-    lax.fori_loop(0, NS_ITERS, sweep, 0)
+    lax.fori_loop(0, NS_ITERS - 1, sweep, 0)
+    every = slice(0, D)
+    store_split(gram[...], (every, every), a_high, a_rest)
+    before = out_ref[...]
+    store_split(before, whole_rows, r_high, r_rest)
+    once = close_product(r, a, slice(0, count), every)
+    store_split(once, whole_rows, r_high, r_rest)
+    twice = close_product(r, a, slice(0, count), every)
+    out_ref[...] = poly_first * before + poly_second * once + poly_third * twice
     both = jnp.concatenate(split_rest(out_ref[...] / scale), axis=0)
     for place in range(0, cols_ref.shape[1], D):
         spot = slice(place, place + D)
@@ -848,10 +889,9 @@
     second_pieces = send_low(sort_high(second_pieces, size), size)
     third_pieces = [third_block, flip(third_block, steps[0], size)]
 
-    spots = pick_core(jnp.array(SPOTS[0], jnp.int32), jnp.array(SPOTS[1], jnp.int32))
     live = jnp.arange(slots) % CAP < counts.reshape(-1)[jnp.arange(slots) // CAP]
     info = jnp.concatenate(
-        [core.reshape(1).astype(jnp.int32), lengths, spots, jnp.where(live, lengths, 0)]
+        [core.reshape(1).astype(jnp.int32), lengths, jnp.where(live, lengths, 0)]
     )
     vec, bias_up, bias_own, bias_other = vector_tables(info, first_own, first_other)
     qkv_own, qkv_other = first_own[:, :qkv_half], first_other[:, :qkv_half]
@@ -881,13 +921,12 @@
         info, vec, xhat_one, branch, matmul_nt(act_other, third_other), cotangent
     )
 
-    full = jnp.float32
     leaving = matmul_tn(branch_low, act_other).astype(low)
     leaving, branch_low = together(leaving, branch_low)
     down_arrived = swap_cores(leaving)
     down_own = matmul_tn(branch_low, act_own)
     down_own, down_arrived, branch_low = together(down_own, down_arrived, branch_low)
-    down_kept, leaving = split_low([down_own + down_arrived.astype(full)], size)
+    down_kept, leaving = split_low([(down_own, down_arrived)], size)
     leaving, branch_low = together(leaving, branch_low)
     down_sent = fly_low(leaving, size)
     pulled = pull_rows(
@@ -916,9 +955,7 @@
     up_own = matmul_tn(hidden_low, pre_own)
     out_own = matmul_tn(context, out_own)
     up_own, out_own, up_arrived, out_arrived = together(up_own, out_own, up_arrived, out_arrived)
-    wide_kept, leaving = split_low(
-        [up_own + up_arrived.astype(full), out_own + out_arrived.astype(full)], size
-    )
+    wide_kept, leaving = split_low([(up_own, up_arrived), (out_own, out_arrived)], size)
     leaving, down_leaving, context_grad = together(leaving, down_leaving, context_grad)
     wide_sent = fly_low(leaving, size)
     down_sent = fly_far(down_leaving, size)
@@ -935,7 +972,7 @@
     (grad_down,) = add_four(down_kept, [down_sent])
     moment_down = moment_decay * mom_down + grad_down
     qkv_part, qkv_arrived, grads, moment_down = together(qkv_part, qkv_arrived, parts, moment_down)
-    qkv_kept, leaving = split_low([qkv_part + qkv_arrived.astype(full)], size)
+    qkv_kept, leaving = split_low([(qkv_part + qkv_arrived.astype(jnp.float32),)], size)
     leaving, grads, down_block = together(leaving, grads, moment_down.astype(low))
     qkv_sent = fly_low(leaving, size)
     down_sent = fly_far(down_block, size)

time: 412 us -> 409 us (level)
  Pallas kernels: 130 us -> 123 us
  local copies, waits for them, and re-layouts: 18.5 us -> 13.8 us
  waiting for transfers between devices: 89.4 us -> 93.8 us
    convert_element_type x0 -> x3, other arithmetic: none -> 7.39 us  [split_four(): part.astype(jnp.bfloat16)]
    ppermute x51, waiting for transfers between devices: 87.9 us -> 92.2 us  [flip(): lax.ppermute(by_rows(values), 'fsdp', [(i, i ^ mask) for i in range(size)])]
    pallas_call x1, Pallas kernels: 25.9 us -> 21.7 us  [attention_pull(): pl.pallas_call(attention_pull_kernel, grid_spec=pltpu.PrefetchScalarGridS...]
    unnamed x126 -> x128, local copies, waits for them, and re-layouts: 11.9 us -> 9.22 us
  transfers between devices with their start and end apart: 60 -> 60, of which waited for: 29 -> 25; matrix products, arithmetic and copies ran while one was open for 17% -> 16% of each run, Pallas kernels for 22% -> 20%
where the time goes in v5:
time: 409 us; the launch traced here: 403 us
  Pallas kernels  123 us (30%)
  waiting for transfers between devices  93.8 us (23%)
  starting transfers between devices  72.4 us (18%)
  matrix products  53.1 us (13%)
  other arithmetic  44.1 us (11%)
  local copies, waits for them, and re-layouts  13.8 us (3%)
    ppermute x51, waiting for transfers between devices, flip(): lax.ppermute(by_rows(values), 'fsdp', [(i, i ^ mask) for i in range(size)])  92.2 us
    ppermute x51, starting transfers between devices, flip(): lax.ppermute(by_rows(values), 'fsdp', [(i, i ^ mask) for i in range(size)])  71.6 us
    pallas_call x3, Pallas kernels, row_call(): pl.pallas_call(kernel, grid=(rows // ROWS,), in_specs=[pl.BlockSpec(memor...  51.2 us
    pallas_call x1, Pallas kernels, polar_rows(): pl.pallas_call(polar_kernel, in_specs=[pl.BlockSpec(memory_space=pltpu.SM...  32.8 us
    dot_general x8, matrix products, matmul_tn(): lax.dot_general(former, latter, (((0,), (0,)), ((), ())), preferred_eleme...  25.1 us
    pallas_call x1, Pallas kernels, attention_pull(): pl.pallas_call(attention_pull_kernel, grid_spec=pltpu.PrefetchScalarGridS...  21.7 us
    dot_general x5, matrix products, matmul_nt(): lax.dot_general(former, latter, (((1,), (1,)), ((), ())), preferred_eleme...  20 us
    pallas_call x1, Pallas kernels, attention(): pl.pallas_call(attention_kernel, grid_spec=pltpu.PrefetchScalarGridSpec(n...  14 us
  transfers between devices with their start and end apart: 60, of which 25 were waited for; matrix products, arithmetic and copies ran while one was open for 16% of the time, Pallas kernels for 20%

profile of v5, /device:TPU:0, one launch (start us, length us, event | category | flops | bytes accessed | tf_op | source)
XLA Modules:
  0.0 402.6 jit_solution(12103772516760898045)
XLA Ops:
  2.6 3.1 collective-permute-start.3
  8.6 3.0 collective-permute-start.1
  13.6 2.3 collective-permute-done
  16.0 4.7 %collective-permute-done.2 = bf16[48,1280]{1,0:T(8,128)(2,1)S(1)} collective-permute-done((bf16[48,1280]{1,0:T(8,128)(2,1)S(1)}, bf16[48,1280]{1,0:T(8,128)(2,1)S(1)}, u32[]{:S(2)}, u32[]{:S(2)}) %collective-permute-start.2) | collective-permute-done | bytes 122912 | tf_op jit(solution)/shard_map/ppermute | solution.py:72
  20.8 1.6 collective-permute-start.4
  24.4 4.3 %collective-permute-start.7 = (bf16[48,1920]{1,0:T(8,128)(2,1)S(1)}, bf16[48,1920]{1,0:T(8,128)(2,1)S(1)}, u32[]{:S(2)}, u32[]{:S(2)}) collective-permute-start(bf16[48,1920]{1,0:T(8,128)(2,1)S(1)} %pad_maximum_fusion.5), channel_id=1, source_target_pairs={{0,16},{2,18},{4,20},{6,22},{8,24},{10,26},{12,28},{14,30},{16,0},... | collective-permute-start | bytes 552968 | tf_op jit(solution)/shard_map/ppermute | solution.py:72
  29.2 11.2 %collective-permute-done.7 = bf16[48,1920]{1,0:T(8,128)(2,1)S(1)} collective-permute-done((bf16[48,1920]{1,0:T(8,128)(2,1)S(1)}, bf16[48,1920]{1,0:T(8,128)(2,1)S(1)}, u32[]{:S(2)}, u32[]{:S(2)}) %collective-permute-start.7) | collective-permute-done | bytes 184352 | tf_op jit(solution)/shard_map/ppermute | solution.py:72
  40.3 3.8 collective-permute-done.5
  50.1 3.7 collective-permute-start.10
  53.8 1.9 vector_tables.1
  57.2 4.3 %fusion.2 = bf16[1024,1152]{1,0:T(8,128)(2,1)S(1)} fusion(f32[1152]{0:T(1024)S(1)} %slice_reduce_fusion.1, bf16[1024,768]{1,0:T(8,128)(2,1)} %x_ref.1, bf16[768,1280]{1,0:T(8,128)(2,1)} %bitcast.361), kind=kOutput, calls=%fused_computation.13 | convolution fusion | flops 1814298624 | bytes 5706240 | tf_op jit(solution)/shard_map/dot_general | solution.py:52
  61.5 3.7 fusion
  65.2 2.5 pad_maximum_fusion.query_ref.key_ref.value_ref
  70.7 14.0 %attention.1 = (bf16[1024,768]{1,0:T(8,128)(2,1)S(1)}, f32[2,6,2,512]{3,2,1,0:T(2,128)S(1)}) custom-call(s32[5]{0:T(128)S(1)} %copy-done.9, bf16[1024,2304]{1,0:T(8,128)(2,1)} %pad_maximum_fusion.query_ref.key_ref.value_ref, bf16[1024,2304]{1,0:T(8,128)(2,1)} %pad_maximum_fusion.query_ref.key_ref.value_ref, ...), custom_call_target="tpu_custom_call" | custom-call | flops 1048576 | bytes 65536 | tf_op jit(solution)/shard_map/attention/pallas_call | solution.py:426
  85.1 2.3 maximum_select_fusion.4
  95.2 21.6 %raise_rows.1 = (f32[1024,768]{1,0:T(8,128)}, f32[1024,128]{1,0:T(8,128)S(1)}, bf16[1024,768]{1,0:T(8,128)(2,1)}, bf16[1024,1536]{1,0:T(8,128)(2,1)}, bf16[1024,...) custom-call(s32[5]{0:T(128)S(1)} %copy-done.9, f32[16,768]{1,0:T(8,128)S(1)} %copy-done.6, f32[8,3072]{1,0:T(8,128)S(1)} %copy-done.7, ...), custom_call_target="tpu_custom_call" | custom-call | flops 1048576 | bytes 65536 | tf_op jit(solution)/shard_map/raise_rows/pallas_call | solution.py:662
  117.2 1.6 collective-permute-done.19
  120.0 2.4 copy-done.21
  122.4 4.4 %fusion.83.first_ref = f32[1024,768]{1,0:T(8,128)} fusion(bf16[1024,1536]{1,0:T(8,128)(2,1)S(1)} %copy-done.21, bf16[768,1536]{1,0:T(8,128)(2,1)S(1)} %bitcast.355), kind=kOutput, calls=%fused_computation.192 | convolution fusion | flops 2415919104 | bytes 8650752 | tf_op jit(solution)/shard_map/dot_general | solution.py:62
  126.8 4.3 %fusion.84.second_ref = f32[1024,768]{1,0:T(8,128)} fusion(bf16[1024,1536]{1,0:T(8,128)(2,1)S(1)} %copy-done.58, bf16[768,1536]{1,0:T(8,128)(2,1)S(1)} %collective-permute-done.20.other), kind=kOutput, calls=%fused_computation.193 | convolution fusion | flops 2415919104 | bytes 8650752 | tf_op jit(solution)/shard_map/dot_general | solution.py:62
  131.1 8.1 %lower_rows.1 = (bf16[1024,768]{1,0:T(8,128)(2,1)}, f32[1024,768]{1,0:T(8,128)}, bf16[1024,768]{1,0:T(8,128)(2,1)S(1)}, f32[8,768]{1,0:T(8,128)S(1)}) custom-call(s32[5]{0:T(128)S(1)} %copy-done.9, f32[16,768]{1,0:T(8,128)S(1)} %copy-done.6, f32[1024,768]{1,0:T(8,128)} %get-tuple-element.227.xhat_ref, f32[1024,768]{1,0:T(8,128)} %fusion.83.first_ref, ...), custom_call_target="tpu_custom_call" | custom-call | flops 1048576 | bytes 65536 | tf_op jit(solution)/shard_map/lower_rows/pallas_call | solution.py:662
  139.2 4.0 convolution_convert_fusion.1
  143.2 4.5 %fusion.85 = f32[768,1536]{1,0:T(8,128)S(1)} fusion(bf16[1024,768]{1,0:T(8,128)(2,1)S(1)} %get-tuple-element.253.low_ref, bf16[1024,1536]{1,0:T(8,128)(2,1)} %get-tuple-element.234), kind=kOutput, calls=%fused_computation.194 | convolution fusion | flops 2415919104 | bytes 9437184 | tf_op jit(solution)/shard_map/dot_general | solution.py:56
  148.1 4.3 %fusion.45 = (bf16[4,48,1536]{2,1,0:T(8,128)(2,1)S(1)}, bf16[4,48,1536]{2,1,0:T(8,128)(2,1)}, bf16[4,48,1536]{2,1,0:T(8,128)(2,1)}) fusion(f32[4,4,48,1536]{3,2,1,0:T(8,128)S(1)} %bitcast.352, s32[]{:T(128)S(6)} %select_n.517, bf16[4,4,48,1536]{3,2,1,0:T(8,128)(2,1)} %bitcast.33, s32[]{:T(128)S(6)} %select_n.516, s32[]{:T(128)S(6)} %select_n.515), kind=kLoop, calls=%fused_computation.85 | loop fusion | flops 2654208 | bytes 7077900 | tf_op jit(solution)/shard_map/convert_element_type | solution.py:142
  155.9 21.5 %pull_rows.1 = (bf16[1024,1536]{1,0:T(8,128)(2,1)}, bf16[1024,1536]{1,0:T(8,128)(2,1)}, f32[1024,768]{1,0:T(8,128)}, bf16[1024,768]{1,0:T(8,128)(2,1)}, bf16[102...) custom-call(s32[5]{0:T(128)S(1)} %copy-done.9, f32[16,768]{1,0:T(8,128)S(1)} %copy-done.6, ...), custom_call_target="tpu_custom_call" | custom-call | flops 1048576 | bytes 65536 | tf_op jit(solution)/shard_map/pull_rows/pallas_call | solution.py:662
  177.4 3.8 collective-permute-done.23
  181.2 2.0 fusion.27
  184.5 4.1 %convolution_convert_fusion = bf16[768,1536]{1,0:T(8,128)(2,1)} fusion(bf16[1024,768]{1,0:T(8,128)(2,1)S(1)} %copy-done.30, bf16[1024,1536]{1,0:T(8,128)(2,1)S(1)} %copy-done.59), kind=kOutput, calls=%fused_computation.6 | convolution fusion | flops 2417098752 | bytes 7077888 | tf_op jit(solution)/shard_map/dot_general | solution.py:56
  188.6 2.9 collective-permute-done.25
  192.2 2.4 convolution_convert_fusion.3
  198.4 2.7 fusion.86
  202.0 2.9 fusion.48
  211.2 2.6 collective-permute-start.28
  213.8 21.7 %attention_pull.1 = (bf16[1024,1152]{1,0:T(8,128)(2,1)}, bf16[1024,1152]{1,0:T(8,128)(2,1)}, f32[2,6,2,128]{3,2,1,0:T(2,128)S(1)}) custom-call(s32[5]{0:T(128)S(1)} %copy-done.9, bf16[1024,2304]{1,0:T(8,128)(2,1)} %pad_maximum_fusion.query_ref.key_ref.value_ref, bf16[1024,2304]{1,0:T(8,128)(2,1)} %pad_maximum_fusion.query_ref.key_ref.value_ref, ...), custom_call_target="tpu_custom_call" | custom-call | flops 1048576 | bytes 65536 | tf_op jit(solution)/shard_map/attention_pull/pallas_call | solution.py:447
  235.5 3.9 fusion.1
  239.4 4.4 %collective-permute-done.30 = bf16[4,48,1920]{2,1,0:T(8,128)(2,1)} collective-permute-done((bf16[4,48,1920]{2,1,0:T(8,128)(2,1)}, bf16[4,48,1920]{2,1,0:T(8,128)(2,1)}, u32[]{:S(2)}, u32[]{:S(2)}) %collective-permute-start.30) | collective-permute-done | bytes 737312 | tf_op jit(solution)/shard_map/ppermute | solution.py:72
  243.9 2.1 fusion.20
  249.0 2.4 convolution_bitcast_fusion
  252.9 2.4 collective-permute-start.37
  257.0 1.7 collective-permute-start.35
  258.7 3.0 collective-permute-done.36
  264.1 1.6 collective-permute-start.38
  266.4 1.6 vector_grads.1
  268.0 7.7 %collective-permute-done.38 = bf16[48,1920]{1,0:T(8,128)(2,1)} collective-permute-done((bf16[48,1920]{1,0:T(8,128)(2,1)}, bf16[48,1920]{1,0:T(8,128)(2,1)}, u32[]{:S(2)}, u32[]{:S(2)}) %collective-permute-start.38) | collective-permute-done | bytes 184352 | tf_op jit(solution)/shard_map/ppermute | solution.py:72
  275.6 1.8 collective-permute-done.34
  279.0 1.8 collective-permute-start.39
  281.1 2.3 collective-permute-start.41
  284.9 1.8 fusion.81
  289.1 1.6 collective-permute-done.40
  290.7 9.3 %collective-permute-done.42 = bf16[48,1920]{1,0:T(8,128)(2,1)S(1)} collective-permute-done((bf16[48,1920]{1,0:T(8,128)(2,1)S(1)}, bf16[48,1920]{1,0:T(8,128)(2,1)S(1)}, u32[]{:S(2)}, u32[]{:S(2)}) %collective-permute-start.42) | collective-permute-done | bytes 184352 | tf_op jit(solution)/shard_map/ppermute | solution.py:72
  300.2 1.9 collective-permute-start.45
  302.1 2.5 collective-permute-start.46
  307.0 4.2 %collective-permute-done.45 = bf16[48,1152]{1,0:T(8,128)(2,1)S(1)} collective-permute-done((bf16[48,1152]{1,0:T(8,128)(2,1)S(1)}, bf16[48,1152]{1,0:T(8,128)(2,1)S(1)}, u32[]{:S(2)}, u32[]{:S(2)}) %collective-permute-start.45) | collective-permute-done | bytes 110624 | tf_op jit(solution)/shard_map/ppermute | solution.py:72
  311.2 5.6 %collective-permute-done.47 = bf16[2,48,1920]{2,1,0:T(8,128)(2,1)S(1)} collective-permute-done((bf16[2,48,1920]{2,1,0:T(8,128)(2,1)S(1)}, bf16[2,48,1920]{2,1,0:T(8,128)(2,1)S(1)}, u32[]{:S(2)}, u32[]{:S(2)}) %collective-permute-start.47) | collective-permute-done | bytes 368672 | tf_op jit(solution)/shard_map/ppermute | solution.py:72
  319.8 1.8 collective-permute-start.52
  321.6 2.2 fusion.6
  324.8 5.7 %add_add_fusion = f32[1024,768]{1,0:T(8,128)} fusion(f32[1024,768]{1,0:T(8,128)S(1)} %copy-done.57, f32[1024,768]{1,0:T(8,128)S(1)} %fusion.6, bf16[1024,1152]{1,0:T(8,128)(2,1)S(1)} %copy-done.60, bf16[768,1280]{1,0:T(8,128)(2,1)} %collective-permute-done.9.other_ref), kind=kOutput, calls=%fused_computation.10 | convolution fusion | flops 1813512192 | bytes 13565952 | tf_op jit(solution)/shard_map/dot_general | solution.py:62
  330.4 15.4 %collective-permute-done.53 = f32[16,768]{1,0:T(8,128)S(1)} collective-permute-done((f32[16,768]{1,0:T(8,128)S(1)}, f32[16,768]{1,0:T(8,128)S(1)}, u32[]{:S(2)}, u32[]{:S(2)}) %collective-permute-start.53) | collective-permute-done | bytes 49184 | tf_op jit(solution)/shard_map/ppermute | solution.py:72
  346.9 3.4 fusion.87.own_ref
  350.3 1.6 collective-permute-start.55
  351.9 2.5 collective-permute-done.55
  355.2 32.8 %polar_rows.1 = bf16[192,1536]{1,0:T(8,128)(2,1)S(1)} custom-call(s32[1]{0:T(128)} %bitcast.96.start_ref, f32[768,768]{1,0:T(8,128)} %fusion.87.own_ref, f32[768,768]{1,0:T(8,128)} %collective-permute-done.54.other_ref, bf16[768,1536]{1,0:T(8,128)(2,1)S(1)} %bitcast.345), custom_call_target="tpu_custom_call" | custom-call | tf_op jit(solution)/shard_map/polar_rows/pallas_call | solution.py:825
  389.4 1.7 collective-permute-start.59
  395.6 4.0 collective-permute-done.58
  (315 shorter events, 77.2 us)
Async XLA Ops:
  0.7 44.3 %copy-start = (s32[1,2]{1,0:T(1,128)S(1)}, s32[1,2]{1,0:T(1,128)}, u32[]{:S(2)}) copy-start(s32[1,2]{1,0:T(1,128)} %param.17) | copy-start | bytes 28
  2.6 18.1 %collective-permute-start.3 = (bf16[48,1920]{1,0:T(8,128)(2,1)S(1)}, bf16[48,1920]{1,0:T(8,128)(2,1)S(1)}, u32[]{:S(2)}, u32[]{:S(2)}) collective-permute-start(bf16[48,1920]{1,0:T(8,128)(2,1)S(1)} %pad_maximum_fusion.5), channel_id=1, source_target_pairs={{0,8},{2,10},{4,12},{6,14},{8,0},{10,2},{12,4},{14,6},{16,24},{18,... | collective-permute-start | bytes 552968 | tf_op jit(solution)/shard_map/ppermute | solution.py:72
  8.5 7.5 %collective-permute-start = (bf16[48,1280]{1,0:T(8,128)(2,1)S(1)}, bf16[48,1280]{1,0:T(8,128)(2,1)S(1)}, u32[]{:S(2)}, u32[]{:S(2)}) collective-permute-start(bf16[48,1280]{1,0:T(8,128)(2,1)S(1)} %fusion.71), channel_id=1, source_target_pairs={{0,8},{2,10},{4,12},{6,14},{8,0},{10,2},{12,4},{14,6},{16,24},{18,... | collective-permute-start | bytes 368648 | tf_op jit(solution)/shard_map/ppermute | solution.py:72
  8.6 7.4 %collective-permute-start.1 = (bf16[48,1280]{1,0:T(8,128)(2,1)S(1)}, bf16[48,1280]{1,0:T(8,128)(2,1)S(1)}, u32[]{:S(2)}, u32[]{:S(2)}) collective-permute-start(bf16[48,1280]{1,0:T(8,128)(2,1)S(1)} %fusion.71), channel_id=1, source_target_pairs={{0,16},{2,18},{4,20},{6,22},{8,24},{10,26},{12,28},{14,30},{16,0},... | collective-permute-start | bytes 368648 | tf_op jit(solution)/shard_map/ppermute | solution.py:72
  11.6 9.1 %collective-permute-start.2 = (bf16[48,1280]{1,0:T(8,128)(2,1)S(1)}, bf16[48,1280]{1,0:T(8,128)(2,1)S(1)}, u32[]{:S(2)}, u32[]{:S(2)}) collective-permute-start(bf16[48,1280]{1,0:T(8,128)(2,1)S(1)} %fusion.71), channel_id=1, source_target_pairs={{0,24},{2,26},{4,28},{6,30},{8,16},{10,18},{12,20},{14,22},{16,8},... | collective-permute-start | bytes 368648 | tf_op jit(solution)/shard_map/ppermute | solution.py:72
  20.8 19.5 %collective-permute-start.4 = (bf16[4,48,1280]{2,1,0:T(8,128)(2,1)S(1)}, bf16[4,48,1280]{2,1,0:T(8,128)(2,1)S(1)}, u32[]{:S(2)}, u32[]{:S(2)}) collective-permute-start(bf16[4,48,1280]{2,1,0:T(8,128)(2,1)S(1)} %maximum_select_fusion.17), channel_id=1, source_target_pairs={{0,2},{2,0},{4,6},{6,4},{8,10},{10,8},{12,14},{14,12},{16,18},{18,... | collective-permute-start | bytes 1474568 | tf_op jit(solution)/shard_map/ppermute | solution.py:72
  22.4 21.6 %collective-permute-start.5 = (bf16[4,48,1280]{2,1,0:T(8,128)(2,1)S(1)}, bf16[4,48,1280]{2,1,0:T(8,128)(2,1)S(1)}, u32[]{:S(2)}, u32[]{:S(2)}) collective-permute-start(bf16[4,48,1280]{2,1,0:T(8,128)(2,1)S(1)} %maximum_select_fusion.17), channel_id=1, source_target_pairs={{0,4},{2,6},{4,0},{6,2},{8,12},{10,14},{12,8},{14,10},{16,20},{18,... | collective-permute-start | bytes 1474568 | tf_op jit(solution)/shard_map/ppermute | solution.py:72
  24.0 20.1 %collective-permute-start.6 = (bf16[4,48,1280]{2,1,0:T(8,128)(2,1)S(1)}, bf16[4,48,1280]{2,1,0:T(8,128)(2,1)S(1)}, u32[]{:S(2)}, u32[]{:S(2)}) collective-permute-start(bf16[4,48,1280]{2,1,0:T(8,128)(2,1)S(1)} %maximum_select_fusion.17), channel_id=1, source_target_pairs={{0,6},{2,4},{4,2},{6,0},{8,14},{10,12},{12,10},{14,8},{16,22},{18,... | collective-permute-start | bytes 1474568 | tf_op jit(solution)/shard_map/ppermute | solution.py:72
  24.4 15.9 %collective-permute-start.7 = (bf16[48,1920]{1,0:T(8,128)(2,1)S(1)}, bf16[48,1920]{1,0:T(8,128)(2,1)S(1)}, u32[]{:S(2)}, u32[]{:S(2)}) collective-permute-start(bf16[48,1920]{1,0:T(8,128)(2,1)S(1)} %pad_maximum_fusion.5), channel_id=1, source_target_pairs={{0,16},{2,18},{4,20},{6,22},{8,24},{10,26},{12,28},{14,30},{16,0},... | collective-permute-start | bytes 552968 | tf_op jit(solution)/shard_map/ppermute | solution.py:72
  28.7 11.6 %collective-permute-start.8 = (bf16[48,1920]{1,0:T(8,128)(2,1)S(1)}, bf16[48,1920]{1,0:T(8,128)(2,1)S(1)}, u32[]{:S(2)}, u32[]{:S(2)}) collective-permute-start(bf16[48,1920]{1,0:T(8,128)(2,1)S(1)} %pad_maximum_fusion.5), channel_id=1, source_target_pairs={{0,24},{2,26},{4,28},{6,30},{8,16},{10,18},{12,20},{14,22},{16,8},... | collective-permute-start | bytes 552968 | tf_op jit(solution)/shard_map/ppermute | solution.py:72
  44.8 8.9 %collective-permute-start.9 = (bf16[768,1280]{1,0:T(8,128)(2,1)S(1)}, bf16[768,1280]{1,0:T(8,128)(2,1)}, u32[]{:S(2)}, u32[]{:S(2)}) collective-permute-start(bf16[768,1280]{1,0:T(8,128)(2,1)S(1)} %bitcast.359), channel_id=1, source_target_pairs={{0,1},{1,0},{2,3},{3,2},{4,5},{5,4},{6,7},{7,6},{8,9},{9,8},{10,11... | collective-permute-start | bytes 5898248 | tf_op jit(solution)/shard_map/ppermute | solution.py:76
  46.5 38.2 %collective-permute-start.11 = (bf16[4,48,1920]{2,1,0:T(8,128)(2,1)S(1)}, bf16[4,48,1920]{2,1,0:T(8,128)(2,1)S(1)}, u32[]{:S(2)}, u32[]{:S(2)}) collective-permute-start(bf16[4,48,1920]{2,1,0:T(8,128)(2,1)S(1)} %maximum_select_fusion.12), channel_id=1, source_target_pairs={{0,2},{2,0},{4,6},{6,4},{8,10},{10,8},{12,14},{14,12},{16,18},{18,... | collective-permute-start | bytes 2211848 | tf_op jit(solution)/shard_map/ppermute | solution.py:72
  47.8 37.0 %collective-permute-start.12 = (bf16[4,48,1920]{2,1,0:T(8,128)(2,1)S(1)}, bf16[4,48,1920]{2,1,0:T(8,128)(2,1)}, u32[]{:S(2)}, u32[]{:S(2)}) collective-permute-start(bf16[4,48,1920]{2,1,0:T(8,128)(2,1)S(1)} %maximum_select_fusion.12), channel_id=1, source_target_pairs={{0,4},{2,6},{4,0},{6,2},{8,12},{10,14},{12,8},{14,10},{16,20},{18,... | collective-permute-start | bytes 2211848 | tf_op jit(solution)/shard_map/ppermute | solution.py:72
  48.6 36.1 %collective-permute-start.13 = (bf16[4,48,1920]{2,1,0:T(8,128)(2,1)S(1)}, bf16[4,48,1920]{2,1,0:T(8,128)(2,1)}, u32[]{:S(2)}, u32[]{:S(2)}) collective-permute-start(bf16[4,48,1920]{2,1,0:T(8,128)(2,1)S(1)} %maximum_select_fusion.12), channel_id=1, source_target_pairs={{0,6},{2,4},{4,2},{6,0},{8,14},{10,12},{12,10},{14,8},{16,22},{18,... | collective-permute-start | bytes 2211848 | tf_op jit(solution)/shard_map/ppermute | solution.py:72
  50.1 17.7 %collective-permute-start.10 = (bf16[48,1536]{1,0:T(8,128)(2,1)}, bf16[48,1536]{1,0:T(8,128)(2,1)}, u32[]{:S(2)}, u32[]{:S(2)}) collective-permute-start(bf16[48,1536]{1,0:T(8,128)(2,1)} %convert_element_type.315), channel_id=1, source_target_pairs={{0,8},{2,10},{4,12},{6,14},{8,0},{10,2},{12,4},{14,6},{16,24},{18,... | collective-permute-start | bytes 442376 | tf_op jit(solution)/shard_map/ppermute | solution.py:72
  67.8 17.0 %collective-permute-start.14 = (bf16[48,1536]{1,0:T(8,128)(2,1)S(1)}, bf16[48,1536]{1,0:T(8,128)(2,1)S(1)}, u32[]{:S(2)}, u32[]{:S(2)}) collective-permute-start(bf16[48,1536]{1,0:T(8,128)(2,1)S(1)} %copy-done.41), channel_id=1, source_target_pairs={{0,16},{2,18},{4,20},{6,22},{8,24},{10,26},{12,28},{14,30},{16,0},... | collective-permute-start | bytes 442376 | tf_op jit(solution)/shard_map/ppermute | solution.py:72
  69.2 15.6 %collective-permute-start.15 = (bf16[48,1536]{1,0:T(8,128)(2,1)S(1)}, bf16[48,1536]{1,0:T(8,128)(2,1)S(1)}, u32[]{:S(2)}, u32[]{:S(2)}) collective-permute-start(bf16[48,1536]{1,0:T(8,128)(2,1)S(1)} %copy-done.41), channel_id=1, source_target_pairs={{0,24},{2,26},{4,28},{6,30},{8,16},{10,18},{12,20},{14,22},{16,8},... | collective-permute-start | bytes 442376 | tf_op jit(solution)/shard_map/ppermute | solution.py:72
  88.2 5.4 %collective-permute-start.16 = (bf16[768,1920]{1,0:T(8,128)(2,1)S(1)}, bf16[768,1920]{1,0:T(8,128)(2,1)S(1)}, u32[]{:S(2)}, u32[]{:S(2)}) collective-permute-start(bf16[768,1920]{1,0:T(8,128)(2,1)S(1)} %bitcast.347), channel_id=1, source_target_pairs={{0,1},{1,0},{2,3},{3,2},{4,5},{5,4},{6,7},{7,6},{8,9},{9,8},{10,11... | collective-permute-start | bytes 8847368 | tf_op jit(solution)/shard_map/ppermute | solution.py:76
  89.9 26.8 %collective-permute-start.17 = (bf16[4,48,1536]{2,1,0:T(8,128)(2,1)S(1)}, bf16[4,48,1536]{2,1,0:T(8,128)(2,1)S(1)}, u32[]{:S(2)}, u32[]{:S(2)}) collective-permute-start(bf16[4,48,1536]{2,1,0:T(8,128)(2,1)S(1)} %maximum_select_fusion.14), channel_id=1, source_target_pairs={{0,2},{2,0},{4,6},{6,4},{8,10},{10,8},{12,14},{14,12},{16,18},{18,... | collective-permute-start | bytes 1769480 | tf_op jit(solution)/shard_map/ppermute | solution.py:72
  91.2 26.0 %collective-permute-start.18 = (bf16[4,48,1536]{2,1,0:T(8,128)(2,1)S(1)}, bf16[4,48,1536]{2,1,0:T(8,128)(2,1)S(1)}, u32[]{:S(2)}, u32[]{:S(2)}) collective-permute-start(bf16[4,48,1536]{2,1,0:T(8,128)(2,1)S(1)} %maximum_select_fusion.14), channel_id=1, source_target_pairs={{0,4},{2,6},{4,0},{6,2},{8,12},{10,14},{12,8},{14,10},{16,20},{18,... | collective-permute-start | bytes 1769480 | tf_op jit(solution)/shard_map/ppermute | solution.py:72
  92.0 26.8 %collective-permute-start.19 = (bf16[4,48,1536]{2,1,0:T(8,128)(2,1)S(1)}, bf16[4,48,1536]{2,1,0:T(8,128)(2,1)S(1)}, u32[]{:S(2)}, u32[]{:S(2)}) collective-permute-start(bf16[4,48,1536]{2,1,0:T(8,128)(2,1)S(1)} %maximum_select_fusion.14), channel_id=1, source_target_pairs={{0,6},{2,4},{4,2},{6,0},{8,14},{10,12},{12,10},{14,8},{16,22},{18,... | collective-permute-start | bytes 1769480 | tf_op jit(solution)/shard_map/ppermute | solution.py:72
  119.9 6.9 %collective-permute-start.20 = (bf16[768,1536]{1,0:T(8,128)(2,1)S(1)}, bf16[768,1536]{1,0:T(8,128)(2,1)S(1)}, u32[]{:S(2)}, u32[]{:S(2)}) collective-permute-start(bf16[768,1536]{1,0:T(8,128)(2,1)S(1)} %bitcast.354), channel_id=1, source_target_pairs={{0,1},{1,0},{2,3},{3,2},{4,5},{5,4},{6,7},{7,6},{8,9},{9,8},{10,11... | collective-permute-start | bytes 7077896 | tf_op jit(solution)/shard_map/ppermute | solution.py:76
  143.2 4.9 %collective-permute-start.21 = (bf16[768,1536]{1,0:T(8,128)(2,1)}, bf16[768,1536]{1,0:T(8,128)(2,1)}, u32[]{:S(2)}, u32[]{:S(2)}) collective-permute-start(bf16[768,1536]{1,0:T(8,128)(2,1)} %convolution_convert_fusion.1), channel_id=1, source_target_pairs={{0,1},{1,0},{2,3},{3,2},{4,5},{5,4},{6,7},{7,6},{8,9},{9,8},{10,11... | collective-permute-start | bytes 7077896 | tf_op jit(solution)/shard_map/ppermute | solution.py:76
  152.4 25.0 %collective-permute-start.22 = (bf16[4,48,1536]{2,1,0:T(8,128)(2,1)}, bf16[4,48,1536]{2,1,0:T(8,128)(2,1)S(1)}, u32[]{:S(2)}, u32[]{:S(2)}) collective-permute-start(bf16[4,48,1536]{2,1,0:T(8,128)(2,1)} %get-tuple-element.261), channel_id=1, source_target_pairs={{0,2},{2,0},{4,6},{6,4},{8,10},{10,8},{12,14},{14,12},{16,18},{18,... | collective-permute-start | bytes 1769480 | tf_op jit(solution)/shard_map/ppermute | solution.py:72
  153.2 28.0 %collective-permute-start.23 = (bf16[4,48,1536]{2,1,0:T(8,128)(2,1)}, bf16[4,48,1536]{2,1,0:T(8,128)(2,1)S(1)}, u32[]{:S(2)}, u32[]{:S(2)}) collective-permute-start(bf16[4,48,1536]{2,1,0:T(8,128)(2,1)} %get-tuple-element.262), channel_id=1, source_target_pairs={{0,4},{2,6},{4,0},{6,2},{8,12},{10,14},{12,8},{14,10},{16,20},{18,... | collective-permute-start | bytes 1769480 | tf_op jit(solution)/shard_map/ppermute | solution.py:72
  154.7 26.5 %collective-permute-start.24 = (bf16[4,48,1536]{2,1,0:T(8,128)(2,1)S(1)}, bf16[4,48,1536]{2,1,0:T(8,128)(2,1)S(1)}, u32[]{:S(2)}, u32[]{:S(2)}) collective-permute-start(bf16[4,48,1536]{2,1,0:T(8,128)(2,1)S(1)} %get-tuple-element.263), channel_id=1, source_target_pairs={{0,6},{2,4},{4,2},{6,0},{8,14},{10,12},{12,10},{14,8},{16,22},{18,... | collective-permute-start | bytes 1769480 | tf_op jit(solution)/shard_map/ppermute | solution.py:72
  183.3 8.1 %collective-permute-start.25 = (bf16[2,48,1536]{2,1,0:T(8,128)(2,1)S(1)}, bf16[2,48,1536]{2,1,0:T(8,128)(2,1)S(1)}, u32[]{:S(2)}, u32[]{:S(2)}) collective-permute-start(bf16[2,48,1536]{2,1,0:T(8,128)(2,1)S(1)} %fusion.52), channel_id=1, source_target_pairs={{0,8},{2,10},{4,12},{6,14},{8,0},{10,2},{12,4},{14,6},{16,24},{18,... | collective-permute-start | bytes 884744 | tf_op jit(solution)/shard_map/ppermute | solution.py:72
  192.2 9.0 %collective-permute-start.26 = (bf16[768,1536]{1,0:T(8,128)(2,1)}, bf16[768,1536]{1,0:T(8,128)(2,1)}, u32[]{:S(2)}, u32[]{:S(2)}) collective-permute-start(bf16[768,1536]{1,0:T(8,128)(2,1)} %convolution_convert_fusion), channel_id=1, source_target_pairs={{0,1},{1,0},{2,3},{3,2},{4,5},{5,4},{6,7},{7,6},{8,9},{9,8},{10,11... | collective-permute-start | bytes 7077896 | tf_op jit(solution)/shard_map/ppermute | solution.py:76
  194.6 6.5 %collective-permute-start.27 = (bf16[768,384]{1,0:T(8,128)(2,1)S(1)}, bf16[768,384]{1,0:T(8,128)(2,1)S(1)}, u32[]{:S(2)}, u32[]{:S(2)}) collective-permute-start(bf16[768,384]{1,0:T(8,128)(2,1)S(1)} %convolution_convert_fusion.3), channel_id=1, source_target_pairs={{0,1},{1,0},{2,3},{3,2},{4,5},{5,4},{6,7},{7,6},{8,9},{9,8},{10,11... | collective-permute-start | bytes 1769480 | tf_op jit(solution)/shard_map/ppermute | solution.py:76
  207.7 31.7 %collective-permute-start.29 = (bf16[4,48,1920]{2,1,0:T(8,128)(2,1)}, bf16[4,48,1920]{2,1,0:T(8,128)(2,1)S(1)}, u32[]{:S(2)}, u32[]{:S(2)}) collective-permute-start(bf16[4,48,1920]{2,1,0:T(8,128)(2,1)} %pad_maximum_fusion.1), channel_id=1, source_target_pairs={{0,2},{2,0},{4,6},{6,4},{8,10},{10,8},{12,14},{14,12},{16,18},{18,... | collective-permute-start | bytes 2211848 | tf_op jit(solution)/shard_map/ppermute | solution.py:72
  209.2 34.7 %collective-permute-start.30 = (bf16[4,48,1920]{2,1,0:T(8,128)(2,1)}, bf16[4,48,1920]{2,1,0:T(8,128)(2,1)}, u32[]{:S(2)}, u32[]{:S(2)}) collective-permute-start(bf16[4,48,1920]{2,1,0:T(8,128)(2,1)} %pad_maximum_fusion.2), channel_id=1, source_target_pairs={{0,4},{2,6},{4,0},{6,2},{8,12},{10,14},{12,8},{14,10},{16,20},{18,... | collective-permute-start | bytes 2211848 | tf_op jit(solution)/shard_map/ppermute | solution.py:72
  209.7 34.2 %collective-permute-start.31 = (bf16[4,48,1920]{2,1,0:T(8,128)(2,1)}, bf16[4,48,1920]{2,1,0:T(8,128)(2,1)}, u32[]{:S(2)}, u32[]{:S(2)}) collective-permute-start(bf16[4,48,1920]{2,1,0:T(8,128)(2,1)} %pad_maximum_fusion.3), channel_id=1, source_target_pairs={{0,6},{2,4},{4,2},{6,0},{8,14},{10,12},{12,10},{14,8},{16,22},{18,... | collective-permute-start | bytes 2211848 | tf_op jit(solution)/shard_map/ppermute | solution.py:72
  211.2 24.3 %collective-permute-start.28 = (bf16[48,1536]{1,0:T(8,128)(2,1)S(1)}, bf16[48,1536]{1,0:T(8,128)(2,1)S(1)}, u32[]{:S(2)}, u32[]{:S(2)}) collective-permute-start(bf16[48,1536]{1,0:T(8,128)(2,1)S(1)} %fusion.66), channel_id=1, source_target_pairs={{0,16},{2,18},{4,20},{6,22},{8,24},{10,26},{12,28},{14,30},{16,0},... | collective-permute-start | bytes 442376 | tf_op jit(solution)/shard_map/ppermute | solution.py:72
  243.9 7.5 %collective-permute-start.32 = (bf16[768,1152]{1,0:T(8,128)(2,1)S(1)}, bf16[768,1152]{1,0:T(8,128)(2,1)S(1)}, u32[]{:S(2)}, u32[]{:S(2)}) collective-permute-start(bf16[768,1152]{1,0:T(8,128)(2,1)S(1)} %fusion.1), channel_id=1, source_target_pairs={{0,1},{1,0},{2,3},{3,2},{4,5},{5,4},{6,7},{7,6},{8,9},{9,8},{10,11... | collective-permute-start | bytes 5308424 | tf_op jit(solution)/shard_map/ppermute | solution.py:76
  247.5 14.2 %collective-permute-start.36 = (bf16[2,48,1920]{2,1,0:T(8,128)(2,1)S(1)}, bf16[2,48,1920]{2,1,0:T(8,128)(2,1)S(1)}, u32[]{:S(2)}, u32[]{:S(2)}) collective-permute-start(bf16[2,48,1920]{2,1,0:T(8,128)(2,1)S(1)} %pad_maximum_fusion.4), channel_id=1, source_target_pairs={{0,8},{2,10},{4,12},{6,14},{8,0},{10,2},{12,4},{14,6},{16,24},{18,... | collective-permute-start | bytes 1105928 | tf_op jit(solution)/shard_map/ppermute | solution.py:72
  252.9 8.9 %collective-permute-start.37 = (bf16[48,1536]{1,0:T(8,128)(2,1)S(1)}, bf16[48,1536]{1,0:T(8,128)(2,1)S(1)}, u32[]{:S(2)}, u32[]{:S(2)}) collective-permute-start(bf16[48,1536]{1,0:T(8,128)(2,1)S(1)} %convert_element_type.381), channel_id=1, source_target_pairs={{0,16},{2,18},{4,20},{6,22},{8,24},{10,26},{12,28},{14,30},{16,0},... | collective-permute-start | bytes 442376 | tf_op jit(solution)/shard_map/ppermute | solution.py:72
  255.2 20.4 %collective-permute-start.33 = (bf16[4,48,1152]{2,1,0:T(8,128)(2,1)}, bf16[4,48,1152]{2,1,0:T(8,128)(2,1)}, u32[]{:S(2)}, u32[]{:S(2)}) collective-permute-start(bf16[4,48,1152]{2,1,0:T(8,128)(2,1)} %get-tuple-element.313), channel_id=1, source_target_pairs={{0,2},{2,0},{4,6},{6,4},{8,10},{10,8},{12,14},{14,12},{16,18},{18,... | collective-permute-start | bytes 1327112 | tf_op jit(solution)/shard_map/ppermute | solution.py:72
  255.8 21.6 %collective-permute-start.34 = (bf16[4,48,1152]{2,1,0:T(8,128)(2,1)}, bf16[4,48,1152]{2,1,0:T(8,128)(2,1)}, u32[]{:S(2)}, u32[]{:S(2)}) collective-permute-start(bf16[4,48,1152]{2,1,0:T(8,128)(2,1)} %get-tuple-element.314), channel_id=1, source_target_pairs={{0,4},{2,6},{4,0},{6,2},{8,12},{10,14},{12,8},{14,10},{16,20},{18,... | collective-permute-start | bytes 1327112 | tf_op jit(solution)/shard_map/ppermute | solution.py:72
  257.0 20.4 %collective-permute-start.35 = (bf16[4,48,1152]{2,1,0:T(8,128)(2,1)}, bf16[4,48,1152]{2,1,0:T(8,128)(2,1)}, u32[]{:S(2)}, u32[]{:S(2)}) collective-permute-start(bf16[4,48,1152]{2,1,0:T(8,128)(2,1)} %get-tuple-element.315), channel_id=1, source_target_pairs={{0,6},{2,4},{4,2},{6,0},{8,14},{10,12},{12,10},{14,8},{16,22},{18,... | collective-permute-start | bytes 1327112 | tf_op jit(solution)/shard_map/ppermute | solution.py:72
  264.1 11.5 %collective-permute-start.38 = (bf16[48,1920]{1,0:T(8,128)(2,1)}, bf16[48,1920]{1,0:T(8,128)(2,1)}, u32[]{:S(2)}, u32[]{:S(2)}) collective-permute-start(bf16[48,1920]{1,0:T(8,128)(2,1)} %pad_maximum_fusion.6), channel_id=1, source_target_pairs={{0,16},{2,18},{4,20},{6,22},{8,24},{10,26},{12,28},{14,30},{16,0},... | collective-permute-start | bytes 552968 | tf_op jit(solution)/shard_map/ppermute | solution.py:72
  279.0 10.1 %collective-permute-start.39 = (bf16[48,1152]{1,0:T(8,128)(2,1)S(1)}, bf16[48,1152]{1,0:T(8,128)(2,1)S(1)}, u32[]{:S(2)}, u32[]{:S(2)}) collective-permute-start(bf16[48,1152]{1,0:T(8,128)(2,1)S(1)} %get-tuple-element.325), channel_id=1, source_target_pairs={{0,8},{2,10},{4,12},{6,14},{8,0},{10,2},{12,4},{14,6},{16,24},{18,... | collective-permute-start | bytes 331784 | tf_op jit(solution)/shard_map/ppermute | solution.py:72
  280.7 9.9 %collective-permute-start.40 = (bf16[48,1152]{1,0:T(8,128)(2,1)S(1)}, bf16[48,1152]{1,0:T(8,128)(2,1)S(1)}, u32[]{:S(2)}, u32[]{:S(2)}) collective-permute-start(bf16[48,1152]{1,0:T(8,128)(2,1)S(1)} %get-tuple-element.326), channel_id=1, source_target_pairs={{0,16},{2,18},{4,20},{6,22},{8,24},{10,26},{12,28},{14,30},{16,0},... | collective-permute-start | bytes 331784 | tf_op jit(solution)/shard_map/ppermute | solution.py:72
  281.1 9.5 %collective-permute-start.41 = (bf16[48,1152]{1,0:T(8,128)(2,1)S(1)}, bf16[48,1152]{1,0:T(8,128)(2,1)S(1)}, u32[]{:S(2)}, u32[]{:S(2)}) collective-permute-start(bf16[48,1152]{1,0:T(8,128)(2,1)S(1)} %get-tuple-element.327), channel_id=1, source_target_pairs={{0,24},{2,26},{4,28},{6,30},{8,16},{10,18},{12,20},{14,22},{16,8},... | collective-permute-start | bytes 331784 | tf_op jit(solution)/shard_map/ppermute | solution.py:72
  286.8 13.1 %collective-permute-start.43 = (bf16[2,48,1536]{2,1,0:T(8,128)(2,1)S(1)}, bf16[2,48,1536]{2,1,0:T(8,128)(2,1)S(1)}, u32[]{:S(2)}, u32[]{:S(2)}) collective-permute-start(bf16[2,48,1536]{2,1,0:T(8,128)(2,1)S(1)} %maximum_select_fusion.24), channel_id=1, source_target_pairs={{0,8},{2,10},{4,12},{6,14},{8,0},{10,2},{12,4},{14,6},{16,24},{18,... | collective-permute-start | bytes 884744 | tf_op jit(solution)/shard_map/ppermute | solution.py:72
  287.7 12.2 %collective-permute-start.42 = (bf16[48,1920]{1,0:T(8,128)(2,1)S(1)}, bf16[48,1920]{1,0:T(8,128)(2,1)S(1)}, u32[]{:S(2)}, u32[]{:S(2)}) collective-permute-start(bf16[48,1920]{1,0:T(8,128)(2,1)S(1)} %get-tuple-element.421), channel_id=1, source_target_pairs={{0,16},{2,18},{4,20},{6,22},{8,24},{10,26},{12,28},{14,30},{16,0},... | collective-permute-start | bytes 552968 | tf_op jit(solution)/shard_map/ppermute | solution.py:72
  300.1 6.9 %collective-permute-start.44 = (bf16[48,1152]{1,0:T(8,128)(2,1)S(1)}, bf16[48,1152]{1,0:T(8,128)(2,1)S(1)}, u32[]{:S(2)}, u32[]{:S(2)}) collective-permute-start(bf16[48,1152]{1,0:T(8,128)(2,1)S(1)} %get-tuple-element.348), channel_id=1, source_target_pairs={{0,8},{2,10},{4,12},{6,14},{8,0},{10,2},{12,4},{14,6},{16,24},{18,... | collective-permute-start | bytes 331784 | tf_op jit(solution)/shard_map/ppermute | solution.py:72
  300.2 11.0 %collective-permute-start.45 = (bf16[48,1152]{1,0:T(8,128)(2,1)S(1)}, bf16[48,1152]{1,0:T(8,128)(2,1)S(1)}, u32[]{:S(2)}, u32[]{:S(2)}) collective-permute-start(bf16[48,1152]{1,0:T(8,128)(2,1)S(1)} %get-tuple-element.348), channel_id=1, source_target_pairs={{0,16},{2,18},{4,20},{6,22},{8,24},{10,26},{12,28},{14,30},{16,0},... | collective-permute-start | bytes 331784 | tf_op jit(solution)/shard_map/ppermute | solution.py:72
  302.1 9.2 %collective-permute-start.46 = (bf16[48,1152]{1,0:T(8,128)(2,1)S(1)}, bf16[48,1152]{1,0:T(8,128)(2,1)S(1)}, u32[]{:S(2)}, u32[]{:S(2)}) collective-permute-start(bf16[48,1152]{1,0:T(8,128)(2,1)S(1)} %get-tuple-element.348), channel_id=1, source_target_pairs={{0,24},{2,26},{4,28},{6,30},{8,16},{10,18},{12,20},{14,22},{16,8},... | collective-permute-start | bytes 331784 | tf_op jit(solution)/shard_map/ppermute | solution.py:72
  304.6 12.3 %collective-permute-start.47 = (bf16[2,48,1920]{2,1,0:T(8,128)(2,1)S(1)}, bf16[2,48,1920]{2,1,0:T(8,128)(2,1)S(1)}, u32[]{:S(2)}, u32[]{:S(2)}) collective-permute-start(bf16[2,48,1920]{2,1,0:T(8,128)(2,1)S(1)} %maximum_select_fusion.21), channel_id=1, source_target_pairs={{0,8},{2,10},{4,12},{6,14},{8,0},{10,2},{12,4},{14,6},{16,24},{18,... | collective-permute-start | bytes 1105928 | tf_op jit(solution)/shard_map/ppermute | solution.py:72
  304.6 1.2 collective-permute-start.48
  305.8 12.3 %collective-permute-start.49 = (f32[16,768]{1,0:T(8,128)S(1)}, f32[16,768]{1,0:T(8,128)S(1)}, u32[]{:S(2)}, u32[]{:S(2)}) collective-permute-start(f32[16,768]{1,0:T(8,128)S(1)} %add.371), channel_id=1, source_target_pairs={{0,2},{2,0},{4,6},{6,4},{8,10},{10,8},{12,14},{14,12},{16,18},{18,... | collective-permute-start | bytes 147464 | tf_op jit(solution)/shard_map/ppermute | solution.py:72
  318.1 27.8 %collective-permute-start.50 = (bf16[4,48,1536]{2,1,0:T(8,128)(2,1)S(1)}, bf16[4,48,1536]{2,1,0:T(8,128)(2,1)S(1)}, u32[]{:S(2)}, u32[]{:S(2)}) collective-permute-start(bf16[4,48,1536]{2,1,0:T(8,128)(2,1)S(1)} %bitcast.398), channel_id=1, source_target_pairs={{0,2},{2,0},{4,6},{6,4},{8,10},{10,8},{12,14},{14,12},{16,18},{18,... | collective-permute-start | bytes 1769480 | tf_op jit(solution)/shard_map/ppermute | solution.py:72
  318.8 27.1 %collective-permute-start.51 = (bf16[4,48,1536]{2,1,0:T(8,128)(2,1)S(1)}, bf16[4,48,1536]{2,1,0:T(8,128)(2,1)S(1)}, u32[]{:S(2)}, u32[]{:S(2)}) collective-permute-start(bf16[4,48,1536]{2,1,0:T(8,128)(2,1)S(1)} %bitcast.397), channel_id=1, source_target_pairs={{0,4},{2,6},{4,0},{6,2},{8,12},{10,14},{12,8},{14,10},{16,20},{18,... | collective-permute-start | bytes 1769480 | tf_op jit(solution)/shard_map/ppermute | solution.py:72
  319.8 26.1 %collective-permute-start.52 = (bf16[4,48,1536]{2,1,0:T(8,128)(2,1)S(1)}, bf16[4,48,1536]{2,1,0:T(8,128)(2,1)S(1)}, u32[]{:S(2)}, u32[]{:S(2)}) collective-permute-start(bf16[4,48,1536]{2,1,0:T(8,128)(2,1)S(1)} %bitcast.396), channel_id=1, source_target_pairs={{0,6},{2,4},{4,2},{6,0},{8,14},{10,12},{12,10},{14,8},{16,22},{18,... | collective-permute-start | bytes 1769480 | tf_op jit(solution)/shard_map/ppermute | solution.py:72
  323.9 22.0 %collective-permute-start.53 = (f32[16,768]{1,0:T(8,128)S(1)}, f32[16,768]{1,0:T(8,128)S(1)}, u32[]{:S(2)}, u32[]{:S(2)}) collective-permute-start(f32[16,768]{1,0:T(8,128)S(1)} %add.374), channel_id=1, source_target_pairs={{0,4},{2,6},{4,0},{6,2},{8,12},{10,14},{12,8},{14,10},{16,20},{18,... | collective-permute-start | bytes 147464 | tf_op jit(solution)/shard_map/ppermute | solution.py:72
  350.3 4.9 %collective-permute-start.54 = (f32[768,768]{1,0:T(8,128)}, f32[768,768]{1,0:T(8,128)}, u32[]{:S(2)}, u32[]{:S(2)}) collective-permute-start(f32[768,768]{1,0:T(8,128)} %fusion.87.own_ref), channel_id=1, source_target_pairs={{0,1},{1,0},{2,3},{3,2},{4,5},{5,4},{6,7},{7,6},{8,9},{9,8},{10,11... | collective-permute-start | bytes 7077896 | tf_op jit(solution)/shard_map/ppermute | solution.py:76
  350.3 4.2 %collective-permute-start.55 = (f32[16,768]{1,0:T(8,128)S(1)}, f32[16,768]{1,0:T(8,128)S(1)}, u32[]{:S(2)}, u32[]{:S(2)}) collective-permute-start(f32[16,768]{1,0:T(8,128)S(1)} %add.375), channel_id=1, source_target_pairs={{0,8},{2,10},{4,12},{6,14},{8,0},{10,2},{12,4},{14,6},{16,24},{18,... | collective-permute-start | bytes 147464 | tf_op jit(solution)/shard_map/ppermute | solution.py:72
  355.2 39.0 %copy-start.53 = (f32[6,48]{1,0:T(8,128)S(1)}, f32[6,48]{1,0:T(8,128)}, u32[]{:S(2)}) copy-start(f32[6,48]{1,0:T(8,128)} %param.23) | copy-start | bytes 3460
  355.2 39.0 %copy-start.54 = (f32[6,48]{1,0:T(8,128)S(1)}, f32[6,48]{1,0:T(8,128)}, u32[]{:S(2)}) copy-start(f32[6,48]{1,0:T(8,128)} %param.29) | copy-start | bytes 3460
  355.2 39.0 %copy-start.55 = (f32[6,48]{1,0:T(8,128)S(1)}, f32[6,48]{1,0:T(8,128)}, u32[]{:S(2)}) copy-start(f32[6,48]{1,0:T(8,128)} %param.28) | copy-start | bytes 3460
  388.1 6.1 %collective-permute-start.56 = (f32[16,768]{1,0:T(8,128)S(1)}, f32[16,768]{1,0:T(8,128)S(1)}, u32[]{:S(2)}, u32[]{:S(2)}) collective-permute-start(f32[16,768]{1,0:T(8,128)S(1)} %add.376), channel_id=1, source_target_pairs={{0,16},{2,18},{4,20},{6,22},{8,24},{10,26},{12,28},{14,30},{16,0},... | collective-permute-start | bytes 147464 | tf_op jit(solution)/shard_map/ppermute | solution.py:72
  389.4 6.2 %collective-permute-start.59 = (bf16[48,1536]{1,0:T(8,128)(2,1)S(1)}, bf16[48,1536]{1,0:T(8,128)(2,1)S(1)}, u32[]{:S(2)}, u32[]{:S(2)}) collective-permute-start(bf16[48,1536]{1,0:T(8,128)(2,1)S(1)} %get-tuple-element.418), channel_id=1, source_target_pairs={{0,2},{2,0},{4,6},{6,4},{8,10},{10,8},{12,14},{14,12},{16,18},{18,... | collective-permute-start | bytes 442376 | tf_op jit(solution)/shard_map/ppermute | solution.py:72
  391.1 8.5 %collective-permute-start.58 = (bf16[48,1536]{1,0:T(8,128)(2,1)S(1)}, bf16[48,1536]{1,0:T(8,128)(2,1)S(1)}, u32[]{:S(2)}, u32[]{:S(2)}) collective-permute-start(bf16[48,1536]{1,0:T(8,128)(2,1)S(1)} %get-tuple-element.419), channel_id=1, source_target_pairs={{0,4},{2,6},{4,0},{6,2},{8,12},{10,14},{12,8},{14,10},{16,20},{18,... | collective-permute-start | bytes 442376 | tf_op jit(solution)/shard_map/ppermute | solution.py:72
  391.6 8.0 %collective-permute-start.57 = (bf16[48,1536]{1,0:T(8,128)(2,1)S(1)}, bf16[48,1536]{1,0:T(8,128)(2,1)S(1)}, u32[]{:S(2)}, u32[]{:S(2)}) collective-permute-start(bf16[48,1536]{1,0:T(8,128)(2,1)S(1)} %get-tuple-element.416), channel_id=1, source_target_pairs={{0,6},{2,4},{4,2},{6,0},{8,14},{10,12},{12,10},{14,8},{16,22},{18,... | collective-permute-start | bytes 442376 | tf_op jit(solution)/shard_map/ppermute | solution.py:72
  (62 other events, 385.2 us)

commit v6 on v5

--- a/solution.py
+++ b/solution.py
@@ -586,11 +586,11 @@
 
 
 def lower_kernel(
-    info, vec_ref, xhat_ref, first_ref, second_ref, cot_ref, out_ref, grad_ref, low_ref, sum_ref
+    info, vec_ref, xhat_ref, branch_ref, cot_ref, out_ref, grad_ref, low_ref, sum_ref
 ):
     first = pl.program_id(0) * ROWS
     hidden = xhat_ref[...] * vec_ref[3:4, :] + vec_ref[4:5, :]
-    xhat, rstd = norm_parts(hidden + (first_ref[...] + second_ref[...] + vec_ref[9:10, :]))
+    xhat, rstd = norm_parts(hidden + (branch_ref[...] + vec_ref[9:10, :]))
     gain = vec_ref[10:11, :]
     out_ref[...] = (xhat * gain + vec_ref[11:12, :]).astype(jnp.bfloat16)
     limit = info[INFO + lax.div(first, SEQ)]
@@ -686,17 +686,17 @@
     )
 
 
-def lower_rows(info, vec, xhat, first, second, cotangent):
+def lower_rows(info, vec, xhat, branch, cotangent):
     low, full = jnp.bfloat16, jnp.float32
     return row_call(
         lower_kernel,
         "lower_rows",
-        [whole_spec()] + [row_spec(D)] * 4,
-        first.shape[0],
+        [whole_spec()] + [row_spec(D)] * 3,
+        branch.shape[0],
         [(D, low), (D, full), (D, low)],
         [D],
         4 << 30,
-        (info, vec, xhat, first, second, cotangent),
+        (info, vec, xhat, branch, cotangent),
     )
 
 
@@ -879,10 +879,9 @@
     near, far = size.bit_length() - 3, size.bit_length() - 2
     steps = [1 << near, 1 << far, 3 << near]
     first_pieces = send_high(first_block, size)
-    second_pieces = [second_block, flip(second_block, steps[0], size)]
-    first_pieces, second_pieces, third_block = together(first_pieces, second_pieces, third_block)
+    first_pieces, second_block, third_block = together(first_pieces, second_block, third_block)
     first_pieces = send_low(sort_high(first_pieces, size), size)
-    second_pieces += [flip(second_pieces[0], step, size) for step in steps[1:]]
+    second_pieces = send_high(second_block, size)
     first_pieces, second_pieces, third_block = together(first_pieces, second_pieces, third_block)
     first_own = sort_low(first_pieces)
     first_other = swap_cores(first_own)
@@ -918,7 +917,7 @@
     branch = matmul_nt(act_own, third_own)
     branch, third_other = together(branch, third_other)
     layer_out, top_grad, branch_low, high_sums = lower_rows(
-        info, vec, xhat_one, branch, matmul_nt(act_other, third_other), cotangent
+        info, vec, xhat_one, branch + matmul_nt(act_other, third_other), cotangent
     )
 
     leaving = matmul_tn(branch_low, act_other).astype(low)

time: 409 us -> 405 us (level)
  transfers between devices with their start and end apart: 60 -> 60, of which waited for: 25 -> 25; matrix products, arithmetic and copies ran while one was open for 16% -> 16% of each run, Pallas kernels for 20% -> 21%
where the time goes in v6:
time: 405 us; the launch traced here: 399 us
  Pallas kernels  122 us (30%)
  waiting for transfers between devices  92.6 us (23%)
  starting transfers between devices  70.1 us (17%)
  matrix products  49.5 us (12%)
  other arithmetic  46.6 us (12%)
  local copies, waits for them, and re-layouts  15.2 us (4%)
    ppermute x51, waiting for transfers between devices, flip(): lax.ppermute(by_rows(values), 'fsdp', [(i, i ^ mask) for i in range(size)])  91.1 us
    ppermute x51, starting transfers between devices, flip(): lax.ppermute(by_rows(values), 'fsdp', [(i, i ^ mask) for i in range(size)])  69.3 us
    pallas_call x3, Pallas kernels, row_call(): pl.pallas_call(kernel, grid=(rows // ROWS,), in_specs=[pl.BlockSpec(memor...  50.3 us
    pallas_call x1, Pallas kernels, polar_rows(): pl.pallas_call(polar_kernel, in_specs=[pl.BlockSpec(memory_space=pltpu.SM...  32.8 us
    dot_general x8, matrix products, matmul_tn(): lax.dot_general(former, latter, (((0,), (0,)), ((), ())), preferred_eleme...  25 us
    pallas_call x1, Pallas kernels, attention_pull(): pl.pallas_call(attention_pull_kernel, grid_spec=pltpu.PrefetchScalarGridS...  21.7 us
    dot_general x5, matrix products, matmul_nt(): lax.dot_general(former, latter, (((1,), (1,)), ((), ())), preferred_eleme...  16.6 us
    pallas_call x1, Pallas kernels, attention(): pl.pallas_call(attention_kernel, grid_spec=pltpu.PrefetchScalarGridSpec(n...  14 us
  transfers between devices with their start and end apart: 60, of which 25 were waited for; matrix products, arithmetic and copies ran while one was open for 16% of the time, Pallas kernels for 21%

profile of v6, /device:TPU:0, one launch (start us, length us, event | category | flops | bytes accessed | tf_op | source)
XLA Modules:
  0.0 398.7 jit_solution(2972223040992786609)
XLA Ops:
  3.5 3.1 collective-permute-start
  6.6 2.6 collective-permute-start.1
  11.8 7.1 %collective-permute-done.1 = bf16[48,1280]{1,0:T(8,128)(2,1)S(1)} collective-permute-done((bf16[48,1280]{1,0:T(8,128)(2,1)S(1)}, bf16[48,1280]{1,0:T(8,128)(2,1)S(1)}, u32[]{:S(2)}, u32[]{:S(2)}) %collective-permute-start.1) | collective-permute-done | bytes 122912 | tf_op jit(solution)/shard_map/ppermute | solution.py:72
  22.6 1.9 collective-permute-start.6
  25.6 3.8 collective-permute-done.6
  29.4 2.7 collective-permute-start.8
  32.1 7.5 %collective-permute-done.7 = bf16[48,1920]{1,0:T(8,128)(2,1)S(1)} collective-permute-done((bf16[48,1920]{1,0:T(8,128)(2,1)S(1)}, bf16[48,1920]{1,0:T(8,128)(2,1)S(1)}, u32[]{:S(2)}, u32[]{:S(2)}) %collective-permute-start.7) | collective-permute-done | bytes 184352 | tf_op jit(solution)/shard_map/ppermute | solution.py:72
  39.5 1.9 collective-permute-done.4
  47.5 2.8 collective-permute-start.10
  50.3 1.9 vector_tables.1
  53.8 4.3 %fusion.2 = bf16[1024,1152]{1,0:T(8,128)(2,1)S(1)} fusion(f32[1152]{0:T(1024)S(1)} %slice_reduce_fusion.1, bf16[1024,768]{1,0:T(8,128)(2,1)} %x_ref.1, bf16[768,1280]{1,0:T(8,128)(2,1)} %bitcast.361), kind=kOutput, calls=%fused_computation.13 | convolution fusion | flops 1814298624 | bytes 5706240 | tf_op jit(solution)/shard_map/dot_general | solution.py:52
  58.1 3.7 fusion
  61.8 2.5 pad_maximum_fusion.query_ref.key_ref.value_ref
  67.3 14.0 %attention.1 = (bf16[1024,768]{1,0:T(8,128)(2,1)S(1)}, f32[2,6,2,512]{3,2,1,0:T(2,128)S(1)}) custom-call(s32[5]{0:T(128)S(1)} %copy-done.9, bf16[1024,2304]{1,0:T(8,128)(2,1)} %pad_maximum_fusion.query_ref.key_ref.value_ref, bf16[1024,2304]{1,0:T(8,128)(2,1)} %pad_maximum_fusion.query_ref.key_ref.value_ref, ...), custom_call_target="tpu_custom_call" | custom-call | flops 1048576 | bytes 65536 | tf_op jit(solution)/shard_map/attention/pallas_call | solution.py:426
  81.7 2.3 maximum_select_fusion.4
  90.2 1.6 copy-done.16
  91.8 21.6 %raise_rows.1 = (f32[1024,768]{1,0:T(8,128)}, f32[1024,128]{1,0:T(8,128)S(1)}, bf16[1024,768]{1,0:T(8,128)(2,1)}, bf16[1024,1536]{1,0:T(8,128)(2,1)}, bf16[1024,...) custom-call(s32[5]{0:T(128)S(1)} %copy-done.9, f32[16,768]{1,0:T(8,128)S(1)} %copy-done.6, f32[8,3072]{1,0:T(8,128)S(1)} %copy-done.7, ...), custom_call_target="tpu_custom_call" | custom-call | flops 1048576 | bytes 65536 | tf_op jit(solution)/shard_map/raise_rows/pallas_call | solution.py:662
  113.8 1.6 collective-permute-done.19
  117.0 2.4 copy-done.21
  119.4 2.6 fusion.83
  123.4 2.6 fusion.84
  126.1 2.1 add.319.branch_ref
  128.1 7.1 %lower_rows.1 = (bf16[1024,768]{1,0:T(8,128)(2,1)}, f32[1024,768]{1,0:T(8,128)}, bf16[1024,768]{1,0:T(8,128)(2,1)S(1)}, f32[8,768]{1,0:T(8,128)S(1)}) custom-call(s32[5]{0:T(128)S(1)} %copy-done.9, f32[16,768]{1,0:T(8,128)S(1)} %copy-done.6, f32[1024,768]{1,0:T(8,128)} %get-tuple-element.225.xhat_ref, f32[1024,768]{1,0:T(8,128)} %add.319.branch_ref, ...), custom_call_target="tpu_custom_call" | custom-call | flops 1048576 | bytes 65536 | tf_op jit(solution)/shard_map/lower_rows/pallas_call | solution.py:662
  135.2 4.0 %convolution_convert_fusion.1 = bf16[768,1536]{1,0:T(8,128)(2,1)} fusion(bf16[1024,768]{1,0:T(8,128)(2,1)S(1)} %get-tuple-element.251.low_ref, bf16[1024,1536]{1,0:T(8,128)(2,1)S(1)} %copy-done.58), kind=kOutput, calls=%fused_computation.7 | convolution fusion | flops 2417098752 | bytes 7077888 | tf_op jit(solution)/shard_map/dot_general | solution.py:56
  139.2 4.5 %fusion.85 = f32[768,1536]{1,0:T(8,128)S(1)} fusion(bf16[1024,768]{1,0:T(8,128)(2,1)S(1)} %get-tuple-element.251.low_ref, bf16[1024,1536]{1,0:T(8,128)(2,1)} %get-tuple-element.232), kind=kOutput, calls=%fused_computation.194 | convolution fusion | flops 2415919104 | bytes 9437184 | tf_op jit(solution)/shard_map/dot_general | solution.py:56
  144.1 4.3 %fusion.45 = (bf16[4,48,1536]{2,1,0:T(8,128)(2,1)S(1)}, bf16[4,48,1536]{2,1,0:T(8,128)(2,1)}, bf16[4,48,1536]{2,1,0:T(8,128)(2,1)}) fusion(f32[4,4,48,1536]{3,2,1,0:T(8,128)S(1)} %bitcast.352, s32[]{:T(128)S(6)} %select_n.517, bf16[4,4,48,1536]{3,2,1,0:T(8,128)(2,1)} %bitcast.33, s32[]{:T(128)S(6)} %select_n.516, s32[]{:T(128)S(6)} %select_n.515), kind=kLoop, calls=%fused_computation.85 | loop fusion | flops 2654208 | bytes 7077900 | tf_op jit(solution)/shard_map/convert_element_type | solution.py:142
  151.9 21.7 %pull_rows.1 = (bf16[1024,1536]{1,0:T(8,128)(2,1)}, bf16[1024,1536]{1,0:T(8,128)(2,1)}, f32[1024,768]{1,0:T(8,128)}, bf16[1024,768]{1,0:T(8,128)(2,1)}, bf16[102...) custom-call(s32[5]{0:T(128)S(1)} %copy-done.9, f32[16,768]{1,0:T(8,128)S(1)} %copy-done.6, ...), custom_call_target="tpu_custom_call" | custom-call | flops 1048576 | bytes 65536 | tf_op jit(solution)/shard_map/pull_rows/pallas_call | solution.py:662
  173.6 3.6 collective-permute-done.23
  177.3 2.0 fusion.27
  180.5 3.9 convolution_convert_fusion
  184.4 3.1 collective-permute-done.25
  188.2 2.4 convolution_convert_fusion.3
  194.4 2.7 fusion.86
  198.0 2.9 fusion.48
  207.2 2.6 collective-permute-start.28
  209.9 21.7 %attention_pull.1 = (bf16[1024,1152]{1,0:T(8,128)(2,1)}, bf16[1024,1152]{1,0:T(8,128)(2,1)}, f32[2,6,2,128]{3,2,1,0:T(2,128)S(1)}) custom-call(s32[5]{0:T(128)S(1)} %copy-done.9, bf16[1024,2304]{1,0:T(8,128)(2,1)} %pad_maximum_fusion.query_ref.key_ref.value_ref, bf16[1024,2304]{1,0:T(8,128)(2,1)} %pad_maximum_fusion.query_ref.key_ref.value_ref, ...), custom_call_target="tpu_custom_call" | custom-call | flops 1048576 | bytes 65536 | tf_op jit(solution)/shard_map/attention_pull/pallas_call | solution.py:447
  231.6 3.9 fusion.1
  235.5 4.4 %collective-permute-done.30 = bf16[4,48,1920]{2,1,0:T(8,128)(2,1)} collective-permute-done((bf16[4,48,1920]{2,1,0:T(8,128)(2,1)}, bf16[4,48,1920]{2,1,0:T(8,128)(2,1)}, u32[]{:S(2)}, u32[]{:S(2)}) %collective-permute-start.30) | collective-permute-done | bytes 737312 | tf_op jit(solution)/shard_map/ppermute | solution.py:72
  239.9 2.1 fusion.20
  244.9 2.4 convolution_bitcast_fusion
  248.9 2.4 collective-permute-start.37
  253.1 1.7 collective-permute-start.35
  254.8 3.0 collective-permute-done.36
  262.3 1.6 vector_grads.1
  263.9 7.7 %collective-permute-done.38 = bf16[48,1920]{1,0:T(8,128)(2,1)} collective-permute-done((bf16[48,1920]{1,0:T(8,128)(2,1)}, bf16[48,1920]{1,0:T(8,128)(2,1)}, u32[]{:S(2)}, u32[]{:S(2)}) %collective-permute-start.38) | collective-permute-done | bytes 184352 | tf_op jit(solution)/shard_map/ppermute | solution.py:72
  271.6 1.8 collective-permute-done.34
  275.0 1.8 collective-permute-start.39
  277.2 2.3 collective-permute-start.41
  280.9 1.8 fusion.81
  285.1 1.6 collective-permute-done.40
  286.7 9.2 %collective-permute-done.42 = bf16[48,1920]{1,0:T(8,128)(2,1)S(1)} collective-permute-done((bf16[48,1920]{1,0:T(8,128)(2,1)S(1)}, bf16[48,1920]{1,0:T(8,128)(2,1)S(1)}, u32[]{:S(2)}, u32[]{:S(2)}) %collective-permute-start.42) | collective-permute-done | bytes 184352 | tf_op jit(solution)/shard_map/ppermute | solution.py:72
  296.2 1.8 collective-permute-start.45
  298.0 2.6 collective-permute-start.46
  303.0 4.2 %collective-permute-done.45 = bf16[48,1152]{1,0:T(8,128)(2,1)S(1)} collective-permute-done((bf16[48,1152]{1,0:T(8,128)(2,1)S(1)}, bf16[48,1152]{1,0:T(8,128)(2,1)S(1)}, u32[]{:S(2)}, u32[]{:S(2)}) %collective-permute-start.45) | collective-permute-done | bytes 110624 | tf_op jit(solution)/shard_map/ppermute | solution.py:72
  307.2 5.6 %collective-permute-done.47 = bf16[2,48,1920]{2,1,0:T(8,128)(2,1)S(1)} collective-permute-done((bf16[2,48,1920]{2,1,0:T(8,128)(2,1)S(1)}, bf16[2,48,1920]{2,1,0:T(8,128)(2,1)S(1)}, u32[]{:S(2)}, u32[]{:S(2)}) %collective-permute-start.47) | collective-permute-done | bytes 368672 | tf_op jit(solution)/shard_map/ppermute | solution.py:72
  315.9 1.8 collective-permute-start.52
  317.7 2.2 fusion.6
  320.8 5.7 %add_add_fusion = f32[1024,768]{1,0:T(8,128)} fusion(f32[1024,768]{1,0:T(8,128)S(1)} %copy-done.57, f32[1024,768]{1,0:T(8,128)S(1)} %fusion.6, bf16[1024,1152]{1,0:T(8,128)(2,1)S(1)} %copy-done.60, bf16[768,1280]{1,0:T(8,128)(2,1)} %collective-permute-done.9.other_ref), kind=kOutput, calls=%fused_computation.10 | convolution fusion | flops 1813512192 | bytes 13565952 | tf_op jit(solution)/shard_map/dot_general | solution.py:62
  326.4 15.4 %collective-permute-done.53 = f32[16,768]{1,0:T(8,128)S(1)} collective-permute-done((f32[16,768]{1,0:T(8,128)S(1)}, f32[16,768]{1,0:T(8,128)S(1)}, u32[]{:S(2)}, u32[]{:S(2)}) %collective-permute-start.53) | collective-permute-done | bytes 49184 | tf_op jit(solution)/shard_map/ppermute | solution.py:72
  342.9 3.4 fusion.87.own_ref
  347.6 2.9 collective-permute-done.55
  351.3 32.8 %polar_rows.1 = bf16[192,1536]{1,0:T(8,128)(2,1)S(1)} custom-call(s32[1]{0:T(128)} %bitcast.96.start_ref, f32[768,768]{1,0:T(8,128)} %fusion.87.own_ref, f32[768,768]{1,0:T(8,128)} %collective-permute-done.54.other_ref, bf16[768,1536]{1,0:T(8,128)(2,1)S(1)} %bitcast.345), custom_call_target="tpu_custom_call" | custom-call | tf_op jit(solution)/shard_map/polar_rows/pallas_call | solution.py:825
  385.4 1.7 collective-permute-start.59
  391.7 4.0 collective-permute-done.58
  (316 shorter events, 80.9 us)
Async XLA Ops:
  0.7 41.7 %copy-start = (s32[1,2]{1,0:T(1,128)S(1)}, s32[1,2]{1,0:T(1,128)}, u32[]{:S(2)}) copy-start(s32[1,2]{1,0:T(1,128)} %param.17) | copy-start | bytes 28
  3.5 8.3 %collective-permute-start = (bf16[48,1280]{1,0:T(8,128)(2,1)S(1)}, bf16[48,1280]{1,0:T(8,128)(2,1)S(1)}, u32[]{:S(2)}, u32[]{:S(2)}) collective-permute-start(bf16[48,1280]{1,0:T(8,128)(2,1)S(1)} %fusion.71), channel_id=1, source_target_pairs={{0,8},{2,10},{4,12},{6,14},{8,0},{10,2},{12,4},{14,6},{16,24},{18,... | collective-permute-start | bytes 368648 | tf_op jit(solution)/shard_map/ppermute | solution.py:72
  6.6 12.3 %collective-permute-start.1 = (bf16[48,1280]{1,0:T(8,128)(2,1)S(1)}, bf16[48,1280]{1,0:T(8,128)(2,1)S(1)}, u32[]{:S(2)}, u32[]{:S(2)}) collective-permute-start(bf16[48,1280]{1,0:T(8,128)(2,1)S(1)} %fusion.71), channel_id=1, source_target_pairs={{0,16},{2,18},{4,20},{6,22},{8,24},{10,26},{12,28},{14,30},{16,0},... | collective-permute-start | bytes 368648 | tf_op jit(solution)/shard_map/ppermute | solution.py:72
  9.2 9.7 %collective-permute-start.2 = (bf16[48,1280]{1,0:T(8,128)(2,1)S(1)}, bf16[48,1280]{1,0:T(8,128)(2,1)S(1)}, u32[]{:S(2)}, u32[]{:S(2)}) collective-permute-start(bf16[48,1280]{1,0:T(8,128)(2,1)S(1)} %fusion.71), channel_id=1, source_target_pairs={{0,24},{2,26},{4,28},{6,30},{8,16},{10,18},{12,20},{14,22},{16,8},... | collective-permute-start | bytes 368648 | tf_op jit(solution)/shard_map/ppermute | solution.py:72
  19.1 20.5 %collective-permute-start.3 = (bf16[4,48,1280]{2,1,0:T(8,128)(2,1)S(1)}, bf16[4,48,1280]{2,1,0:T(8,128)(2,1)S(1)}, u32[]{:S(2)}, u32[]{:S(2)}) collective-permute-start(bf16[4,48,1280]{2,1,0:T(8,128)(2,1)S(1)} %maximum_select_fusion.17), channel_id=1, source_target_pairs={{0,2},{2,0},{4,6},{6,4},{8,10},{10,8},{12,14},{14,12},{16,18},{18,... | collective-permute-start | bytes 1474568 | tf_op jit(solution)/shard_map/ppermute | solution.py:72
  20.6 20.9 %collective-permute-start.4 = (bf16[4,48,1280]{2,1,0:T(8,128)(2,1)S(1)}, bf16[4,48,1280]{2,1,0:T(8,128)(2,1)S(1)}, u32[]{:S(2)}, u32[]{:S(2)}) collective-permute-start(bf16[4,48,1280]{2,1,0:T(8,128)(2,1)S(1)} %maximum_select_fusion.17), channel_id=1, source_target_pairs={{0,4},{2,6},{4,0},{6,2},{8,12},{10,14},{12,8},{14,10},{16,20},{18,... | collective-permute-start | bytes 1474568 | tf_op jit(solution)/shard_map/ppermute | solution.py:72
  22.1 19.3 %collective-permute-start.5 = (bf16[4,48,1280]{2,1,0:T(8,128)(2,1)S(1)}, bf16[4,48,1280]{2,1,0:T(8,128)(2,1)S(1)}, u32[]{:S(2)}, u32[]{:S(2)}) collective-permute-start(bf16[4,48,1280]{2,1,0:T(8,128)(2,1)S(1)} %maximum_select_fusion.17), channel_id=1, source_target_pairs={{0,6},{2,4},{4,2},{6,0},{8,14},{10,12},{12,10},{14,8},{16,22},{18,... | collective-permute-start | bytes 1474568 | tf_op jit(solution)/shard_map/ppermute | solution.py:72
  22.6 6.8 %collective-permute-start.6 = (bf16[48,1920]{1,0:T(8,128)(2,1)S(1)}, bf16[48,1920]{1,0:T(8,128)(2,1)S(1)}, u32[]{:S(2)}, u32[]{:S(2)}) collective-permute-start(bf16[48,1920]{1,0:T(8,128)(2,1)S(1)} %pad_maximum_fusion.5), channel_id=1, source_target_pairs={{0,8},{2,10},{4,12},{6,14},{8,0},{10,2},{12,4},{14,6},{16,24},{18,... | collective-permute-start | bytes 552968 | tf_op jit(solution)/shard_map/ppermute | solution.py:72
  24.5 15.0 %collective-permute-start.7 = (bf16[48,1920]{1,0:T(8,128)(2,1)S(1)}, bf16[48,1920]{1,0:T(8,128)(2,1)S(1)}, u32[]{:S(2)}, u32[]{:S(2)}) collective-permute-start(bf16[48,1920]{1,0:T(8,128)(2,1)S(1)} %pad_maximum_fusion.5), channel_id=1, source_target_pairs={{0,16},{2,18},{4,20},{6,22},{8,24},{10,26},{12,28},{14,30},{16,0},... | collective-permute-start | bytes 552968 | tf_op jit(solution)/shard_map/ppermute | solution.py:72
  29.4 10.1 %collective-permute-start.8 = (bf16[48,1920]{1,0:T(8,128)(2,1)S(1)}, bf16[48,1920]{1,0:T(8,128)(2,1)S(1)}, u32[]{:S(2)}, u32[]{:S(2)}) collective-permute-start(bf16[48,1920]{1,0:T(8,128)(2,1)S(1)} %pad_maximum_fusion.5), channel_id=1, source_target_pairs={{0,24},{2,26},{4,28},{6,30},{8,16},{10,18},{12,20},{14,22},{16,8},... | collective-permute-start | bytes 552968 | tf_op jit(solution)/shard_map/ppermute | solution.py:72
  42.2 8.1 %collective-permute-start.9 = (bf16[768,1280]{1,0:T(8,128)(2,1)S(1)}, bf16[768,1280]{1,0:T(8,128)(2,1)}, u32[]{:S(2)}, u32[]{:S(2)}) collective-permute-start(bf16[768,1280]{1,0:T(8,128)(2,1)S(1)} %bitcast.359), channel_id=1, source_target_pairs={{0,1},{1,0},{2,3},{3,2},{4,5},{5,4},{6,7},{7,6},{8,9},{9,8},{10,11... | collective-permute-start | bytes 5898248 | tf_op jit(solution)/shard_map/ppermute | solution.py:76
  43.9 37.5 %collective-permute-start.11 = (bf16[4,48,1920]{2,1,0:T(8,128)(2,1)S(1)}, bf16[4,48,1920]{2,1,0:T(8,128)(2,1)S(1)}, u32[]{:S(2)}, u32[]{:S(2)}) collective-permute-start(bf16[4,48,1920]{2,1,0:T(8,128)(2,1)S(1)} %maximum_select_fusion.12), channel_id=1, source_target_pairs={{0,2},{2,0},{4,6},{6,4},{8,10},{10,8},{12,14},{14,12},{16,18},{18,... | collective-permute-start | bytes 2211848 | tf_op jit(solution)/shard_map/ppermute | solution.py:72
  45.2 36.2 %collective-permute-start.12 = (bf16[4,48,1920]{2,1,0:T(8,128)(2,1)S(1)}, bf16[4,48,1920]{2,1,0:T(8,128)(2,1)}, u32[]{:S(2)}, u32[]{:S(2)}) collective-permute-start(bf16[4,48,1920]{2,1,0:T(8,128)(2,1)S(1)} %maximum_select_fusion.12), channel_id=1, source_target_pairs={{0,4},{2,6},{4,0},{6,2},{8,12},{10,14},{12,8},{14,10},{16,20},{18,... | collective-permute-start | bytes 2211848 | tf_op jit(solution)/shard_map/ppermute | solution.py:72
  46.0 35.4 %collective-permute-start.13 = (bf16[4,48,1920]{2,1,0:T(8,128)(2,1)S(1)}, bf16[4,48,1920]{2,1,0:T(8,128)(2,1)}, u32[]{:S(2)}, u32[]{:S(2)}) collective-permute-start(bf16[4,48,1920]{2,1,0:T(8,128)(2,1)S(1)} %maximum_select_fusion.12), channel_id=1, source_target_pairs={{0,6},{2,4},{4,2},{6,0},{8,14},{10,12},{12,10},{14,8},{16,22},{18,... | collective-permute-start | bytes 2211848 | tf_op jit(solution)/shard_map/ppermute | solution.py:72
  47.5 16.9 %collective-permute-start.10 = (bf16[48,1536]{1,0:T(8,128)(2,1)}, bf16[48,1536]{1,0:T(8,128)(2,1)}, u32[]{:S(2)}, u32[]{:S(2)}) collective-permute-start(bf16[48,1536]{1,0:T(8,128)(2,1)} %convert_element_type.315), channel_id=1, source_target_pairs={{0,8},{2,10},{4,12},{6,14},{8,0},{10,2},{12,4},{14,6},{16,24},{18,... | collective-permute-start | bytes 442376 | tf_op jit(solution)/shard_map/ppermute | solution.py:72
  64.3 17.1 %collective-permute-start.14 = (bf16[48,1536]{1,0:T(8,128)(2,1)S(1)}, bf16[48,1536]{1,0:T(8,128)(2,1)S(1)}, u32[]{:S(2)}, u32[]{:S(2)}) collective-permute-start(bf16[48,1536]{1,0:T(8,128)(2,1)S(1)} %copy-done.41), channel_id=1, source_target_pairs={{0,16},{2,18},{4,20},{6,22},{8,24},{10,26},{12,28},{14,30},{16,0},... | collective-permute-start | bytes 442376 | tf_op jit(solution)/shard_map/ppermute | solution.py:72
  65.8 15.6 %collective-permute-start.15 = (bf16[48,1536]{1,0:T(8,128)(2,1)S(1)}, bf16[48,1536]{1,0:T(8,128)(2,1)S(1)}, u32[]{:S(2)}, u32[]{:S(2)}) collective-permute-start(bf16[48,1536]{1,0:T(8,128)(2,1)S(1)} %copy-done.41), channel_id=1, source_target_pairs={{0,24},{2,26},{4,28},{6,30},{8,16},{10,18},{12,20},{14,22},{16,8},... | collective-permute-start | bytes 442376 | tf_op jit(solution)/shard_map/ppermute | solution.py:72
  84.8 5.4 %collective-permute-start.16 = (bf16[768,1920]{1,0:T(8,128)(2,1)S(1)}, bf16[768,1920]{1,0:T(8,128)(2,1)S(1)}, u32[]{:S(2)}, u32[]{:S(2)}) collective-permute-start(bf16[768,1920]{1,0:T(8,128)(2,1)S(1)} %bitcast.347), channel_id=1, source_target_pairs={{0,1},{1,0},{2,3},{3,2},{4,5},{5,4},{6,7},{7,6},{8,9},{9,8},{10,11... | collective-permute-start | bytes 8847368 | tf_op jit(solution)/shard_map/ppermute | solution.py:76
  86.5 26.8 %collective-permute-start.17 = (bf16[4,48,1536]{2,1,0:T(8,128)(2,1)S(1)}, bf16[4,48,1536]{2,1,0:T(8,128)(2,1)S(1)}, u32[]{:S(2)}, u32[]{:S(2)}) collective-permute-start(bf16[4,48,1536]{2,1,0:T(8,128)(2,1)S(1)} %maximum_select_fusion.14), channel_id=1, source_target_pairs={{0,2},{2,0},{4,6},{6,4},{8,10},{10,8},{12,14},{14,12},{16,18},{18,... | collective-permute-start | bytes 1769480 | tf_op jit(solution)/shard_map/ppermute | solution.py:72
  87.8 26.0 %collective-permute-start.18 = (bf16[4,48,1536]{2,1,0:T(8,128)(2,1)S(1)}, bf16[4,48,1536]{2,1,0:T(8,128)(2,1)S(1)}, u32[]{:S(2)}, u32[]{:S(2)}) collective-permute-start(bf16[4,48,1536]{2,1,0:T(8,128)(2,1)S(1)} %maximum_select_fusion.14), channel_id=1, source_target_pairs={{0,4},{2,6},{4,0},{6,2},{8,12},{10,14},{12,8},{14,10},{16,20},{18,... | collective-permute-start | bytes 1769480 | tf_op jit(solution)/shard_map/ppermute | solution.py:72
  88.6 26.8 %collective-permute-start.19 = (bf16[4,48,1536]{2,1,0:T(8,128)(2,1)S(1)}, bf16[4,48,1536]{2,1,0:T(8,128)(2,1)S(1)}, u32[]{:S(2)}, u32[]{:S(2)}) collective-permute-start(bf16[4,48,1536]{2,1,0:T(8,128)(2,1)S(1)} %maximum_select_fusion.14), channel_id=1, source_target_pairs={{0,6},{2,4},{4,2},{6,0},{8,14},{10,12},{12,10},{14,8},{16,22},{18,... | collective-permute-start | bytes 1769480 | tf_op jit(solution)/shard_map/ppermute | solution.py:72
  116.9 5.2 %collective-permute-start.20 = (bf16[768,1536]{1,0:T(8,128)(2,1)S(1)}, bf16[768,1536]{1,0:T(8,128)(2,1)S(1)}, u32[]{:S(2)}, u32[]{:S(2)}) collective-permute-start(bf16[768,1536]{1,0:T(8,128)(2,1)S(1)} %bitcast.354), channel_id=1, source_target_pairs={{0,1},{1,0},{2,3},{3,2},{4,5},{5,4},{6,7},{7,6},{8,9},{9,8},{10,11... | collective-permute-start | bytes 7077896 | tf_op jit(solution)/shard_map/ppermute | solution.py:76
  139.2 4.9 %collective-permute-start.21 = (bf16[768,1536]{1,0:T(8,128)(2,1)}, bf16[768,1536]{1,0:T(8,128)(2,1)}, u32[]{:S(2)}, u32[]{:S(2)}) collective-permute-start(bf16[768,1536]{1,0:T(8,128)(2,1)} %convolution_convert_fusion.1), channel_id=1, source_target_pairs={{0,1},{1,0},{2,3},{3,2},{4,5},{5,4},{6,7},{7,6},{8,9},{9,8},{10,11... | collective-permute-start | bytes 7077896 | tf_op jit(solution)/shard_map/ppermute | solution.py:76
  148.4 25.2 %collective-permute-start.22 = (bf16[4,48,1536]{2,1,0:T(8,128)(2,1)}, bf16[4,48,1536]{2,1,0:T(8,128)(2,1)S(1)}, u32[]{:S(2)}, u32[]{:S(2)}) collective-permute-start(bf16[4,48,1536]{2,1,0:T(8,128)(2,1)} %get-tuple-element.259), channel_id=1, source_target_pairs={{0,2},{2,0},{4,6},{6,4},{8,10},{10,8},{12,14},{14,12},{16,18},{18,... | collective-permute-start | bytes 1769480 | tf_op jit(solution)/shard_map/ppermute | solution.py:72
  149.2 28.0 %collective-permute-start.23 = (bf16[4,48,1536]{2,1,0:T(8,128)(2,1)}, bf16[4,48,1536]{2,1,0:T(8,128)(2,1)S(1)}, u32[]{:S(2)}, u32[]{:S(2)}) collective-permute-start(bf16[4,48,1536]{2,1,0:T(8,128)(2,1)} %get-tuple-element.260), channel_id=1, source_target_pairs={{0,4},{2,6},{4,0},{6,2},{8,12},{10,14},{12,8},{14,10},{16,20},{18,... | collective-permute-start | bytes 1769480 | tf_op jit(solution)/shard_map/ppermute | solution.py:72
  150.7 26.5 %collective-permute-start.24 = (bf16[4,48,1536]{2,1,0:T(8,128)(2,1)S(1)}, bf16[4,48,1536]{2,1,0:T(8,128)(2,1)S(1)}, u32[]{:S(2)}, u32[]{:S(2)}) collective-permute-start(bf16[4,48,1536]{2,1,0:T(8,128)(2,1)S(1)} %get-tuple-element.261), channel_id=1, source_target_pairs={{0,6},{2,4},{4,2},{6,0},{8,14},{10,12},{12,10},{14,8},{16,22},{18,... | collective-permute-start | bytes 1769480 | tf_op jit(solution)/shard_map/ppermute | solution.py:72
  179.3 8.2 %collective-permute-start.25 = (bf16[2,48,1536]{2,1,0:T(8,128)(2,1)S(1)}, bf16[2,48,1536]{2,1,0:T(8,128)(2,1)S(1)}, u32[]{:S(2)}, u32[]{:S(2)}) collective-permute-start(bf16[2,48,1536]{2,1,0:T(8,128)(2,1)S(1)} %fusion.52), channel_id=1, source_target_pairs={{0,8},{2,10},{4,12},{6,14},{8,0},{10,2},{12,4},{14,6},{16,24},{18,... | collective-permute-start | bytes 884744 | tf_op jit(solution)/shard_map/ppermute | solution.py:72
  188.2 9.0 %collective-permute-start.26 = (bf16[768,1536]{1,0:T(8,128)(2,1)}, bf16[768,1536]{1,0:T(8,128)(2,1)}, u32[]{:S(2)}, u32[]{:S(2)}) collective-permute-start(bf16[768,1536]{1,0:T(8,128)(2,1)} %convolution_convert_fusion), channel_id=1, source_target_pairs={{0,1},{1,0},{2,3},{3,2},{4,5},{5,4},{6,7},{7,6},{8,9},{9,8},{10,11... | collective-permute-start | bytes 7077896 | tf_op jit(solution)/shard_map/ppermute | solution.py:76
  190.7 6.5 %collective-permute-start.27 = (bf16[768,384]{1,0:T(8,128)(2,1)S(1)}, bf16[768,384]{1,0:T(8,128)(2,1)S(1)}, u32[]{:S(2)}, u32[]{:S(2)}) collective-permute-start(bf16[768,384]{1,0:T(8,128)(2,1)S(1)} %convolution_convert_fusion.3), channel_id=1, source_target_pairs={{0,1},{1,0},{2,3},{3,2},{4,5},{5,4},{6,7},{7,6},{8,9},{9,8},{10,11... | collective-permute-start | bytes 1769480 | tf_op jit(solution)/shard_map/ppermute | solution.py:76
  203.7 31.7 %collective-permute-start.29 = (bf16[4,48,1920]{2,1,0:T(8,128)(2,1)}, bf16[4,48,1920]{2,1,0:T(8,128)(2,1)S(1)}, u32[]{:S(2)}, u32[]{:S(2)}) collective-permute-start(bf16[4,48,1920]{2,1,0:T(8,128)(2,1)} %pad_maximum_fusion.1), channel_id=1, source_target_pairs={{0,2},{2,0},{4,6},{6,4},{8,10},{10,8},{12,14},{14,12},{16,18},{18,... | collective-permute-start | bytes 2211848 | tf_op jit(solution)/shard_map/ppermute | solution.py:72
  205.2 34.7 %collective-permute-start.30 = (bf16[4,48,1920]{2,1,0:T(8,128)(2,1)}, bf16[4,48,1920]{2,1,0:T(8,128)(2,1)}, u32[]{:S(2)}, u32[]{:S(2)}) collective-permute-start(bf16[4,48,1920]{2,1,0:T(8,128)(2,1)} %pad_maximum_fusion.2), channel_id=1, source_target_pairs={{0,4},{2,6},{4,0},{6,2},{8,12},{10,14},{12,8},{14,10},{16,20},{18,... | collective-permute-start | bytes 2211848 | tf_op jit(solution)/shard_map/ppermute | solution.py:72
  205.7 34.2 %collective-permute-start.31 = (bf16[4,48,1920]{2,1,0:T(8,128)(2,1)}, bf16[4,48,1920]{2,1,0:T(8,128)(2,1)}, u32[]{:S(2)}, u32[]{:S(2)}) collective-permute-start(bf16[4,48,1920]{2,1,0:T(8,128)(2,1)} %pad_maximum_fusion.3), channel_id=1, source_target_pairs={{0,6},{2,4},{4,2},{6,0},{8,14},{10,12},{12,10},{14,8},{16,22},{18,... | collective-permute-start | bytes 2211848 | tf_op jit(solution)/shard_map/ppermute | solution.py:72
  207.2 24.3 %collective-permute-start.28 = (bf16[48,1536]{1,0:T(8,128)(2,1)S(1)}, bf16[48,1536]{1,0:T(8,128)(2,1)S(1)}, u32[]{:S(2)}, u32[]{:S(2)}) collective-permute-start(bf16[48,1536]{1,0:T(8,128)(2,1)S(1)} %fusion.66), channel_id=1, source_target_pairs={{0,16},{2,18},{4,20},{6,22},{8,24},{10,26},{12,28},{14,30},{16,0},... | collective-permute-start | bytes 442376 | tf_op jit(solution)/shard_map/ppermute | solution.py:72
  239.9 7.4 %collective-permute-start.32 = (bf16[768,1152]{1,0:T(8,128)(2,1)S(1)}, bf16[768,1152]{1,0:T(8,128)(2,1)S(1)}, u32[]{:S(2)}, u32[]{:S(2)}) collective-permute-start(bf16[768,1152]{1,0:T(8,128)(2,1)S(1)} %fusion.1), channel_id=1, source_target_pairs={{0,1},{1,0},{2,3},{3,2},{4,5},{5,4},{6,7},{7,6},{8,9},{9,8},{10,11... | collective-permute-start | bytes 5308424 | tf_op jit(solution)/shard_map/ppermute | solution.py:76
  243.6 14.2 %collective-permute-start.36 = (bf16[2,48,1920]{2,1,0:T(8,128)(2,1)S(1)}, bf16[2,48,1920]{2,1,0:T(8,128)(2,1)S(1)}, u32[]{:S(2)}, u32[]{:S(2)}) collective-permute-start(bf16[2,48,1920]{2,1,0:T(8,128)(2,1)S(1)} %pad_maximum_fusion.4), channel_id=1, source_target_pairs={{0,8},{2,10},{4,12},{6,14},{8,0},{10,2},{12,4},{14,6},{16,24},{18,... | collective-permute-start | bytes 1105928 | tf_op jit(solution)/shard_map/ppermute | solution.py:72
  248.9 8.9 %collective-permute-start.37 = (bf16[48,1536]{1,0:T(8,128)(2,1)S(1)}, bf16[48,1536]{1,0:T(8,128)(2,1)S(1)}, u32[]{:S(2)}, u32[]{:S(2)}) collective-permute-start(bf16[48,1536]{1,0:T(8,128)(2,1)S(1)} %convert_element_type.381), channel_id=1, source_target_pairs={{0,16},{2,18},{4,20},{6,22},{8,24},{10,26},{12,28},{14,30},{16,0},... | collective-permute-start | bytes 442376 | tf_op jit(solution)/shard_map/ppermute | solution.py:72
  251.3 20.4 %collective-permute-start.33 = (bf16[4,48,1152]{2,1,0:T(8,128)(2,1)}, bf16[4,48,1152]{2,1,0:T(8,128)(2,1)}, u32[]{:S(2)}, u32[]{:S(2)}) collective-permute-start(bf16[4,48,1152]{2,1,0:T(8,128)(2,1)} %get-tuple-element.311), channel_id=1, source_target_pairs={{0,2},{2,0},{4,6},{6,4},{8,10},{10,8},{12,14},{14,12},{16,18},{18,... | collective-permute-start | bytes 1327112 | tf_op jit(solution)/shard_map/ppermute | solution.py:72
  251.9 21.6 %collective-permute-start.34 = (bf16[4,48,1152]{2,1,0:T(8,128)(2,1)}, bf16[4,48,1152]{2,1,0:T(8,128)(2,1)}, u32[]{:S(2)}, u32[]{:S(2)}) collective-permute-start(bf16[4,48,1152]{2,1,0:T(8,128)(2,1)} %get-tuple-element.312), channel_id=1, source_target_pairs={{0,4},{2,6},{4,0},{6,2},{8,12},{10,14},{12,8},{14,10},{16,20},{18,... | collective-permute-start | bytes 1327112 | tf_op jit(solution)/shard_map/ppermute | solution.py:72
  253.1 20.4 %collective-permute-start.35 = (bf16[4,48,1152]{2,1,0:T(8,128)(2,1)}, bf16[4,48,1152]{2,1,0:T(8,128)(2,1)}, u32[]{:S(2)}, u32[]{:S(2)}) collective-permute-start(bf16[4,48,1152]{2,1,0:T(8,128)(2,1)} %get-tuple-element.313), channel_id=1, source_target_pairs={{0,6},{2,4},{4,2},{6,0},{8,14},{10,12},{12,10},{14,8},{16,22},{18,... | collective-permute-start | bytes 1327112 | tf_op jit(solution)/shard_map/ppermute | solution.py:72
  260.1 11.5 %collective-permute-start.38 = (bf16[48,1920]{1,0:T(8,128)(2,1)}, bf16[48,1920]{1,0:T(8,128)(2,1)}, u32[]{:S(2)}, u32[]{:S(2)}) collective-permute-start(bf16[48,1920]{1,0:T(8,128)(2,1)} %pad_maximum_fusion.6), channel_id=1, source_target_pairs={{0,16},{2,18},{4,20},{6,22},{8,24},{10,26},{12,28},{14,30},{16,0},... | collective-permute-start | bytes 552968 | tf_op jit(solution)/shard_map/ppermute | solution.py:72
  275.0 10.1 %collective-permute-start.39 = (bf16[48,1152]{1,0:T(8,128)(2,1)S(1)}, bf16[48,1152]{1,0:T(8,128)(2,1)S(1)}, u32[]{:S(2)}, u32[]{:S(2)}) collective-permute-start(bf16[48,1152]{1,0:T(8,128)(2,1)S(1)} %get-tuple-element.323), channel_id=1, source_target_pairs={{0,8},{2,10},{4,12},{6,14},{8,0},{10,2},{12,4},{14,6},{16,24},{18,... | collective-permute-start | bytes 331784 | tf_op jit(solution)/shard_map/ppermute | solution.py:72
  276.8 9.9 %collective-permute-start.40 = (bf16[48,1152]{1,0:T(8,128)(2,1)S(1)}, bf16[48,1152]{1,0:T(8,128)(2,1)S(1)}, u32[]{:S(2)}, u32[]{:S(2)}) collective-permute-start(bf16[48,1152]{1,0:T(8,128)(2,1)S(1)} %get-tuple-element.324), channel_id=1, source_target_pairs={{0,16},{2,18},{4,20},{6,22},{8,24},{10,26},{12,28},{14,30},{16,0},... | collective-permute-start | bytes 331784 | tf_op jit(solution)/shard_map/ppermute | solution.py:72
  277.2 9.6 %collective-permute-start.41 = (bf16[48,1152]{1,0:T(8,128)(2,1)S(1)}, bf16[48,1152]{1,0:T(8,128)(2,1)S(1)}, u32[]{:S(2)}, u32[]{:S(2)}) collective-permute-start(bf16[48,1152]{1,0:T(8,128)(2,1)S(1)} %get-tuple-element.325), channel_id=1, source_target_pairs={{0,24},{2,26},{4,28},{6,30},{8,16},{10,18},{12,20},{14,22},{16,8},... | collective-permute-start | bytes 331784 | tf_op jit(solution)/shard_map/ppermute | solution.py:72
  282.8 13.1 %collective-permute-start.43 = (bf16[2,48,1536]{2,1,0:T(8,128)(2,1)S(1)}, bf16[2,48,1536]{2,1,0:T(8,128)(2,1)S(1)}, u32[]{:S(2)}, u32[]{:S(2)}) collective-permute-start(bf16[2,48,1536]{2,1,0:T(8,128)(2,1)S(1)} %maximum_select_fusion.24), channel_id=1, source_target_pairs={{0,8},{2,10},{4,12},{6,14},{8,0},{10,2},{12,4},{14,6},{16,24},{18,... | collective-permute-start | bytes 884744 | tf_op jit(solution)/shard_map/ppermute | solution.py:72
  283.8 12.2 %collective-permute-start.42 = (bf16[48,1920]{1,0:T(8,128)(2,1)S(1)}, bf16[48,1920]{1,0:T(8,128)(2,1)S(1)}, u32[]{:S(2)}, u32[]{:S(2)}) collective-permute-start(bf16[48,1920]{1,0:T(8,128)(2,1)S(1)} %get-tuple-element.419), channel_id=1, source_target_pairs={{0,16},{2,18},{4,20},{6,22},{8,24},{10,26},{12,28},{14,30},{16,0},... | collective-permute-start | bytes 552968 | tf_op jit(solution)/shard_map/ppermute | solution.py:72
  296.1 6.9 %collective-permute-start.44 = (bf16[48,1152]{1,0:T(8,128)(2,1)S(1)}, bf16[48,1152]{1,0:T(8,128)(2,1)S(1)}, u32[]{:S(2)}, u32[]{:S(2)}) collective-permute-start(bf16[48,1152]{1,0:T(8,128)(2,1)S(1)} %get-tuple-element.346), channel_id=1, source_target_pairs={{0,8},{2,10},{4,12},{6,14},{8,0},{10,2},{12,4},{14,6},{16,24},{18,... | collective-permute-start | bytes 331784 | tf_op jit(solution)/shard_map/ppermute | solution.py:72
  296.2 11.0 %collective-permute-start.45 = (bf16[48,1152]{1,0:T(8,128)(2,1)S(1)}, bf16[48,1152]{1,0:T(8,128)(2,1)S(1)}, u32[]{:S(2)}, u32[]{:S(2)}) collective-permute-start(bf16[48,1152]{1,0:T(8,128)(2,1)S(1)} %get-tuple-element.346), channel_id=1, source_target_pairs={{0,16},{2,18},{4,20},{6,22},{8,24},{10,26},{12,28},{14,30},{16,0},... | collective-permute-start | bytes 331784 | tf_op jit(solution)/shard_map/ppermute | solution.py:72
  298.0 9.2 %collective-permute-start.46 = (bf16[48,1152]{1,0:T(8,128)(2,1)S(1)}, bf16[48,1152]{1,0:T(8,128)(2,1)S(1)}, u32[]{:S(2)}, u32[]{:S(2)}) collective-permute-start(bf16[48,1152]{1,0:T(8,128)(2,1)S(1)} %get-tuple-element.346), channel_id=1, source_target_pairs={{0,24},{2,26},{4,28},{6,30},{8,16},{10,18},{12,20},{14,22},{16,8},... | collective-permute-start | bytes 331784 | tf_op jit(solution)/shard_map/ppermute | solution.py:72
  300.6 12.3 %collective-permute-start.47 = (bf16[2,48,1920]{2,1,0:T(8,128)(2,1)S(1)}, bf16[2,48,1920]{2,1,0:T(8,128)(2,1)S(1)}, u32[]{:S(2)}, u32[]{:S(2)}) collective-permute-start(bf16[2,48,1920]{2,1,0:T(8,128)(2,1)S(1)} %maximum_select_fusion.21), channel_id=1, source_target_pairs={{0,8},{2,10},{4,12},{6,14},{8,0},{10,2},{12,4},{14,6},{16,24},{18,... | collective-permute-start | bytes 1105928 | tf_op jit(solution)/shard_map/ppermute | solution.py:72
  300.6 1.2 collective-permute-start.48
  301.8 12.2 %collective-permute-start.49 = (f32[16,768]{1,0:T(8,128)S(1)}, f32[16,768]{1,0:T(8,128)S(1)}, u32[]{:S(2)}, u32[]{:S(2)}) collective-permute-start(f32[16,768]{1,0:T(8,128)S(1)} %add.375), channel_id=1, source_target_pairs={{0,2},{2,0},{4,6},{6,4},{8,10},{10,8},{12,14},{14,12},{16,18},{18,... | collective-permute-start | bytes 147464 | tf_op jit(solution)/shard_map/ppermute | solution.py:72
  314.1 27.8 %collective-permute-start.50 = (bf16[4,48,1536]{2,1,0:T(8,128)(2,1)S(1)}, bf16[4,48,1536]{2,1,0:T(8,128)(2,1)S(1)}, u32[]{:S(2)}, u32[]{:S(2)}) collective-permute-start(bf16[4,48,1536]{2,1,0:T(8,128)(2,1)S(1)} %bitcast.398), channel_id=1, source_target_pairs={{0,2},{2,0},{4,6},{6,4},{8,10},{10,8},{12,14},{14,12},{16,18},{18,... | collective-permute-start | bytes 1769480 | tf_op jit(solution)/shard_map/ppermute | solution.py:72
  314.8 27.1 %collective-permute-start.51 = (bf16[4,48,1536]{2,1,0:T(8,128)(2,1)S(1)}, bf16[4,48,1536]{2,1,0:T(8,128)(2,1)S(1)}, u32[]{:S(2)}, u32[]{:S(2)}) collective-permute-start(bf16[4,48,1536]{2,1,0:T(8,128)(2,1)S(1)} %bitcast.397), channel_id=1, source_target_pairs={{0,4},{2,6},{4,0},{6,2},{8,12},{10,14},{12,8},{14,10},{16,20},{18,... | collective-permute-start | bytes 1769480 | tf_op jit(solution)/shard_map/ppermute | solution.py:72
  315.9 26.0 %collective-permute-start.52 = (bf16[4,48,1536]{2,1,0:T(8,128)(2,1)S(1)}, bf16[4,48,1536]{2,1,0:T(8,128)(2,1)S(1)}, u32[]{:S(2)}, u32[]{:S(2)}) collective-permute-start(bf16[4,48,1536]{2,1,0:T(8,128)(2,1)S(1)} %bitcast.396), channel_id=1, source_target_pairs={{0,6},{2,4},{4,2},{6,0},{8,14},{10,12},{12,10},{14,8},{16,22},{18,... | collective-permute-start | bytes 1769480 | tf_op jit(solution)/shard_map/ppermute | solution.py:72
  319.9 22.0 %collective-permute-start.53 = (f32[16,768]{1,0:T(8,128)S(1)}, f32[16,768]{1,0:T(8,128)S(1)}, u32[]{:S(2)}, u32[]{:S(2)}) collective-permute-start(f32[16,768]{1,0:T(8,128)S(1)} %add.378), channel_id=1, source_target_pairs={{0,4},{2,6},{4,0},{6,2},{8,12},{10,14},{12,8},{14,10},{16,20},{18,... | collective-permute-start | bytes 147464 | tf_op jit(solution)/shard_map/ppermute | solution.py:72
  346.3 4.9 %collective-permute-start.54 = (f32[768,768]{1,0:T(8,128)}, f32[768,768]{1,0:T(8,128)}, u32[]{:S(2)}, u32[]{:S(2)}) collective-permute-start(f32[768,768]{1,0:T(8,128)} %fusion.87.own_ref), channel_id=1, source_target_pairs={{0,1},{1,0},{2,3},{3,2},{4,5},{5,4},{6,7},{7,6},{8,9},{9,8},{10,11... | collective-permute-start | bytes 7077896 | tf_op jit(solution)/shard_map/ppermute | solution.py:76
  346.3 4.2 %collective-permute-start.55 = (f32[16,768]{1,0:T(8,128)S(1)}, f32[16,768]{1,0:T(8,128)S(1)}, u32[]{:S(2)}, u32[]{:S(2)}) collective-permute-start(f32[16,768]{1,0:T(8,128)S(1)} %add.379), channel_id=1, source_target_pairs={{0,8},{2,10},{4,12},{6,14},{8,0},{10,2},{12,4},{14,6},{16,24},{18,... | collective-permute-start | bytes 147464 | tf_op jit(solution)/shard_map/ppermute | solution.py:72
  351.2 38.8 %copy-start.53 = (f32[6,48]{1,0:T(8,128)S(1)}, f32[6,48]{1,0:T(8,128)}, u32[]{:S(2)}) copy-start(f32[6,48]{1,0:T(8,128)} %param.23) | copy-start | bytes 3460
  351.2 38.8 %copy-start.54 = (f32[6,48]{1,0:T(8,128)S(1)}, f32[6,48]{1,0:T(8,128)}, u32[]{:S(2)}) copy-start(f32[6,48]{1,0:T(8,128)} %param.29) | copy-start | bytes 3460
  351.2 38.8 %copy-start.55 = (f32[6,48]{1,0:T(8,128)S(1)}, f32[6,48]{1,0:T(8,128)}, u32[]{:S(2)}) copy-start(f32[6,48]{1,0:T(8,128)} %param.28) | copy-start | bytes 3460
  384.1 5.9 %collective-permute-start.56 = (f32[16,768]{1,0:T(8,128)S(1)}, f32[16,768]{1,0:T(8,128)S(1)}, u32[]{:S(2)}, u32[]{:S(2)}) collective-permute-start(f32[16,768]{1,0:T(8,128)S(1)} %add.380), channel_id=1, source_target_pairs={{0,16},{2,18},{4,20},{6,22},{8,24},{10,26},{12,28},{14,30},{16,0},... | collective-permute-start | bytes 147464 | tf_op jit(solution)/shard_map/ppermute | solution.py:72
  385.4 6.2 %collective-permute-start.59 = (bf16[48,1536]{1,0:T(8,128)(2,1)S(1)}, bf16[48,1536]{1,0:T(8,128)(2,1)S(1)}, u32[]{:S(2)}, u32[]{:S(2)}) collective-permute-start(bf16[48,1536]{1,0:T(8,128)(2,1)S(1)} %get-tuple-element.416), channel_id=1, source_target_pairs={{0,2},{2,0},{4,6},{6,4},{8,10},{10,8},{12,14},{14,12},{16,18},{18,... | collective-permute-start | bytes 442376 | tf_op jit(solution)/shard_map/ppermute | solution.py:72
  387.2 8.5 %collective-permute-start.58 = (bf16[48,1536]{1,0:T(8,128)(2,1)S(1)}, bf16[48,1536]{1,0:T(8,128)(2,1)S(1)}, u32[]{:S(2)}, u32[]{:S(2)}) collective-permute-start(bf16[48,1536]{1,0:T(8,128)(2,1)S(1)} %get-tuple-element.417), channel_id=1, source_target_pairs={{0,4},{2,6},{4,0},{6,2},{8,12},{10,14},{12,8},{14,10},{16,20},{18,... | collective-permute-start | bytes 442376 | tf_op jit(solution)/shard_map/ppermute | solution.py:72
  387.6 8.1 %collective-permute-start.57 = (bf16[48,1536]{1,0:T(8,128)(2,1)S(1)}, bf16[48,1536]{1,0:T(8,128)(2,1)S(1)}, u32[]{:S(2)}, u32[]{:S(2)}) collective-permute-start(bf16[48,1536]{1,0:T(8,128)(2,1)S(1)} %get-tuple-element.414), channel_id=1, source_target_pairs={{0,6},{2,4},{4,2},{6,0},{8,14},{10,12},{12,10},{14,8},{16,22},{18,... | collective-permute-start | bytes 442376 | tf_op jit(solution)/shard_map/ppermute | solution.py:72
  (62 other events, 377.3 us)
